TPU v7x, 32 devices: a whole 2x2x4 slice. The times are simulated.
32 devices in a mesh: dp: 8 (over z, y), tensor: 4 (over x, core).
Axes of the slice: x: 2, y: 2, z: 4, core: 2. Of those that a mesh axis runs over, the one named last changes fastest.
Arguments:
- tokens: bfloat16 [12608, 768], P('dp'), may hold values from -6 to 6
- ln1_gain: float32 [768], P('dp'), may hold values from 0.5 to 1.5
- ln1_bias: float32 [768], P('dp'), may hold values from -1 to 1
- w_qkv: float32 [768, 3, 768], P('dp', None, 'tensor'), may hold values from -0.21875 to 0.21875
- w_attn_out: float32 [768, 768], P('tensor', 'dp'), may hold values from -0.625 to 0.625
- ln2_gain: float32 [768], P('dp'), may hold values from 0.5 to 1.5
- ln2_bias: float32 [768], P('dp'), may hold values from -1 to 1
- router_weight: float32 [768, 8], P('dp'), may hold values from -0.15625 to 0.15625
- w_in: float32 [8, 768, 3072], P(None, 'dp', 'tensor'), may hold values from -0.21875 to 0.21875
- w_expert_out: float32 [8, 3072, 768], P(None, 'tensor', 'dp'), may hold values from -0.875 to 0.875
- router_noise: float32 [12608, 8], P('dp'), may hold values from -1.5 to 1.5
- routes: int32 [12608, 2], P('dp'), may hold values from 0 to 7, all different within a row; in each aligned block of 1576 rows (0 to 1575, 1576 to 3151, ...) at most 788 rows name the same one
- cotangent: bfloat16 [12608, 768], P('dp'), may hold values from -6 to 6
Outputs:
- output: bfloat16 [12608, 768], P('dp')
- d_tokens: bfloat16 [12608, 768], P('dp')
- g_ln1_gain: float32 [768], P('dp')
- g_ln1_bias: float32 [768], P('dp')
- g_w_qkv: float32 [768, 3, 768], P('dp', None, 'tensor')
- g_w_attn_out: float32 [768, 768], P('tensor', 'dp')
- g_ln2_gain: float32 [768], P('dp')
- g_ln2_bias: float32 [768], P('dp')
- g_router: float32 [768, 8], P('dp')
- g_w_in: float32 [8, 768, 3072], P(None, 'dp', 'tensor')
- g_w_expert_out: float32 [8, 3072, 768], P(None, 'tensor', 'dp')
Inputs may be any that keep to these rules, and one draw needn't show every extreme that they name: `routes`: each row names 2 different experts; in the rows of one index of dp no expert is named more than 788 times, a bound that some block reaches.
All inputs are finite; a program needn't handle non-finite values.
Results may differ from a plain program's by a relative error of at most 0.023.
Values may be sent and summed in bfloat16 or wider, within the bound.
A program may use at most 320 MiB of HBM per device.

v0:
```python
import jax
import jax.numpy as jnp
from jax import lax
from jax.sharding import PartitionSpec as P

D = 768
HD = 64
E = 8
TOP = 2
SEQ = 197
CAP = 689


EPS = 1e-06


def layer_norm(values, norm_gain, norm_bias):
    centred = values - jnp.mean(values, axis=-1, keepdims=True)
    variance = jnp.mean(centred * centred, axis=-1, keepdims=True)
    return centred * lax.rsqrt(variance + EPS) * norm_gain + norm_bias


def gelu_tanh(values):
    return jax.nn.gelu(values, approximate=True)


def slot_table(routes):
    chosen = jnp.transpose(routes).reshape(-1)
    onehot = (chosen[:, None] == jnp.arange(E, dtype=jnp.int32)[None, :]).astype(jnp.int32)
    earlier = jnp.cumsum(onehot, axis=0) - onehot
    position = jnp.sum(earlier * onehot, axis=1)
    flat_slot = jnp.where(position < CAP, chosen * CAP + position, E * CAP)
    return jnp.transpose(flat_slot.reshape(TOP, routes.shape[0]))


def softmax_rows(scores):
    row_max = jnp.max(scores, axis=-1, keepdims=True)
    shifted = jnp.exp(scores - row_max)
    totals = jnp.sum(shifted, axis=-1, keepdims=True)
    return (shifted / totals, row_max + jnp.log(totals))


def body(
    tokens,
    ln1_gain,
    ln1_bias,
    w_qkv,
    w_attn_out,
    ln2_gain,
    ln2_bias,
    router_weight,
    w_in,
    w_expert_out,
    router_noise,
    routes,
    cotangent,
):
    token_count = tokens.shape[0]
    image_count = token_count // SEQ
    local_heads = w_qkv.shape[2] // HD
    score_scale = HD ** (-0.5)
    qkv_low, attn_out_low, gain_one_low, bias_one_low = (
        lax.all_gather(w_qkv.astype(jnp.bfloat16), "dp", axis=0, tiled=True),
        lax.all_gather(w_attn_out.astype(jnp.bfloat16), "dp", axis=1, tiled=True),
        lax.all_gather(ln1_gain.astype(jnp.bfloat16), "dp", axis=0, tiled=True),
        lax.all_gather(ln1_bias.astype(jnp.bfloat16), "dp", axis=0, tiled=True),
    )
    gain_one = gain_one_low.astype(jnp.float32)
    bias_one = bias_one_low.astype(jnp.float32)
    residual_in = tokens.astype(jnp.float32)
    normed_f, ln_one_back = jax.vjp(layer_norm, residual_in, gain_one, bias_one)
    normed_one = normed_f.astype(jnp.bfloat16)
    packed = jnp.dot(normed_one, qkv_low.reshape(D, -1), preferred_element_type=jnp.float32).astype(
        jnp.bfloat16
    )
    packed = packed.reshape(image_count, SEQ, 3, local_heads, HD)
    query = packed[:, :, 0]
    key_heads = packed[:, :, 1]
    value_heads = packed[:, :, 2]
    scores = (
        jnp.einsum("bqhd,bkhd->bhqk", query, key_heads, preferred_element_type=jnp.float32)
        * score_scale
    )
    att_weights, log_total = softmax_rows(scores)
    mixed = jnp.einsum(
        "bhqk,bkhd->bqhd",
        att_weights.astype(jnp.bfloat16),
        value_heads,
        preferred_element_type=jnp.float32,
    )
    mixed = mixed.astype(jnp.bfloat16).reshape(token_count, local_heads * HD)
    attn_part = jnp.dot(mixed, attn_out_low, preferred_element_type=jnp.float32)
    router_low, expert_in_low, expert_out_low, gain_two_low, bias_two_low = (
        lax.all_gather(router_weight.astype(jnp.bfloat16), "dp", axis=0, tiled=True),
        lax.all_gather(w_in.astype(jnp.bfloat16), "dp", axis=1, tiled=True),
        lax.all_gather(w_expert_out.astype(jnp.bfloat16), "dp", axis=2, tiled=True),
        lax.all_gather(ln2_gain.astype(jnp.bfloat16), "dp", axis=0, tiled=True),
        lax.all_gather(ln2_bias.astype(jnp.bfloat16), "dp", axis=0, tiled=True),
    )
    gain_two = gain_two_low.astype(jnp.float32)
    bias_two = bias_two_low.astype(jnp.float32)
    attended = lax.psum(attn_part.astype(jnp.bfloat16), "tensor").astype(jnp.float32)
    residual_mid = residual_in + attended
    normed_two_f, ln_two_back = jax.vjp(layer_norm, residual_mid, gain_two, bias_two)
    normed_two = normed_two_f.astype(jnp.bfloat16)
    logits = jnp.dot(normed_two, router_low, preferred_element_type=jnp.float32) + router_noise
    router_probs, unused_total = softmax_rows(logits)
    route_onehot = (routes[:, :, None] == jnp.arange(E, dtype=jnp.int32)[None, None, :]).astype(
        jnp.float32
    )
    gates = jnp.sum(router_probs[:, None, :] * route_onehot, axis=-1)
    slot_index = slot_table(routes)
    owners = jnp.broadcast_to(
        jnp.arange(token_count, dtype=jnp.int32)[:, None], slot_index.shape
    ).reshape(-1)
    slot_token = (
        jnp.full((E * CAP + 1,), token_count, jnp.int32)
        .at[slot_index.reshape(-1)]
        .set(owners)[: E * CAP]
    )
    padded_two = jnp.concatenate([normed_two, jnp.zeros((1, D), jnp.bfloat16)], axis=0)
    expert_rows = padded_two[slot_token].reshape(E, CAP, D)
    pre_act = jnp.einsum(
        "ecd,edf->ecf", expert_rows, expert_in_low, preferred_element_type=jnp.float32
    )
    hidden_f, gelu_back = jax.vjp(gelu_tanh, pre_act)
    hidden = hidden_f.astype(jnp.bfloat16)
    expert_part = jnp.einsum(
        "ecf,efd->ecd", hidden, expert_out_low, preferred_element_type=jnp.float32
    )
    part_padded = jnp.concatenate(
        [expert_part.reshape(E * CAP, D), jnp.zeros((1, D), jnp.float32)], axis=0
    )
    picked = part_padded[slot_index]
    moe_part = jnp.sum(gates[:, :, None] * picked, axis=1)
    mixture = lax.psum(moe_part.astype(jnp.bfloat16), "tensor").astype(jnp.float32)
    output = (residual_mid + mixture).astype(jnp.bfloat16)
    router_low, expert_in_low, expert_out_low = (
        lax.all_gather(router_weight.astype(jnp.bfloat16), "dp", axis=0, tiled=True),
        lax.all_gather(w_in.astype(jnp.bfloat16), "dp", axis=1, tiled=True),
        lax.all_gather(w_expert_out.astype(jnp.bfloat16), "dp", axis=2, tiled=True),
    )
    grad_out = cotangent.astype(jnp.float32)
    grad_padded = jnp.concatenate([grad_out, jnp.zeros((1, D), jnp.float32)], axis=0)
    gate_slot = (
        jnp.zeros((E * CAP + 1,), jnp.float32)
        .at[slot_index.reshape(-1)]
        .set(gates.reshape(-1))[: E * CAP]
    )
    grad_slots = (
        (grad_padded[slot_token] * gate_slot[:, None]).astype(jnp.bfloat16).reshape(E, CAP, D)
    )
    grad_hidden = jnp.einsum(
        "ecd,efd->ecf", grad_slots, expert_out_low, preferred_element_type=jnp.float32
    )
    grad_pre = gelu_back(grad_hidden)[0].astype(jnp.bfloat16)
    g_w_expert_out = jnp.einsum(
        "ecf,ecd->efd", hidden, grad_slots, preferred_element_type=jnp.float32
    )
    g_w_in = jnp.einsum("ecd,ecf->edf", expert_rows, grad_pre, preferred_element_type=jnp.float32)
    grad_rows = jnp.einsum(
        "ecf,edf->ecd", grad_pre, expert_in_low, preferred_element_type=jnp.float32
    )
    grad_rows = jnp.concatenate(
        [grad_rows.reshape(E * CAP, D), jnp.zeros((1, D), jnp.float32)], axis=0
    )
    grad_two_part = jnp.sum(grad_rows[slot_index], axis=1)
    grad_gate_part = jnp.sum(grad_out[:, None, :] * picked, axis=-1)
    grad_two_expert, grad_gate = (
        lax.psum(grad_two_part.astype(jnp.bfloat16), "tensor").astype(jnp.float32),
        lax.psum(grad_gate_part.astype(jnp.bfloat16), "tensor").astype(jnp.float32),
    )
    grad_probs = jnp.sum(route_onehot * grad_gate[:, :, None], axis=1)
    grad_logits = router_probs * (
        grad_probs - jnp.sum(router_probs * grad_probs, axis=-1, keepdims=True)
    )
    grad_logits = grad_logits.astype(jnp.bfloat16)
    g_router = jnp.dot(jnp.transpose(normed_two), grad_logits, preferred_element_type=jnp.float32)
    grad_two = grad_two_expert + jnp.dot(
        grad_logits, jnp.transpose(router_low), preferred_element_type=jnp.float32
    )
    grad_mid_norm, g_ln2_gain, g_ln2_bias = ln_two_back(grad_two)
    grad_mid = grad_out + grad_mid_norm
    grad_attn = grad_mid.astype(jnp.bfloat16)
    qkv_low, attn_out_low = (
        lax.all_gather(w_qkv.astype(jnp.bfloat16), "dp", axis=0, tiled=True),
        lax.all_gather(w_attn_out.astype(jnp.bfloat16), "dp", axis=1, tiled=True),
    )
    g_w_attn_out = jnp.dot(jnp.transpose(mixed), grad_attn, preferred_element_type=jnp.float32)
    grad_mixed = jnp.dot(grad_attn, jnp.transpose(attn_out_low), preferred_element_type=jnp.float32)
    grad_mixed = grad_mixed.astype(jnp.bfloat16).reshape(image_count, SEQ, local_heads, HD)
    scores_again = (
        jnp.einsum("bqhd,bkhd->bhqk", query, key_heads, preferred_element_type=jnp.float32)
        * score_scale
    )
    probs_again = jnp.exp(scores_again - log_total)
    grad_values = jnp.einsum(
        "bhqk,bqhd->bkhd",
        probs_again.astype(jnp.bfloat16),
        grad_mixed,
        preferred_element_type=jnp.float32,
    )
    grad_att = jnp.einsum(
        "bqhd,bkhd->bhqk", grad_mixed, value_heads, preferred_element_type=jnp.float32
    )
    row_dots = jnp.sum(probs_again * grad_att, axis=-1, keepdims=True)
    grad_scores = (probs_again * (grad_att - row_dots)).astype(jnp.bfloat16)
    grad_query = (
        jnp.einsum("bhqk,bkhd->bqhd", grad_scores, key_heads, preferred_element_type=jnp.float32)
        * score_scale
    )
    grad_keys = (
        jnp.einsum("bhqk,bqhd->bkhd", grad_scores, query, preferred_element_type=jnp.float32)
        * score_scale
    )
    grad_packed = jnp.stack([grad_query, grad_keys, grad_values], axis=2).astype(jnp.bfloat16)
    grad_packed = grad_packed.reshape(token_count, 3 * local_heads * HD)
    g_w_qkv = jnp.dot(
        jnp.transpose(normed_one), grad_packed, preferred_element_type=jnp.float32
    ).reshape(D, 3, local_heads * HD)
    grad_one = jnp.dot(
        grad_packed, jnp.transpose(qkv_low.reshape(D, -1)), preferred_element_type=jnp.float32
    )
    grad_in_part, gain_one_part, bias_one_part = ln_one_back(grad_one)
    grad_in, g_ln1_gain, g_ln1_bias = (
        lax.psum(grad_in_part.astype(jnp.bfloat16), "tensor").astype(jnp.float32),
        lax.psum(gain_one_part.astype(jnp.bfloat16), "tensor").astype(jnp.float32),
        lax.psum(bias_one_part.astype(jnp.bfloat16), "tensor").astype(jnp.float32),
    )
    d_tokens = (grad_mid + grad_in).astype(jnp.bfloat16)
    (
        out_router,
        out_w_in,
        out_expert_out,
        out_ln2_gain,
        out_ln2_bias,
        out_qkv,
        out_attn_out,
        out_ln1_gain,
        out_ln1_bias,
    ) = (
        lax.psum_scatter(g_router, "dp", scatter_dimension=0, tiled=True),
        lax.psum_scatter(g_w_in, "dp", scatter_dimension=1, tiled=True),
        lax.psum_scatter(g_w_expert_out, "dp", scatter_dimension=2, tiled=True),
        lax.psum_scatter(g_ln2_gain, "dp", scatter_dimension=0, tiled=True),
        lax.psum_scatter(g_ln2_bias, "dp", scatter_dimension=0, tiled=True),
        lax.psum_scatter(g_w_qkv, "dp", scatter_dimension=0, tiled=True),
        lax.psum_scatter(g_w_attn_out, "dp", scatter_dimension=1, tiled=True),
        lax.psum_scatter(g_ln1_gain, "dp", scatter_dimension=0, tiled=True),
        lax.psum_scatter(g_ln1_bias, "dp", scatter_dimension=0, tiled=True),
    )
    return (
        output,
        d_tokens,
        out_ln1_gain,
        out_ln1_bias,
        out_qkv,
        out_attn_out,
        out_ln2_gain,
        out_ln2_bias,
        out_router,
        out_w_in,
        out_expert_out,
    )


def solution(mesh):
    in_specs = (
        P("dp", None),
        P("dp"),
        P("dp"),
        P("dp", None, "tensor"),
        P("tensor", "dp"),
        P("dp"),
        P("dp"),
        P("dp", None),
        P(None, "dp", "tensor"),
        P(None, "tensor", "dp"),
        P("dp", None),
        P("dp", None),
        P("dp", None),
    )
    out_specs = (
        P("dp", None),
        P("dp", None),
        P("dp"),
        P("dp"),
        P("dp", None, "tensor"),
        P("tensor", "dp"),
        P("dp"),
        P("dp"),
        P("dp", None),
        P(None, "dp", "tensor"),
        P(None, "tensor", "dp"),
    )
    return jax.shard_map(body, mesh=mesh, in_specs=in_specs, out_specs=out_specs, check_vma=False)
```

profile of v0, /device:TPU:24, one launch (start us, length us, event | category | flops | bytes accessed | tf_op | source)
XLA Modules:
  0.0 1492.9 jit_solution(2298947369979918682)
XLA Ops:
  9.4 35.8 %all_gather.34 = bf16[768,3,192]{2,1,0:T(4,128)(2,1)} all-gather(bf16[96,3,192]{2,1,0:T(4,128)(2,1)S(1)} %copy.114), channel_id=1, replica_groups=mesh['dp'=8,'tensor'=4] {'dp'}, dimensions={0}, use_global_device_ids=true | all-gather | bytes 995328 | tf_op jit(solution)/shard_map/all_gather | solution.py:63
  50.1 17.8 %all-reduce.14 = (bf16[768]{0:T(1024)(128)(2,1)S(1)}, bf16[768]{0:T(1024)(128)(2,1)S(1)}, bf16[768]{0:T(1024)(128)(2,1)S(1)}, bf16[768]{0:T(1024)(128)(2,1)S(1)}) all-reduce(bf16[768]{0:T(1024)(128)(2,1)S(1)} %dynamic-update-slice.1, bf16[768]{0:T(1024)(128)(2,1)S(1)} %dynamic-update-slice, ...), channel_id=1, replica_groups=mesh['dp'=8,'tensor'=4] {'dp'}, use_global_device_ids=true, to_apply=%add.6 | all-reduce | flops 3072 | bytes 12288
  89.2 32.8 %all_gather.35 = bf16[192,768]{0,1:T(8,128)(2,1)S(1)} all-gather(bf16[192,96]{0,1:T(8,128)(2,1)S(1)} %copy.121), channel_id=1, replica_groups=mesh['dp'=8,'tensor'=4] {'dp'}, dimensions={1}, use_global_device_ids=true | all-gather | bytes 331776 | tf_op jit(solution)/shard_map/all_gather | solution.py:64
  142.3 24.7 %all-gather = bf16[8,96,8]{1,2,0:T(8,128)(2,1)S(1)} all-gather(bf16[1,96,8]{1,2,0:T(8,128)(2,1)S(1)} %convert_bitcast_fusion.1), channel_id=1, replica_groups=mesh['dp'=8,'tensor'=4] {'dp'}, dimensions={0}, use_global_device_ids=true | all-gather | bytes 13824 | tf_op jit(solution)/shard_map/all_gather | solution.py:94
  171.4 15.9 %scatter_custom_fusion = s32[5513]{0:T(1024)S(1)} fusion(s32[3152]{0:T(1024)S(1)} %fusion.47, s32[3152]{0:T(1024)S(1)} %reshape.249, s32[]{:T(128)} %constant.15.clone.1), kind=kCustom, calls=%fused_computation.110 | custom fusion | bytes 22056 | tf_op jit(solution)/shard_map/scatter | solution.py:119
  187.3 23.7 %gather_fusion.2 = f32[5512,768]{1,0:T(8,128)} fusion(f32[1577,768]{1,0:T(8,128)} %concatenate.14, s32[6144]{0:T(1024)S(1)} %pad_clamp_fusion), kind=kCustom, calls=%fused_computation.2 | custom fusion | bytes 33887776 | tf_op jit(solution)/shard_map/gather | solution.py:151
  211.0 13.9 gather.17
  232.4 17.3 %gather_fusion = bf16[5512,768]{1,0:T(8,128)(2,1)} fusion(bf16[1577,768]{1,0:T(8,128)(2,1)S(1)} %concatenate.12, s32[6144]{0:T(1024)S(1)} %pad_clamp_fusion), kind=kCustom, calls=%fused_computation | custom fusion | bytes 16954912 | tf_op jit(solution)/shard_map/gather | solution.py:122
  249.7 9.4 reshape.207
  261.2 16.1 %scatter_custom_fusion.1 = f32[5513]{0:T(1024)S(1)} fusion(s32[3152]{0:T(1024)S(1)} %fusion.47, f32[3152]{0:T(1024)S(1)} %reshape.257, f32[]{:T(128)} %constant.20.clone.1), kind=kCustom, calls=%fused_computation.108 | custom fusion | bytes 22056 | tf_op jit(solution)/shard_map/scatter | solution.py:148
  277.4 15.7 %fusion.65 = f32[8,689,768]{2,1,0:T(8,128)} fusion(bf16[8,689,768]{2,1,0:T(8,128)(2,1)} %reshape.207, bf16[8,768,768]{2,1,0:T(8,128)(2,1)} %all-gather.4.cloned.1.call-done), kind=kOutput, calls=%fused_computation.131 | convolution fusion | flops 6502219776 | bytes 34836480 | tf_op jit(solution)/shard_map/ecd,edf->ecf/dot_general | solution.py:123
  293.2 110.4 %all-gather.6.cloned.1.call-done = bf16[8,768,768]{1,2,0:T(8,128)(2,1)} async-done(((bf16[8,768,96]{1,2,0:T(8,128)(2,1)}), bf16[8,768,768]{1,2,0:T(8,128)(2,1)}) %all-gather.6.cloned.1.call-update) | async-done | bytes 9437200 | tf_op jit(solution)/shard_map/all_gather | solution.py:96
  403.6 15.9 %fusion.58 = f32[8,689,768]{2,1,0:T(8,128)} fusion(bf16[8,768,768]{1,2,0:T(8,128)(2,1)} %all-gather.6.cloned.1.call-done, f32[8,689,768]{2,1,0:T(8,128)} %fusion.65), kind=kOutput, calls=%fused_computation.125 | convolution fusion | flops 6540318720 | bytes 43302912 | tf_op jit(solution)/shard_map/ecf,efd->ecd/dot_general | solution.py:128
  419.5 14.4 reshape.208
  433.9 11.5 concatenate.13
  445.4 18.8 %gather_fusion.1 = f32[3152,768]{1,0:T(8,128)} fusion(f32[5513,768]{1,0:T(8,128)} %concatenate.13, s32[4096]{0:T(1024)S(1)} %pad_clamp_fusion.1), kind=kCustom, calls=%fused_computation.1 | custom fusion | bytes 19378496 | tf_op jit(solution)/shard_map/gather | solution.py:134
  464.2 12.1 reshape.222
  476.3 24.0 %fusion.6 = bf16[8,689,768]{2,1,0:T(8,128)(2,1)} fusion(f32[8,689,768]{2,1,0:T(8,128)} %fusion.65, bf16[8,768,768]{1,2,0:T(8,128)(2,1)} %all-gather.6.cloned.1.call-done, f32[8,689,768]{2,1,0:T(8,128)} %gather.17, f32[8,689]{1,0:T(8,128)S(1)} %mul.249), kind=kOutput, calls=%fused_computation.14 | convolution fusion | flops 6595350528 | bytes 51791392 | tf_op jit(solution)/shard_map/ecd,efd->ecf/dot_general | solution.py:153
  500.3 15.4 %fusion.66 = f32[8,689,768]{2,1,0:T(8,128)} fusion(bf16[8,689,768]{2,1,0:T(8,128)(2,1)} %fusion.6, bf16[8,768,768]{2,1,0:T(8,128)(2,1)} %all-gather.4.cloned.1.call-done), kind=kOutput, calls=%fused_computation.132 | convolution fusion | flops 6502219776 | bytes 34836480 | tf_op jit(solution)/shard_map/ecf,edf->ecd/dot_general | solution.py:161
  515.7 14.4 reshape.210
  530.1 11.5 concatenate.15
  541.5 18.8 %gather_fusion.3 = f32[3152,768]{1,0:T(8,128)} fusion(f32[5513,768]{1,0:T(8,128)} %concatenate.15, s32[4096]{0:T(1024)S(1)} %pad_clamp_fusion.1), kind=kCustom, calls=%fused_computation.3 | custom fusion | bytes 19378496 | tf_op jit(solution)/shard_map/gather | solution.py:167
  560.3 12.6 reshape.242
  572.9 44.4 %reduce_sum.242 = bf16[1576,768]{1,0:T(8,128)(2,1)} reduce(f32[1576,2,768]{2,1,0:T(2,128)} %reshape.242, f32[]{:T(128)} %constant.20.clone.1), dimensions={1}, to_apply=%region_17.18 | reduce | flops 1210368 | bytes 12103684 | tf_op jit(solution)/shard_map/reduce_sum | solution.py:167
  617.4 24.4 %multiply_reduce_fusion = (bf16[1576,2]{1,0:T(8,128)(2,1)S(1)}, bf16[1576,768]{1,0:T(8,128)(2,1)}) fusion(f32[1576,2,768]{2,1,0:T(2,128)} %reshape.222, f32[1576,768]{1,0:T(8,128)} %convert_element_type.187, f32[1576,2]{1,0:T(8,128)S(1)} %copy-done.12), kind=kLoop, calls=%fused_computation.17 | loop fusion | flops 8469424 | bytes 16964064 | tf_op jit(solution)/shard_map/reduce_sum | solution.py:168
  652.9 21.4 %all-reduce.23.cloned.1.call-done = bf16[1576,768]{1,0:T(8,128)(2,1)} async-done(((bf16[1576,768]{1,0:T(8,128)(2,1)}), bf16[1576,768]{1,0:T(8,128)(2,1)}) %all-reduce.23.cloned.1.call-update) | async-done | bytes 2420752 | tf_op jit(solution)/shard_map/psum | solution.py:170
  733.7 16.7 %fusion.68 = f32[8,768,768]{2,1,0:T(8,128)} fusion(bf16[8,689,768]{2,1,0:T(8,128)(2,1)} %reshape.207, bf16[8,689,768]{2,1,0:T(8,128)(2,1)} %fusion.6), kind=kOutput, calls=%fused_computation.134 | convolution fusion | flops 6502219776 | bytes 35807232 | tf_op jit(solution)/shard_map/ecd,ecf->edf/dot_general | solution.py:160
  750.5 24.2 %fusion.21 = f32[8,768,768]{1,2,0:T(8,128)} fusion(f32[8,689,768]{2,1,0:T(8,128)} %gather.17, f32[8,689]{1,0:T(8,128)S(1)} %mul.249, f32[8,689,768]{2,1,0:T(8,128)} %fusion.65), kind=kOutput, calls=%fused_computation.55 | convolution fusion | flops 6548785152 | bytes 52762144 | tf_op jit(solution)/shard_map/ecf,ecd->efd/dot_general | solution.py:157
  783.7 33.0 %all-reduce.13 = (f32[768]{0:T(1024)S(1)}, f32[768]{0:T(1024)S(1)}, f32[768]{0:T(1024)S(1)}, f32[768]{0:T(1024)S(1)}) all-reduce(bf16[768]{0:T(1024)(128)(2,1)S(1)} %get-tuple-element.27, bf16[768]{0:T(1024)(128)(2,1)S(1)} %get-tuple-element.28, f32[768]{0:T(1024)S(1)} %get-tuple-element.11, ...), channel_id=2, replica_groups=mesh['dp'=8,'tensor'=4] {'dp'}, use_global_device_ids=true, to_apply=%region_31.32.clone | all-reduce | flops 3072 | bytes 21504
  833.7 21.9 %reduce-scatter.10.cloned.1.call-done = f32[96,3,192]{2,0,1:T(8,128)} async-done(((f32[768,3,192]{2,0,1:T(8,128)}), f32[96,3,192]{2,0,1:T(8,128)}) %reduce-scatter.10.cloned.1.call-update) | async-done | bytes 221200 | tf_op jit(solution)/shard_map/reduce_scatter | solution.py:247
  855.6 314.9 %reduce-scatter.12.cloned.1.call-done = f32[8,96,768]{2,1,0:T(8,128)} async-done(((f32[8,768,768]{2,1,0:T(8,128)}), f32[8,96,768]{2,1,0:T(8,128)}) %reduce-scatter.12.cloned.1.call-update) | async-done | bytes 2359312 | tf_op jit(solution)/shard_map/reduce_scatter | solution.py:243
  1170.5 314.9 %reduce-scatter.14.cloned.1.call-done = f32[8,768,96]{1,2,0:T(8,128)} async-done(((f32[8,768,768]{1,2,0:T(8,128)}), f32[8,768,96]{1,2,0:T(8,128)}) %reduce-scatter.14.cloned.1.call-update) | async-done | bytes 2359312 | tf_op jit(solution)/shard_map/reduce_scatter | solution.py:244
  (275 shorter events, 156.3 us)
Async XLA Ops:
  8.0 39.9 %copy-start.58 = (u32[32]{0:T(128)S(1)}, u32[32]{0:T(128)}, u32[]{:S(2)}) copy-start(u32[32]{0:T(128)} %constant.73) | copy-start | bytes 388
  8.0 39.8 %copy-start.59 = (f32[96]{0:T(128)S(1)}, f32[96]{0:T(128)}, u32[]{:S(2)}) copy-start(f32[96]{0:T(128)} %param.15) | copy-start | bytes 1156
  8.0 39.8 %copy-start.60 = (f32[96]{0:T(128)S(1)}, f32[96]{0:T(128)}, u32[]{:S(2)}) copy-start(f32[96]{0:T(128)} %param.14) | copy-start | bytes 1156
  8.0 39.8 %copy-start.61 = (f32[96]{0:T(128)S(1)}, f32[96]{0:T(128)}, u32[]{:S(2)}) copy-start(f32[96]{0:T(128)} %param.19) | copy-start | bytes 1156
  8.1 39.8 %copy-start.62 = (f32[96]{0:T(128)S(1)}, f32[96]{0:T(128)}, u32[]{:S(2)}) copy-start(f32[96]{0:T(128)} %param.18) | copy-start | bytes 1156
  8.1 59.9 %copy-start = (bf16[1576,768]{1,0:T(8,128)(2,1)S(1)}, bf16[1576,768]{1,0:T(8,128)(2,1)}, u32[]{:S(2)}) copy-start(bf16[1576,768]{1,0:T(8,128)(2,1)} %param.13) | copy-start | bytes 7262212
  8.1 217.5 %all-reduce.21.cloned.1.call-start = ((), (), s32[]{:S(2)}) async-start(), calls=%async_computation.5 | async-start | bytes 4841472 | tf_op jit(solution)/shard_map/psum | solution.py:102
  126.1 151.3 %all-gather.4.cloned.1.call-start = ((), (), s32[]{:S(2)}) async-start(), calls=%async_computation.6 | async-start | bytes 10616832 | tf_op jit(solution)/shard_map/all_gather | solution.py:95
  129.0 274.6 %all-gather.6.cloned.1.call-start = ((), (), s32[]{:S(2)}) async-start(), calls=%async_computation.7 | async-start | bytes 10616832 | tf_op jit(solution)/shard_map/all_gather | solution.py:96
  132.2 542.1 %all-reduce.23.cloned.1.call-start = ((), (), s32[]{:S(2)}) async-start(), calls=%async_computation.8 | async-start | bytes 4841472 | tf_op jit(solution)/shard_map/psum | solution.py:170
  132.3 96.9 %copy-start.49 = (f32[768]{0:T(1024)}, f32[768]{0:T(1024)S(1)}, u32[]{:S(2)}) copy-start(f32[768]{0:T(1024)S(1)} %convert_element_type.175) | copy-start | bytes 9220
  167.1 92.0 %copy-start.47 = (bf16[768,8]{0,1:T(8,128)(2,1)}, bf16[768,8]{0,1:T(8,128)(2,1)S(1)}, u32[]{:S(2)}) copy-start(bf16[768,8]{0,1:T(8,128)(2,1)S(1)} %reshape.280) | copy-start | bytes 36868
  259.9 33.3 %copy-start.31 = (f32[1576]{0:T(1024)}, f32[1576]{0:T(1024)S(1)}, u32[]{:S(2)}) copy-start(f32[1576]{0:T(1024)S(1)} %get-tuple-element.44) | copy-start | bytes 18916
  259.9 33.3 %copy-start.33 = (f32[1576]{0:T(1024)}, f32[1576]{0:T(1024)S(1)}, u32[]{:S(2)}) copy-start(f32[1576]{0:T(1024)S(1)} %fusion.45) | copy-start | bytes 18916
  260.9 32.3 %copy-start.11 = (f32[1576,2]{1,0:T(8,128)}, f32[1576,2]{1,0:T(8,128)S(1)}, u32[]{:S(2)}) copy-start(f32[1576,2]{1,0:T(8,128)S(1)} %copy.123) | copy-start | bytes 37828
  572.9 44.5 %copy-start.12 = (f32[1576,2]{1,0:T(8,128)S(1)}, f32[1576,2]{1,0:T(8,128)}, u32[]{:S(2)}) copy-start(f32[1576,2]{1,0:T(8,128)} %copy-done.11) | copy-start | bytes 37828
  617.3 31.8 %copy-start.30 = (s32[1576,2]{0,1:T(2,128)S(1)}, s32[1576,2]{0,1:T(2,128)}, u32[]{:S(2)}) copy-start(s32[1576,2]{0,1:T(2,128)} %param.24) | copy-start | bytes 37828
  617.3 31.8 %copy-start.25 = (f32[1576,8]{0,1:T(8,128)S(1)}, f32[1576,8]{0,1:T(8,128)}, u32[]{:S(2)}) copy-start(f32[1576,8]{0,1:T(8,128)} %copy-done.24) | copy-start | bytes 151300
  617.4 31.8 %copy-start.32 = (f32[1576]{0:T(1024)S(1)}, f32[1576]{0:T(1024)}, u32[]{:S(2)}) copy-start(f32[1576]{0:T(1024)} %copy-done.31) | copy-start | bytes 18916
  617.4 31.8 %copy-start.34 = (f32[1576]{0:T(1024)S(1)}, f32[1576]{0:T(1024)}, u32[]{:S(2)}) copy-start(f32[1576]{0:T(1024)} %copy-done.33) | copy-start | bytes 18916
  617.4 158.1 %reduce-scatter.18.cloned.1.call-start = ((), (), s32[]{:S(2)}) async-start(), calls=%async_computation.13 | async-start | bytes 442368
  641.8 32.5 %copy-start.1 = (bf16[1576,768]{1,0:T(8,128)(2,1)S(1)}, bf16[1576,768]{1,0:T(8,128)(2,1)}, u32[]{:S(2)}) copy-start(bf16[1576,768]{1,0:T(8,128)(2,1)} %param.13) | copy-start | bytes 7262212
  641.8 32.5 %copy-start.36 = (f32[1576]{0:T(1024)S(1)}, f32[1576]{0:T(1024)}, u32[]{:S(2)}) copy-start(f32[1576]{0:T(1024)} %copy-done.35) | copy-start | bytes 18916
  641.8 32.5 %copy-start.45 = (f32[1576]{0:T(1024)S(1)}, f32[1576]{0:T(1024)}, u32[]{:S(2)}) copy-start(f32[1576]{0:T(1024)} %copy-done.44) | copy-start | bytes 18916
  641.8 32.5 %copy-start.48 = (bf16[768,8]{0,1:T(8,128)(2,1)S(1)}, bf16[768,8]{0,1:T(8,128)(2,1)}, u32[]{:S(2)}) copy-start(bf16[768,8]{0,1:T(8,128)(2,1)} %copy-done.47) | copy-start | bytes 36868
  641.8 32.5 %copy-start.50 = (f32[768]{0:T(1024)S(1)}, f32[768]{0:T(1024)}, u32[]{:S(2)}) copy-start(f32[768]{0:T(1024)} %copy-done.49) | copy-start | bytes 9220
  652.6 26.8 %copy-start.43 = (f32[1576]{0:T(1024)S(1)}, f32[1576]{0:T(1024)}, u32[]{:S(2)}) copy-start(f32[1576]{0:T(1024)} %copy-done.42) | copy-start | bytes 18916
  652.6 166.4 %reduce-scatter.16.cloned.1.call-start = ((), (), s32[]{:S(2)}) async-start(), calls=%async_computation.12 | async-start | bytes 884736
  721.4 102.6 %all-reduce.25.cloned.1.call-start = ((), (), s32[]{:S(2)}) async-start(), calls=%async_computation.14 | async-start | bytes 9682944 | tf_op jit(solution)/shard_map/psum | solution.py:136
  727.4 128.2 %reduce-scatter.10.cloned.1.call-start = ((), (), s32[]{:S(2)}) async-start(), calls=%async_computation.9 | async-start | bytes 2654208 | tf_op jit(solution)/shard_map/reduce_scatter | solution.py:247
  733.6 436.8 %reduce-scatter.12.cloned.1.call-start = ((), (), s32[]{:S(2)}) async-start(), calls=%async_computation.10 | async-start | bytes 21233664 | tf_op jit(solution)/shard_map/reduce_scatter | solution.py:243
  750.4 734.9 %reduce-scatter.14.cloned.1.call-start = ((), (), s32[]{:S(2)}) async-start(), calls=%async_computation.11 | async-start | bytes 21233664 | tf_op jit(solution)/shard_map/reduce_scatter | solution.py:244
  (45 other events, 203.9 us)
Sparse Core Ops, SparseCore 0:
  126.2 56.7 all-reduce.20
  617.4 56.8 all-reduce.22
  727.6 96.4 all-reduce.24
Sparse Core Ops, SparseCore 1:
  129.6 135.6 all-gather.3
  268.1 135.4 all-gather.5
  652.7 59.7 reduce-scatter.17
  721.5 61.6 reduce-scatter.15
  787.7 67.9 reduce-scatter.9
  860.6 309.8 reduce-scatter.11
  1175.3 310.0 reduce-scatter.13
where the time goes:
time: 1510 us; the launch traced here: 1490 us
  waiting for transfers between devices  787 us (52%)
  local copies, waits for them, and re-layouts  257 us (17%)
  matrix products  160 us (11%)
  blocking collectives  158 us (10%)
  other arithmetic  113 us (7%)
  between operations  18.2 us (1%)
    reduce_scatter x1, waiting for transfers between devices, body(): lax.psum_scatter(g_w_expert_out, 'dp', scatter_dimension=2, tiled=True)  315 us
    reduce_scatter x1, waiting for transfers between devices, body(): lax.psum_scatter(g_w_in, 'dp', scatter_dimension=1, tiled=True)  315 us
    all_gather x1, waiting for transfers between devices, body(): lax.all_gather(w_expert_out.astype(jnp.bfloat16), 'dp', axis=2, tiled=True)  110 us
    unnamed x2, blocking collectives  50.8 us
    reduce_sum x1, other arithmetic, body(): grad_two_part = jnp.sum(grad_rows[slot_index], axis=1)  44.4 us
    gather x2, local copies, waits for them, and re-layouts, body(): grad_padded[slot_token] * gate_slot[:, None]  37.5 us
    all_gather x1, blocking collectives, body(): lax.all_gather(w_qkv.astype(jnp.bfloat16), 'dp', axis=0, tiled=True)  35.8 us
    all_gather x1, blocking collectives, body(): lax.all_gather(w_attn_out.astype(jnp.bfloat16), 'dp', axis=1, tiled=True)  32.8 us
  transfers between devices with their start and end apart: 10, of which 6 were waited for; matrix products, arithmetic and copies ran while one was open for 19% of the time, Pallas kernels for 0%

commit v1 on v0

v1 whole, which is shorter than its diff:
```python
import functools

import jax
import jax.numpy as jnp
from jax import lax
from jax.experimental import pallas as pl
from jax.experimental.pallas import tpu as pltpu
from jax.sharding import PartitionSpec as P

D = 768
HD = 64
E = 8
TOP = 2
SEQ = 197
CAP = 689
PAD = 208
META = 200
TILE = 256
FFS = 768
EPS = 1e-06
VMEM_LIMIT = 60 * 1024 * 1024

F32 = jnp.float32
BF16 = jnp.bfloat16


def dot(a, b):
    return jnp.dot(a, b, preferred_element_type=F32)


def dot_nt(a, b):
    return lax.dot_general(a, b, (((1,), (1,)), ((), ())), preferred_element_type=F32)


def dot_tn(a, b):
    return lax.dot_general(a, b, (((0,), (0,)), ((), ())), preferred_element_type=F32)


def iota(shape, dim):
    return lax.broadcasted_iota(jnp.int32, shape, dim)


def normalise(values):
    centred = values - jnp.mean(values, axis=-1, keepdims=True)
    scale = lax.rsqrt(jnp.mean(centred * centred, axis=-1, keepdims=True) + EPS)
    return centred * scale, scale


def norm_back(grad, unit, scale, gain):
    g = grad * gain
    return scale * (
        g - jnp.mean(g, axis=-1, keepdims=True) - unit * jnp.mean(g * unit, axis=-1, keepdims=True)
    )


def attn_forward_kernel(
    x_ref, par_ref, wa_ref, wb_ref, noise_ref, keep_ref,
    chunk_ref, x1_ref, qkv_ref, o_ref, lse_ref, probs_ref,
):
    par = par_ref[...].astype(F32)
    x = x_ref[...].astype(F32)
    unit, _ = normalise(x)
    h1 = (unit * par[0:1] + par[1:2]).astype(BF16)
    acc = x
    lse = jnp.zeros((PAD, 128), F32)
    key_ok = iota((PAD, PAD), 1) < SEQ
    lane = iota((PAD, 128), 1)
    for r in range(4):
        w = wa_ref[r] if r < 2 else wb_ref[r - 2]
        qkv = dot(h1, w[:, : 9 * HD]).astype(BF16)
        qkv_ref[r] = qkv
        outs = []
        for h in range(3):
            q = qkv[:, h * HD : (h + 1) * HD]
            k = qkv[:, (3 + h) * HD : (4 + h) * HD]
            v = qkv[:, (6 + h) * HD : (7 + h) * HD]
            s = jnp.where(key_ok, dot_nt(q, k) * HD ** (-0.5), -1e30)
            top = jnp.max(s, axis=-1, keepdims=True)
            p = jnp.exp(s - top)
            total = jnp.sum(p, axis=-1, keepdims=True)
            outs.append(dot((p * (1.0 / total)).astype(BF16), v).astype(BF16))
            lse = jnp.where(lane == 3 * r + h, top + jnp.log(total), lse)
        o = jnp.concatenate(outs, axis=1)
        o_ref[r] = o
        acc = acc + dot_nt(o, w[:, 9 * HD :])
    lse_ref[...] = lse
    x1_ref[...] = acc
    unit2, _ = normalise(acc)
    h2 = (unit2 * par[2:3] + par[3:4]).astype(BF16)
    logits = dot_nt(par_ref[8:16, :], h2) + noise_ref[...]
    e = jnp.exp(logits - jnp.max(logits, axis=0, keepdims=True))
    probs = e / jnp.sum(e, axis=0, keepdims=True)
    probs_ref[...] = probs
    gates = jnp.where(keep_ref[...] > 0, probs, -1.0)
    chunk_ref[...] = h2
    tail = jnp.concatenate([gates, jnp.zeros((8, D - PAD), F32)], axis=1)
    low = h2[PAD - 16 :, :].astype(F32)
    chunk_ref[PAD - 16 :, :] = jnp.concatenate([low[:8], tail], axis=0).astype(BF16)


def attn_forward(x, par, wa, wb, noise, keep):
    vm = pl.BlockSpec(memory_space=pltpu.VMEM)
    return pl.pallas_call(
        attn_forward_kernel,
        out_shape=(
            jax.ShapeDtypeStruct((PAD, D), BF16),
            jax.ShapeDtypeStruct((PAD, D), F32),
            jax.ShapeDtypeStruct((4, PAD, 9 * HD), BF16),
            jax.ShapeDtypeStruct((4, PAD, 3 * HD), BF16),
            jax.ShapeDtypeStruct((PAD, 128), F32),
            jax.ShapeDtypeStruct((E, PAD), F32),
        ),
        in_specs=[vm] * 6,
        out_specs=(vm,) * 6,
        compiler_params=pltpu.CompilerParams(vmem_limit_bytes=VMEM_LIMIT),
        cost_estimate=pl.CostEstimate(flops=3 * 10**9, bytes_accessed=10**7, transcendentals=10**6),
        name="attn_forward",
    )(x, par, wa, wb, noise, keep)


def expert_kernel(nb, me_ref, *refs):
    h_in, dy_in = refs[:nb], refs[nb : 2 * nb]
    wa_ref, wb_ref = refs[2 * nb : 2 * nb + 2]
    outs = refs[2 * nb + 2 :]
    y_out, dx_out = outs[:nb], outs[nb : 2 * nb]
    rows_out, hid_out, tiles_ref = outs[2 * nb : 2 * nb + 3]
    (h, dy, y_t, dx_t, gate_s, slot_s, dgate_s, xs, dys, hid_s, rows_s, lo_s, hi_s, in_sem, out_sem, row_sem, hid_sem) = outs[2 * nb + 3 :]
    me = me_ref[0]
    loads = []
    for b in range(nb):
        for ref, table, c in ((h_in[b], h, 0), (dy_in[b], dy, 1)):
            copy = pltpu.make_async_copy(ref, table.at[b], in_sem.at[c, b])
            copy.start()
            loads.append(copy)
    y_t[...] = jnp.zeros_like(y_t)
    dx_t[...] = jnp.zeros_like(dx_t)
    dgate_s[...] = jnp.zeros_like(dgate_s)
    for copy in loads:
        copy.wait()

    row16 = iota((16, D), 0)
    for b in range(nb):
        meta = h[b, PAD - 16 : PAD, :].astype(F32)
        gate_s[b : b + 1, :] = jnp.sum(jnp.where(row16 == 8 + me, meta, 0.0), axis=0, keepdims=True)[:, :PAD]
    gates = gate_s[...]
    named = (gates >= 0) & (iota((nb, PAD), 1) < SEQ)
    ones = named.astype(F32).astype(BF16)
    upto = dot(ones, (iota((PAD, PAD), 0) <= iota((PAD, PAD), 1)).astype(F32).astype(BF16))
    count = dot(ones, jnp.ones((PAD, PAD), BF16)).astype(BF16)
    before = dot((iota((nb, nb), 0) > iota((nb, nb), 1)).astype(F32).astype(BF16), count)
    slot_s[...] = jnp.where(named, before + upto - 1.0, -1.0).astype(jnp.int32)
    ends = jnp.where(named, before + upto, before)
    for b in range(nb):
        lo_s[b] = jnp.max(before[b : b + 1, :]).astype(jnp.int32)
        hi_s[b] = jnp.max(ends[b : b + 1, :]).astype(jnp.int32)
    tiles = lax.div(hi_s[nb - 1] + TILE - 1, TILE)
    tiles_ref[0] = tiles

    def meets(b, first):
        return (lo_s[b] < first + TILE) & (hi_s[b] > first) & (hi_s[b] > lo_s[b])

    def place(b, first):
        return iota((TILE, PAD), 0) + first == slot_s[pl.ds(b, 1), :]

    def step(t, carry):
        first = t * TILE
        slot = lax.rem(t, 2)
        xs[...] = jnp.zeros_like(xs)
        dys[...] = jnp.zeros_like(dys)

        def collect(b, gcol):
            def one(gcol):
                hit = place(b, first)
                p = hit.astype(F32).astype(BF16)
                xs[...] += dot(p, h[b])
                dys[...] += dot(p, dy[b])
                return gcol + jnp.sum(jnp.where(hit, gate_s[pl.ds(b, 1), :], 0.0), axis=1, keepdims=True)

            return lax.cond(meets(b, first), one, lambda g: g, gcol)

        gcol = lax.fori_loop(0, nb, collect, jnp.zeros((TILE, 1), F32))

        def drain(s):
            pltpu.make_async_copy(rows_s.at[s], rows_out.at[:, pl.ds(0, TILE)], row_sem.at[s]).wait()
            pltpu.make_async_copy(hid_s.at[s], hid_out.at[:, pl.ds(0, TILE)], hid_sem.at[s]).wait()

        @pl.when(t >= 2)
        def _():
            drain(slot)

        x = xs[...].astype(BF16)
        g_rows = (dys[...] * gcol).astype(BF16)
        rows_s[slot, 0] = x
        rows_s[slot, 1] = g_rows
        y = jnp.zeros((TILE, D), F32)
        dx = jnp.zeros((TILE, D), F32)
        for r in range(4):
            w1, w2 = (wa_ref.at[r, 0], wa_ref.at[r, 1]) if r < 2 else (wb_ref.at[r - 2, 0], wb_ref.at[r - 2, 1])
            a = dot(x, w1[...])
            a2 = a * a
            th = jnp.tanh(0.7978845608028654 * a * (1.0 + 0.044715 * a2))
            half = 0.5 * (1.0 + th)
            hid = (a * half).astype(BF16)
            slope = half + 0.5 * a * (1.0 - th * th) * (0.7978845608028654 * (1.0 + 3 * 0.044715 * a2))
            da = (dot(g_rows, w2[...]) * slope).astype(BF16)
            y = y + dot_nt(hid, w2[...])
            dx = dx + dot_nt(da, w1[...])
            hid_s[slot, 0, :, r * FFS : (r + 1) * FFS] = da
            hid_s[slot, 1, :, r * FFS : (r + 1) * FFS] = hid
        at = pl.ds(pl.multiple_of(first, TILE), TILE)
        pltpu.make_async_copy(rows_s.at[slot], rows_out.at[:, at], row_sem.at[slot]).start()
        pltpu.make_async_copy(hid_s.at[slot], hid_out.at[:, at], hid_sem.at[slot]).start()
        dgate = jnp.sum(dys[...] * y, axis=1, keepdims=True)
        y_low = (y * gcol).astype(BF16)
        dx_low = dx.astype(BF16)

        def give(b, carry):
            @pl.when(meets(b, first))
            def _():
                hit = place(b, first)
                p = hit.astype(F32).astype(BF16)
                y_t[b] = y_t[b] + dot_tn(p, y_low).astype(BF16)
                dx_t[b] = dx_t[b] + dot_tn(p, dx_low).astype(BF16)
                dgate_s[pl.ds(b, 1), :] += jnp.sum(jnp.where(hit, dgate, 0.0), axis=0, keepdims=True)

            return carry

        lax.fori_loop(0, nb, give, 0)
        return carry

    lax.fori_loop(0, tiles, step, 0)
    for back in (1, 2):

        @pl.when(tiles >= back)
        def _():
            s = lax.rem(tiles - back, 2)
            pltpu.make_async_copy(rows_s.at[s], rows_out.at[:, pl.ds(0, TILE)], row_sem.at[s]).wait()
            pltpu.make_async_copy(hid_s.at[s], hid_out.at[:, pl.ds(0, TILE)], hid_sem.at[s]).wait()

    stores = []
    for b in range(nb):
        tail = dx_t[b, PAD - 16 : PAD, :].astype(F32)
        line = jnp.concatenate([dgate_s[b : b + 1, :], jnp.zeros((1, D - PAD), F32)], axis=1)
        dx_t[b, PAD - 16 : PAD, :] = (tail + jnp.where(row16 == 8 + me, line, 0.0)).astype(BF16)
        for table, ref, c in ((y_t, y_out[b], 0), (dx_t, dx_out[b], 1)):
            copy = pltpu.make_async_copy(table.at[b], ref, out_sem.at[c, b])
            copy.start()
            stores.append(copy)
    for copy in stores:
        copy.wait()


def expert_rows(nb):
    return -(-nb * SEQ // TILE) * TILE


def experts(me, h_blocks, dy_blocks, wa, wb):
    nb = len(h_blocks)
    rows = expert_rows(nb)
    hbm = pl.BlockSpec(memory_space=pl.ANY)
    vm = pl.BlockSpec(memory_space=pltpu.VMEM)
    sm = pl.BlockSpec(memory_space=pltpu.SMEM)
    block = jax.ShapeDtypeStruct((PAD, D), BF16)
    outs = pl.pallas_call(
        functools.partial(expert_kernel, nb),
        out_shape=[block] * (2 * nb)
        + [
            jax.ShapeDtypeStruct((2, rows, D), BF16),
            jax.ShapeDtypeStruct((2, rows, 4 * FFS), BF16),
            jax.ShapeDtypeStruct((1,), jnp.int32),
        ],
        in_specs=[sm] + [hbm] * (2 * nb) + [vm, vm],
        out_specs=[hbm] * (2 * nb + 2) + [sm],
        scratch_shapes=[
            pltpu.VMEM((nb, PAD, D), BF16),
            pltpu.VMEM((nb, PAD, D), BF16),
            pltpu.VMEM((nb, PAD, D), BF16),
            pltpu.VMEM((nb, PAD, D), BF16),
            pltpu.VMEM((nb, PAD), F32),
            pltpu.VMEM((nb, PAD), jnp.int32),
            pltpu.VMEM((nb, PAD), F32),
            pltpu.VMEM((TILE, D), F32),
            pltpu.VMEM((TILE, D), F32),
            pltpu.VMEM((2, 2, TILE, 4 * FFS), BF16),
            pltpu.VMEM((2, 2, TILE, D), BF16),
            pltpu.SMEM((nb,), jnp.int32),
            pltpu.SMEM((nb,), jnp.int32),
            pltpu.SemaphoreType.DMA((2, nb)),
            pltpu.SemaphoreType.DMA((2, nb)),
            pltpu.SemaphoreType.DMA((2,)),
            pltpu.SemaphoreType.DMA((2,)),
        ],
        compiler_params=pltpu.CompilerParams(vmem_limit_bytes=VMEM_LIMIT),
        cost_estimate=pl.CostEstimate(flops=30 * 10**9, bytes_accessed=4 * 10**7, transcendentals=4 * 10**6),
        name="experts",
    )(me.reshape(1), *h_blocks, *dy_blocks, wa, wb)
    return outs[:nb], outs[nb : 2 * nb], outs[2 * nb], outs[2 * nb + 1], outs[2 * nb + 2]


def expert_grad_kernel(tiles_ref, rows_ref, hid_ref, out_ref, acc):
    acc[...] = jnp.zeros_like(acc)

    def step(t, carry):
        at = pl.ds(pl.multiple_of(t * TILE, TILE), TILE)
        acc[...] += dot_tn(rows_ref[0, at, :], hid_ref[0, at, :])
        return carry

    lax.fori_loop(0, tiles_ref[0], step, 0)
    out_ref[0, 0] = acc[...].astype(BF16)


def expert_grads(tiles, rows, hid, base):
    n = rows.shape[1]
    return pl.pallas_call(
        expert_grad_kernel,
        grid_spec=pltpu.PrefetchScalarGridSpec(
            num_scalar_prefetch=1,
            grid=(2, 2),
            in_specs=[
                pl.BlockSpec((1, n, D), lambda k, s, _: (k, 0, 0)),
                pl.BlockSpec((1, n, FFS), lambda k, s, _: (k, 0, base + s)),
            ],
            out_specs=pl.BlockSpec((1, 1, D, FFS), lambda k, s, _: (s, k, 0, 0)),
            scratch_shapes=[pltpu.VMEM((D, FFS), F32)],
        ),
        out_shape=jax.ShapeDtypeStruct((2, 2, D, FFS), BF16),
        compiler_params=pltpu.CompilerParams(vmem_limit_bytes=VMEM_LIMIT),
        cost_estimate=pl.CostEstimate(flops=8 * 10**9, bytes_accessed=3 * 10**7, transcendentals=0),
        name="expert_grads",
    )(tiles, rows, hid)


def attn_backward_kernel(imgs, *refs):
    dh_in, x1_in, x_in, dy_in, probs_in, qkv_in, o_in, lse_in = (
        refs[i * imgs : (i + 1) * imgs] for i in range(8)
    )
    par_ref, wa_ref, wb_ref = refs[8 * imgs : 8 * imgs + 3]
    grads_ref, small_ref, dtok_ref = refs[8 * imgs + 3 : 8 * imgs + 6]
    dx1_s, low_s, h1_s, dh1_s, dqkv_s, o_s = refs[8 * imgs + 6 :]
    par = par_ref[...].astype(F32)
    router = par_ref[8:16, :]
    row_ok = iota((PAD, 1), 0) < SEQ
    lane_ok = iota((E, PAD), 1) < SEQ
    key_ok = iota((PAD, PAD), 1) < SEQ
    small2g = jnp.zeros((1, D), F32)
    small2b = jnp.zeros((1, D), F32)
    g_router = jnp.zeros((E, D), F32)
    for c in range(imgs):
        span = slice(c * PAD, (c + 1) * PAD)
        arrived = dh_in[c][...].astype(F32)
        dgate = arrived[PAD - 8 :, :PAD]
        probs = probs_in[c][...]
        dlogits = probs * (dgate - jnp.sum(probs * dgate, axis=0, keepdims=True))
        dlogits = jnp.where(lane_ok, dlogits, 0.0).astype(BF16)
        unit, scale = normalise(x1_in[c][...])
        h2 = (unit * par[2:3] + par[3:4]).astype(BF16)
        g_router = g_router + dot(dlogits, h2)
        dh2 = jnp.where(row_ok, arrived + dot_tn(dlogits, router), 0.0)
        small2g = small2g + jnp.sum(dh2 * unit, axis=0, keepdims=True)
        small2b = small2b + jnp.sum(dh2, axis=0, keepdims=True)
        dx1 = dy_in[c][...].astype(F32) + norm_back(dh2, unit, scale, par[2:3])
        dx1_s[span, :] = dx1
        low_s[span, :] = dx1.astype(BF16)
        unit1, _ = normalise(x_in[c][...].astype(F32))
        h1_s[span, :] = (unit1 * par[0:1] + par[1:2]).astype(BF16)
    low = low_s[...]
    h1 = h1_s[...]
    for r in range(4):
        w = wa_ref[r] if r < 2 else wb_ref[r - 2]
        dout = dot(low, w[:, 9 * HD :]).astype(BF16)
        for c in range(imgs):
            span = slice(c * PAD, (c + 1) * PAD)
            qkv = qkv_in[c][r]
            lse = lse_in[c][...]
            o_s[span, :] = o_in[c][r]
            dqs, dks, dvs = [], [], []
            for h in range(3):
                q = qkv[:, h * HD : (h + 1) * HD]
                k = qkv[:, (3 + h) * HD : (4 + h) * HD]
                v = qkv[:, (6 + h) * HD : (7 + h) * HD]
                do = dout[span, h * HD : (h + 1) * HD]
                s = dot_nt(q, k) * HD ** (-0.5)
                p = jnp.where(key_ok, jnp.exp(s - lse[:, 3 * r + h : 3 * r + h + 1]), 0.0)
                dvs.append(dot_tn(p.astype(BF16), do).astype(BF16))
                dp = dot_nt(do, v)
                ds = (p * (dp - jnp.sum(p * dp, axis=-1, keepdims=True))).astype(BF16)
                dqs.append((dot(ds, k) * HD ** (-0.5)).astype(BF16))
                dks.append((dot_tn(ds, q) * HD ** (-0.5)).astype(BF16))
            dqkv_s[span, :] = jnp.concatenate(dqs + dks + dvs, axis=1)
        dqkv = dqkv_s[...]
        part = dot_nt(dqkv, w[:, : 9 * HD])
        dh1_s[...] = part if r == 0 else dh1_s[...] + part
        grads_ref[r] = jnp.concatenate([dot_tn(h1, dqkv), dot_tn(low, o_s[...])], axis=1).astype(BF16)
    small1g = jnp.zeros((1, D), F32)
    small1b = jnp.zeros((1, D), F32)
    for c in range(imgs):
        span = slice(c * PAD, (c + 1) * PAD)
        dh1 = jnp.where(row_ok, dh1_s[span, :], 0.0)
        unit1, scale1 = normalise(x_in[c][...].astype(F32))
        small1g = small1g + jnp.sum(dh1 * unit1, axis=0, keepdims=True)
        small1b = small1b + jnp.sum(dh1, axis=0, keepdims=True)
        dtok_ref[c] = (dx1_s[span, :] + norm_back(dh1, unit1, scale1, par[0:1])).astype(BF16)
    small_ref[...] = jnp.concatenate(
        [small1g, small1b, small2g, small2b, jnp.zeros((4, D), F32), g_router], axis=0
    ).astype(BF16)


def attn_backward(dh, x1, x, dy, probs, qkv, o, lse, par, wa, wb):
    imgs = len(dh)
    vm = pl.BlockSpec(memory_space=pltpu.VMEM)
    rows = imgs * PAD
    return pl.pallas_call(
        functools.partial(attn_backward_kernel, imgs),
        out_shape=(
            jax.ShapeDtypeStruct((4, D, D), BF16),
            jax.ShapeDtypeStruct((16, D), BF16),
            jax.ShapeDtypeStruct((imgs, PAD, D), BF16),
        ),
        in_specs=[vm] * (8 * imgs + 3),
        out_specs=(vm,) * 3,
        scratch_shapes=[
            pltpu.VMEM((rows, D), F32),
            pltpu.VMEM((rows, D), BF16),
            pltpu.VMEM((rows, D), BF16),
            pltpu.VMEM((rows, D), F32),
            pltpu.VMEM((rows, 9 * HD), BF16),
            pltpu.VMEM((rows, 3 * HD), BF16),
        ],
        compiler_params=pltpu.CompilerParams(vmem_limit_bytes=VMEM_LIMIT),
        cost_estimate=pl.CostEstimate(flops=12 * 10**9, bytes_accessed=2 * 10**7, transcendentals=2 * 10**6),
        name="attn_backward",
    )(*dh, *x1, *x, *dy, *probs, *qkv, *o, *lse, par, wa, wb)


RING = (0, 2, 4, 6, 7, 5, 3, 1)


def ring_place(member):
    even = lax.rem(member, 2) == 0
    return jnp.where(even, lax.div(member, 2), E - 1 - lax.div(member, 2))


def ring_member(place):
    return jnp.where(place < E // 2, 2 * place, 2 * E - 1 - 2 * place)


class Mover:
    def __init__(self, n_dp):
        self.n_dp = n_dp
        self.groups = n_dp // E
        self.me = lax.axis_index("dp")
        self.member = lax.rem(self.me, E)
        self.group = lax.div(self.me, E)
        self.tensor = lax.axis_index("tensor")
        self.place = ring_place(self.member)
        bases = range(0, n_dp, E)
        self.ring = (
            [(b + RING[i], b + RING[(i + 1) % E]) for b in bases for i in range(E)],
            [(b + RING[(i + 1) % E], b + RING[i]) for b in bases for i in range(E)],
        )

    def along(self, value, way):
        return lax.ppermute(value, "dp", self.ring[way])

    def shift(self, value, by):
        perm = [(b + i, b + (i + by) % E) for b in range(0, self.n_dp, E) for i in range(E)]
        return lax.ppermute(value, "dp", perm)

    def shift_group(self, value, by):
        return lax.ppermute(value, "dp", [(k, (k + by * E) % self.n_dp) for k in range(self.n_dp)])

    def other(self, value, mask):
        return lax.ppermute(value, "tensor", [(k, k ^ mask) for k in range(4)])

    def behind(self, way, k):
        step = -k if way == 0 else k
        return ring_member(lax.rem(self.place + step + E, E))

    def ring_blocks(self, block, way):
        blocks = [block]
        for _ in range(E - 1):
            blocks.append(self.along(blocks[-1], way))
        return blocks

    def ring_sum(self, blocks, way):
        total = blocks[1]
        for k in range(2, E + 1):
            total = self.along(total, way)
            total = (total.astype(F32) + blocks[k % E].astype(F32)).astype(BF16)
        return total

    def both_ways(self, block):
        found = [(self.member, block)]
        ahead = back = block
        for k in range(1, E // 2 + 1):
            ahead = self.along(ahead, 0)
            found.append((self.behind(0, k), ahead))
            if k < E // 2:
                back = self.along(back, 1)
                found.append((self.behind(1, k), back))
        return found

    def sum_both_ways(self, block_for):
        def chain(way, steps):
            total = block_for(self.behind(1 - way, steps))
            for k in range(steps - 1, -1, -1):
                total = self.along(total, way)
                if k:
                    total = (total.astype(F32) + block_for(self.behind(1 - way, k)).astype(F32)).astype(BF16)
            return total

        ahead = chain(0, E // 2)
        back = chain(1, E // 2 - 1)
        return ahead.astype(F32) + back.astype(F32) + block_for(self.member).astype(F32)

    def all_groups(self, part, dim):
        if self.groups == 1:
            return part
        size = part.shape[dim]
        shape = part.shape[:dim] + (size * self.groups,) + part.shape[dim + 1 :]
        whole = lax.dynamic_update_slice_in_dim(jnp.zeros(shape, part.dtype), part, self.group * size, dim)
        for by in range(1, self.groups):
            came = lax.rem(self.group - by + self.groups, self.groups)
            whole = lax.dynamic_update_slice_in_dim(whole, self.shift_group(part, by), came * size, dim)
        return whole

    def sum_groups(self, whole, dim):
        if self.groups == 1:
            return whole
        size = whole.shape[dim] // self.groups
        total = lax.dynamic_slice_in_dim(whole, self.group * size, size, dim).astype(F32)
        for by in range(1, self.groups):
            to = lax.rem(self.group + by, self.groups)
            part = lax.dynamic_slice_in_dim(whole, to * size, size, dim)
            total = total + self.shift_group(part, by).astype(F32)
        return total.astype(whole.dtype)


def image_blocks(rows, tensor, imgs):
    first = tensor * (imgs * SEQ)
    return [
        jnp.pad(lax.dynamic_slice_in_dim(rows, first + c * SEQ, SEQ, 0), ((0, PAD - SEQ), (0, 0)))
        for c in range(imgs)
    ]


def image_lanes(lanes, tensor, imgs):
    first = tensor * (imgs * SEQ)
    return [
        jnp.pad(lax.dynamic_slice_in_dim(lanes, first + c * SEQ, SEQ, 1), ((0, 0), (0, PAD - SEQ)))
        for c in range(imgs)
    ]


def kept_pairs(routes):
    chosen = jnp.transpose(routes).reshape(1, -1)
    named = (chosen == jnp.arange(E, dtype=jnp.int32)[:, None]).astype(jnp.int32)
    kept = named * (jnp.cumsum(named, axis=1) <= CAP)
    return jnp.sum(kept.reshape(E, TOP, -1), axis=1).astype(F32)


def body(
    n_dp,
    tokens,
    ln1_gain,
    ln1_bias,
    w_qkv,
    w_attn_out,
    ln2_gain,
    ln2_bias,
    router_weight,
    w_in,
    w_expert_out,
    router_noise,
    routes,
    cotangent,
):
    move = Mover(n_dp)
    token_count = tokens.shape[0]
    imgs = token_count // SEQ // 4
    d_own = w_qkv.shape[0]
    ways = [c % 2 for c in range(imgs)]

    pack = jnp.concatenate(
        [w_qkv[:, 0], w_qkv[:, 1], w_qkv[:, 2], jnp.transpose(w_attn_out)], axis=1
    ).astype(BF16)
    vectors = jnp.stack([ln1_gain, ln1_bias, ln2_gain, ln2_bias] + [jnp.zeros_like(ln1_gain)] * 4)
    small = jnp.concatenate([vectors, jnp.transpose(router_weight)], axis=0).astype(BF16)
    small = jnp.pad(small, ((0, 0), (0, D - d_own)))
    pack = jnp.concatenate([pack, small], axis=0)
    w_own = jnp.zeros((E * d_own, D), BF16)
    par = jnp.zeros((E, 16, d_own), BF16)
    for member, block in move.both_ways(pack):
        w_own = lax.dynamic_update_slice_in_dim(w_own, block[:d_own], member * d_own, 0)
        par = lax.dynamic_update_slice_in_dim(par, block[None, d_own:, :d_own], member, 0)
    w_own = move.all_groups(w_own, 0)
    par = move.all_groups(par, 0)
    par = jnp.transpose(par, (1, 0, 2)).reshape(16, D)
    wa = jnp.stack([w_own, move.other(w_own, 2)])
    wb = move.other(wa, 1)

    x = image_blocks(tokens, move.tensor, imgs)
    dy = image_blocks(cotangent, move.tensor, imgs)
    dy_ring = [move.ring_blocks(dy[c], ways[c]) for c in range(imgs)]
    out_rows = jnp.transpose(w_expert_out, (0, 2, 1))
    ew = jnp.zeros((2, E * d_own, FFS), BF16)
    for by in range(E):
        to = lax.rem(move.member + by, E)
        block = jnp.stack(
            [lax.dynamic_index_in_dim(w, to, 0, False).astype(BF16) for w in (w_in, out_rows)]
        )
        came = lax.rem(move.member - by + E, E)
        ew = lax.dynamic_update_slice_in_dim(ew, move.shift(block, by) if by else block, came * d_own, 1)
    ew = move.all_groups(ew, 1)
    ewa = jnp.stack([ew, move.other(ew, 2)])
    ewb = move.other(ewa, 1)

    keep = image_lanes(kept_pairs(routes), move.tensor, imgs)
    noise = image_lanes(jnp.transpose(router_noise), move.tensor, imgs)
    fwd = [attn_forward(x[c], par, wa, wb, noise[c], keep[c]) for c in range(imgs)]
    chunk, x1, qkv, o, lse, probs = (list(part) for part in zip(*fwd))

    h_ring = [move.ring_blocks(chunk[c], ways[c]) for c in range(imgs)]
    y, dh, rows, hid, tiles = experts(
        move.member, sum(h_ring, []), sum(dy_ring, []), ewa, ewb
    )
    dh_sum = [move.ring_sum(dh[c * E : (c + 1) * E], ways[c]) for c in range(imgs)]
    y_sum = [move.ring_sum(y[c * E : (c + 1) * E], ways[c]) for c in range(imgs)]
    grads_b = expert_grads(tiles, rows, hid, 2)
    grads_a = expert_grads(tiles, rows, hid, 0)
    pair = (grads_a.astype(F32) + move.other(grads_b, 1).astype(F32)).astype(BF16)
    g_exp = (pair[0].astype(F32) + move.other(pair[1], 2).astype(F32)).astype(BF16)
    g_exp = move.sum_groups(g_exp, 1)
    g_in = jnp.zeros((E, d_own, FFS), F32)
    g_out = jnp.zeros((E, d_own, FFS), F32)
    for by in range(E):
        to = lax.rem(move.member + by, E)
        block = lax.dynamic_slice_in_dim(g_exp, to * d_own, d_own, 1)
        came = lax.rem(move.member - by + E, E)
        block = (move.shift(block, by) if by else block).astype(F32)
        g_in = lax.dynamic_update_slice_in_dim(g_in, block[0:1], came, 0)
        g_out = lax.dynamic_update_slice_in_dim(g_out, block[1:2], came, 0)

    g_attn, g_small, d_tok = attn_backward(dh_sum, x1, x, dy, probs, qkv, o, lse, par, wa, wb)
    spread = jnp.transpose(g_small.reshape(16, n_dp, d_own), (1, 0, 2))
    spread = jnp.pad(spread, ((0, 0), (0, 0), (0, D - d_own)))
    packs = jnp.concatenate(
        [g_attn.reshape(4, n_dp, d_own, D), jnp.broadcast_to(spread[None], (4,) + spread.shape)], axis=2
    )
    pair = (packs[:2].astype(F32) + move.other(packs[2:], 1).astype(F32)).astype(BF16)
    packs = (pair[0].astype(F32) + move.other(pair[1], 2).astype(F32)).astype(BF16)
    packs = move.sum_groups(packs, 0)
    total = move.sum_both_ways(lambda member: lax.dynamic_index_in_dim(packs, member, 0, False))
    g_qkv = total[:d_own, : 9 * HD].reshape(d_own, 3, 3 * HD)
    g_attn_out = jnp.transpose(total[:d_own, 9 * HD :])
    g_small = total[d_own:, :d_own]

    def all_rows(blocks):
        own = jnp.concatenate([b[:SEQ] for b in blocks], axis=0)
        n = own.shape[0]
        two = jnp.stack([own, move.other(own, 2)])
        four = jnp.concatenate([two, move.other(two, 1)], axis=0)
        whole = jnp.zeros((4 * n, D), BF16)
        for at, mask in enumerate((0, 2, 1, 3)):
            whole = lax.dynamic_update_slice_in_dim(whole, four[at], (move.tensor ^ mask) * n, 0)
        return whole

    output = all_rows([(x1[c] + y_sum[c].astype(F32)).astype(BF16) for c in range(imgs)])
    d_tokens = all_rows([d_tok[c] for c in range(imgs)])
    return (
        output,
        d_tokens,
        g_small[0],
        g_small[1],
        g_qkv,
        g_attn_out,
        g_small[2],
        g_small[3],
        jnp.transpose(g_small[8:16]),
        g_in,
        jnp.transpose(g_out, (0, 2, 1)),
    )


def solution(mesh):
    in_specs = (
        P("dp", None),
        P("dp"),
        P("dp"),
        P("dp", None, "tensor"),
        P("tensor", "dp"),
        P("dp"),
        P("dp"),
        P("dp", None),
        P(None, "dp", "tensor"),
        P(None, "tensor", "dp"),
        P("dp", None),
        P("dp", None),
        P("dp", None),
    )
    out_specs = (
        P("dp", None),
        P("dp", None),
        P("dp"),
        P("dp"),
        P("dp", None, "tensor"),
        P("tensor", "dp"),
        P("dp"),
        P("dp"),
        P("dp", None),
        P(None, "dp", "tensor"),
        P(None, "tensor", "dp"),
    )
    return jax.shard_map(
        functools.partial(body, mesh.shape["dp"]),
        mesh=mesh,
        in_specs=in_specs,
        out_specs=out_specs,
        check_vma=False,
    )
```

time: 1510 us -> 699 us (0.46)
  waiting for transfers between devices: 787 us -> 221 us
  matrix products: 160 us -> 0 us
  blocking collectives: 158 us -> 0 us
  starting transfers between devices: 0.95 us -> 155 us
  local copies, waits for them, and re-layouts: 257 us -> 109 us
  Pallas kernels: 0 us -> 140 us
  other arithmetic: 113 us -> 60.4 us
  between operations: 18.2 us -> 2.82 us
    reduce_scatter x3 -> x0, waiting for transfers between devices: 652 us -> none  [the longest x1 315 us: body(): lax.psum_scatter(g_w_expert_out, 'dp', scatter_dimension=2, tiled=True)]
    ppermute x0 -> x96, waiting for transfers between devices: none -> 221 us  [the longest x70 161 us: along(): return lax.ppermute(value, 'dp', self.ring[way])]
    ppermute x0 -> x96, starting transfers between devices: none -> 155 us  [the longest x70 76.5 us: along(): return lax.ppermute(value, 'dp', self.ring[way])]
    dot_general x19 -> x0, matrix products: 154 us -> none  [the longest x1 24.2 us: body(): jnp.einsum('ecf,ecd->efd', hidden, grad_slots, preferred_element_type=jnp...]
    pallas_call x0 -> x6, Pallas kernels: none -> 140 us  [the longest x1 60 us: experts(): pl.pallas_call(functools.partial(expert_kernel, nb), out_shape=[block] *...]
    gather x7 -> x0, local copies, waits for them, and re-layouts: 117 us -> none  [the longest x2 37.5 us: body(): grad_padded[slot_token] * gate_slot[:, None]]
    all_gather x2 -> x0, waiting for transfers between devices: 110 us -> none  [the longest x1 110 us: body(): lax.all_gather(w_expert_out.astype(jnp.bfloat16), 'dp', axis=2, tiled=True)]
    all_gather x3 -> x0, blocking collectives: 93.3 us -> none  [the longest x1 35.8 us: body(): lax.all_gather(w_qkv.astype(jnp.bfloat16), 'dp', axis=0, tiled=True)]
  transfers between devices with their start and end apart: 10 -> 96, of which waited for: 6 -> 41; matrix products, arithmetic and copies ran while one was open for 19% -> 22% of each run, Pallas kernels for 0% -> 12%
where the time goes in v1:
time: 699 us; the launch traced here: 688 us
  waiting for transfers between devices  221 us (32%)
  starting transfers between devices  155 us (22%)
  Pallas kernels  140 us (20%)
  local copies, waits for them, and re-layouts  109 us (16%)
  other arithmetic  60.4 us (9%)
    ppermute x70, waiting for transfers between devices, along(): return lax.ppermute(value, 'dp', self.ring[way])  161 us
    ppermute x70, starting transfers between devices, along(): return lax.ppermute(value, 'dp', self.ring[way])  76.5 us
    ppermute x14, starting transfers between devices, shift(): return lax.ppermute(value, 'dp', perm)  69.9 us
    pallas_call x1, Pallas kernels, experts(): pl.pallas_call(functools.partial(expert_kernel, nb), out_shape=[block] *...  60 us
    ppermute x12, waiting for transfers between devices, other(): return lax.ppermute(value, 'tensor', [(k, k ^ mask) for k in range(4)])  51 us
    pallas_call x2, Pallas kernels, expert_grads(): pl.pallas_call(expert_grad_kernel, grid_spec=pltpu.PrefetchScalarGridSpec...  38.3 us
    dynamic_update_slice x8, local copies, waits for them, and re-layouts, all_rows(): lax.dynamic_update_slice_in_dim(whole, four[at], (move.tensor ^ mask) * n...  32.9 us
    pallas_call x1, Pallas kernels, attn_backward(): pl.pallas_call(functools.partial(attn_backward_kernel, imgs), out_shape=(...  24.8 us
  transfers between devices with their start and end apart: 96, of which 41 were waited for; matrix products, arithmetic and copies ran while one was open for 22% of the time, Pallas kernels for 12%

profile of v1, /device:TPU:24, one launch (start us, length us, event | category | flops | bytes accessed | tf_op | source)
XLA Modules:
  0.0 687.9 jit_solution(10253956580815122204)
XLA Ops:
  34.1 22.4 %collective-permute-start.43 = (bf16[2,96,768]{2,1,0:T(8,128)(2,1)S(1)}, bf16[2,96,768]{2,1,0:T(8,128)(2,1)S(1)}, u32[]{:S(2)}, u32[]{:S(2)}) collective-permute-start(bf16[2,96,768]{2,1,0:T(8,128)(2,1)S(1)} %copy-done.51), channel_id=1, source_target_pairs={{0,28},{4,0},{8,4},{12,8},{16,12},{20,16},{24,20},{28,24},{1,29},{... | collective-permute-start | bytes 884744 | tf_op jit(solution)/shard_map/ppermute | solution.py:467
  71.2 7.2 %collective-permute-done.2 = bf16[112,768]{1,0:T(8,128)(2,1)S(1)} collective-permute-done((bf16[112,768]{1,0:T(8,128)(2,1)}, bf16[112,768]{1,0:T(8,128)(2,1)S(1)}, u32[]{:S(2)}, u32[]{:S(2)}) %collective-permute-start.2) | collective-permute-done | bytes 172064 | tf_op jit(solution)/shard_map/ppermute | solution.py:463
  85.1 5.3 collective-permute-done.6
  92.8 5.2 reduce-window.6
  102.3 45.6 %collective-permute-done.7 = bf16[768,768]{1,0:T(8,128)(2,1)} collective-permute-done((bf16[768,768]{1,0:T(8,128)(2,1)S(1)}, bf16[768,768]{1,0:T(8,128)(2,1)}, u32[]{:S(2)}, u32[]{:S(2)}) %collective-permute-start.7) | collective-permute-done | bytes 1179680 | tf_op jit(solution)/shard_map/ppermute | solution.py:473
  166.6 8.3 %attn_forward.2 = (bf16[208,768]{1,0:T(8,128)(2,1)}, f32[208,768]{1,0:T(8,128)}, bf16[4,208,576]{2,1,0:T(8,128)(2,1)}, bf16[4,208,192]{2,1,0:T(8,128)(2,1)}, f32[208,128]{1,0:T(8,128)}, /*index=5*/f32[8,208]{1,0:T(8,128)}) custom-call(bf16[208,768]{1,0:T(8,128)(2,1)} %pad.37.x_ref.refs_4_, bf16[16,768]{1,0:T(8,128)(2,1)} %reshape.155.par_ref.refs_16_, ...), custom_call_target="tpu_custom_call" | custom-call | flops 3000000000 | bytes 10000000 | tf_op jit(solution)/shard_map/attn_forward/pallas_call | solution.py:103
  176.8 8.3 %attn_forward.3 = (bf16[208,768]{1,0:T(8,128)(2,1)}, f32[208,768]{1,0:T(8,128)}, bf16[4,208,576]{2,1,0:T(8,128)(2,1)}, bf16[4,208,192]{2,1,0:T(8,128)(2,1)}, f32[208,128]{1,0:T(8,128)}, /*index=5*/f32[8,208]{1,0:T(8,128)}) custom-call(bf16[208,768]{1,0:T(8,128)(2,1)} %pad.42.x_ref.refs_5_, bf16[16,768]{1,0:T(8,128)(2,1)} %reshape.155.par_ref.refs_16_, ...), custom_call_target="tpu_custom_call" | custom-call | flops 3000000000 | bytes 10000000 | tf_op jit(solution)/shard_map/attn_forward/pallas_call | solution.py:103
  189.2 6.6 collective-permute-done.16.refs_9_
  204.7 4.8 collective-permute-done.17.refs_10_
  218.4 4.8 collective-permute-done.18.refs_11_
  232.1 4.8 collective-permute-done.19.refs_12_
  264.6 6.5 collective-permute-done.36.refs_31_
  271.1 5.5 collective-permute-done.22.refs_15_
  277.5 60.0 %experts.1 = (bf16[208,768]{1,0:T(8,128)(2,1)}, bf16[208,768]{1,0:T(8,128)(2,1)}, bf16[208,768]{1,0:T(8,128)(2,1)}, bf16[208,768]{1,0:T(8,128)(2,1)}, bf16[208,7...) custom-call(s32[1]{0:T(128)} %bitcast.27.me_ref, ...), custom_call_target="tpu_custom_call" | custom-call | flops 30000001024 | bytes 40000000 | tf_op jit(solution)/shard_map/experts/pallas_call | solution.py:264
  339.6 7.2 %collective-permute-done.69 = bf16[208,768]{1,0:T(8,128)(2,1)S(1)} collective-permute-done((bf16[208,768]{1,0:T(8,128)(2,1)}, bf16[208,768]{1,0:T(8,128)(2,1)S(1)}, u32[]{:S(2)}, u32[]{:S(2)}) %collective-permute-start.69) | collective-permute-done | bytes 319520 | tf_op jit(solution)/shard_map/ppermute | solution.py:463
  351.1 19.2 %expert_grads.3 = bf16[2,2,768,768]{3,2,1,0:T(8,128)(2,1)} custom-call(s32[1]{0:T(128)} %get-tuple-element.108.tiles_ref, bf16[2,3328,768]{2,1,0:T(8,128)(2,1)} %get-tuple-element.109.rows_ref, bf16[2,3328,3072]{2,1,0:T(8,128)(2,1)} %get-tuple-element.110.hid_ref), custom_call_target="tpu_custom_call" | custom-call | flops 8000000000 | bytes 30000000 | tf_op jit(solution)/shard_map/expert_grads/pallas_call | solution.py:314
  377.7 6.0 collective-permute-done.46
  383.9 5.5 collective-permute-done.71
  394.3 5.7 collective-permute-done.72
  404.0 7.8 %collective-permute-done.73 = bf16[208,768]{1,0:T(8,128)(2,1)S(1)} collective-permute-done((bf16[208,768]{1,0:T(8,128)(2,1)S(1)}, bf16[208,768]{1,0:T(8,128)(2,1)S(1)}, u32[]{:S(2)}, u32[]{:S(2)}) %collective-permute-start.73) | collective-permute-done | bytes 319520 | tf_op jit(solution)/shard_map/ppermute | solution.py:463
  417.4 5.0 collective-permute-done.74
  428.1 5.3 collective-permute-done.75
  437.9 24.8 %attn_backward.1 = (bf16[4,768,768]{2,1,0:T(8,128)(2,1)}, bf16[16,768]{1,0:T(8,128)(2,1)}, bf16[2,208,768]{2,1,0:T(8,128)(2,1)}) custom-call(bf16[208,768]{1,0:T(8,128)(2,1)} %add_convert_fusion.9.refs_0_, bf16[208,768]{1,0:T(8,128)(2,1)} %add_convert_fusion.2.refs_1_, f32[208,768]{1,0:T(8,128)} %get-tuple-element.61.refs_2_, ...), custom_call_target="tpu_custom_call" | custom-call | flops 12000000000 | bytes 20000000 | tf_op jit(solution)/shard_map/attn_backward/pallas_call | solution.py:412
  463.7 8.0 %copy.70 = bf16[4,8,96,768]{2,3,1,0:T(8,128)(2,1)} copy(bf16[4,8,96,768]{3,2,1,0:T(8,128)(2,1)} %bitcast.159) | data formatting | bytes 9437184 | tf_op jit(solution)/shard_map/reshape | solution.py:648
  485.1 6.6 collective-permute-done.56
  494.9 6.1 collective-permute-done.57
  503.8 5.5 collective-permute-done.58
  531.1 19.1 %expert_grads.2 = bf16[2,2,768,768]{3,2,1,0:T(8,128)(2,1)} custom-call(s32[1]{0:T(128)} %get-tuple-element.108.tiles_ref, bf16[2,3328,768]{2,1,0:T(8,128)(2,1)} %get-tuple-element.109.rows_ref, bf16[2,3328,3072]{2,1,0:T(8,128)(2,1)} %get-tuple-element.110.hid_ref), custom_call_target="tpu_custom_call" | custom-call | flops 8000000000 | bytes 30000000 | tf_op jit(solution)/shard_map/expert_grads/pallas_call | solution.py:314
  557.3 6.0 add_convert_fusion
  563.3 5.4 collective-permute-done.79
  648.6 26.5 %collective-permute-start.94 = (bf16[2,96,768]{2,1,0:T(8,128)(2,1)S(1)}, bf16[2,96,768]{2,1,0:T(8,128)(2,1)S(1)}, u32[]{:S(2)}, u32[]{:S(2)}) collective-permute-start(bf16[2,96,768]{2,1,0:T(8,128)(2,1)S(1)} %get-tuple-element.175), channel_id=1, source_target_pairs={{0,24},{4,28},{8,0},{12,4},{16,8},{20,12},{24,16},{28,20},{1,25},{... | collective-permute-start | bytes 884744 | tf_op jit(solution)/shard_map/ppermute | solution.py:467
  675.2 5.2 collective-permute-start.95
  (524 shorter events, 314.8 us)
Async XLA Ops:
  16.5 45.7 %collective-permute-start.39 = (bf16[2,96,768]{2,1,0:T(8,128)(2,1)}, bf16[2,96,768]{2,1,0:T(8,128)(2,1)}, u32[]{:S(2)}, u32[]{:S(2)}) collective-permute-start(bf16[2,96,768]{2,1,0:T(8,128)(2,1)} %pad_maximum_fusion.9), channel_id=1, source_target_pairs={{0,12},{4,16},{8,20},{12,24},{16,28},{20,0},{24,4},{28,8},{1,13},{... | collective-permute-start | bytes 884744 | tf_op jit(solution)/shard_map/ppermute | solution.py:467
  27.7 35.6 %collective-permute-start.40 = (bf16[2,96,768]{2,1,0:T(8,128)(2,1)}, bf16[2,96,768]{2,1,0:T(8,128)(2,1)S(1)}, u32[]{:S(2)}, u32[]{:S(2)}) collective-permute-start(bf16[2,96,768]{2,1,0:T(8,128)(2,1)} %pad_maximum_fusion.10), channel_id=1, source_target_pairs={{0,16},{4,20},{8,24},{12,28},{16,0},{20,4},{24,8},{28,12},{1,17},{... | collective-permute-start | bytes 884744 | tf_op jit(solution)/shard_map/ppermute | solution.py:467
  28.8 36.6 %collective-permute-start.41 = (bf16[2,96,768]{2,1,0:T(8,128)(2,1)}, bf16[2,96,768]{2,1,0:T(8,128)(2,1)S(1)}, u32[]{:S(2)}, u32[]{:S(2)}) collective-permute-start(bf16[2,96,768]{2,1,0:T(8,128)(2,1)} %pad_maximum_fusion.11), channel_id=1, source_target_pairs={{0,20},{4,24},{8,28},{12,0},{16,4},{20,8},{24,12},{28,16},{1,21},{... | collective-permute-start | bytes 884744 | tf_op jit(solution)/shard_map/ppermute | solution.py:467
  32.6 36.8 %collective-permute-start.42 = (bf16[2,96,768]{2,1,0:T(8,128)(2,1)S(1)}, bf16[2,96,768]{2,1,0:T(8,128)(2,1)S(1)}, u32[]{:S(2)}, u32[]{:S(2)}) collective-permute-start(bf16[2,96,768]{2,1,0:T(8,128)(2,1)S(1)} %copy-done.52), channel_id=1, source_target_pairs={{0,24},{4,28},{8,0},{12,4},{16,8},{20,12},{24,16},{28,20},{1,25},{... | collective-permute-start | bytes 884744 | tf_op jit(solution)/shard_map/ppermute | solution.py:467
  34.1 35.4 %collective-permute-start.43 = (bf16[2,96,768]{2,1,0:T(8,128)(2,1)S(1)}, bf16[2,96,768]{2,1,0:T(8,128)(2,1)S(1)}, u32[]{:S(2)}, u32[]{:S(2)}) collective-permute-start(bf16[2,96,768]{2,1,0:T(8,128)(2,1)S(1)} %copy-done.51), channel_id=1, source_target_pairs={{0,28},{4,0},{8,4},{12,8},{16,12},{20,16},{24,20},{28,24},{1,29},{... | collective-permute-start | bytes 884744 | tf_op jit(solution)/shard_map/ppermute | solution.py:467
  62.3 123.1 %collective-permute-start.23 = (bf16[208,768]{1,0:T(8,128)(2,1)}, bf16[208,768]{1,0:T(8,128)(2,1)}, u32[]{:S(2)}, u32[]{:S(2)}) collective-permute-start(bf16[208,768]{1,0:T(8,128)(2,1)} %pad.45.refs_16_.refs_6_), channel_id=1, source_target_pairs={{0,8},{8,16},{16,24},{24,28},{28,20},{20,12},{12,4},{4,0},{1,9},{9... | collective-permute-start | bytes 958472 | tf_op jit(solution)/shard_map/ppermute | solution.py:463
  63.3 123.9 %collective-permute-start.30 = (bf16[208,768]{1,0:T(8,128)(2,1)}, bf16[208,768]{1,0:T(8,128)(2,1)}, u32[]{:S(2)}, u32[]{:S(2)}) collective-permute-start(bf16[208,768]{1,0:T(8,128)(2,1)} %pad.46.refs_24_.refs_7_), channel_id=1, source_target_pairs={{8,0},{16,8},{24,16},{28,24},{20,28},{12,20},{4,12},{0,4},{9,1},{1... | collective-permute-start | bytes 958472 | tf_op jit(solution)/shard_map/ppermute | solution.py:463
  69.6 81.2 %collective-permute-start.44 = (bf16[2,768,768]{2,1,0:T(8,128)(2,1)S(1)}, bf16[2,768,768]{2,1,0:T(8,128)(2,1)}, u32[]{:S(2)}, u32[]{:S(2)}) collective-permute-start(bf16[2,768,768]{2,1,0:T(8,128)(2,1)S(1)} %constant_dynamic-update-slice_fusion), channel_id=1, source_target_pairs={{0,2},{1,3},{2,0},{3,1},{4,6},{5,7},{6,4},{7,5},{8,10},{9,11},{10,... | collective-permute-start | bytes 7077896 | tf_op jit(solution)/shard_map/ppermute | solution.py:473
  90.5 57.5 %collective-permute-start.7 = (bf16[768,768]{1,0:T(8,128)(2,1)S(1)}, bf16[768,768]{1,0:T(8,128)(2,1)}, u32[]{:S(2)}, u32[]{:S(2)}) collective-permute-start(bf16[768,768]{1,0:T(8,128)(2,1)S(1)} %slice_dynamic-update-slice_fusion.16), channel_id=1, source_target_pairs={{0,2},{1,3},{2,0},{3,1},{4,6},{5,7},{6,4},{7,5},{8,10},{9,11},{10,... | collective-permute-start | bytes 3538952 | tf_op jit(solution)/shard_map/ppermute | solution.py:473
  155.2 121.5 %collective-permute-start.45 = (bf16[2,2,768,768]{3,2,1,0:T(8,128)(2,1)}, bf16[2,2,768,768]{3,2,1,0:T(8,128)(2,1)}, u32[]{:S(2)}, u32[]{:S(2)}) collective-permute-start(bf16[2,2,768,768]{3,2,1,0:T(8,128)(2,1)} %pad_maximum_fusion.refs_32_), channel_id=1, source_target_pairs={{0,1},{1,0},{2,3},{3,2},{4,5},{5,4},{6,7},{7,6},{8,9},{9,8},{10,11... | collective-permute-start | bytes 14155784 | tf_op jit(solution)/shard_map/ppermute | solution.py:473
  347.9 27.5 %collective-permute-start.70 = (bf16[208,768]{1,0:T(8,128)(2,1)S(1)}, bf16[208,768]{1,0:T(8,128)(2,1)S(1)}, u32[]{:S(2)}, u32[]{:S(2)}) collective-permute-start(bf16[208,768]{1,0:T(8,128)(2,1)S(1)} %add_convert_fusion.8), channel_id=1, source_target_pairs={{8,0},{16,8},{24,16},{28,24},{20,28},{12,20},{4,12},{0,4},{9,1},{1... | collective-permute-start | bytes 958472 | tf_op jit(solution)/shard_map/ppermute | solution.py:463
  349.0 28.5 %collective-permute-start.63 = (bf16[208,768]{1,0:T(8,128)(2,1)S(1)}, bf16[208,768]{1,0:T(8,128)(2,1)S(1)}, u32[]{:S(2)}, u32[]{:S(2)}) collective-permute-start(bf16[208,768]{1,0:T(8,128)(2,1)S(1)} %add_convert_fusion.15), channel_id=1, source_target_pairs={{0,8},{8,16},{16,24},{24,28},{28,20},{20,12},{12,4},{4,0},{1,9},{9... | collective-permute-start | bytes 958472 | tf_op jit(solution)/shard_map/ppermute | solution.py:463
  370.3 186.9 %collective-permute-start.87 = (bf16[2,2,768,768]{3,2,1,0:T(8,128)(2,1)}, bf16[2,2,768,768]{3,2,1,0:T(8,128)(2,1)}, u32[]{:S(2)}, u32[]{:S(2)}) collective-permute-start(bf16[2,2,768,768]{3,2,1,0:T(8,128)(2,1)} %expert_grads.3), channel_id=1, source_target_pairs={{0,1},{1,0},{2,3},{3,2},{4,5},{5,4},{6,7},{7,6},{8,9},{9,8},{10,11... | collective-permute-start | bytes 14155784 | tf_op jit(solution)/shard_map/ppermute | solution.py:473
  392.2 22.4 %collective-permute-start.54 = (bf16[208,768]{1,0:T(8,128)(2,1)S(1)}, bf16[208,768]{1,0:T(8,128)(2,1)S(1)}, u32[]{:S(2)}, u32[]{:S(2)}) collective-permute-start(bf16[208,768]{1,0:T(8,128)(2,1)S(1)} %add_convert_fusion.21), channel_id=1, source_target_pairs={{8,0},{16,8},{24,16},{28,24},{20,28},{12,20},{4,12},{0,4},{9,1},{1... | collective-permute-start | bytes 958472 | tf_op jit(solution)/shard_map/ppermute | solution.py:463
  403.9 23.0 %collective-permute-start.48 = (bf16[208,768]{1,0:T(8,128)(2,1)S(1)}, bf16[208,768]{1,0:T(8,128)(2,1)S(1)}, u32[]{:S(2)}, u32[]{:S(2)}) collective-permute-start(bf16[208,768]{1,0:T(8,128)(2,1)S(1)} %add_convert_fusion.26), channel_id=1, source_target_pairs={{0,8},{8,16},{16,24},{24,28},{28,20},{20,12},{12,4},{4,0},{1,9},{9... | collective-permute-start | bytes 958472 | tf_op jit(solution)/shard_map/ppermute | solution.py:463
  415.4 65.1 %collective-permute-start.55 = (bf16[208,768]{1,0:T(8,128)(2,1)}, bf16[208,768]{1,0:T(8,128)(2,1)}, u32[]{:S(2)}, u32[]{:S(2)}) collective-permute-start(bf16[208,768]{1,0:T(8,128)(2,1)} %add_convert_fusion.20), channel_id=1, source_target_pairs={{8,0},{16,8},{24,16},{28,24},{20,28},{12,20},{4,12},{0,4},{9,1},{1... | collective-permute-start | bytes 958472 | tf_op jit(solution)/shard_map/ppermute | solution.py:463
  427.7 55.6 %collective-permute-start.49 = (bf16[208,768]{1,0:T(8,128)(2,1)}, bf16[208,768]{1,0:T(8,128)(2,1)}, u32[]{:S(2)}, u32[]{:S(2)}) collective-permute-start(bf16[208,768]{1,0:T(8,128)(2,1)} %add_convert_fusion.25), channel_id=1, source_target_pairs={{0,8},{8,16},{16,24},{24,28},{28,20},{20,12},{12,4},{4,0},{1,9},{9... | collective-permute-start | bytes 958472 | tf_op jit(solution)/shard_map/ppermute | solution.py:463
  480.6 37.7 %collective-permute-start.78 = (bf16[2,8,112,768]{3,2,1,0:T(8,128)(2,1)}, bf16[2,8,112,768]{3,2,1,0:T(8,128)(2,1)}, u32[]{:S(2)}, u32[]{:S(2)}) collective-permute-start(bf16[2,8,112,768]{3,2,1,0:T(8,128)(2,1)} %copy.71), channel_id=1, source_target_pairs={{0,1},{1,0},{2,3},{3,2},{4,5},{5,4},{6,7},{7,6},{8,9},{9,8},{10,11... | collective-permute-start | bytes 8257544 | tf_op jit(solution)/shard_map/ppermute | solution.py:473
  512.3 37.9 %collective-permute-start.76 = (bf16[394,768]{1,0:T(8,128)(2,1)}, bf16[394,768]{1,0:T(8,128)(2,1)}, u32[]{:S(2)}, u32[]{:S(2)}) collective-permute-start(bf16[394,768]{1,0:T(8,128)(2,1)} %get-tuple-element.211), channel_id=1, source_target_pairs={{0,2},{1,3},{2,0},{3,1},{4,6},{5,7},{6,4},{7,5},{8,10},{9,11},{10,... | collective-permute-start | bytes 1815560 | tf_op jit(solution)/shard_map/ppermute | solution.py:473
  518.3 35.2 %collective-permute-start.60 = (bf16[394,768]{1,0:T(8,128)(2,1)}, bf16[394,768]{1,0:T(8,128)(2,1)}, u32[]{:S(2)}, u32[]{:S(2)}) collective-permute-start(bf16[394,768]{1,0:T(8,128)(2,1)} %get-tuple-element.213), channel_id=1, source_target_pairs={{0,2},{1,3},{2,0},{3,1},{4,6},{5,7},{6,4},{7,5},{8,10},{9,11},{10,... | collective-permute-start | bytes 1815560 | tf_op jit(solution)/shard_map/ppermute | solution.py:473
  529.1 39.5 %collective-permute-start.79 = (bf16[8,112,768]{2,1,0:T(8,128)(2,1)}, bf16[8,112,768]{2,1,0:T(8,128)(2,1)}, u32[]{:S(2)}, u32[]{:S(2)}) collective-permute-start(bf16[8,112,768]{2,1,0:T(8,128)(2,1)} %copy.73), channel_id=1, source_target_pairs={{0,2},{1,3},{2,0},{3,1},{4,6},{5,7},{6,4},{7,5},{8,10},{9,11},{10,... | collective-permute-start | bytes 4128776 | tf_op jit(solution)/shard_map/ppermute | solution.py:473
  553.5 50.7 %collective-permute-start.77 = (bf16[2,394,768]{2,0,1:T(2,128)(2,1)}, bf16[2,394,768]{2,0,1:T(2,128)(2,1)}, u32[]{:S(2)}, u32[]{:S(2)}) collective-permute-start(bf16[2,394,768]{2,0,1:T(2,128)(2,1)} %copy.66), channel_id=1, source_target_pairs={{0,1},{1,0},{2,3},{3,2},{4,5},{5,4},{6,7},{7,6},{8,9},{9,8},{10,11... | collective-permute-start | bytes 3631112 | tf_op jit(solution)/shard_map/ppermute | solution.py:473
  556.8 55.4 %collective-permute-start.61 = (bf16[2,394,768]{2,0,1:T(2,128)(2,1)}, bf16[2,394,768]{2,0,1:T(2,128)(2,1)}, u32[]{:S(2)}, u32[]{:S(2)}) collective-permute-start(bf16[2,394,768]{2,0,1:T(2,128)(2,1)} %copy.63), channel_id=1, source_target_pairs={{0,1},{1,0},{2,3},{3,2},{4,5},{5,4},{6,7},{7,6},{8,9},{9,8},{10,11... | collective-permute-start | bytes 3631112 | tf_op jit(solution)/shard_map/ppermute | solution.py:473
  575.6 61.4 %collective-permute-start.88 = (bf16[2,768,768]{2,1,0:T(8,128)(2,1)}, bf16[2,768,768]{2,1,0:T(8,128)(2,1)}, u32[]{:S(2)}, u32[]{:S(2)}) collective-permute-start(bf16[2,768,768]{2,1,0:T(8,128)(2,1)} %slice_bitcast_fusion), channel_id=1, source_target_pairs={{0,2},{1,3},{2,0},{3,1},{4,6},{5,7},{6,4},{7,5},{8,10},{9,11},{10,... | collective-permute-start | bytes 7077896 | tf_op jit(solution)/shard_map/ppermute | solution.py:473
  575.9 25.9 %collective-permute-start.84 = (bf16[112,768]{0,1:T(8,128)(2,1)S(1)}, bf16[112,768]{0,1:T(8,128)(2,1)S(1)}, u32[]{:S(2)}, u32[]{:S(2)}) collective-permute-start(bf16[112,768]{0,1:T(8,128)(2,1)S(1)} %get-tuple-element.203), channel_id=1, source_target_pairs={{8,0},{16,8},{24,16},{28,24},{20,28},{12,20},{4,12},{0,4},{9,1},{1... | collective-permute-start | bytes 516104 | tf_op jit(solution)/shard_map/ppermute | solution.py:463
  610.1 22.7 %collective-permute-start.83 = (bf16[112,768]{0,1:T(8,128)(2,1)}, bf16[112,768]{0,1:T(8,128)(2,1)}, u32[]{:S(2)}, u32[]{:S(2)}) collective-permute-start(bf16[112,768]{0,1:T(8,128)(2,1)} %get-tuple-element.198), channel_id=1, source_target_pairs={{0,8},{8,16},{16,24},{24,28},{28,20},{20,12},{12,4},{4,0},{1,9},{9... | collective-permute-start | bytes 516104 | tf_op jit(solution)/shard_map/ppermute | solution.py:463
  610.4 22.4 %collective-permute-start.86 = (bf16[112,768]{0,1:T(8,128)(2,1)}, bf16[112,768]{0,1:T(8,128)(2,1)}, u32[]{:S(2)}, u32[]{:S(2)}) collective-permute-start(bf16[112,768]{0,1:T(8,128)(2,1)} %get-tuple-element.199), channel_id=1, source_target_pairs={{8,0},{16,8},{24,16},{28,24},{20,28},{12,20},{4,12},{0,4},{9,1},{1... | collective-permute-start | bytes 516104 | tf_op jit(solution)/shard_map/ppermute | solution.py:463
  640.6 34.6 %collective-permute-start.90 = (bf16[2,96,768]{2,1,0:T(8,128)(2,1)S(1)}, bf16[2,96,768]{2,1,0:T(8,128)(2,1)S(1)}, u32[]{:S(2)}, u32[]{:S(2)}) collective-permute-start(bf16[2,96,768]{2,1,0:T(8,128)(2,1)S(1)} %get-tuple-element.179), channel_id=1, source_target_pairs={{0,8},{4,12},{8,16},{12,20},{16,24},{20,28},{24,0},{28,4},{1,9},{5... | collective-permute-start | bytes 884744 | tf_op jit(solution)/shard_map/ppermute | solution.py:467
  644.7 38.4 %collective-permute-start.91 = (bf16[2,96,768]{2,1,0:T(8,128)(2,1)S(1)}, bf16[2,96,768]{2,1,0:T(8,128)(2,1)S(1)}, u32[]{:S(2)}, u32[]{:S(2)}) collective-permute-start(bf16[2,96,768]{2,1,0:T(8,128)(2,1)S(1)} %get-tuple-element.178), channel_id=1, source_target_pairs={{0,12},{4,16},{8,20},{12,24},{16,28},{20,0},{24,4},{28,8},{1,13},{... | collective-permute-start | bytes 884744 | tf_op jit(solution)/shard_map/ppermute | solution.py:467
  645.7 37.6 %collective-permute-start.92 = (bf16[2,96,768]{2,1,0:T(8,128)(2,1)S(1)}, bf16[2,96,768]{2,1,0:T(8,128)(2,1)S(1)}, u32[]{:S(2)}, u32[]{:S(2)}) collective-permute-start(bf16[2,96,768]{2,1,0:T(8,128)(2,1)S(1)} %get-tuple-element.177), channel_id=1, source_target_pairs={{0,16},{4,20},{8,24},{12,28},{16,0},{20,4},{24,8},{28,12},{1,17},{... | collective-permute-start | bytes 884744 | tf_op jit(solution)/shard_map/ppermute | solution.py:467
  648.0 35.5 %collective-permute-start.93 = (bf16[2,96,768]{2,1,0:T(8,128)(2,1)S(1)}, bf16[2,96,768]{2,1,0:T(8,128)(2,1)S(1)}, u32[]{:S(2)}, u32[]{:S(2)}) collective-permute-start(bf16[2,96,768]{2,1,0:T(8,128)(2,1)S(1)} %get-tuple-element.176), channel_id=1, source_target_pairs={{0,20},{4,24},{8,28},{12,0},{16,4},{20,8},{24,12},{28,16},{1,21},{... | collective-permute-start | bytes 884744 | tf_op jit(solution)/shard_map/ppermute | solution.py:467
  648.6 34.9 %collective-permute-start.94 = (bf16[2,96,768]{2,1,0:T(8,128)(2,1)S(1)}, bf16[2,96,768]{2,1,0:T(8,128)(2,1)S(1)}, u32[]{:S(2)}, u32[]{:S(2)}) collective-permute-start(bf16[2,96,768]{2,1,0:T(8,128)(2,1)S(1)} %get-tuple-element.175), channel_id=1, source_target_pairs={{0,24},{4,28},{8,0},{12,4},{16,8},{20,12},{24,16},{28,20},{1,25},{... | collective-permute-start | bytes 884744 | tf_op jit(solution)/shard_map/ppermute | solution.py:467
  (156 other events, 2540.2 us)

commit v2 on v1

--- a/solution.py
+++ b/solution.py
@@ -53,10 +53,24 @@
     )
 
 
+def load_attn_weights(order_ref, wa_ref, wb_ref, w_s, sem):
+    rows = D // E
+    copies = []
+    for r in range(4):
+        src = wa_ref if r < 2 else wb_ref
+        for b in range(E):
+            at = pl.ds(pl.multiple_of(order_ref[b] * rows, 16), rows)
+            copies.append(pltpu.make_async_copy(src.at[r % 2, b, pl.ds(0, rows)], w_s.at[r, at], sem.at[r, b]))
+            copies[-1].start()
+    return [copies[r * E : (r + 1) * E] for r in range(4)]
+
+
 def attn_forward_kernel(
-    x_ref, par_ref, wa_ref, wb_ref, noise_ref, keep_ref,
+    order_ref, x_ref, par_ref, wa_ref, wb_ref, noise_ref, keep_ref,
     chunk_ref, x1_ref, qkv_ref, o_ref, lse_ref, probs_ref,
+    w_s, sem,
 ):
+    copies = load_attn_weights(order_ref, wa_ref, wb_ref, w_s, sem)
     par = par_ref[...].astype(F32)
     x = x_ref[...].astype(F32)
     unit, _ = normalise(x)
@@ -66,7 +80,9 @@
     key_ok = iota((PAD, PAD), 1) < SEQ
     lane = iota((PAD, 128), 1)
     for r in range(4):
-        w = wa_ref[r] if r < 2 else wb_ref[r - 2]
+        for copy in copies[r]:
+            copy.wait()
+        w = w_s[r]
         qkv = dot(h1, w[:, : 9 * HD]).astype(BF16)
         qkv_ref[r] = qkv
         outs = []
@@ -98,8 +114,10 @@
     chunk_ref[PAD - 16 :, :] = jnp.concatenate([low[:8], tail], axis=0).astype(BF16)
 
 
-def attn_forward(x, par, wa, wb, noise, keep):
+def attn_forward(order, x, par, wa, wb, noise, keep):
     vm = pl.BlockSpec(memory_space=pltpu.VMEM)
+    hbm = pl.BlockSpec(memory_space=pl.ANY)
+    sm = pl.BlockSpec(memory_space=pltpu.SMEM)
     return pl.pallas_call(
         attn_forward_kernel,
         out_shape=(
@@ -110,26 +128,33 @@
             jax.ShapeDtypeStruct((PAD, 128), F32),
             jax.ShapeDtypeStruct((E, PAD), F32),
         ),
-        in_specs=[vm] * 6,
+        in_specs=[sm, vm, vm, hbm, hbm, vm, vm],
         out_specs=(vm,) * 6,
+        scratch_shapes=[pltpu.VMEM((4, D, D), BF16), pltpu.SemaphoreType.DMA((4, E))],
         compiler_params=pltpu.CompilerParams(vmem_limit_bytes=VMEM_LIMIT),
         cost_estimate=pl.CostEstimate(flops=3 * 10**9, bytes_accessed=10**7, transcendentals=10**6),
         name="attn_forward",
-    )(x, par, wa, wb, noise, keep)
-
-
-def expert_kernel(nb, me_ref, *refs):
-    h_in, dy_in = refs[:nb], refs[nb : 2 * nb]
-    wa_ref, wb_ref = refs[2 * nb : 2 * nb + 2]
-    outs = refs[2 * nb + 2 :]
-    y_out, dx_out = outs[:nb], outs[nb : 2 * nb]
-    rows_out, hid_out, tiles_ref = outs[2 * nb : 2 * nb + 3]
-    (h, dy, y_t, dx_t, gate_s, slot_s, dgate_s, xs, dys, hid_s, rows_s, lo_s, hi_s, in_sem, out_sem, row_sem, hid_sem) = outs[2 * nb + 3 :]
-    me = me_ref[0]
+    )(order, x, par, wa, wb, noise, keep)
+
+
+def expert_kernel(nb, who_ref, *refs):
+    h_in = refs[:nb]
+    dy_in, w_in = refs[nb], refs[nb + 1 : nb + 5]
+    outs = refs[nb + 5 :]
+    dx_out = outs[:nb]
+    y_out, rows_out, hid_out, tiles_ref = outs[nb : nb + 4]
+    (h, dy, y_t, dx_t, w_s, gate_s, slot_s, dgate_s, xs, dys, hid_s, rows_s, lo_s, hi_s, in_sem, out_sem, row_sem, hid_sem, w_sem) = outs[nb + 4 :]
+    me = who_ref[nb]
     loads = []
     for b in range(nb):
-        for ref, table, c in ((h_in[b], h, 0), (dy_in[b], dy, 1)):
+        for ref, table, c in ((h_in[b], h, 0), (dy_in.at[who_ref[b]], dy, 1)):
             copy = pltpu.make_async_copy(ref, table.at[b], in_sem.at[c, b])
+            copy.start()
+            loads.append(copy)
+    for b in range(E):
+        at = pl.ds(pl.multiple_of(who_ref[nb + 1 + b] * (D // E), 16), D // E)
+        for r in range(4):
+            copy = pltpu.make_async_copy(w_in[r].at[b], w_s.at[r, :, at], w_sem.at[r, b])
             copy.start()
             loads.append(copy)
     y_t[...] = jnp.zeros_like(y_t)
@@ -195,7 +220,7 @@
         y = jnp.zeros((TILE, D), F32)
         dx = jnp.zeros((TILE, D), F32)
         for r in range(4):
-            w1, w2 = (wa_ref.at[r, 0], wa_ref.at[r, 1]) if r < 2 else (wb_ref.at[r - 2, 0], wb_ref.at[r - 2, 1])
+            w1, w2 = w_s.at[r, 0], w_s.at[r, 1]
             a = dot(x, w1[...])
             a2 = a * a
             th = jnp.tanh(0.7978845608028654 * a * (1.0 + 0.044715 * a2))
@@ -242,7 +267,7 @@
         tail = dx_t[b, PAD - 16 : PAD, :].astype(F32)
         line = jnp.concatenate([dgate_s[b : b + 1, :], jnp.zeros((1, D - PAD), F32)], axis=1)
         dx_t[b, PAD - 16 : PAD, :] = (tail + jnp.where(row16 == 8 + me, line, 0.0)).astype(BF16)
-        for table, ref, c in ((y_t, y_out[b], 0), (dx_t, dx_out[b], 1)):
+        for table, ref, c in ((y_t, y_out.at[who_ref[b]], 0), (dx_t, dx_out[b], 1)):
             copy = pltpu.make_async_copy(table.at[b], ref, out_sem.at[c, b])
             copy.start()
             stores.append(copy)
@@ -254,28 +279,29 @@
     return -(-nb * SEQ // TILE) * TILE
 
 
-def experts(me, h_blocks, dy_blocks, wa, wb):
+def experts(who, h_blocks, dy_all, weights):
     nb = len(h_blocks)
     rows = expert_rows(nb)
     hbm = pl.BlockSpec(memory_space=pl.ANY)
-    vm = pl.BlockSpec(memory_space=pltpu.VMEM)
     sm = pl.BlockSpec(memory_space=pltpu.SMEM)
     block = jax.ShapeDtypeStruct((PAD, D), BF16)
     outs = pl.pallas_call(
         functools.partial(expert_kernel, nb),
-        out_shape=[block] * (2 * nb)
+        out_shape=[block] * nb
         + [
+            jax.ShapeDtypeStruct((nb, PAD, D), BF16),
             jax.ShapeDtypeStruct((2, rows, D), BF16),
             jax.ShapeDtypeStruct((2, rows, 4 * FFS), BF16),
             jax.ShapeDtypeStruct((1,), jnp.int32),
         ],
-        in_specs=[sm] + [hbm] * (2 * nb) + [vm, vm],
-        out_specs=[hbm] * (2 * nb + 2) + [sm],
+        in_specs=[sm] + [hbm] * (nb + 5),
+        out_specs=[hbm] * (nb + 3) + [sm],
         scratch_shapes=[
             pltpu.VMEM((nb, PAD, D), BF16),
             pltpu.VMEM((nb, PAD, D), BF16),
             pltpu.VMEM((nb, PAD, D), BF16),
             pltpu.VMEM((nb, PAD, D), BF16),
+            pltpu.VMEM((4, 2, D, FFS), BF16),
             pltpu.VMEM((nb, PAD), F32),
             pltpu.VMEM((nb, PAD), jnp.int32),
             pltpu.VMEM((nb, PAD), F32),
@@ -289,12 +315,13 @@
             pltpu.SemaphoreType.DMA((2, nb)),
             pltpu.SemaphoreType.DMA((2,)),
             pltpu.SemaphoreType.DMA((2,)),
+            pltpu.SemaphoreType.DMA((4, E)),
         ],
         compiler_params=pltpu.CompilerParams(vmem_limit_bytes=VMEM_LIMIT),
         cost_estimate=pl.CostEstimate(flops=30 * 10**9, bytes_accessed=4 * 10**7, transcendentals=4 * 10**6),
         name="experts",
-    )(me.reshape(1), *h_blocks, *dy_blocks, wa, wb)
-    return outs[:nb], outs[nb : 2 * nb], outs[2 * nb], outs[2 * nb + 1], outs[2 * nb + 2]
+    )(who, *h_blocks, dy_all, *weights)
+    return outs[:nb], *outs[nb:]
 
 
 def expert_grad_kernel(tiles_ref, rows_ref, hid_ref, out_ref, acc):
@@ -306,37 +333,88 @@
         return carry
 
     lax.fori_loop(0, tiles_ref[0], step, 0)
-    out_ref[0, 0] = acc[...].astype(BF16)
-
-
-def expert_grads(tiles, rows, hid, base):
+    out_ref[0] = acc[...].astype(BF16)
+
+
+def expert_grads(tiles, rows, hid, kind, base):
     n = rows.shape[1]
     return pl.pallas_call(
         expert_grad_kernel,
         grid_spec=pltpu.PrefetchScalarGridSpec(
             num_scalar_prefetch=1,
-            grid=(2, 2),
+            grid=(2,),
             in_specs=[
-                pl.BlockSpec((1, n, D), lambda k, s, _: (k, 0, 0)),
-                pl.BlockSpec((1, n, FFS), lambda k, s, _: (k, 0, base + s)),
+                pl.BlockSpec((1, n, D), lambda s, _: (kind, 0, 0)),
+                pl.BlockSpec((1, n, FFS), lambda s, _: (kind, 0, base + s)),
             ],
-            out_specs=pl.BlockSpec((1, 1, D, FFS), lambda k, s, _: (s, k, 0, 0)),
+            out_specs=pl.BlockSpec((1, D, FFS), lambda s, _: (s, 0, 0)),
             scratch_shapes=[pltpu.VMEM((D, FFS), F32)],
         ),
-        out_shape=jax.ShapeDtypeStruct((2, 2, D, FFS), BF16),
+        out_shape=jax.ShapeDtypeStruct((2, D, FFS), BF16),
         compiler_params=pltpu.CompilerParams(vmem_limit_bytes=VMEM_LIMIT),
-        cost_estimate=pl.CostEstimate(flops=8 * 10**9, bytes_accessed=3 * 10**7, transcendentals=0),
+        cost_estimate=pl.CostEstimate(flops=4 * 10**9, bytes_accessed=15 * 10**6, transcendentals=0),
         name="expert_grads",
     )(tiles, rows, hid)
+
+
+def unpack_kernel(who_ref, *refs):
+    blocks, out_ref = refs[:E], refs[E]
+    for by in range(E):
+        out_ref[who_ref[by]] = blocks[by][...].astype(F32)
+
+
+def unpack(who, blocks):
+    vm = pl.BlockSpec(memory_space=pltpu.VMEM)
+    return pl.pallas_call(
+        unpack_kernel,
+        out_shape=jax.ShapeDtypeStruct((E,) + blocks[0].shape, F32),
+        in_specs=[pl.BlockSpec(memory_space=pltpu.SMEM)] + [vm] * E,
+        out_specs=vm,
+        compiler_params=pltpu.CompilerParams(vmem_limit_bytes=VMEM_LIMIT),
+        cost_estimate=pl.CostEstimate(flops=10**6, bytes_accessed=4 * 10**6, transcendentals=0),
+        name="unpack",
+    )(who, *blocks)
+
+
+def lay_out_kernel(imgs, at_ref, *refs):
+    parts, out_ref, held, sem = refs[:4], refs[4], refs[5], refs[6]
+    copies = [pltpu.make_async_copy(parts[s], held.at[s], sem.at[s]) for s in range(4)]
+    for copy in copies:
+        copy.start()
+    for copy in copies:
+        copy.wait()
+    for i in range(4 * imgs):
+        out_ref[i * SEQ : (i + 1) * SEQ, :] = held[at_ref[i // imgs], i % imgs, :SEQ, :]
+
+
+def lay_out(at, parts):
+    imgs = parts[0].shape[0]
+    hbm = pl.BlockSpec(memory_space=pl.ANY)
+    return pl.pallas_call(
+        functools.partial(lay_out_kernel, imgs),
+        out_shape=jax.ShapeDtypeStruct((4 * imgs * SEQ, D), BF16),
+        in_specs=[pl.BlockSpec(memory_space=pltpu.SMEM)] + [hbm] * 4,
+        out_specs=pl.BlockSpec(memory_space=pltpu.VMEM),
+        scratch_shapes=[pltpu.VMEM((4, imgs, PAD, D), BF16), pltpu.SemaphoreType.DMA((4,))],
+        compiler_params=pltpu.CompilerParams(vmem_limit_bytes=VMEM_LIMIT),
+        cost_estimate=pl.CostEstimate(flops=10**6, bytes_accessed=5 * 10**6, transcendentals=0),
+        name="lay_out",
+    )(at, *parts)
 
 
 def attn_backward_kernel(imgs, *refs):
     dh_in, x1_in, x_in, dy_in, probs_in, qkv_in, o_in, lse_in = (
         refs[i * imgs : (i + 1) * imgs] for i in range(8)
     )
-    par_ref, wa_ref, wb_ref = refs[8 * imgs : 8 * imgs + 3]
-    grads_ref, small_ref, dtok_ref = refs[8 * imgs + 3 : 8 * imgs + 6]
-    dx1_s, low_s, h1_s, dh1_s, dqkv_s, o_s = refs[8 * imgs + 6 :]
+    order_ref, par_ref, wa_ref, wb_ref = refs[8 * imgs : 8 * imgs + 4]
+    packs, dtok_ref = refs[8 * imgs + 4 : 8 * imgs + 7], refs[8 * imgs + 7]
+    dx1_s, low_s, h1_s, dh1_s, dqkv_s, o_s, w_s, sem = refs[8 * imgs + 8 :]
+    n_dp, d_own = packs[0].shape[0], packs[0].shape[1] - 16
+    copies = load_attn_weights(order_ref, wa_ref, wb_ref, w_s, sem)
+
+    def pack_of(r):
+        return packs[r] if r < 2 else packs[2].at[:, r - 2]
+
     par = par_ref[...].astype(F32)
     router = par_ref[8:16, :]
     row_ok = iota((PAD, 1), 0) < SEQ
@@ -366,7 +444,9 @@
     low = low_s[...]
     h1 = h1_s[...]
     for r in range(4):
-        w = wa_ref[r] if r < 2 else wb_ref[r - 2]
+        for copy in copies[r]:
+            copy.wait()
+        w = w_s[r]
         dout = dot(low, w[:, 9 * HD :]).astype(BF16)
         for c in range(imgs):
             span = slice(c * PAD, (c + 1) * PAD)
@@ -390,7 +470,9 @@
         dqkv = dqkv_s[...]
         part = dot_nt(dqkv, w[:, : 9 * HD])
         dh1_s[...] = part if r == 0 else dh1_s[...] + part
-        grads_ref[r] = jnp.concatenate([dot_tn(h1, dqkv), dot_tn(low, o_s[...])], axis=1).astype(BF16)
+        grad = jnp.concatenate([dot_tn(h1, dqkv), dot_tn(low, o_s[...])], axis=1).astype(BF16)
+        for i in range(n_dp):
+            pack_of(r)[i, :d_own, :] = grad[i * d_own : (i + 1) * d_own]
     small1g = jnp.zeros((1, D), F32)
     small1b = jnp.zeros((1, D), F32)
     for c in range(imgs):
@@ -400,24 +482,30 @@
         small1g = small1g + jnp.sum(dh1 * unit1, axis=0, keepdims=True)
         small1b = small1b + jnp.sum(dh1, axis=0, keepdims=True)
         dtok_ref[c] = (dx1_s[span, :] + norm_back(dh1, unit1, scale1, par[0:1])).astype(BF16)
-    small_ref[...] = jnp.concatenate(
-        [small1g, small1b, small2g, small2b, jnp.zeros((4, D), F32), g_router], axis=0
-    ).astype(BF16)
-
-
-def attn_backward(dh, x1, x, dy, probs, qkv, o, lse, par, wa, wb):
+    small = jnp.concatenate([small1g, small1b, small2g, small2b, jnp.zeros((4, D), F32), g_router], axis=0)
+    for i in range(n_dp):
+        line = jnp.concatenate([small[:, i * d_own : (i + 1) * d_own], jnp.zeros((16, D - d_own), F32)], axis=1)
+        for r in range(4):
+            pack_of(r)[i, d_own:, :] = line.astype(BF16)
+
+
+def attn_backward(dh, x1, x, dy, probs, qkv, o, lse, order, par, wa, wb, n_dp):
     imgs = len(dh)
+    hbm = pl.BlockSpec(memory_space=pl.ANY)
+    sm = pl.BlockSpec(memory_space=pltpu.SMEM)
+    pack = (n_dp, D // n_dp + 16, D)
     vm = pl.BlockSpec(memory_space=pltpu.VMEM)
     rows = imgs * PAD
     return pl.pallas_call(
         functools.partial(attn_backward_kernel, imgs),
         out_shape=(
-            jax.ShapeDtypeStruct((4, D, D), BF16),
-            jax.ShapeDtypeStruct((16, D), BF16),
+            jax.ShapeDtypeStruct(pack, BF16),
+            jax.ShapeDtypeStruct(pack, BF16),
+            jax.ShapeDtypeStruct((n_dp, 2) + pack[1:], BF16),
             jax.ShapeDtypeStruct((imgs, PAD, D), BF16),
         ),
-        in_specs=[vm] * (8 * imgs + 3),
-        out_specs=(vm,) * 3,
+        in_specs=[vm] * (8 * imgs) + [sm, vm, hbm, hbm],
+        out_specs=(vm,) * 4,
         scratch_shapes=[
             pltpu.VMEM((rows, D), F32),
             pltpu.VMEM((rows, D), BF16),
@@ -425,11 +513,13 @@
             pltpu.VMEM((rows, D), F32),
             pltpu.VMEM((rows, 9 * HD), BF16),
             pltpu.VMEM((rows, 3 * HD), BF16),
+            pltpu.VMEM((4, D, D), BF16),
+            pltpu.SemaphoreType.DMA((4, E)),
         ],
         compiler_params=pltpu.CompilerParams(vmem_limit_bytes=VMEM_LIMIT),
         cost_estimate=pl.CostEstimate(flops=12 * 10**9, bytes_accessed=2 * 10**7, transcendentals=2 * 10**6),
         name="attn_backward",
-    )(*dh, *x1, *x, *dy, *probs, *qkv, *o, *lse, par, wa, wb)
+    )(*dh, *x1, *x, *dy, *probs, *qkv, *o, *lse, order, par, wa, wb)
 
 
 RING = (0, 2, 4, 6, 7, 5, 3, 1)
@@ -476,6 +566,19 @@
         step = -k if way == 0 else k
         return ring_member(lax.rem(self.place + step + E, E))
 
+    def group_lists(self):
+        if self.groups == 1:
+            return None
+        return [[b + i for i in range(E)] for b in range(0, self.n_dp, E)]
+
+    def gather(self, value):
+        return lax.all_gather(value, "dp", axis=0, tiled=False, axis_index_groups=self.group_lists())
+
+    def scatter_sum(self, value):
+        return lax.psum_scatter(
+            value, "dp", scatter_dimension=0, tiled=False, axis_index_groups=self.group_lists()
+        )
+
     def ring_blocks(self, block, way):
         blocks = [block]
         for _ in range(E - 1):
@@ -502,7 +605,7 @@
 
     def sum_both_ways(self, block_for):
         def chain(way, steps):
-            total = block_for(self.behind(1 - way, steps))
+            total = block_for(self.behind(1 - way, steps)).astype(BF16)
             for k in range(steps - 1, -1, -1):
                 total = self.along(total, way)
                 if k:
@@ -512,6 +615,17 @@
         ahead = chain(0, E // 2)
         back = chain(1, E // 2 - 1)
         return ahead.astype(F32) + back.astype(F32) + block_for(self.member).astype(F32)
+
+    def in_order(self, members, parts, d_own):
+        if self.groups == 1:
+            return jnp.stack(members), jnp.stack([jnp.stack(blocks) for blocks in parts])
+        wholes = []
+        for blocks in parts:
+            rows = jnp.zeros((E * d_own,) + blocks[0].shape[1:], BF16)
+            for member, block in zip(members, blocks):
+                rows = lax.dynamic_update_slice_in_dim(rows, block[:d_own], member * d_own, 0)
+            wholes.append(self.all_groups(rows, 0).reshape((E, D // E) + blocks[0].shape[1:]))
+        return jnp.arange(E, dtype=jnp.int32), jnp.stack(wholes)
 
     def all_groups(self, part, dim):
         if self.groups == 1:
@@ -534,6 +648,15 @@
             part = lax.dynamic_slice_in_dim(whole, to * size, size, dim)
             total = total + self.shift_group(part, by).astype(F32)
         return total.astype(whole.dtype)
+
+
+def after(value, *first):
+    return lax.optimization_barrier((value, first))[0]
+
+
+def _slot(tensor, t):
+    apart = lax.bitwise_xor(tensor, t)
+    return lax.div(apart, 2) + 2 * lax.rem(apart, 2)
 
 
 def image_blocks(rows, tensor, imgs):
@@ -588,85 +711,98 @@
     small = jnp.concatenate([vectors, jnp.transpose(router_weight)], axis=0).astype(BF16)
     small = jnp.pad(small, ((0, 0), (0, D - d_own)))
     pack = jnp.concatenate([pack, small], axis=0)
-    w_own = jnp.zeros((E * d_own, D), BF16)
+    found = move.both_ways(pack)
     par = jnp.zeros((E, 16, d_own), BF16)
-    for member, block in move.both_ways(pack):
-        w_own = lax.dynamic_update_slice_in_dim(w_own, block[:d_own], member * d_own, 0)
+    for member, block in found:
         par = lax.dynamic_update_slice_in_dim(par, block[None, d_own:, :d_own], member, 0)
-    w_own = move.all_groups(w_own, 0)
-    par = move.all_groups(par, 0)
-    par = jnp.transpose(par, (1, 0, 2)).reshape(16, D)
-    wa = jnp.stack([w_own, move.other(w_own, 2)])
+    par = jnp.transpose(move.all_groups(par, 0), (1, 0, 2)).reshape(16, D)
+    order, wa = move.in_order(
+        [member for member, _ in found], [[b for _, b in found], [move.other(b, 2) for _, b in found]], d_own
+    )
     wb = move.other(wa, 1)
 
     x = image_blocks(tokens, move.tensor, imgs)
     dy = image_blocks(cotangent, move.tensor, imgs)
-    dy_ring = [move.ring_blocks(dy[c], ways[c]) for c in range(imgs)]
+    keep = image_lanes(kept_pairs(routes), move.tensor, imgs)
+    noise = image_lanes(jnp.transpose(router_noise), move.tensor, imgs)
     out_rows = jnp.transpose(w_expert_out, (0, 2, 1))
-    ew = jnp.zeros((2, E * d_own, FFS), BF16)
+    blocks = []
     for by in range(E):
         to = lax.rem(move.member + by, E)
-        block = jnp.stack(
-            [lax.dynamic_index_in_dim(w, to, 0, False).astype(BF16) for w in (w_in, out_rows)]
+        blocks.append(
+            jnp.stack([lax.dynamic_index_in_dim(w, to, 0, False).astype(BF16) for w in (w_in, out_rows)])
         )
-        came = lax.rem(move.member - by + E, E)
-        ew = lax.dynamic_update_slice_in_dim(ew, move.shift(block, by) if by else block, came * d_own, 1)
-    ew = move.all_groups(ew, 1)
-    ewa = jnp.stack([ew, move.other(ew, 2)])
-    ewb = move.other(ewa, 1)
-
-    keep = image_lanes(kept_pairs(routes), move.tensor, imgs)
-    noise = image_lanes(jnp.transpose(router_noise), move.tensor, imgs)
-    fwd = [attn_forward(x[c], par, wa, wb, noise[c], keep[c]) for c in range(imgs)]
+    blocks, dy_own, x, keep, noise, wb = lax.optimization_barrier((blocks, jnp.stack(dy), x, keep, noise, wb))
+    dy_all = move.gather(dy_own)
+    came = [lax.rem(move.member - by + E, E) for by in range(E)]
+    blocks = [move.shift(blocks[by], by) if by else blocks[by] for by in range(E)]
+
+    fwd = [attn_forward(order, x[c], par, wa, wb, noise[c], keep[c]) for c in range(imgs)]
     chunk, x1, qkv, o, lse, probs = (list(part) for part in zip(*fwd))
 
+    blocks = after(blocks, chunk)
+    e_order, e_own = move.in_order(came, [[b[kind] for b in blocks] for kind in range(2)], d_own)
+    e_own = jnp.swapaxes(e_own, 0, 1)
+    e_x = move.other(e_own, 2)
+    weights = [e_own, e_x, move.other(e_own, 1), move.other(e_x, 1)]
     h_ring = [move.ring_blocks(chunk[c], ways[c]) for c in range(imgs)]
-    y, dh, rows, hid, tiles = experts(
-        move.member, sum(h_ring, []), sum(dy_ring, []), ewa, ewb
+    who = [move.behind(ways[c], k) * imgs + c for c in range(imgs) for k in range(E)] + [move.member]
+    who = jnp.concatenate([jnp.stack(who), e_order])
+    dh, y_all, rows, hid, tiles = experts(who, sum(h_ring, []), dy_all.reshape(imgs * E, PAD, D), weights)
+    dh = [dh[c * E : (c + 1) * E] for c in range(imgs)]
+    dh_sum = [dh[c][1] for c in range(imgs)]
+    g_work = {3: (1, 2), 4: (1, 0), 5: (0, 2), 6: (0, 0)}
+    g_part = {}
+    for k in range(2, E + 1):
+        if k in g_work:
+            part = expert_grads(tiles, rows, hid, *g_work[k])
+            dh_sum, g_part[g_work[k]] = lax.optimization_barrier((dh_sum, part))
+        for c in range(imgs):
+            passed = move.along(dh_sum[c], ways[c])
+            dh_sum[c] = (passed.astype(F32) + dh[c][k % E].astype(F32)).astype(BF16)
+    y_all = after(y_all, dh_sum)
+    y_sum = move.scatter_sum(y_all.reshape(E, imgs, PAD, D))
+    g_exp = {}
+    for kind in (1, 0):
+        passed = move.other(g_part[kind, 2], 1).astype(F32)
+        pair = [(g_part[kind, 0][s].astype(F32) + passed[s]).astype(BF16) for s in range(2)]
+        total = (pair[0].astype(F32) + move.other(pair[1], 2).astype(F32)).astype(BF16)
+        total = move.sum_groups(total, 0)
+        blocks = []
+        for by in range(E):
+            to = lax.rem(move.member + by, E)
+            block = lax.dynamic_slice_in_dim(total, to * d_own, d_own, 0)
+            blocks.append(move.shift(block, by) if by else block)
+        g_exp[kind] = blocks
+
+    pack0, pack1, packs, d_tok = attn_backward(
+        dh_sum, x1, x, dy, probs, qkv, o, lse, order, par, wa, wb, n_dp
     )
-    dh_sum = [move.ring_sum(dh[c * E : (c + 1) * E], ways[c]) for c in range(imgs)]
-    y_sum = [move.ring_sum(y[c * E : (c + 1) * E], ways[c]) for c in range(imgs)]
-    grads_b = expert_grads(tiles, rows, hid, 2)
-    grads_a = expert_grads(tiles, rows, hid, 0)
-    pair = (grads_a.astype(F32) + move.other(grads_b, 1).astype(F32)).astype(BF16)
-    g_exp = (pair[0].astype(F32) + move.other(pair[1], 2).astype(F32)).astype(BF16)
-    g_exp = move.sum_groups(g_exp, 1)
-    g_in = jnp.zeros((E, d_own, FFS), F32)
-    g_out = jnp.zeros((E, d_own, FFS), F32)
-    for by in range(E):
-        to = lax.rem(move.member + by, E)
-        block = lax.dynamic_slice_in_dim(g_exp, to * d_own, d_own, 1)
-        came = lax.rem(move.member - by + E, E)
-        block = (move.shift(block, by) if by else block).astype(F32)
-        g_in = lax.dynamic_update_slice_in_dim(g_in, block[0:1], came, 0)
-        g_out = lax.dynamic_update_slice_in_dim(g_out, block[1:2], came, 0)
-
-    g_attn, g_small, d_tok = attn_backward(dh_sum, x1, x, dy, probs, qkv, o, lse, par, wa, wb)
-    spread = jnp.transpose(g_small.reshape(16, n_dp, d_own), (1, 0, 2))
-    spread = jnp.pad(spread, ((0, 0), (0, 0), (0, D - d_own)))
-    packs = jnp.concatenate(
-        [g_attn.reshape(4, n_dp, d_own, D), jnp.broadcast_to(spread[None], (4,) + spread.shape)], axis=2
-    )
-    pair = (packs[:2].astype(F32) + move.other(packs[2:], 1).astype(F32)).astype(BF16)
-    packs = (pair[0].astype(F32) + move.other(pair[1], 2).astype(F32)).astype(BF16)
-    packs = move.sum_groups(packs, 0)
-    total = move.sum_both_ways(lambda member: lax.dynamic_index_in_dim(packs, member, 0, False))
+    passed = move.other(packs, 1)
+    if move.groups > 1:
+        pack0 = move.sum_groups((pack0.astype(F32) + passed[:, 0].astype(F32)).astype(BF16), 0)
+        pack1 = move.sum_groups((pack1.astype(F32) + passed[:, 1].astype(F32)).astype(BF16), 0)
+        passed = jnp.zeros((E, 2) + pack0.shape[1:], BF16)
+
+    def pack_for(member):
+        one, two = (lax.dynamic_index_in_dim(p, member, 0, False).astype(F32) for p in (pack0, pack1))
+        came = lax.dynamic_index_in_dim(passed, member, 0, False).astype(F32)
+        return one + came[0] + move.other((two + came[1]).astype(BF16), 2).astype(F32)
+
+    total = move.sum_both_ways(pack_for)
     g_qkv = total[:d_own, : 9 * HD].reshape(d_own, 3, 3 * HD)
     g_attn_out = jnp.transpose(total[:d_own, 9 * HD :])
     g_small = total[d_own:, :d_own]
 
-    def all_rows(blocks):
-        own = jnp.concatenate([b[:SEQ] for b in blocks], axis=0)
-        n = own.shape[0]
-        two = jnp.stack([own, move.other(own, 2)])
-        four = jnp.concatenate([two, move.other(two, 1)], axis=0)
-        whole = jnp.zeros((4 * n, D), BF16)
-        for at, mask in enumerate((0, 2, 1, 3)):
-            whole = lax.dynamic_update_slice_in_dim(whole, four[at], (move.tensor ^ mask) * n, 0)
-        return whole
-
-    output = all_rows([(x1[c] + y_sum[c].astype(F32)).astype(BF16) for c in range(imgs)])
-    d_tokens = all_rows([d_tok[c] for c in range(imgs)])
+    at = jnp.stack([_slot(move.tensor, t) for t in range(4)])
+
+    def all_rows(own):
+        across = move.other(own, 2)
+        return lay_out(at, [own, across, move.other(own, 1), move.other(across, 1)])
+
+    d_tokens = all_rows(d_tok)
+    output = all_rows((jnp.stack(x1) + y_sum.astype(F32)).astype(BF16))
+    g_out, g_in = (unpack(jnp.stack(came), g_exp[kind]) for kind in (1, 0))
     return (
         output,
         d_tokens,

time: 699 us -> 630 us (0.901)
  local copies, waits for them, and re-layouts: 109 us -> 31.6 us
  other arithmetic: 60.4 us -> 35.3 us
  starting transfers between devices: 155 us -> 179 us
  between operations: 2.82 us -> 16.1 us
    ppermute x70 -> x42, waiting for transfers between devices: 161 us -> 77.7 us  [along(): return lax.ppermute(value, 'dp', self.ring[way])]
    ppermute x12 -> x31, waiting for transfers between devices: 51 us -> 109 us  [other(): return lax.ppermute(value, 'tensor', [(k, k ^ mask) for k in range(4)])]
    dynamic_update_slice x31 -> x0, local copies, waits for them, and re-layouts: 38.3 us -> none  [the longest x8 32.9 us: all_rows(): lax.dynamic_update_slice_in_dim(whole, four[at], (move.tensor ^ mask) * n...]
    ppermute x14 -> x21, waiting for transfers between devices: 8.98 us -> 31.4 us  [shift(): return lax.ppermute(value, 'dp', perm)]
    another operation x12 -> x6, other arithmetic: 23.5 us -> 6.61 us
    pallas_call x0 -> x4, Pallas kernels: none -> 14.3 us  [the longest x2 8.46 us: lay_out(): pl.pallas_call(functools.partial(lay_out_kernel, imgs), out_shape=jax.Sha...]
    pallas_call x1, Pallas kernels: 60 us -> 45.8 us  [experts(): pl.pallas_call(functools.partial(expert_kernel, nb), out_shape=[block] *...]
    slice x6 -> x1, local copies, waits for them, and re-layouts: 12.8 us -> 0.3 us  [the longest x2 7.49 us: all_rows(): four[at]]
  transfers between devices with their start and end apart: 96 -> 96, of which waited for: 41 -> 35; matrix products, arithmetic and copies ran while one was open for 22% -> 8% of each run, Pallas kernels for 12% -> 15%
where the time goes in v2:
time: 630 us; the launch traced here: 621 us
  waiting for transfers between devices  218 us (35%)
  starting transfers between devices  179 us (28%)
  Pallas kernels  141 us (22%)
  other arithmetic  35.3 us (6%)
  local copies, waits for them, and re-layouts  31.6 us (5%)
  between operations  16.1 us (3%)
    ppermute x31, waiting for transfers between devices, other(): return lax.ppermute(value, 'tensor', [(k, k ^ mask) for k in range(4)])  109 us
    ppermute x42, starting transfers between devices, along(): return lax.ppermute(value, 'dp', self.ring[way])  88.2 us
    ppermute x42, waiting for transfers between devices, along(): return lax.ppermute(value, 'dp', self.ring[way])  77.7 us
    ppermute x21, starting transfers between devices, shift(): return lax.ppermute(value, 'dp', perm)  70.5 us
    pallas_call x1, Pallas kernels, experts(): pl.pallas_call(functools.partial(expert_kernel, nb), out_shape=[block] *...  45.8 us
    pallas_call x4, Pallas kernels, expert_grads(): pl.pallas_call(expert_grad_kernel, grid_spec=pltpu.PrefetchScalarGridSpec...  37.6 us
    ppermute x21, waiting for transfers between devices, shift(): return lax.ppermute(value, 'dp', perm)  31.4 us
    pallas_call x1, Pallas kernels, attn_backward(): pl.pallas_call(functools.partial(attn_backward_kernel, imgs), out_shape=(...  26 us
  transfers between devices with their start and end apart: 96, of which 35 were waited for; matrix products, arithmetic and copies ran while one was open for 8% of the time, Pallas kernels for 15%

profile of v2, /device:TPU:24, one launch (start us, length us, event | category | flops | bytes accessed | tf_op | source)
XLA Modules:
  0.0 620.6 jit_solution(13033483538736558131)
XLA Ops:
  30.1 4.3 collective-permute-done.4
  80.1 7.9 %collective-permute-done.30 = bf16[2,96,768]{2,1,0:T(8,128)(2,1)S(1)} collective-permute-done((bf16[2,96,768]{2,1,0:T(8,128)(2,1)}, bf16[2,96,768]{2,1,0:T(8,128)(2,1)S(1)}, u32[]{:S(2)}, u32[]{:S(2)}) %collective-permute-start.30) | collective-permute-done | bytes 294944 | tf_op jit(solution)/shard_map/ppermute | solution.py:557
  88.0 4.3 collective-permute-done.31
  92.3 40.2 %collective-permute-start.36 = (bf16[2,96,768]{2,1,0:T(8,128)(2,1)S(1)}, bf16[2,96,768]{2,1,0:T(8,128)(2,1)S(1)}, u32[]{:S(2)}, u32[]{:S(2)}) collective-permute-start(bf16[2,96,768]{2,1,0:T(8,128)(2,1)S(1)} %get-tuple-element.103), channel_id=1, source_target_pairs={{0,28},{4,0},{8,4},{12,8},{16,12},{20,16},{24,20},{28,24},{1,29},{... | collective-permute-start | bytes 884744 | tf_op jit(solution)/shard_map/ppermute | solution.py:557
  132.5 8.5 %attn_forward.2 = (bf16[208,768]{1,0:T(8,128)(2,1)}, f32[208,768]{1,0:T(8,128)}, bf16[4,208,576]{2,1,0:T(8,128)(2,1)}, bf16[4,208,192]{2,1,0:T(8,128)(2,1)}, f32[208,128]{1,0:T(8,128)}, /*index=5*/f32[8,208]{1,0:T(8,128)}) custom-call(s32[8]{0:T(128)} %stack.300.order_ref.refs_16_, bf16[208,768]{1,0:T(8,128)(2,1)} %pad.35.x_ref.refs_4_, ...), custom_call_target="tpu_custom_call" | custom-call | flops 3000000000 | bytes 10000000 | tf_op jit(solution)/shard_map/attn_forward/pallas_call | solution.py:121
  141.0 8.7 %attn_forward.3 = (bf16[208,768]{1,0:T(8,128)(2,1)}, f32[208,768]{1,0:T(8,128)}, bf16[4,208,576]{2,1,0:T(8,128)(2,1)}, bf16[4,208,192]{2,1,0:T(8,128)(2,1)}, f32[208,128]{1,0:T(8,128)}, /*index=5*/f32[8,208]{1,0:T(8,128)}) custom-call(s32[8]{0:T(128)} %stack.300.order_ref.refs_16_, bf16[208,768]{1,0:T(8,128)(2,1)} %pad.36.x_ref.refs_5_, ...), custom_call_target="tpu_custom_call" | custom-call | flops 3000000000 | bytes 10000000 | tf_op jit(solution)/shard_map/attn_forward/pallas_call | solution.py:121
  150.4 46.3 %collective-permute-done.37.refs_18_ = bf16[8,2,96,768]{3,2,1,0:T(8,128)(2,1)} collective-permute-done((bf16[8,2,96,768]{3,2,1,0:T(8,128)(2,1)S(1)}, bf16[8,2,96,768]{3,2,1,0:T(8,128)(2,1)}, u32[]{:S(2)}, u32[]{:S(2)}) %collective-permute-start.37) | collective-permute-done | bytes 2359328 | tf_op jit(solution)/shard_map/ppermute | solution.py:563
  196.7 16.3 %collective-permute-start.16 = (bf16[208,768]{1,0:T(8,128)(2,1)S(1)}, bf16[208,768]{1,0:T(8,128)(2,1)S(1)}, u32[]{:S(2)}, u32[]{:S(2)}) collective-permute-start(bf16[208,768]{1,0:T(8,128)(2,1)S(1)} %copy-done.64), channel_id=1, source_target_pairs={{0,8},{8,16},{16,24},{24,28},{28,20},{20,12},{12,4},{4,0},{1,9},{9... | collective-permute-start | bytes 958472 | tf_op jit(solution)/shard_map/ppermute | solution.py:553
  213.0 7.5 %collective-permute-done.16.refs_1_ = bf16[208,768]{1,0:T(8,128)(2,1)S(1)} collective-permute-done((bf16[208,768]{1,0:T(8,128)(2,1)S(1)}, bf16[208,768]{1,0:T(8,128)(2,1)S(1)}, u32[]{:S(2)}, u32[]{:S(2)}) %collective-permute-start.16) | collective-permute-done | bytes 319520 | tf_op jit(solution)/shard_map/ppermute | solution.py:553
  223.0 6.7 %collective-permute-done.17.refs_2_ = bf16[208,768]{1,0:T(8,128)(2,1)S(1)} collective-permute-done((bf16[208,768]{1,0:T(8,128)(2,1)S(1)}, bf16[208,768]{1,0:T(8,128)(2,1)S(1)}, u32[]{:S(2)}, u32[]{:S(2)}) %collective-permute-start.17) | collective-permute-done | bytes 319520 | tf_op jit(solution)/shard_map/ppermute | solution.py:553
  232.2 5.8 collective-permute-done.18.refs_3_
  240.5 5.1 collective-permute-done.19.refs_4_
  248.7 5.1 collective-permute-done.20.refs_5_
  256.4 5.7 collective-permute-done.21.refs_6_
  272.5 45.8 %experts.1 = (bf16[208,768]{1,0:T(8,128)(2,1)}, bf16[208,768]{1,0:T(8,128)(2,1)}, bf16[208,768]{1,0:T(8,128)(2,1)}, bf16[208,768]{1,0:T(8,128)(2,1)}, bf16[208,7...) custom-call(s32[25]{0:T(128)} %concatenate.50.who_ref, ...), custom_call_target="tpu_custom_call" | custom-call | flops 30000001024 | bytes 40000000 | tf_op jit(solution)/shard_map/experts/pallas_call | solution.py:288
  318.4 17.1 %collective-permute-start.40 = (bf16[208,768]{1,0:T(8,128)(2,1)}, bf16[208,768]{1,0:T(8,128)(2,1)S(1)}, u32[]{:S(2)}, u32[]{:S(2)}) collective-permute-start(bf16[208,768]{1,0:T(8,128)(2,1)} %get-tuple-element.113), channel_id=1, source_target_pairs={{0,8},{8,16},{16,24},{24,28},{28,20},{20,12},{12,4},{4,0},{1,9},{9... | collective-permute-start | bytes 958472 | tf_op jit(solution)/shard_map/ppermute | solution.py:553
  335.5 9.4 %expert_grads.4 = bf16[2,768,768]{2,1,0:T(8,128)(2,1)} custom-call(s32[1]{0:T(128)} %get-tuple-element.117.tiles_ref, bf16[2,3328,768]{2,1,0:T(8,128)(2,1)} %get-tuple-element.118.rows_ref, bf16[2,3328,3072]{2,1,0:T(8,128)(2,1)} %get-tuple-element.119.hid_ref), custom_call_target="tpu_custom_call" | custom-call | flops 4000000000 | bytes 15000000 | tf_op jit(solution)/shard_map/expert_grads/pallas_call | solution.py:341
  349.3 9.4 %expert_grads.5 = bf16[2,768,768]{2,1,0:T(8,128)(2,1)} custom-call(s32[1]{0:T(128)} %get-tuple-element.117.tiles_ref, bf16[2,3328,768]{2,1,0:T(8,128)(2,1)} %get-tuple-element.118.rows_ref, bf16[2,3328,3072]{2,1,0:T(8,128)(2,1)} %get-tuple-element.119.hid_ref), custom_call_target="tpu_custom_call" | custom-call | flops 4000000000 | bytes 15000000 | tf_op jit(solution)/shard_map/expert_grads/pallas_call | solution.py:341
  363.0 9.3 %expert_grads.6 = bf16[2,768,768]{2,1,0:T(8,128)(2,1)} custom-call(s32[1]{0:T(128)} %get-tuple-element.117.tiles_ref, bf16[2,3328,768]{2,1,0:T(8,128)(2,1)} %get-tuple-element.118.rows_ref, bf16[2,3328,3072]{2,1,0:T(8,128)(2,1)} %get-tuple-element.119.hid_ref), custom_call_target="tpu_custom_call" | custom-call | flops 4000000000 | bytes 15000000 | tf_op jit(solution)/shard_map/expert_grads/pallas_call | solution.py:341
  376.7 9.4 %expert_grads.7 = bf16[2,768,768]{2,1,0:T(8,128)(2,1)} custom-call(s32[1]{0:T(128)} %get-tuple-element.117.tiles_ref, bf16[2,3328,768]{2,1,0:T(8,128)(2,1)} %get-tuple-element.118.rows_ref, bf16[2,3328,3072]{2,1,0:T(8,128)(2,1)} %get-tuple-element.119.hid_ref), custom_call_target="tpu_custom_call" | custom-call | flops 4000000000 | bytes 15000000 | tf_op jit(solution)/shard_map/expert_grads/pallas_call | solution.py:341
  390.5 5.6 collective-permute-done.48
  399.0 6.4 %collective-permute-done.49 = bf16[208,768]{1,0:T(8,128)(2,1)S(1)} collective-permute-done((bf16[208,768]{1,0:T(8,128)(2,1)S(1)}, bf16[208,768]{1,0:T(8,128)(2,1)S(1)}, u32[]{:S(2)}, u32[]{:S(2)}) %collective-permute-start.49) | collective-permute-done | bytes 319520 | tf_op jit(solution)/shard_map/ppermute | solution.py:553
  408.5 7.4 %collective-permute-done.50 = bf16[208,768]{1,0:T(8,128)(2,1)S(1)} collective-permute-done((bf16[208,768]{1,0:T(8,128)(2,1)S(1)}, bf16[208,768]{1,0:T(8,128)(2,1)S(1)}, u32[]{:S(2)}, u32[]{:S(2)}) %collective-permute-start.50) | collective-permute-done | bytes 319520 | tf_op jit(solution)/shard_map/ppermute | solution.py:553
  419.4 26.0 %attn_backward.1 = (bf16[8,112,768]{2,1,0:T(8,128)(2,1)}, bf16[8,112,768]{2,1,0:T(8,128)(2,1)}, bf16[8,2,112,768]{3,2,1,0:T(8,128)(2,1)}, bf16[2,208,768]{2,1,0:T(8,128)(2,1)}) custom-call(bf16[208,768]{1,0:T(8,128)(2,1)} %add_convert_fusion.3.refs_0_, bf16[208,768]{1,0:T(8,128)(2,1)} %add_convert_fusion.refs_1_, f32[208,768]{1,0:T(8,128)} %get-tuple-element.88.refs_2_, ...), custom_call_target="tpu_custom_call" | custom-call | flops 12000000000 | bytes 20000000 | tf_op jit(solution)/shard_map/attn_backward/pallas_call | solution.py:499
  446.1 8.2 %collective-permute-done.85 = bf16[2,768,768]{2,1,0:T(8,128)(2,1)} collective-permute-done((bf16[2,768,768]{2,1,0:T(8,128)(2,1)}, bf16[2,768,768]{2,1,0:T(8,128)(2,1)}, u32[]{:S(2)}, u32[]{:S(2)}) %collective-permute-start.85) | collective-permute-done | bytes 2359328 | tf_op jit(solution)/shard_map/ppermute | solution.py:563
  470.4 22.2 %collective-permute-done.61 = bf16[112,768]{1,0:T(8,128)(2,1)} collective-permute-done((bf16[112,768]{1,0:T(8,128)(2,1)}, bf16[112,768]{1,0:T(8,128)(2,1)}, u32[]{:S(2)}, u32[]{:S(2)}) %collective-permute-start.61) | collective-permute-done | bytes 172064 | tf_op jit(solution)/shard_map/ppermute | solution.py:563
  495.9 25.6 %collective-permute-done.69 = bf16[112,768]{1,0:T(8,128)(2,1)S(1)} collective-permute-done((bf16[112,768]{1,0:T(8,128)(2,1)}, bf16[112,768]{1,0:T(8,128)(2,1)S(1)}, u32[]{:S(2)}, u32[]{:S(2)}) %collective-permute-start.69) | collective-permute-done | bytes 172064 | tf_op jit(solution)/shard_map/ppermute | solution.py:563
  530.9 6.2 collective-permute-done.92.refs_6_
  552.0 4.8 collective-permute-start.83
  579.1 5.7 collective-permute-done.81.refs_4_
  593.0 4.2 lay_out.3
  609.2 4.2 lay_out.2
  (452 shorter events, 205.2 us)
Async XLA Ops:
  7.2 265.3 %all-gather.3.cloned.1.call-start = ((), (), s32[]{:S(2)}) async-start(), calls=%async_computation.2 | async-start | bytes 5750784 | tf_op jit(solution)/shard_map/all_gather | solution.py:575
  50.1 17.3 %collective-permute-start.15 = (bf16[2,8,112,768]{3,2,1,0:T(8,128)(2,1)S(1)}, bf16[2,8,112,768]{3,2,1,0:T(8,128)(2,1)}, u32[]{:S(2)}, u32[]{:S(2)}) collective-permute-start(bf16[2,8,112,768]{3,2,1,0:T(8,128)(2,1)S(1)} %pad_maximum_fusion.wa_ref.refs_18_), channel_id=1, source_target_pairs={{0,1},{1,0},{2,3},{3,2},{4,5},{5,4},{6,7},{7,6},{8,9},{9,8},{10,11... | collective-permute-start | bytes 8257544 | tf_op jit(solution)/shard_map/ppermute | solution.py:563
  67.5 498.4 %reduce-scatter.2.cloned.1.call-start = ((), (), s32[]{:S(2)}) async-start(), calls=%async_computation.1 | async-start | bytes 5750784 | tf_op jit(solution)/shard_map/reduce_scatter | solution.py:578
  71.1 16.9 %collective-permute-start.30 = (bf16[2,96,768]{2,1,0:T(8,128)(2,1)}, bf16[2,96,768]{2,1,0:T(8,128)(2,1)S(1)}, u32[]{:S(2)}, u32[]{:S(2)}) collective-permute-start(bf16[2,96,768]{2,1,0:T(8,128)(2,1)} %get-tuple-element.97), channel_id=1, source_target_pairs={{0,4},{4,8},{8,12},{12,16},{16,20},{20,24},{24,28},{28,0},{1,5},{5... | collective-permute-start | bytes 884744 | tf_op jit(solution)/shard_map/ppermute | solution.py:557
  72.6 19.7 %collective-permute-start.31 = (bf16[2,96,768]{2,1,0:T(8,128)(2,1)}, bf16[2,96,768]{2,1,0:T(8,128)(2,1)S(1)}, u32[]{:S(2)}, u32[]{:S(2)}) collective-permute-start(bf16[2,96,768]{2,1,0:T(8,128)(2,1)} %get-tuple-element.98), channel_id=1, source_target_pairs={{0,8},{4,12},{8,16},{12,20},{16,24},{20,28},{24,0},{28,4},{1,9},{5... | collective-permute-start | bytes 884744 | tf_op jit(solution)/shard_map/ppermute | solution.py:557
  74.8 74.9 %collective-permute-start.32 = (bf16[2,96,768]{2,1,0:T(8,128)(2,1)}, bf16[2,96,768]{2,1,0:T(8,128)(2,1)S(1)}, u32[]{:S(2)}, u32[]{:S(2)}) collective-permute-start(bf16[2,96,768]{2,1,0:T(8,128)(2,1)} %get-tuple-element.99), channel_id=1, source_target_pairs={{0,12},{4,16},{8,20},{12,24},{16,28},{20,0},{24,4},{28,8},{1,13},{... | collective-permute-start | bytes 884744 | tf_op jit(solution)/shard_map/ppermute | solution.py:557
  77.5 72.2 %collective-permute-start.33 = (bf16[2,96,768]{2,1,0:T(8,128)(2,1)}, bf16[2,96,768]{2,1,0:T(8,128)(2,1)S(1)}, u32[]{:S(2)}, u32[]{:S(2)}) collective-permute-start(bf16[2,96,768]{2,1,0:T(8,128)(2,1)} %get-tuple-element.100), channel_id=1, source_target_pairs={{0,16},{4,20},{8,24},{12,28},{16,0},{20,4},{24,8},{28,12},{1,17},{... | collective-permute-start | bytes 884744 | tf_op jit(solution)/shard_map/ppermute | solution.py:557
  77.7 72.0 %collective-permute-start.34 = (bf16[2,96,768]{2,1,0:T(8,128)(2,1)}, bf16[2,96,768]{2,1,0:T(8,128)(2,1)S(1)}, u32[]{:S(2)}, u32[]{:S(2)}) collective-permute-start(bf16[2,96,768]{2,1,0:T(8,128)(2,1)} %get-tuple-element.101), channel_id=1, source_target_pairs={{0,20},{4,24},{8,28},{12,0},{16,4},{20,8},{24,12},{28,16},{1,21},{... | collective-permute-start | bytes 884744 | tf_op jit(solution)/shard_map/ppermute | solution.py:557
  88.0 61.8 %collective-permute-start.35 = (bf16[2,96,768]{2,1,0:T(8,128)(2,1)}, bf16[2,96,768]{2,1,0:T(8,128)(2,1)S(1)}, u32[]{:S(2)}, u32[]{:S(2)}) collective-permute-start(bf16[2,96,768]{2,1,0:T(8,128)(2,1)} %get-tuple-element.102), channel_id=1, source_target_pairs={{0,24},{4,28},{8,0},{12,4},{16,8},{20,12},{24,16},{28,20},{1,25},{... | collective-permute-start | bytes 884744 | tf_op jit(solution)/shard_map/ppermute | solution.py:557
  92.3 57.4 %collective-permute-start.36 = (bf16[2,96,768]{2,1,0:T(8,128)(2,1)S(1)}, bf16[2,96,768]{2,1,0:T(8,128)(2,1)S(1)}, u32[]{:S(2)}, u32[]{:S(2)}) collective-permute-start(bf16[2,96,768]{2,1,0:T(8,128)(2,1)S(1)} %get-tuple-element.103), channel_id=1, source_target_pairs={{0,28},{4,0},{8,4},{12,8},{16,12},{20,16},{24,20},{28,24},{1,29},{... | collective-permute-start | bytes 884744 | tf_op jit(solution)/shard_map/ppermute | solution.py:557
  150.3 46.5 %collective-permute-start.37 = (bf16[8,2,96,768]{3,2,1,0:T(8,128)(2,1)S(1)}, bf16[8,2,96,768]{3,2,1,0:T(8,128)(2,1)}, u32[]{:S(2)}, u32[]{:S(2)}) collective-permute-start(bf16[8,2,96,768]{3,2,1,0:T(8,128)(2,1)S(1)} %maximum_bitcast_fusion.refs_17_), channel_id=1, source_target_pairs={{0,2},{1,3},{2,0},{3,1},{4,6},{5,7},{6,4},{7,5},{8,10},{9,11},{10,... | collective-permute-start | bytes 7077896 | tf_op jit(solution)/shard_map/ppermute | solution.py:563
  150.3 122.1 %collective-permute-start.38 = (bf16[8,2,96,768]{3,2,1,0:T(8,128)(2,1)S(1)}, bf16[8,2,96,768]{3,2,1,0:T(8,128)(2,1)}, u32[]{:S(2)}, u32[]{:S(2)}) collective-permute-start(bf16[8,2,96,768]{3,2,1,0:T(8,128)(2,1)S(1)} %maximum_bitcast_fusion.refs_17_), channel_id=1, source_target_pairs={{0,1},{1,0},{2,3},{3,2},{4,5},{5,4},{6,7},{7,6},{8,9},{9,8},{10,11... | collective-permute-start | bytes 7077896 | tf_op jit(solution)/shard_map/ppermute | solution.py:563
  196.7 75.8 %collective-permute-start.39 = (bf16[8,2,96,768]{3,2,1,0:T(8,128)(2,1)}, bf16[8,2,96,768]{3,2,1,0:T(8,128)(2,1)}, u32[]{:S(2)}, u32[]{:S(2)}) collective-permute-start(bf16[8,2,96,768]{3,2,1,0:T(8,128)(2,1)} %collective-permute-done.37.refs_18_), channel_id=1, source_target_pairs={{0,1},{1,0},{2,3},{3,2},{4,5},{5,4},{6,7},{7,6},{8,9},{9,8},{10,11... | collective-permute-start | bytes 7077896 | tf_op jit(solution)/shard_map/ppermute | solution.py:563
  196.7 23.8 %collective-permute-start.16 = (bf16[208,768]{1,0:T(8,128)(2,1)S(1)}, bf16[208,768]{1,0:T(8,128)(2,1)S(1)}, u32[]{:S(2)}, u32[]{:S(2)}) collective-permute-start(bf16[208,768]{1,0:T(8,128)(2,1)S(1)} %copy-done.64), channel_id=1, source_target_pairs={{0,8},{8,16},{16,24},{24,28},{28,20},{20,12},{12,4},{4,0},{1,9},{9... | collective-permute-start | bytes 958472 | tf_op jit(solution)/shard_map/ppermute | solution.py:553
  318.4 26.5 %collective-permute-start.40 = (bf16[208,768]{1,0:T(8,128)(2,1)}, bf16[208,768]{1,0:T(8,128)(2,1)S(1)}, u32[]{:S(2)}, u32[]{:S(2)}) collective-permute-start(bf16[208,768]{1,0:T(8,128)(2,1)} %get-tuple-element.113), channel_id=1, source_target_pairs={{0,8},{8,16},{16,24},{24,28},{28,20},{20,12},{12,4},{4,0},{1,9},{9... | collective-permute-start | bytes 958472 | tf_op jit(solution)/shard_map/ppermute | solution.py:553
  445.4 15.5 %collective-permute-start.60 = (bf16[8,2,112,768]{3,2,1,0:T(8,128)(2,1)}, bf16[8,2,112,768]{3,2,1,0:T(8,128)(2,1)S(1)}, u32[]{:S(2)}, u32[]{:S(2)}) collective-permute-start(bf16[8,2,112,768]{3,2,1,0:T(8,128)(2,1)} %get-tuple-element.151), channel_id=1, source_target_pairs={{0,1},{1,0},{2,3},{3,2},{4,5},{5,4},{6,7},{7,6},{8,9},{9,8},{10,11... | collective-permute-start | bytes 8257544 | tf_op jit(solution)/shard_map/ppermute | solution.py:563
  446.1 23.8 %collective-permute-start.57 = (bf16[2,208,768]{2,1,0:T(8,128)(2,1)}, bf16[2,208,768]{2,1,0:T(8,128)(2,1)}, u32[]{:S(2)}, u32[]{:S(2)}) collective-permute-start(bf16[2,208,768]{2,1,0:T(8,128)(2,1)} %get-tuple-element.149.refs_0_), channel_id=1, source_target_pairs={{0,2},{1,3},{2,0},{3,1},{4,6},{5,7},{6,4},{7,5},{8,10},{9,11},{10,... | collective-permute-start | bytes 1916936 | tf_op jit(solution)/shard_map/ppermute | solution.py:563
  458.8 35.0 %collective-permute-start.86 = (bf16[768,768]{1,0:T(8,128)(2,1)}, bf16[768,768]{1,0:T(8,128)(2,1)}, u32[]{:S(2)}, u32[]{:S(2)}) collective-permute-start(bf16[768,768]{1,0:T(8,128)(2,1)} %fusion.10), channel_id=1, source_target_pairs={{0,2},{1,3},{2,0},{3,1},{4,6},{5,7},{6,4},{7,5},{8,10},{9,11},{10,... | collective-permute-start | bytes 3538952 | tf_op jit(solution)/shard_map/ppermute | solution.py:563
  464.5 28.2 %collective-permute-start.61 = (bf16[112,768]{1,0:T(8,128)(2,1)}, bf16[112,768]{1,0:T(8,128)(2,1)}, u32[]{:S(2)}, u32[]{:S(2)}) collective-permute-start(bf16[112,768]{1,0:T(8,128)(2,1)} %get-tuple-element.226), channel_id=1, source_target_pairs={{0,2},{1,3},{2,0},{3,1},{4,6},{5,7},{6,4},{7,5},{8,10},{9,11},{10,... | collective-permute-start | bytes 516104 | tf_op jit(solution)/shard_map/ppermute | solution.py:563
  467.8 69.2 %collective-permute-start.77 = (bf16[768,768]{1,0:T(8,128)(2,1)}, bf16[768,768]{1,0:T(8,128)(2,1)}, u32[]{:S(2)}, u32[]{:S(2)}) collective-permute-start(bf16[768,768]{1,0:T(8,128)(2,1)} %fusion.8), channel_id=1, source_target_pairs={{0,2},{1,3},{2,0},{3,1},{4,6},{5,7},{6,4},{7,5},{8,10},{9,11},{10,... | collective-permute-start | bytes 3538952 | tf_op jit(solution)/shard_map/ppermute | solution.py:563
  469.9 57.4 %collective-permute-start.58 = (bf16[2,208,768]{2,1,0:T(8,128)(2,1)}, bf16[2,208,768]{2,1,0:T(8,128)(2,1)S(1)}, u32[]{:S(2)}, u32[]{:S(2)}) collective-permute-start(bf16[2,208,768]{2,1,0:T(8,128)(2,1)} %get-tuple-element.149.refs_0_), channel_id=1, source_target_pairs={{0,1},{1,0},{2,3},{3,2},{4,5},{5,4},{6,7},{7,6},{8,9},{9,8},{10,11... | collective-permute-start | bytes 1916936 | tf_op jit(solution)/shard_map/ppermute | solution.py:563
  469.9 58.4 %collective-permute-start.59 = (bf16[2,208,768]{2,1,0:T(8,128)(2,1)}, bf16[2,208,768]{2,1,0:T(8,128)(2,1)S(1)}, u32[]{:S(2)}, u32[]{:S(2)}) collective-permute-start(bf16[2,208,768]{2,1,0:T(8,128)(2,1)} %collective-permute-done.57.refs_1_), channel_id=1, source_target_pairs={{0,1},{1,0},{2,3},{3,2},{4,5},{5,4},{6,7},{7,6},{8,9},{9,8},{10,11... | collective-permute-start | bytes 1916936 | tf_op jit(solution)/shard_map/ppermute | solution.py:563
  492.6 28.9 %collective-permute-start.69 = (bf16[112,768]{1,0:T(8,128)(2,1)}, bf16[112,768]{1,0:T(8,128)(2,1)S(1)}, u32[]{:S(2)}, u32[]{:S(2)}) collective-permute-start(bf16[112,768]{1,0:T(8,128)(2,1)} %get-tuple-element.230), channel_id=1, source_target_pairs={{0,2},{1,3},{2,0},{3,1},{4,6},{5,7},{6,4},{7,5},{8,10},{9,11},{10,... | collective-permute-start | bytes 516104 | tf_op jit(solution)/shard_map/ppermute | solution.py:563
  493.9 31.9 %collective-permute-start.63 = (bf16[112,768]{1,0:T(8,128)(2,1)S(1)}, bf16[112,768]{1,0:T(8,128)(2,1)S(1)}, u32[]{:S(2)}, u32[]{:S(2)}) collective-permute-start(bf16[112,768]{1,0:T(8,128)(2,1)S(1)} %get-tuple-element.233), channel_id=1, source_target_pairs={{0,2},{1,3},{2,0},{3,1},{4,6},{5,7},{6,4},{7,5},{8,10},{9,11},{10,... | collective-permute-start | bytes 516104 | tf_op jit(solution)/shard_map/ppermute | solution.py:563
  528.3 16.2 %collective-permute-start.71 = (bf16[112,768]{1,0:T(8,128)(2,1)}, bf16[112,768]{1,0:T(8,128)(2,1)S(1)}, u32[]{:S(2)}, u32[]{:S(2)}) collective-permute-start(bf16[112,768]{1,0:T(8,128)(2,1)} %get-tuple-element.229), channel_id=1, source_target_pairs={{0,2},{1,3},{2,0},{3,1},{4,6},{5,7},{6,4},{7,5},{8,10},{9,11},{10,... | collective-permute-start | bytes 516104 | tf_op jit(solution)/shard_map/ppermute | solution.py:563
  544.6 16.0 %collective-permute-start.88 = (bf16[96,768]{1,0:T(8,128)(2,1)S(1)}, bf16[96,768]{1,0:T(8,128)(2,1)S(1)}, u32[]{:S(2)}, u32[]{:S(2)}) collective-permute-start(bf16[96,768]{1,0:T(8,128)(2,1)S(1)} %get-tuple-element.239), channel_id=1, source_target_pairs={{0,8},{4,12},{8,16},{12,20},{16,24},{20,28},{24,0},{28,4},{1,9},{5... | collective-permute-start | bytes 442376 | tf_op jit(solution)/shard_map/ppermute | solution.py:557
  552.0 15.1 %collective-permute-start.83 = (bf16[96,768]{1,0:T(8,128)(2,1)}, bf16[96,768]{1,0:T(8,128)(2,1)}, u32[]{:S(2)}, u32[]{:S(2)}) collective-permute-start(bf16[96,768]{1,0:T(8,128)(2,1)} %get-tuple-element.243), channel_id=1, source_target_pairs={{0,24},{4,28},{8,0},{12,4},{16,8},{20,12},{24,16},{28,20},{1,25},{... | collective-permute-start | bytes 442376 | tf_op jit(solution)/shard_map/ppermute | solution.py:557
  571.6 17.4 %collective-permute-start.80 = (bf16[96,768]{1,0:T(8,128)(2,1)}, bf16[96,768]{1,0:T(8,128)(2,1)S(1)}, u32[]{:S(2)}, u32[]{:S(2)}) collective-permute-start(bf16[96,768]{1,0:T(8,128)(2,1)} %get-tuple-element.246), channel_id=1, source_target_pairs={{0,12},{4,16},{8,20},{12,24},{16,28},{20,0},{24,4},{28,8},{1,13},{... | collective-permute-start | bytes 442376 | tf_op jit(solution)/shard_map/ppermute | solution.py:557
  574.5 16.1 %collective-permute-start.79 = (bf16[96,768]{1,0:T(8,128)(2,1)}, bf16[96,768]{1,0:T(8,128)(2,1)S(1)}, u32[]{:S(2)}, u32[]{:S(2)}) collective-permute-start(bf16[96,768]{1,0:T(8,128)(2,1)} %get-tuple-element.247), channel_id=1, source_target_pairs={{0,8},{4,12},{8,16},{12,20},{16,24},{20,28},{24,0},{28,4},{1,9},{5... | collective-permute-start | bytes 442376 | tf_op jit(solution)/shard_map/ppermute | solution.py:557
  574.9 30.0 %collective-permute-start.54 = (bf16[2,208,768]{2,1,0:T(8,128)(2,1)S(1)}, bf16[2,208,768]{2,1,0:T(8,128)(2,1)S(1)}, u32[]{:S(2)}, u32[]{:S(2)}) collective-permute-start(bf16[2,208,768]{2,1,0:T(8,128)(2,1)S(1)} %fusion.6.refs_0_), channel_id=1, source_target_pairs={{0,2},{1,3},{2,0},{3,1},{4,6},{5,7},{6,4},{7,5},{8,10},{9,11},{10,... | collective-permute-start | bytes 1916936 | tf_op jit(solution)/shard_map/ppermute | solution.py:563
  578.0 25.8 %collective-permute-start.75 = (bf16[112,768]{1,0:T(8,128)(2,1)S(1)}, bf16[112,768]{1,0:T(8,128)(2,1)S(1)}, u32[]{:S(2)}, u32[]{:S(2)}) collective-permute-start(bf16[112,768]{1,0:T(8,128)(2,1)S(1)} %get-tuple-element.227), channel_id=1, source_target_pairs={{0,2},{1,3},{2,0},{3,1},{4,6},{5,7},{6,4},{7,5},{8,10},{9,11},{10,... | collective-permute-start | bytes 516104 | tf_op jit(solution)/shard_map/ppermute | solution.py:563
  585.5 18.3 %collective-permute-start.68 = (bf16[112,768]{1,0:T(8,128)(2,1)}, bf16[112,768]{1,0:T(8,128)(2,1)S(1)}, u32[]{:S(2)}, u32[]{:S(2)}) collective-permute-start(bf16[112,768]{1,0:T(8,128)(2,1)} %get-tuple-element.220), channel_id=1, source_target_pairs={{0,8},{8,16},{16,24},{24,28},{28,20},{20,12},{12,4},{4,0},{1,9},{9... | collective-permute-start | bytes 516104 | tf_op jit(solution)/shard_map/ppermute | solution.py:553
  (142 other events, 1678.3 us)
Sparse Core Ops, SparseCore 0:
  67.6 120.4 all-gather.2
  419.6 98.6 reduce-scatter.1

commit v3 on v2

--- a/solution.py
+++ b/solution.py
@@ -53,26 +53,12 @@
     )
 
 
-def load_attn_weights(order_ref, wa_ref, wb_ref, w_s, sem):
-    rows = D // E
-    copies = []
-    for r in range(4):
-        src = wa_ref if r < 2 else wb_ref
-        for b in range(E):
-            at = pl.ds(pl.multiple_of(order_ref[b] * rows, 16), rows)
-            copies.append(pltpu.make_async_copy(src.at[r % 2, b, pl.ds(0, rows)], w_s.at[r, at], sem.at[r, b]))
-            copies[-1].start()
-    return [copies[r * E : (r + 1) * E] for r in range(4)]
-
-
-def attn_forward_kernel(
-    order_ref, x_ref, par_ref, wa_ref, wb_ref, noise_ref, keep_ref,
-    chunk_ref, x1_ref, qkv_ref, o_ref, lse_ref, probs_ref,
-    w_s, sem,
-):
-    copies = load_attn_weights(order_ref, wa_ref, wb_ref, w_s, sem)
-    par = par_ref[...].astype(F32)
-    x = x_ref[...].astype(F32)
+def params_of(w_own):
+    return jnp.transpose(w_own[:, D:].astype(F32))[:16]
+
+
+def attend(x, par, w_of, noise, keep, chunk_ref, x1_ref, qkv_ref, o_ref, lse_ref, probs_ref):
+    x = x.astype(F32)
     unit, _ = normalise(x)
     h1 = (unit * par[0:1] + par[1:2]).astype(BF16)
     acc = x
@@ -80,9 +66,7 @@
     key_ok = iota((PAD, PAD), 1) < SEQ
     lane = iota((PAD, 128), 1)
     for r in range(4):
-        for copy in copies[r]:
-            copy.wait()
-        w = w_s[r]
+        w = w_of(r)
         qkv = dot(h1, w[:, : 9 * HD]).astype(BF16)
         qkv_ref[r] = qkv
         outs = []
@@ -98,65 +82,286 @@
             lse = jnp.where(lane == 3 * r + h, top + jnp.log(total), lse)
         o = jnp.concatenate(outs, axis=1)
         o_ref[r] = o
-        acc = acc + dot_nt(o, w[:, 9 * HD :])
+        acc = acc + dot_nt(o, w[:, 9 * HD : D])
     lse_ref[...] = lse
     x1_ref[...] = acc
     unit2, _ = normalise(acc)
     h2 = (unit2 * par[2:3] + par[3:4]).astype(BF16)
-    logits = dot_nt(par_ref[8:16, :], h2) + noise_ref[...]
+    logits = dot_nt(par[8:16].astype(BF16), h2) + noise
     e = jnp.exp(logits - jnp.max(logits, axis=0, keepdims=True))
     probs = e / jnp.sum(e, axis=0, keepdims=True)
     probs_ref[...] = probs
-    gates = jnp.where(keep_ref[...] > 0, probs, -1.0)
+    gates = jnp.where(keep > 0, probs, -1.0)
     chunk_ref[...] = h2
     tail = jnp.concatenate([gates, jnp.zeros((8, D - PAD), F32)], axis=1)
     low = h2[PAD - 16 :, :].astype(F32)
     chunk_ref[PAD - 16 :, :] = jnp.concatenate([low[:8], tail], axis=0).astype(BF16)
 
 
-def attn_forward(order, x, par, wa, wb, noise, keep):
+def attn_shapes(imgs):
+    return (
+        jax.ShapeDtypeStruct((imgs, PAD, D), F32),
+        jax.ShapeDtypeStruct((imgs, 4, PAD, 9 * HD), BF16),
+        jax.ShapeDtypeStruct((imgs, 4, PAD, 3 * HD), BF16),
+        jax.ShapeDtypeStruct((imgs, PAD, 128), F32),
+        jax.ShapeDtypeStruct((imgs, E, PAD), F32),
+    )
+
+
+def attn_forward_kernel(imgs, x_ref, w_ref, noise_ref, keep_ref, chunk_ref, *saved):
+    par = params_of(w_ref[0])
+    for c in range(imgs):
+        attend(
+            x_ref[c], par, lambda r: w_ref[r], noise_ref[c], keep_ref[c],
+            chunk_ref.at[c], *(ref.at[c] for ref in saved),
+        )
+
+
+def attn_forward(x, w, noise, keep):
+    imgs = x.shape[0]
+    vm = pl.BlockSpec(memory_space=pltpu.VMEM)
+    return pl.pallas_call(
+        functools.partial(attn_forward_kernel, imgs),
+        out_shape=(jax.ShapeDtypeStruct((imgs, PAD, D), BF16),) + attn_shapes(imgs),
+        in_specs=[vm] * 4,
+        out_specs=(vm,) * 6,
+        compiler_params=pltpu.CompilerParams(vmem_limit_bytes=VMEM_LIMIT),
+        cost_estimate=pl.CostEstimate(flops=6 * 10**9, bytes_accessed=10**7, transcendentals=2 * 10**6),
+        name="attn_forward",
+    )(x, w, noise, keep)
+
+
+def ring_place(member):
+    odd = lax.rem(member, 2)
+    half = lax.div(member, 2)
+    return half + odd * (E - 1 - 2 * half)
+
+
+def ring_member(place):
+    late = lax.div(place, E // 2)
+    return 2 * place + late * (2 * E - 1 - 4 * place)
+
+
+class Peers:
+    def __init__(self):
+        dp = lax.axis_index("dp")
+        tensor = lax.axis_index("tensor")
+        self.member = lax.rem(dp, E)
+        self.base = dp - self.member
+        self.place = ring_place(self.member)
+        self.across = {"tensor": lax.rem(tensor + 2, 4)}
+        self.core = {"tensor": tensor + 1 - 2 * lax.rem(tensor, 2)}
+        self.next = ({"dp": self.base + self.behind(1, 1)}, {"dp": self.base + self.behind(0, 1)})
+        self.sends = []
+
+    def behind(self, way, k):
+        step = E - k if way == 0 else k
+        return ring_member(lax.rem(self.place + step, E))
+
+    def ahead(self, by):
+        return lax.rem(self.member + by, E)
+
+    def came(self, by):
+        return lax.rem(self.member + E - by, E)
+
+    def meet(self):
+        barrier = pltpu.get_barrier_semaphore()
+        others = [{"dp": self.base + self.ahead(by)} for by in range(1, E)] + [self.across, self.core]
+        for device in others:
+            pl.semaphore_signal(barrier, inc=1, device_id=device, device_id_type=pl.DeviceIdType.MESH)
+        pl.semaphore_wait(barrier, len(others))
+
+    def send(self, src, dst, sems, at, device):
+        copy = pltpu.make_async_remote_copy(
+            src_ref=src,
+            dst_ref=dst,
+            send_sem=sems[0].at[at],
+            recv_sem=sems[1].at[at],
+            device_id=device,
+            device_id_type=pl.DeviceIdType.MESH,
+        )
+        copy.start()
+        self.sends.append(copy)
+        return copy
+
+
+def front_kernel(
+    imgs, pack_ref, ew_ref, dy_ref, x_ref, noise_ref, keep_ref,
+    h_out, dy_out, ew_out, w_out, x1_ref, qkv_ref, o_ref, lse_ref, probs_ref,
+    w_s, chunk_s, p_s, p_r, px_s, px_r, pc_s, pc_r, d_s, d_r, h_s, h_r, e_s, e_r, ex_s, ex_r, ec_s, ec_r, local,
+):
+    peers = Peers()
+    member = peers.member
+    d_own = pack_ref.shape[0]
+    half = E // 2
+    peers.meet()
+
+    def rows(of):
+        return pl.ds(pl.multiple_of(of * d_own, 16), d_own)
+
+    locals_ = [pltpu.make_async_copy(pack_ref, w_s.at[0, rows(member)], local.at[0])]
+    locals_[0].start()
+
+    ring, px, pc = {}, {}, {}
+
+    def pass_pack(number, of, src, way=None, k=None):
+        if way is not None:
+            ring[way, k] = peers.send(src, w_s.at[0, rows(of)], (p_s, p_r), (way, k), peers.next[way])
+        px[number] = peers.send(src, w_s.at[1, rows(of)], (px_s, px_r), number, peers.across)
+        pc[0, number] = peers.send(src, w_s.at[2, rows(of)], (pc_s, pc_r), (0, number), peers.core)
+
+    arrivals = [(0, k) if i == 0 else (1, k) for k in range(1, half + 1) for i in range(2 if k < half else 1)]
+    owners = [member] + [peers.behind(way, k) for way, k in arrivals]
+    ring[0, 0] = peers.send(pack_ref, w_s.at[0, rows(member)], (p_s, p_r), (0, 0), peers.next[0])
+    pass_pack(0, member, pack_ref, 1, 0)
+
+    def pass_x(number):
+        px[number].wait_recv()
+        at = rows(owners[number])
+        pc[1, number] = peers.send(w_s.at[1, at], w_s.at[3, at], (pc_s, pc_r), (1, number), peers.core)
+
+    for number, (way, k) in enumerate(arrivals, 1):
+        ring[way, k - 1].wait_recv()
+        of = owners[number]
+        last = half if way == 0 else half - 1
+        pass_pack(number, of, w_s.at[0, rows(of)], way if k < last else None, k)
+        if number >= 2:
+            pass_x(number - 2)
+
+    e_copy = {}
+    for by in range(1, E):
+        to = peers.ahead(by)
+        e_copy[by] = peers.send(ew_ref.at[to], ew_out.at[0, member], (e_s, e_r), by, {"dp": peers.base + to})
+
+    d_ring, h_ring = {}, {}
+
+    def row_ring(c, k, src, out, kept, sems):
+        at = peers.behind(c % 2, k) * imgs + c if k else member * imgs + c
+        kept[c, k] = peers.send(src if k == 0 else out.at[at], out.at[at], sems, (c, k), peers.next[c % 2])
+
+    for c in range(imgs):
+        row_ring(c, 0, dy_ref.at[c], dy_out, d_ring, (d_s, d_r))
+    for number in range(len(arrivals) - 1, len(arrivals) + 1):
+        pass_x(number)
+
+    ex, ec = {}, {}
+
+    def pass_e(by):
+        if by:
+            e_copy[by].wait_recv()
+        of = peers.came(by)
+        src = ew_out.at[0, of] if by else ew_ref.at[member]
+        ex[by] = peers.send(src, ew_out.at[1, of], (ex_s, ex_r), by, peers.across)
+        ec[0, by] = peers.send(src, ew_out.at[2, of], (ec_s, ec_r), (0, by), peers.core)
+
+    def pass_ex(by):
+        ex[by].wait_recv()
+        of = peers.came(by)
+        ec[1, by] = peers.send(ew_out.at[1, of], ew_out.at[3, of], (ec_s, ec_r), (1, by), peers.core)
+
+    for number in range(E):
+        pc[0, number].wait_recv()
+        pc[1, number].wait_recv()
+    locals_[0].wait()
+    pass_e(0)
+    keepers = [
+        pltpu.make_async_copy(w_s, w_out, local.at[1]),
+        pltpu.make_async_copy(ew_ref.at[member], ew_out.at[0, member], local.at[2]),
+    ] + [
+        pltpu.make_async_copy(dy_ref.at[c], dy_out.at[member * imgs + c], local.at[3 + c]) for c in range(imgs)
+    ]
+    for copy in keepers:
+        copy.start()
+
+    par = params_of(w_s[0])
+    for c in range(imgs):
+        attend(
+            x_ref[c], par, lambda r: w_s[r], noise_ref[c], keep_ref[c],
+            chunk_s.at[c], *(ref.at[c] for ref in (x1_ref, qkv_ref, o_ref, lse_ref, probs_ref)),
+        )
+        row_ring(c, 0, chunk_s.at[c], h_out, h_ring, (h_s, h_r))
+        keepers.append(
+            pltpu.make_async_copy(chunk_s.at[c], h_out.at[member * imgs + c], local.at[3 + imgs + c])
+        )
+        keepers[-1].start()
+        if c == 0:
+            for i in range(imgs):
+                d_ring[i, 0].wait_recv()
+                row_ring(i, 1, None, dy_out, d_ring, (d_s, d_r))
+
+    for k in range(1, E):
+        for c in range(imgs):
+            h_ring[c, k - 1].wait_recv()
+            if k < E - 1:
+                row_ring(c, k, None, h_out, h_ring, (h_s, h_r))
+        if k < E - 1:
+            for c in range(imgs):
+                d_ring[c, k].wait_recv()
+                if k + 1 < E - 1:
+                    row_ring(c, k + 1, None, dy_out, d_ring, (d_s, d_r))
+        for by in {2: (1, 7), 3: (2, 6), 4: (3, 5), 5: (4,)}.get(k, ()):
+            pass_e(by)
+        for by in {2: (0,), 3: (1, 7), 4: (2, 6), 5: (3, 5), 6: (4,)}.get(k, ()):
+            pass_ex(by)
+    for by in range(E):
+        ec[0, by].wait_recv()
+        ec[1, by].wait_recv()
+    for copy in keepers:
+        copy.wait()
+    for copy in peers.sends:
+        copy.wait_send()
+
+
+def front(pack, ew, dy, x, noise, keep):
+    imgs = x.shape[0]
+    d_own = pack.shape[0]
     vm = pl.BlockSpec(memory_space=pltpu.VMEM)
     hbm = pl.BlockSpec(memory_space=pl.ANY)
-    sm = pl.BlockSpec(memory_space=pltpu.SMEM)
+    table = jax.ShapeDtypeStruct((E * imgs, PAD, D), BF16)
+    dma = pltpu.SemaphoreType.DMA
     return pl.pallas_call(
-        attn_forward_kernel,
+        functools.partial(front_kernel, imgs),
         out_shape=(
-            jax.ShapeDtypeStruct((PAD, D), BF16),
-            jax.ShapeDtypeStruct((PAD, D), F32),
-            jax.ShapeDtypeStruct((4, PAD, 9 * HD), BF16),
-            jax.ShapeDtypeStruct((4, PAD, 3 * HD), BF16),
-            jax.ShapeDtypeStruct((PAD, 128), F32),
-            jax.ShapeDtypeStruct((E, PAD), F32),
+            table,
+            table,
+            jax.ShapeDtypeStruct((4, E, 2, d_own, FFS), BF16),
+            jax.ShapeDtypeStruct((4, E * d_own, D + 128), BF16),
+        )
+        + attn_shapes(imgs),
+        in_specs=[vm, hbm, hbm, vm, vm, vm],
+        out_specs=(hbm,) * 4 + (vm,) * 5,
+        scratch_shapes=[
+            pltpu.VMEM((4, E * d_own, D + 128), BF16),
+            pltpu.VMEM((imgs, PAD, D), BF16),
+            dma((2, 4)), dma((2, 4)), dma((E,)), dma((E,)), dma((2, E)), dma((2, E)),
+            dma((imgs, E - 1)), dma((imgs, E - 1)), dma((imgs, E - 1)), dma((imgs, E - 1)),
+            dma((E,)), dma((E,)), dma((E,)), dma((E,)), dma((2, E)), dma((2, E)),
+            dma((3 + 2 * imgs,)),
+        ],
+        compiler_params=pltpu.CompilerParams(
+            vmem_limit_bytes=VMEM_LIMIT, collective_id=0, has_side_effects=True
         ),
-        in_specs=[sm, vm, vm, hbm, hbm, vm, vm],
-        out_specs=(vm,) * 6,
-        scratch_shapes=[pltpu.VMEM((4, D, D), BF16), pltpu.SemaphoreType.DMA((4, E))],
-        compiler_params=pltpu.CompilerParams(vmem_limit_bytes=VMEM_LIMIT),
-        cost_estimate=pl.CostEstimate(flops=3 * 10**9, bytes_accessed=10**7, transcendentals=10**6),
-        name="attn_forward",
-    )(order, x, par, wa, wb, noise, keep)
+        cost_estimate=pl.CostEstimate(flops=6 * 10**9, bytes_accessed=10**8, transcendentals=2 * 10**6),
+        name="front",
+    )(pack, ew, dy, x, noise, keep)
 
 
 def expert_kernel(nb, who_ref, *refs):
-    h_in = refs[:nb]
-    dy_in, w_in = refs[nb], refs[nb + 1 : nb + 5]
-    outs = refs[nb + 5 :]
-    dx_out = outs[:nb]
-    y_out, rows_out, hid_out, tiles_ref = outs[nb : nb + 4]
-    (h, dy, y_t, dx_t, w_s, gate_s, slot_s, dgate_s, xs, dys, hid_s, rows_s, lo_s, hi_s, in_sem, out_sem, row_sem, hid_sem, w_sem) = outs[nb + 4 :]
-    me = who_ref[nb]
-    loads = []
-    for b in range(nb):
-        for ref, table, c in ((h_in[b], h, 0), (dy_in.at[who_ref[b]], dy, 1)):
-            copy = pltpu.make_async_copy(ref, table.at[b], in_sem.at[c, b])
-            copy.start()
-            loads.append(copy)
+    h_in, dy_in, w_in = refs[:3]
+    outs = refs[3:]
+    dx_out, y_out, rows_out, hid_out, tiles_ref = outs[:5]
+    (h, dy, y_t, dx_t, w_s, gate_s, slot_s, dgate_s, xs, dys, hid_s, rows_s, lo_s, hi_s, in_sem, out_sem, row_sem, hid_sem, w_sem) = outs[5:]
+    me = who_ref[0]
+    loads = [
+        pltpu.make_async_copy(h_in, h, in_sem.at[0]),
+        pltpu.make_async_copy(dy_in, dy, in_sem.at[1]),
+    ]
     for b in range(E):
-        at = pl.ds(pl.multiple_of(who_ref[nb + 1 + b] * (D // E), 16), D // E)
+        at = pl.ds(b * (D // E), D // E)
         for r in range(4):
-            copy = pltpu.make_async_copy(w_in[r].at[b], w_s.at[r, :, at], w_sem.at[r, b])
-            copy.start()
-            loads.append(copy)
+            loads.append(pltpu.make_async_copy(w_in.at[r, b], w_s.at[r, :, at], w_sem.at[r, b]))
+    for copy in loads:
+        copy.start()
     y_t[...] = jnp.zeros_like(y_t)
     dx_t[...] = jnp.zeros_like(dx_t)
     dgate_s[...] = jnp.zeros_like(dgate_s)
@@ -262,15 +467,16 @@
             pltpu.make_async_copy(rows_s.at[s], rows_out.at[:, pl.ds(0, TILE)], row_sem.at[s]).wait()
             pltpu.make_async_copy(hid_s.at[s], hid_out.at[:, pl.ds(0, TILE)], hid_sem.at[s]).wait()
 
-    stores = []
     for b in range(nb):
         tail = dx_t[b, PAD - 16 : PAD, :].astype(F32)
         line = jnp.concatenate([dgate_s[b : b + 1, :], jnp.zeros((1, D - PAD), F32)], axis=1)
         dx_t[b, PAD - 16 : PAD, :] = (tail + jnp.where(row16 == 8 + me, line, 0.0)).astype(BF16)
-        for table, ref, c in ((y_t, y_out.at[who_ref[b]], 0), (dx_t, dx_out[b], 1)):
-            copy = pltpu.make_async_copy(table.at[b], ref, out_sem.at[c, b])
-            copy.start()
-            stores.append(copy)
+    stores = [
+        pltpu.make_async_copy(dx_t, dx_out, out_sem.at[0]),
+        pltpu.make_async_copy(y_t, y_out, out_sem.at[1]),
+    ]
+    for copy in stores:
+        copy.start()
     for copy in stores:
         copy.wait()
 
@@ -279,23 +485,23 @@
     return -(-nb * SEQ // TILE) * TILE
 
 
-def experts(who, h_blocks, dy_all, weights):
-    nb = len(h_blocks)
+def experts(member, h_all, dy_all, weights):
+    nb = h_all.shape[0]
     rows = expert_rows(nb)
     hbm = pl.BlockSpec(memory_space=pl.ANY)
     sm = pl.BlockSpec(memory_space=pltpu.SMEM)
-    block = jax.ShapeDtypeStruct((PAD, D), BF16)
-    outs = pl.pallas_call(
+    table = jax.ShapeDtypeStruct((nb, PAD, D), BF16)
+    return pl.pallas_call(
         functools.partial(expert_kernel, nb),
-        out_shape=[block] * nb
-        + [
-            jax.ShapeDtypeStruct((nb, PAD, D), BF16),
+        out_shape=[
+            table,
+            table,
             jax.ShapeDtypeStruct((2, rows, D), BF16),
             jax.ShapeDtypeStruct((2, rows, 4 * FFS), BF16),
             jax.ShapeDtypeStruct((1,), jnp.int32),
         ],
-        in_specs=[sm] + [hbm] * (nb + 5),
-        out_specs=[hbm] * (nb + 3) + [sm],
+        in_specs=[sm, hbm, hbm, hbm],
+        out_specs=[hbm] * 4 + [sm],
         scratch_shapes=[
             pltpu.VMEM((nb, PAD, D), BF16),
             pltpu.VMEM((nb, PAD, D), BF16),
@@ -311,8 +517,8 @@
             pltpu.VMEM((2, 2, TILE, D), BF16),
             pltpu.SMEM((nb,), jnp.int32),
             pltpu.SMEM((nb,), jnp.int32),
-            pltpu.SemaphoreType.DMA((2, nb)),
-            pltpu.SemaphoreType.DMA((2, nb)),
+            pltpu.SemaphoreType.DMA((2,)),
+            pltpu.SemaphoreType.DMA((2,)),
             pltpu.SemaphoreType.DMA((2,)),
             pltpu.SemaphoreType.DMA((2,)),
             pltpu.SemaphoreType.DMA((4, E)),
@@ -320,8 +526,7 @@
         compiler_params=pltpu.CompilerParams(vmem_limit_bytes=VMEM_LIMIT),
         cost_estimate=pl.CostEstimate(flops=30 * 10**9, bytes_accessed=4 * 10**7, transcendentals=4 * 10**6),
         name="experts",
-    )(who, *h_blocks, dy_all, *weights)
-    return outs[:nb], *outs[nb:]
+    )(member.reshape(1), h_all, dy_all, weights)
 
 
 def expert_grad_kernel(tiles_ref, rows_ref, hid_ref, out_ref, acc):
@@ -403,20 +608,17 @@
 
 
 def attn_backward_kernel(imgs, *refs):
-    dh_in, x1_in, x_in, dy_in, probs_in, qkv_in, o_in, lse_in = (
-        refs[i * imgs : (i + 1) * imgs] for i in range(8)
-    )
-    order_ref, par_ref, wa_ref, wb_ref = refs[8 * imgs : 8 * imgs + 4]
-    packs, dtok_ref = refs[8 * imgs + 4 : 8 * imgs + 7], refs[8 * imgs + 7]
-    dx1_s, low_s, h1_s, dh1_s, dqkv_s, o_s, w_s, sem = refs[8 * imgs + 8 :]
+    dh_in = refs[:imgs]
+    x1_in, x_in, dy_in, probs_in, qkv_in, o_in, lse_in, w_ref = refs[imgs : imgs + 8]
+    packs, dtok_ref = refs[imgs + 8 : imgs + 11], refs[imgs + 11]
+    dx1_s, low_s, h1_s, dh1_s, dqkv_s, o_s = refs[imgs + 12 :]
     n_dp, d_own = packs[0].shape[0], packs[0].shape[1] - 16
-    copies = load_attn_weights(order_ref, wa_ref, wb_ref, w_s, sem)
 
     def pack_of(r):
         return packs[r] if r < 2 else packs[2].at[:, r - 2]
 
-    par = par_ref[...].astype(F32)
-    router = par_ref[8:16, :]
+    par = params_of(w_ref[0])
+    router = par[8:16].astype(BF16)
     row_ok = iota((PAD, 1), 0) < SEQ
     lane_ok = iota((E, PAD), 1) < SEQ
     key_ok = iota((PAD, PAD), 1) < SEQ
@@ -427,32 +629,30 @@
         span = slice(c * PAD, (c + 1) * PAD)
         arrived = dh_in[c][...].astype(F32)
         dgate = arrived[PAD - 8 :, :PAD]
-        probs = probs_in[c][...]
+        probs = probs_in[c]
         dlogits = probs * (dgate - jnp.sum(probs * dgate, axis=0, keepdims=True))
         dlogits = jnp.where(lane_ok, dlogits, 0.0).astype(BF16)
-        unit, scale = normalise(x1_in[c][...])
+        unit, scale = normalise(x1_in[c])
         h2 = (unit * par[2:3] + par[3:4]).astype(BF16)
         g_router = g_router + dot(dlogits, h2)
         dh2 = jnp.where(row_ok, arrived + dot_tn(dlogits, router), 0.0)
         small2g = small2g + jnp.sum(dh2 * unit, axis=0, keepdims=True)
         small2b = small2b + jnp.sum(dh2, axis=0, keepdims=True)
-        dx1 = dy_in[c][...].astype(F32) + norm_back(dh2, unit, scale, par[2:3])
+        dx1 = dy_in[c].astype(F32) + norm_back(dh2, unit, scale, par[2:3])
         dx1_s[span, :] = dx1
         low_s[span, :] = dx1.astype(BF16)
-        unit1, _ = normalise(x_in[c][...].astype(F32))
+        unit1, _ = normalise(x_in[c].astype(F32))
         h1_s[span, :] = (unit1 * par[0:1] + par[1:2]).astype(BF16)
     low = low_s[...]
     h1 = h1_s[...]
     for r in range(4):
-        for copy in copies[r]:
-            copy.wait()
-        w = w_s[r]
-        dout = dot(low, w[:, 9 * HD :]).astype(BF16)
+        w = w_ref[r]
+        dout = dot(low, w[:, 9 * HD : D]).astype(BF16)
         for c in range(imgs):
             span = slice(c * PAD, (c + 1) * PAD)
-            qkv = qkv_in[c][r]
-            lse = lse_in[c][...]
-            o_s[span, :] = o_in[c][r]
+            qkv = qkv_in[c, r]
+            lse = lse_in[c]
+            o_s[span, :] = o_in[c, r]
             dqs, dks, dvs = [], [], []
             for h in range(3):
                 q = qkv[:, h * HD : (h + 1) * HD]
@@ -478,7 +678,7 @@
     for c in range(imgs):
         span = slice(c * PAD, (c + 1) * PAD)
         dh1 = jnp.where(row_ok, dh1_s[span, :], 0.0)
-        unit1, scale1 = normalise(x_in[c][...].astype(F32))
+        unit1, scale1 = normalise(x_in[c].astype(F32))
         small1g = small1g + jnp.sum(dh1 * unit1, axis=0, keepdims=True)
         small1b = small1b + jnp.sum(dh1, axis=0, keepdims=True)
         dtok_ref[c] = (dx1_s[span, :] + norm_back(dh1, unit1, scale1, par[0:1])).astype(BF16)
@@ -489,10 +689,8 @@
             pack_of(r)[i, d_own:, :] = line.astype(BF16)
 
 
-def attn_backward(dh, x1, x, dy, probs, qkv, o, lse, order, par, wa, wb, n_dp):
+def attn_backward(dh, saved, w, n_dp):
     imgs = len(dh)
-    hbm = pl.BlockSpec(memory_space=pl.ANY)
-    sm = pl.BlockSpec(memory_space=pltpu.SMEM)
     pack = (n_dp, D // n_dp + 16, D)
     vm = pl.BlockSpec(memory_space=pltpu.VMEM)
     rows = imgs * PAD
@@ -504,7 +702,7 @@
             jax.ShapeDtypeStruct((n_dp, 2) + pack[1:], BF16),
             jax.ShapeDtypeStruct((imgs, PAD, D), BF16),
         ),
-        in_specs=[vm] * (8 * imgs) + [sm, vm, hbm, hbm],
+        in_specs=[vm] * (imgs + 8),
         out_specs=(vm,) * 4,
         scratch_shapes=[
             pltpu.VMEM((rows, D), F32),
@@ -513,25 +711,14 @@
             pltpu.VMEM((rows, D), F32),
             pltpu.VMEM((rows, 9 * HD), BF16),
             pltpu.VMEM((rows, 3 * HD), BF16),
-            pltpu.VMEM((4, D, D), BF16),
-            pltpu.SemaphoreType.DMA((4, E)),
         ],
         compiler_params=pltpu.CompilerParams(vmem_limit_bytes=VMEM_LIMIT),
         cost_estimate=pl.CostEstimate(flops=12 * 10**9, bytes_accessed=2 * 10**7, transcendentals=2 * 10**6),
         name="attn_backward",
-    )(*dh, *x1, *x, *dy, *probs, *qkv, *o, *lse, order, par, wa, wb)
+    )(*dh, *saved, w)
 
 
 RING = (0, 2, 4, 6, 7, 5, 3, 1)
-
-
-def ring_place(member):
-    even = lax.rem(member, 2) == 0
-    return jnp.where(even, lax.div(member, 2), E - 1 - lax.div(member, 2))
-
-
-def ring_member(place):
-    return jnp.where(place < E // 2, 2 * place, 2 * E - 1 - 2 * place)
 
 
 class Mover:
@@ -579,29 +766,24 @@
             value, "dp", scatter_dimension=0, tiled=False, axis_index_groups=self.group_lists()
         )
 
-    def ring_blocks(self, block, way):
-        blocks = [block]
-        for _ in range(E - 1):
-            blocks.append(self.along(blocks[-1], way))
-        return blocks
-
-    def ring_sum(self, blocks, way):
-        total = blocks[1]
-        for k in range(2, E + 1):
-            total = self.along(total, way)
-            total = (total.astype(F32) + blocks[k % E].astype(F32)).astype(BF16)
-        return total
-
-    def both_ways(self, block):
-        found = [(self.member, block)]
-        ahead = back = block
-        for k in range(1, E // 2 + 1):
-            ahead = self.along(ahead, 0)
-            found.append((self.behind(0, k), ahead))
-            if k < E // 2:
-                back = self.along(back, 1)
-                found.append((self.behind(1, k), back))
-        return found
+    def front(self, pack, ew, dy, x, noise, keep):
+        own = lax.all_gather(pack, "dp", axis=0, tiled=True)
+        two = jnp.stack([own, self.other(own, 2)])
+        w = jnp.concatenate([two, self.other(two, 1)], axis=0)
+        blocks = jnp.zeros((2, E * pack.shape[0], FFS), BF16)
+        for by in range(E):
+            to = lax.rem(self.member + by, E)
+            block = lax.dynamic_index_in_dim(ew, to, 0, False)
+            came = lax.rem(self.member - by + E, E)
+            block = self.shift(block, by) if by else block
+            blocks = lax.dynamic_update_slice_in_dim(blocks, block, came * pack.shape[0], 1)
+        blocks = self.all_groups(blocks, 1)
+        blocks = jnp.swapaxes(blocks.reshape(2, E, D // E, FFS), 0, 1)
+        two = jnp.stack([blocks, self.other(blocks, 2)])
+        weights = jnp.concatenate([two, self.other(two, 1)], axis=0)
+        chunk, *saved = attn_forward(x, w, noise, keep)
+        table = (E * x.shape[0], PAD, D)
+        return self.gather(chunk).reshape(table), self.gather(dy).reshape(table), weights, w, *saved
 
     def sum_both_ways(self, block_for):
         def chain(way, steps):
@@ -615,17 +797,6 @@
         ahead = chain(0, E // 2)
         back = chain(1, E // 2 - 1)
         return ahead.astype(F32) + back.astype(F32) + block_for(self.member).astype(F32)
-
-    def in_order(self, members, parts, d_own):
-        if self.groups == 1:
-            return jnp.stack(members), jnp.stack([jnp.stack(blocks) for blocks in parts])
-        wholes = []
-        for blocks in parts:
-            rows = jnp.zeros((E * d_own,) + blocks[0].shape[1:], BF16)
-            for member, block in zip(members, blocks):
-                rows = lax.dynamic_update_slice_in_dim(rows, block[:d_own], member * d_own, 0)
-            wholes.append(self.all_groups(rows, 0).reshape((E, D // E) + blocks[0].shape[1:]))
-        return jnp.arange(E, dtype=jnp.int32), jnp.stack(wholes)
 
     def all_groups(self, part, dim):
         if self.groups == 1:
@@ -704,53 +875,28 @@
     d_own = w_qkv.shape[0]
     ways = [c % 2 for c in range(imgs)]
 
+    vectors = jnp.stack([ln1_gain, ln1_bias, ln2_gain, ln2_bias] + [jnp.zeros_like(ln1_gain)] * 4, axis=1)
     pack = jnp.concatenate(
-        [w_qkv[:, 0], w_qkv[:, 1], w_qkv[:, 2], jnp.transpose(w_attn_out)], axis=1
-    ).astype(BF16)
-    vectors = jnp.stack([ln1_gain, ln1_bias, ln2_gain, ln2_bias] + [jnp.zeros_like(ln1_gain)] * 4)
-    small = jnp.concatenate([vectors, jnp.transpose(router_weight)], axis=0).astype(BF16)
-    small = jnp.pad(small, ((0, 0), (0, D - d_own)))
-    pack = jnp.concatenate([pack, small], axis=0)
-    found = move.both_ways(pack)
-    par = jnp.zeros((E, 16, d_own), BF16)
-    for member, block in found:
-        par = lax.dynamic_update_slice_in_dim(par, block[None, d_own:, :d_own], member, 0)
-    par = jnp.transpose(move.all_groups(par, 0), (1, 0, 2)).reshape(16, D)
-    order, wa = move.in_order(
-        [member for member, _ in found], [[b for _, b in found], [move.other(b, 2) for _, b in found]], d_own
+        [w_qkv[:, 0], w_qkv[:, 1], w_qkv[:, 2], jnp.transpose(w_attn_out), vectors, router_weight], axis=1
     )
-    wb = move.other(wa, 1)
-
-    x = image_blocks(tokens, move.tensor, imgs)
-    dy = image_blocks(cotangent, move.tensor, imgs)
-    keep = image_lanes(kept_pairs(routes), move.tensor, imgs)
-    noise = image_lanes(jnp.transpose(router_noise), move.tensor, imgs)
-    out_rows = jnp.transpose(w_expert_out, (0, 2, 1))
-    blocks = []
-    for by in range(E):
-        to = lax.rem(move.member + by, E)
-        blocks.append(
-            jnp.stack([lax.dynamic_index_in_dim(w, to, 0, False).astype(BF16) for w in (w_in, out_rows)])
-        )
-    blocks, dy_own, x, keep, noise, wb = lax.optimization_barrier((blocks, jnp.stack(dy), x, keep, noise, wb))
-    dy_all = move.gather(dy_own)
-    came = [lax.rem(move.member - by + E, E) for by in range(E)]
-    blocks = [move.shift(blocks[by], by) if by else blocks[by] for by in range(E)]
-
-    fwd = [attn_forward(order, x[c], par, wa, wb, noise[c], keep[c]) for c in range(imgs)]
-    chunk, x1, qkv, o, lse, probs = (list(part) for part in zip(*fwd))
-
-    blocks = after(blocks, chunk)
-    e_order, e_own = move.in_order(came, [[b[kind] for b in blocks] for kind in range(2)], d_own)
-    e_own = jnp.swapaxes(e_own, 0, 1)
-    e_x = move.other(e_own, 2)
-    weights = [e_own, e_x, move.other(e_own, 1), move.other(e_x, 1)]
-    h_ring = [move.ring_blocks(chunk[c], ways[c]) for c in range(imgs)]
-    who = [move.behind(ways[c], k) * imgs + c for c in range(imgs) for k in range(E)] + [move.member]
-    who = jnp.concatenate([jnp.stack(who), e_order])
-    dh, y_all, rows, hid, tiles = experts(who, sum(h_ring, []), dy_all.reshape(imgs * E, PAD, D), weights)
-    dh = [dh[c * E : (c + 1) * E] for c in range(imgs)]
-    dh_sum = [dh[c][1] for c in range(imgs)]
+    pack = jnp.pad(pack, ((0, 0), (0, 128 - 16))).astype(BF16)
+    ew = jnp.stack([w_in, jnp.transpose(w_expert_out, (0, 2, 1))], axis=1).astype(BF16)
+    x = jnp.stack(image_blocks(tokens, move.tensor, imgs))
+    dy = jnp.stack(image_blocks(cotangent, move.tensor, imgs))
+    keep = jnp.stack(image_lanes(kept_pairs(routes), move.tensor, imgs))
+    noise = jnp.stack(image_lanes(jnp.transpose(router_noise), move.tensor, imgs))
+    if move.groups == 1:
+        h_all, dy_all, weights, w, *saved = front(pack, ew, dy, x, noise, keep)
+    else:
+        h_all, dy_all, weights, w, *saved = move.front(pack, ew, dy, x, noise, keep)
+    x1, qkv, o, lse, probs = saved
+
+    dh, y_all, rows, hid, tiles = experts(move.member, h_all, dy_all, weights)
+
+    def dh_for(c, k):
+        return lax.dynamic_index_in_dim(dh, move.behind(ways[c], k) * imgs + c, 0, False)
+
+    dh_sum = [dh_for(c, 1) for c in range(imgs)]
     g_work = {3: (1, 2), 4: (1, 0), 5: (0, 2), 6: (0, 0)}
     g_part = {}
     for k in range(2, E + 1):
@@ -759,7 +905,7 @@
             dh_sum, g_part[g_work[k]] = lax.optimization_barrier((dh_sum, part))
         for c in range(imgs):
             passed = move.along(dh_sum[c], ways[c])
-            dh_sum[c] = (passed.astype(F32) + dh[c][k % E].astype(F32)).astype(BF16)
+            dh_sum[c] = (passed.astype(F32) + dh_for(c, k % E).astype(F32)).astype(BF16)
     y_all = after(y_all, dh_sum)
     y_sum = move.scatter_sum(y_all.reshape(E, imgs, PAD, D))
     g_exp = {}
@@ -776,7 +922,7 @@
         g_exp[kind] = blocks
 
     pack0, pack1, packs, d_tok = attn_backward(
-        dh_sum, x1, x, dy, probs, qkv, o, lse, order, par, wa, wb, n_dp
+        dh_sum, (x1, x, dy, probs, qkv, o, lse), w, n_dp
     )
     passed = move.other(packs, 1)
     if move.groups > 1:
@@ -801,8 +947,9 @@
         return lay_out(at, [own, across, move.other(own, 1), move.other(across, 1)])
 
     d_tokens = all_rows(d_tok)
-    output = all_rows((jnp.stack(x1) + y_sum.astype(F32)).astype(BF16))
-    g_out, g_in = (unpack(jnp.stack(came), g_exp[kind]) for kind in (1, 0))
+    output = all_rows((x1 + y_sum.astype(F32)).astype(BF16))
+    came = jnp.stack([lax.rem(move.member - by + E, E) for by in range(E)])
+    g_out, g_in = (unpack(came, g_exp[kind]) for kind in (1, 0))
     return (
         output,
         d_tokens,

time: 630 us -> 575 us (0.913)
  Pallas kernels: 141 us -> 301 us
  waiting for transfers between devices: 218 us -> 108 us
  starting transfers between devices: 179 us -> 81.7 us
    pallas_call x3 -> x2, Pallas kernels: 63 us -> 223 us  [the longest x1 178 us: front(): pl.pallas_call(functools.partial(front_kernel, imgs), out_shape=(table, t...]
    ppermute x42 -> x21, waiting for transfers between devices: 77.7 us -> 23.4 us  [along(): return lax.ppermute(value, 'dp', self.ring[way])]
    ppermute x31 -> x19, waiting for transfers between devices: 109 us -> 55.7 us  [other(): return lax.ppermute(value, 'tensor', [(k, k ^ mask) for k in range(4)])]
    ppermute x21 -> x14, starting transfers between devices: 70.5 us -> 19.6 us  [shift(): return lax.ppermute(value, 'dp', perm)]
    ppermute x42 -> x21, starting transfers between devices: 88.2 us -> 47.6 us  [along(): return lax.ppermute(value, 'dp', self.ring[way])]
    convert_element_type x15 -> x8, other arithmetic: 3.76 us -> 10.9 us  [the longest x7 9.59 us: body(): dh_sum[c] = (passed.astype(F32) + dh_for(c, k % E).astype(F32)).astype(BF16)]
    ppermute x31 -> x19, starting transfers between devices: 20 us -> 14.5 us  [other(): return lax.ppermute(value, 'tensor', [(k, k ^ mask) for k in range(4)])]
    ppermute x21 -> x14, waiting for transfers between devices: 31.4 us -> 28.4 us  [shift(): return lax.ppermute(value, 'dp', perm)]
  transfers between devices with their start and end apart: 96 -> 55, of which waited for: 35 -> 13; matrix products, arithmetic and copies ran while one was open for 8% -> 5% of each run, Pallas kernels for 15% -> 13%
where the time goes in v3:
time: 575 us; the launch traced here: 569 us
  Pallas kernels  301 us (52%)
  waiting for transfers between devices  108 us (19%)
  starting transfers between devices  81.7 us (14%)
  other arithmetic  38.7 us (7%)
  local copies, waits for them, and re-layouts  25.5 us (4%)
  between operations  15.2 us (3%)
    pallas_call x1, Pallas kernels, front(): pl.pallas_call(functools.partial(front_kernel, imgs), out_shape=(table, t...  178 us
    ppermute x19, waiting for transfers between devices, other(): return lax.ppermute(value, 'tensor', [(k, k ^ mask) for k in range(4)])  55.7 us
    ppermute x21, starting transfers between devices, along(): return lax.ppermute(value, 'dp', self.ring[way])  47.6 us
    pallas_call x1, Pallas kernels, experts(): pl.pallas_call(functools.partial(expert_kernel, nb), out_shape=[table, ta...  45.3 us
    pallas_call x4, Pallas kernels, expert_grads(): pl.pallas_call(expert_grad_kernel, grid_spec=pltpu.PrefetchScalarGridSpec...  37.4 us
    ppermute x14, waiting for transfers between devices, shift(): return lax.ppermute(value, 'dp', perm)  28.4 us
    pallas_call x1, Pallas kernels, attn_backward(): pl.pallas_call(functools.partial(attn_backward_kernel, imgs), out_shape=(...  25.7 us
    ppermute x21, waiting for transfers between devices, along(): return lax.ppermute(value, 'dp', self.ring[way])  23.4 us
  transfers between devices with their start and end apart: 55, of which 13 were waited for; matrix products, arithmetic and copies ran while one was open for 5% of the time, Pallas kernels for 13%

profile of v3, /device:TPU:24, one launch (start us, length us, event | category | flops | bytes accessed | tf_op | source)
XLA Modules:
  0.0 569.2 jit_solution(10031714441117739176)
XLA Ops:
  26.7 178.0 %front.1 = (bf16[16,208,768]{2,1,0:T(8,128)(2,1)}, bf16[16,208,768]{2,1,0:T(8,128)(2,1)}, bf16[4,8,2,96,768]{4,3,2,1,0:T(8,128)(2,1)}, bf16[4,768,896]{2,1,0:T(8...) custom-call(bf16[96,896]{1,0:T(8,128)(2,1)} %pad.34.pack_ref, ...), custom_call_target="tpu_custom_call" | custom-call | flops 6000000000 | bytes 100000000 | tf_op jit(solution)/shard_map/front/pallas_call | solution.py:322
  204.7 45.3 %experts.1 = (bf16[16,208,768]{2,1,0:T(8,128)(2,1)}, bf16[16,208,768]{2,1,0:T(8,128)(2,1)}, bf16[2,3328,768]{2,1,0:T(8,128)(2,1)}, bf16[2,3328,3072]{2,1,0:T(8,128)(2,1)}, s32[1]{0:T(128)}) custom-call(s32[1]{0:T(128)} %bitcast.27.who_ref, bf16[16,208,768]{2,1,0:T(8,128)(2,1)} %get-tuple-element.43.refs_0_, bf16[16,208,768]{2,1,0:T(8,128)(2,1)} %get-tuple-element.44.refs_1_, ...), custom_call_target="tpu_custom_call" | custom-call | flops 30000001024 | bytes 40000000 | tf_op jit(solution)/shard_map/experts/pallas_call | solution.py:494
  251.2 6.4 %collective-permute-start = (bf16[208,768]{1,0:T(8,128)(2,1)S(1)}, bf16[208,768]{1,0:T(8,128)(2,1)S(1)}, u32[]{:S(2)}, u32[]{:S(2)}) collective-permute-start(bf16[208,768]{1,0:T(8,128)(2,1)S(1)} %get-tuple-element.110), channel_id=1, source_target_pairs={{0,8},{8,16},{16,24},{24,28},{28,20},{20,12},{12,4},{4,0},{1,9},{9... | collective-permute-start | bytes 958472 | tf_op jit(solution)/shard_map/ppermute | solution.py:740
  257.5 9.3 %expert_grads.4 = bf16[2,768,768]{2,1,0:T(8,128)(2,1)} custom-call(s32[1]{0:T(128)} %get-tuple-element.48.tiles_ref, bf16[2,3328,768]{2,1,0:T(8,128)(2,1)} %get-tuple-element.49.rows_ref, bf16[2,3328,3072]{2,1,0:T(8,128)(2,1)} %get-tuple-element.50.hid_ref), custom_call_target="tpu_custom_call" | custom-call | flops 4000000000 | bytes 15000000 | tf_op jit(solution)/shard_map/expert_grads/pallas_call | solution.py:546
  270.2 10.9 %collective-permute-start.3 = (bf16[208,768]{1,0:T(8,128)(2,1)S(1)}, bf16[208,768]{1,0:T(8,128)(2,1)S(1)}, u32[]{:S(2)}, u32[]{:S(2)}) collective-permute-start(bf16[208,768]{1,0:T(8,128)(2,1)S(1)} %get-tuple-element.52), channel_id=1, source_target_pairs={{8,0},{16,8},{24,16},{28,24},{20,28},{12,20},{4,12},{0,4},{9,1},{1... | collective-permute-start | bytes 958472 | tf_op jit(solution)/shard_map/ppermute | solution.py:740
  281.1 9.3 %expert_grads.5 = bf16[2,768,768]{2,1,0:T(8,128)(2,1)} custom-call(s32[1]{0:T(128)} %get-tuple-element.48.tiles_ref, bf16[2,3328,768]{2,1,0:T(8,128)(2,1)} %get-tuple-element.49.rows_ref, bf16[2,3328,3072]{2,1,0:T(8,128)(2,1)} %get-tuple-element.50.hid_ref), custom_call_target="tpu_custom_call" | custom-call | flops 4000000000 | bytes 15000000 | tf_op jit(solution)/shard_map/expert_grads/pallas_call | solution.py:546
  292.4 3.8 collective-permute-start.5
  296.1 9.3 %expert_grads.6 = bf16[2,768,768]{2,1,0:T(8,128)(2,1)} custom-call(s32[1]{0:T(128)} %get-tuple-element.48.tiles_ref, bf16[2,3328,768]{2,1,0:T(8,128)(2,1)} %get-tuple-element.49.rows_ref, bf16[2,3328,3072]{2,1,0:T(8,128)(2,1)} %get-tuple-element.50.hid_ref), custom_call_target="tpu_custom_call" | custom-call | flops 4000000000 | bytes 15000000 | tf_op jit(solution)/shard_map/expert_grads/pallas_call | solution.py:546
  307.1 4.4 collective-permute-start.7
  311.5 9.3 %expert_grads.7 = bf16[2,768,768]{2,1,0:T(8,128)(2,1)} custom-call(s32[1]{0:T(128)} %get-tuple-element.48.tiles_ref, bf16[2,3328,768]{2,1,0:T(8,128)(2,1)} %get-tuple-element.49.rows_ref, bf16[2,3328,3072]{2,1,0:T(8,128)(2,1)} %get-tuple-element.50.hid_ref), custom_call_target="tpu_custom_call" | custom-call | flops 4000000000 | bytes 15000000 | tf_op jit(solution)/shard_map/expert_grads/pallas_call | solution.py:546
  322.1 4.1 collective-permute-start.11
  326.2 4.5 collective-permute-done.11
  330.7 4.5 collective-permute-done.8
  338.5 5.0 collective-permute-done.12
  343.5 4.7 collective-permute-done.9
  349.5 3.6 collective-permute-start.13
  353.1 4.7 collective-permute-done.10
  359.9 25.7 %attn_backward.1 = (bf16[8,112,768]{2,1,0:T(8,128)(2,1)}, bf16[8,112,768]{2,1,0:T(8,128)(2,1)}, bf16[8,2,112,768]{3,2,1,0:T(8,128)(2,1)}, bf16[2,208,768]{2,1,0:T(8,128)(2,1)}) custom-call(bf16[208,768]{1,0:T(8,128)(2,1)} %get-tuple-element.96.refs_0_, bf16[208,768]{1,0:T(8,128)(2,1)} %get-tuple-element.95.refs_1_, ...), custom_call_target="tpu_custom_call" | custom-call | flops 12000000000 | bytes 20000000 | tf_op jit(solution)/shard_map/attn_backward/pallas_call | solution.py:697
  386.8 7.6 %collective-permute-done.45 = bf16[2,768,768]{2,1,0:T(8,128)(2,1)} collective-permute-done((bf16[2,768,768]{2,1,0:T(8,128)(2,1)}, bf16[2,768,768]{2,1,0:T(8,128)(2,1)}, u32[]{:S(2)}, u32[]{:S(2)}) %collective-permute-start.45) | collective-permute-done | bytes 2359328 | tf_op jit(solution)/shard_map/ppermute | solution.py:750
  410.6 22.0 %collective-permute-done.21 = bf16[112,768]{1,0:T(8,128)(2,1)} collective-permute-done((bf16[112,768]{1,0:T(8,128)(2,1)}, bf16[112,768]{1,0:T(8,128)(2,1)}, u32[]{:S(2)}, u32[]{:S(2)}) %collective-permute-start.21) | collective-permute-done | bytes 172064 | tf_op jit(solution)/shard_map/ppermute | solution.py:750
  435.9 25.6 %collective-permute-done.23 = bf16[112,768]{1,0:T(8,128)(2,1)S(1)} collective-permute-done((bf16[112,768]{1,0:T(8,128)(2,1)}, bf16[112,768]{1,0:T(8,128)(2,1)S(1)}, u32[]{:S(2)}, u32[]{:S(2)}) %collective-permute-start.23) | collective-permute-done | bytes 172064 | tf_op jit(solution)/shard_map/ppermute | solution.py:750
  467.6 4.8 collective-permute-start.48
  475.9 3.5 collective-permute-start.24
  482.2 2.8 collective-permute-done.49.refs_3_
  485.4 2.8 collective-permute-start.51
  493.2 11.7 %collective-permute-done.50.refs_4_ = bf16[96,768]{1,0:T(8,128)(2,1)S(1)} collective-permute-done((bf16[96,768]{1,0:T(8,128)(2,1)S(1)}, bf16[96,768]{1,0:T(8,128)(2,1)S(1)}, u32[]{:S(2)}, u32[]{:S(2)}) %collective-permute-start.50) | collective-permute-done | bytes 147488 | tf_op jit(solution)/shard_map/ppermute | solution.py:744
  506.9 3.7 collective-permute-start.26
  520.5 12.8 %collective-permute-done.40.refs_3_ = bf16[96,768]{1,0:T(8,128)(2,1)S(1)} collective-permute-done((bf16[96,768]{1,0:T(8,128)(2,1)S(1)}, bf16[96,768]{1,0:T(8,128)(2,1)S(1)}, u32[]{:S(2)}, u32[]{:S(2)}) %collective-permute-start.40) | collective-permute-done | bytes 147488 | tf_op jit(solution)/shard_map/ppermute | solution.py:744
  540.9 4.2 lay_out.3
  545.1 2.9 unpack.3
  548.7 2.9 unpack.2
  557.9 4.2 lay_out.2
  (287 shorter events, 99.8 us)
Async XLA Ops:
  7.2 504.1 %reduce-scatter.2.cloned.1.call-start = ((), (), s32[]{:S(2)}) async-start(), calls=%async_computation.1 | async-start | bytes 5750784 | tf_op jit(solution)/shard_map/reduce_scatter | solution.py:765
  251.2 15.7 %collective-permute-start = (bf16[208,768]{1,0:T(8,128)(2,1)S(1)}, bf16[208,768]{1,0:T(8,128)(2,1)S(1)}, u32[]{:S(2)}, u32[]{:S(2)}) collective-permute-start(bf16[208,768]{1,0:T(8,128)(2,1)S(1)} %get-tuple-element.110), channel_id=1, source_target_pairs={{0,8},{8,16},{16,24},{24,28},{28,20},{20,12},{12,4},{4,0},{1,9},{9... | collective-permute-start | bytes 958472 | tf_op jit(solution)/shard_map/ppermute | solution.py:740
  268.1 22.3 %collective-permute-start.2 = (bf16[208,768]{1,0:T(8,128)(2,1)S(1)}, bf16[208,768]{1,0:T(8,128)(2,1)S(1)}, u32[]{:S(2)}, u32[]{:S(2)}) collective-permute-start(bf16[208,768]{1,0:T(8,128)(2,1)S(1)} %get-tuple-element.51), channel_id=1, source_target_pairs={{0,8},{8,16},{16,24},{24,28},{28,20},{20,12},{12,4},{4,0},{1,9},{9... | collective-permute-start | bytes 958472 | tf_op jit(solution)/shard_map/ppermute | solution.py:740
  270.2 20.2 %collective-permute-start.3 = (bf16[208,768]{1,0:T(8,128)(2,1)S(1)}, bf16[208,768]{1,0:T(8,128)(2,1)S(1)}, u32[]{:S(2)}, u32[]{:S(2)}) collective-permute-start(bf16[208,768]{1,0:T(8,128)(2,1)S(1)} %get-tuple-element.52), channel_id=1, source_target_pairs={{8,0},{16,8},{24,16},{28,24},{20,28},{12,20},{4,12},{0,4},{9,1},{1... | collective-permute-start | bytes 958472 | tf_op jit(solution)/shard_map/ppermute | solution.py:740
  291.6 13.8 %collective-permute-start.4 = (bf16[208,768]{1,0:T(8,128)(2,1)S(1)}, bf16[208,768]{1,0:T(8,128)(2,1)S(1)}, u32[]{:S(2)}, u32[]{:S(2)}) collective-permute-start(bf16[208,768]{1,0:T(8,128)(2,1)S(1)} %get-tuple-element.53), channel_id=1, source_target_pairs={{0,8},{8,16},{16,24},{24,28},{28,20},{20,12},{12,4},{4,0},{1,9},{9... | collective-permute-start | bytes 958472 | tf_op jit(solution)/shard_map/ppermute | solution.py:740
  306.7 14.1 %collective-permute-start.6 = (bf16[208,768]{1,0:T(8,128)(2,1)S(1)}, bf16[208,768]{1,0:T(8,128)(2,1)S(1)}, u32[]{:S(2)}, u32[]{:S(2)}) collective-permute-start(bf16[208,768]{1,0:T(8,128)(2,1)S(1)} %get-tuple-element.55), channel_id=1, source_target_pairs={{0,8},{8,16},{16,24},{24,28},{28,20},{20,12},{12,4},{4,0},{1,9},{9... | collective-permute-start | bytes 958472 | tf_op jit(solution)/shard_map/ppermute | solution.py:740
  307.1 13.7 %collective-permute-start.7 = (bf16[208,768]{1,0:T(8,128)(2,1)S(1)}, bf16[208,768]{1,0:T(8,128)(2,1)S(1)}, u32[]{:S(2)}, u32[]{:S(2)}) collective-permute-start(bf16[208,768]{1,0:T(8,128)(2,1)S(1)} %get-tuple-element.56), channel_id=1, source_target_pairs={{8,0},{16,8},{24,16},{28,24},{20,28},{12,20},{4,12},{0,4},{9,1},{1... | collective-permute-start | bytes 958472 | tf_op jit(solution)/shard_map/ppermute | solution.py:740
  385.6 16.2 %collective-permute-start.20 = (bf16[8,2,112,768]{3,2,1,0:T(8,128)(2,1)}, bf16[8,2,112,768]{3,2,1,0:T(8,128)(2,1)S(1)}, u32[]{:S(2)}, u32[]{:S(2)}) collective-permute-start(bf16[8,2,112,768]{3,2,1,0:T(8,128)(2,1)} %get-tuple-element.67), channel_id=1, source_target_pairs={{0,1},{1,0},{2,3},{3,2},{4,5},{5,4},{6,7},{7,6},{8,9},{9,8},{10,11... | collective-permute-start | bytes 8257544 | tf_op jit(solution)/shard_map/ppermute | solution.py:750
  386.1 13.6 %collective-permute-start.36 = (bf16[2,768,768]{2,1,0:T(8,128)(2,1)}, bf16[2,768,768]{2,1,0:T(8,128)(2,1)}, u32[]{:S(2)}, u32[]{:S(2)}) collective-permute-start(bf16[2,768,768]{2,1,0:T(8,128)(2,1)} %expert_grads.6), channel_id=1, source_target_pairs={{0,1},{1,0},{2,3},{3,2},{4,5},{5,4},{6,7},{7,6},{8,9},{9,8},{10,11... | collective-permute-start | bytes 7077896 | tf_op jit(solution)/shard_map/ppermute | solution.py:750
  386.2 24.0 %collective-permute-start.17 = (bf16[2,208,768]{2,1,0:T(8,128)(2,1)}, bf16[2,208,768]{2,1,0:T(8,128)(2,1)}, u32[]{:S(2)}, u32[]{:S(2)}) collective-permute-start(bf16[2,208,768]{2,1,0:T(8,128)(2,1)} %get-tuple-element.65.refs_0_), channel_id=1, source_target_pairs={{0,2},{1,3},{2,0},{3,1},{4,6},{5,7},{6,4},{7,5},{8,10},{9,11},{10,... | collective-permute-start | bytes 1916936 | tf_op jit(solution)/shard_map/ppermute | solution.py:750
  399.1 35.4 %collective-permute-start.46 = (bf16[768,768]{1,0:T(8,128)(2,1)}, bf16[768,768]{1,0:T(8,128)(2,1)}, u32[]{:S(2)}, u32[]{:S(2)}) collective-permute-start(bf16[768,768]{1,0:T(8,128)(2,1)} %fusion.10), channel_id=1, source_target_pairs={{0,2},{1,3},{2,0},{3,1},{4,6},{5,7},{6,4},{7,5},{8,10},{9,11},{10,... | collective-permute-start | bytes 3538952 | tf_op jit(solution)/shard_map/ppermute | solution.py:750
  405.3 27.3 %collective-permute-start.21 = (bf16[112,768]{1,0:T(8,128)(2,1)}, bf16[112,768]{1,0:T(8,128)(2,1)}, u32[]{:S(2)}, u32[]{:S(2)}) collective-permute-start(bf16[112,768]{1,0:T(8,128)(2,1)} %get-tuple-element.129), channel_id=1, source_target_pairs={{0,2},{1,3},{2,0},{3,1},{4,6},{5,7},{6,4},{7,5},{8,10},{9,11},{10,... | collective-permute-start | bytes 516104 | tf_op jit(solution)/shard_map/ppermute | solution.py:750
  408.7 70.7 %collective-permute-start.37 = (bf16[768,768]{1,0:T(8,128)(2,1)}, bf16[768,768]{1,0:T(8,128)(2,1)}, u32[]{:S(2)}, u32[]{:S(2)}) collective-permute-start(bf16[768,768]{1,0:T(8,128)(2,1)} %fusion.8), channel_id=1, source_target_pairs={{0,2},{1,3},{2,0},{3,1},{4,6},{5,7},{6,4},{7,5},{8,10},{9,11},{10,... | collective-permute-start | bytes 3538952 | tf_op jit(solution)/shard_map/ppermute | solution.py:750
  410.1 62.5 %collective-permute-start.18 = (bf16[2,208,768]{2,1,0:T(8,128)(2,1)}, bf16[2,208,768]{2,1,0:T(8,128)(2,1)S(1)}, u32[]{:S(2)}, u32[]{:S(2)}) collective-permute-start(bf16[2,208,768]{2,1,0:T(8,128)(2,1)} %get-tuple-element.65.refs_0_), channel_id=1, source_target_pairs={{0,1},{1,0},{2,3},{3,2},{4,5},{5,4},{6,7},{7,6},{8,9},{9,8},{10,11... | collective-permute-start | bytes 1916936 | tf_op jit(solution)/shard_map/ppermute | solution.py:750
  410.1 62.6 %collective-permute-start.19 = (bf16[2,208,768]{2,1,0:T(8,128)(2,1)}, bf16[2,208,768]{2,1,0:T(8,128)(2,1)S(1)}, u32[]{:S(2)}, u32[]{:S(2)}) collective-permute-start(bf16[2,208,768]{2,1,0:T(8,128)(2,1)} %collective-permute-done.17.refs_1_), channel_id=1, source_target_pairs={{0,1},{1,0},{2,3},{3,2},{4,5},{5,4},{6,7},{7,6},{8,9},{9,8},{10,11... | collective-permute-start | bytes 1916936 | tf_op jit(solution)/shard_map/ppermute | solution.py:750
  432.6 28.9 %collective-permute-start.23 = (bf16[112,768]{1,0:T(8,128)(2,1)}, bf16[112,768]{1,0:T(8,128)(2,1)S(1)}, u32[]{:S(2)}, u32[]{:S(2)}) collective-permute-start(bf16[112,768]{1,0:T(8,128)(2,1)} %get-tuple-element.136), channel_id=1, source_target_pairs={{0,2},{1,3},{2,0},{3,1},{4,6},{5,7},{6,4},{7,5},{8,10},{9,11},{10,... | collective-permute-start | bytes 516104 | tf_op jit(solution)/shard_map/ppermute | solution.py:750
  434.5 30.6 %collective-permute-start.29 = (bf16[112,768]{1,0:T(8,128)(2,1)S(1)}, bf16[112,768]{1,0:T(8,128)(2,1)S(1)}, u32[]{:S(2)}, u32[]{:S(2)}) collective-permute-start(bf16[112,768]{1,0:T(8,128)(2,1)S(1)} %get-tuple-element.133), channel_id=1, source_target_pairs={{0,2},{1,3},{2,0},{3,1},{4,6},{5,7},{6,4},{7,5},{8,10},{9,11},{10,... | collective-permute-start | bytes 516104 | tf_op jit(solution)/shard_map/ppermute | solution.py:750
  473.3 14.9 %collective-permute-start.31 = (bf16[112,768]{1,0:T(8,128)(2,1)}, bf16[112,768]{1,0:T(8,128)(2,1)S(1)}, u32[]{:S(2)}, u32[]{:S(2)}) collective-permute-start(bf16[112,768]{1,0:T(8,128)(2,1)} %get-tuple-element.132), channel_id=1, source_target_pairs={{0,2},{1,3},{2,0},{3,1},{4,6},{5,7},{6,4},{7,5},{8,10},{9,11},{10,... | collective-permute-start | bytes 516104 | tf_op jit(solution)/shard_map/ppermute | solution.py:750
  475.9 14.3 %collective-permute-start.24 = (bf16[112,768]{1,0:T(8,128)(2,1)S(1)}, bf16[112,768]{1,0:T(8,128)(2,1)S(1)}, u32[]{:S(2)}, u32[]{:S(2)}) collective-permute-start(bf16[112,768]{1,0:T(8,128)(2,1)S(1)} %get-tuple-element.127), channel_id=1, source_target_pairs={{0,8},{8,16},{16,24},{24,28},{28,20},{20,12},{12,4},{4,0},{1,9},{9... | collective-permute-start | bytes 516104 | tf_op jit(solution)/shard_map/ppermute | solution.py:740
  485.0 19.8 %collective-permute-start.50 = (bf16[96,768]{1,0:T(8,128)(2,1)S(1)}, bf16[96,768]{1,0:T(8,128)(2,1)S(1)}, u32[]{:S(2)}, u32[]{:S(2)}) collective-permute-start(bf16[96,768]{1,0:T(8,128)(2,1)S(1)} %get-tuple-element.140), channel_id=1, source_target_pairs={{0,16},{4,20},{8,24},{12,28},{16,0},{20,4},{24,8},{28,12},{1,17},{... | collective-permute-start | bytes 442376 | tf_op jit(solution)/shard_map/ppermute | solution.py:744
  485.4 19.5 %collective-permute-start.51 = (bf16[96,768]{1,0:T(8,128)(2,1)S(1)}, bf16[96,768]{1,0:T(8,128)(2,1)S(1)}, u32[]{:S(2)}, u32[]{:S(2)}) collective-permute-start(bf16[96,768]{1,0:T(8,128)(2,1)S(1)} %get-tuple-element.139), channel_id=1, source_target_pairs={{0,20},{4,24},{8,28},{12,0},{16,4},{20,8},{24,12},{28,16},{1,21},{... | collective-permute-start | bytes 442376 | tf_op jit(solution)/shard_map/ppermute | solution.py:744
  488.2 17.4 %collective-permute-start.52 = (bf16[96,768]{1,0:T(8,128)(2,1)S(1)}, bf16[96,768]{1,0:T(8,128)(2,1)S(1)}, u32[]{:S(2)}, u32[]{:S(2)}) collective-permute-start(bf16[96,768]{1,0:T(8,128)(2,1)S(1)} %get-tuple-element.138), channel_id=1, source_target_pairs={{0,24},{4,28},{8,0},{12,4},{16,8},{20,12},{24,16},{28,20},{1,25},{... | collective-permute-start | bytes 442376 | tf_op jit(solution)/shard_map/ppermute | solution.py:744
  490.2 16.7 %collective-permute-start.53 = (bf16[96,768]{1,0:T(8,128)(2,1)S(1)}, bf16[96,768]{1,0:T(8,128)(2,1)S(1)}, u32[]{:S(2)}, u32[]{:S(2)}) collective-permute-start(bf16[96,768]{1,0:T(8,128)(2,1)S(1)} %get-tuple-element.137), channel_id=1, source_target_pairs={{0,28},{4,0},{8,4},{12,8},{16,12},{20,16},{24,20},{28,24},{1,29},{... | collective-permute-start | bytes 442376 | tf_op jit(solution)/shard_map/ppermute | solution.py:744
  491.2 19.4 %collective-permute-start.38 = (bf16[96,768]{1,0:T(8,128)(2,1)S(1)}, bf16[96,768]{1,0:T(8,128)(2,1)S(1)}, u32[]{:S(2)}, u32[]{:S(2)}) collective-permute-start(bf16[96,768]{1,0:T(8,128)(2,1)S(1)} %get-tuple-element.151), channel_id=1, source_target_pairs={{0,4},{4,8},{8,12},{12,16},{16,20},{20,24},{24,28},{28,0},{1,5},{5... | collective-permute-start | bytes 442376 | tf_op jit(solution)/shard_map/ppermute | solution.py:744
  512.6 20.6 %collective-permute-start.40 = (bf16[96,768]{1,0:T(8,128)(2,1)S(1)}, bf16[96,768]{1,0:T(8,128)(2,1)S(1)}, u32[]{:S(2)}, u32[]{:S(2)}) collective-permute-start(bf16[96,768]{1,0:T(8,128)(2,1)S(1)} %copy-done.35), channel_id=1, source_target_pairs={{0,12},{4,16},{8,20},{12,24},{16,28},{20,0},{24,4},{28,8},{1,13},{... | collective-permute-start | bytes 442376 | tf_op jit(solution)/shard_map/ppermute | solution.py:744
  513.4 22.2 %collective-permute-start.41 = (bf16[96,768]{1,0:T(8,128)(2,1)S(1)}, bf16[96,768]{1,0:T(8,128)(2,1)S(1)}, u32[]{:S(2)}, u32[]{:S(2)}) collective-permute-start(bf16[96,768]{1,0:T(8,128)(2,1)S(1)} %copy-done.34), channel_id=1, source_target_pairs={{0,16},{4,20},{8,24},{12,28},{16,0},{20,4},{24,8},{28,12},{1,17},{... | collective-permute-start | bytes 442376 | tf_op jit(solution)/shard_map/ppermute | solution.py:744
  515.7 20.6 %collective-permute-start.42 = (bf16[96,768]{1,0:T(8,128)(2,1)S(1)}, bf16[96,768]{1,0:T(8,128)(2,1)S(1)}, u32[]{:S(2)}, u32[]{:S(2)}) collective-permute-start(bf16[96,768]{1,0:T(8,128)(2,1)S(1)} %copy-done.33), channel_id=1, source_target_pairs={{0,20},{4,24},{8,28},{12,0},{16,4},{20,8},{24,12},{28,16},{1,21},{... | collective-permute-start | bytes 442376 | tf_op jit(solution)/shard_map/ppermute | solution.py:744
  516.7 22.2 %collective-permute-start.43 = (bf16[96,768]{1,0:T(8,128)(2,1)S(1)}, bf16[96,768]{1,0:T(8,128)(2,1)S(1)}, u32[]{:S(2)}, u32[]{:S(2)}) collective-permute-start(bf16[96,768]{1,0:T(8,128)(2,1)S(1)} %copy-done.32), channel_id=1, source_target_pairs={{0,24},{4,28},{8,0},{12,4},{16,8},{20,12},{24,16},{28,20},{1,25},{... | collective-permute-start | bytes 442376 | tf_op jit(solution)/shard_map/ppermute | solution.py:744
  517.4 36.3 %collective-permute-start.14 = (bf16[2,208,768]{2,1,0:T(8,128)(2,1)S(1)}, bf16[2,208,768]{2,1,0:T(8,128)(2,1)S(1)}, u32[]{:S(2)}, u32[]{:S(2)}) collective-permute-start(bf16[2,208,768]{2,1,0:T(8,128)(2,1)S(1)} %fusion.6.refs_0_), channel_id=1, source_target_pairs={{0,2},{1,3},{2,0},{3,1},{4,6},{5,7},{6,4},{7,5},{8,10},{9,11},{10,... | collective-permute-start | bytes 1916936 | tf_op jit(solution)/shard_map/ppermute | solution.py:750
  533.9 17.7 %collective-permute-start.35 = (bf16[112,768]{1,0:T(8,128)(2,1)S(1)}, bf16[112,768]{1,0:T(8,128)(2,1)S(1)}, u32[]{:S(2)}, u32[]{:S(2)}) collective-permute-start(bf16[112,768]{1,0:T(8,128)(2,1)S(1)} %get-tuple-element.130), channel_id=1, source_target_pairs={{0,2},{1,3},{2,0},{3,1},{4,6},{5,7},{6,4},{7,5},{8,10},{9,11},{10,... | collective-permute-start | bytes 516104 | tf_op jit(solution)/shard_map/ppermute | solution.py:750
  536.2 15.4 %collective-permute-start.28 = (bf16[112,768]{1,0:T(8,128)(2,1)}, bf16[112,768]{1,0:T(8,128)(2,1)S(1)}, u32[]{:S(2)}, u32[]{:S(2)}) collective-permute-start(bf16[112,768]{1,0:T(8,128)(2,1)} %get-tuple-element.123), channel_id=1, source_target_pairs={{0,8},{8,16},{16,24},{24,28},{28,20},{20,12},{12,4},{4,0},{1,9},{9... | collective-permute-start | bytes 516104 | tf_op jit(solution)/shard_map/ppermute | solution.py:740
  536.9 14.7 %collective-permute-start.34 = (bf16[112,768]{1,0:T(8,128)(2,1)}, bf16[112,768]{1,0:T(8,128)(2,1)S(1)}, u32[]{:S(2)}, u32[]{:S(2)}) collective-permute-start(bf16[112,768]{1,0:T(8,128)(2,1)} %get-tuple-element.124), channel_id=1, source_target_pairs={{8,0},{16,8},{24,16},{28,24},{20,28},{12,20},{4,12},{0,4},{9,1},{1... | collective-permute-start | bytes 516104 | tf_op jit(solution)/shard_map/ppermute | solution.py:740
  (82 other events, 634.2 us)
Sparse Core Ops, SparseCore 0:
  360.1 100.7 reduce-scatter.1

commit v4 on v3

--- a/solution.py
+++ b/solution.py
@@ -18,7 +18,7 @@
 TILE = 256
 FFS = 768
 EPS = 1e-06
-VMEM_LIMIT = 60 * 1024 * 1024
+VMEM_LIMIT = 62 * 1024 * 1024
 
 F32 = jnp.float32
 BF16 = jnp.bfloat16
@@ -185,10 +185,39 @@
         return copy
 
 
+def expert_step(x, dy, gate, w_ref, g_ref, y_ref, dx_ref):
+    weight = jnp.maximum(gate, 0.0)
+    d_rows = (dy.astype(F32) * weight).astype(BF16)
+
+    def hidden(r, carry):
+        w1 = w_ref[r, :, 0].reshape(D, FFS)
+        w2 = w_ref[r, :, 1].reshape(D, FFS)
+        a = dot(x, w1)
+        a2 = a * a
+        th = jnp.tanh(0.7978845608028654 * a * (1.0 + 0.044715 * a2))
+        half = 0.5 * (1.0 + th)
+        hid = (a * half).astype(BF16)
+        slope = half + 0.5 * a * (1.0 - th * th) * (0.7978845608028654 * (1.0 + 3 * 0.044715 * a2))
+        da = (dot(d_rows, w2) * slope).astype(BF16)
+        y_ref[...] += dot_nt(hid, w2)
+        dx_ref[...] += dot_nt(da, w1)
+        g_ref[r, 0] += dot_tn(x, da)
+        g_ref[r, 1] += dot_tn(d_rows, hid)
+        return carry
+
+    y_ref[...] = jnp.zeros_like(y_ref)
+    dx_ref[...] = jnp.zeros_like(dx_ref)
+    lax.fori_loop(0, 4, hidden, 0)
+    y = y_ref[...]
+    dgate = jnp.where(gate >= 0, jnp.sum(dy.astype(F32) * y, axis=1, keepdims=True), 0.0)
+    return (y * weight).astype(BF16), dx_ref[...], dgate
+
+
 def front_kernel(
     imgs, pack_ref, ew_ref, dy_ref, x_ref, noise_ref, keep_ref,
-    h_out, dy_out, ew_out, w_out, x1_ref, qkv_ref, o_ref, lse_ref, probs_ref,
-    w_s, chunk_s, p_s, p_r, px_s, px_r, pc_s, pc_r, d_s, d_r, h_s, h_r, e_s, e_r, ex_s, ex_r, ec_s, ec_r, local,
+    h_out, dy_out, t_in, g_out, sums_out, w_out, x1_ref, qkv_ref, o_ref, lse_ref, probs_ref,
+    w_s, chunk_s, we_s, g_s, xs, dys, y_s, dx_s, t_s, pass_s, g_low,
+    p_s, p_r, px_s, px_r, pc_s, pc_r, d_s, d_r, h_s, h_r, e_s, e_r, ex_s, ex_r, ec_s, ec_r, t_ss, t_r, local, stage, g_sem,
 ):
     peers = Peers()
     member = peers.member
@@ -199,8 +228,8 @@
     def rows(of):
         return pl.ds(pl.multiple_of(of * d_own, 16), d_own)
 
-    locals_ = [pltpu.make_async_copy(pack_ref, w_s.at[0, rows(member)], local.at[0])]
-    locals_[0].start()
+    own_pack = pltpu.make_async_copy(pack_ref, w_s.at[0, rows(member)], local.at[0])
+    own_pack.start()
 
     ring, px, pc = {}, {}, {}
 
@@ -231,16 +260,25 @@
     e_copy = {}
     for by in range(1, E):
         to = peers.ahead(by)
-        e_copy[by] = peers.send(ew_ref.at[to], ew_out.at[0, member], (e_s, e_r), by, {"dp": peers.base + to})
-
-    d_ring, h_ring = {}, {}
-
-    def row_ring(c, k, src, out, kept, sems):
-        at = peers.behind(c % 2, k) * imgs + c if k else member * imgs + c
-        kept[c, k] = peers.send(src if k == 0 else out.at[at], out.at[at], sems, (c, k), peers.next[c % 2])
-
+        e_copy[by] = peers.send(ew_ref.at[to], we_s.at[0, member], (e_s, e_r), by, {"dp": peers.base + to})
+
+    def block_at(c, k):
+        return peers.behind(c % 2, k) * imgs + c
+
+    def row_copy(out, sems, c, k, src=None):
+        at = block_at(c, k)
+        return pltpu.make_async_remote_copy(
+            src_ref=out.at[at] if src is None else src,
+            dst_ref=out.at[at],
+            send_sem=sems[0].at[c, k],
+            recv_sem=sems[1].at[c, k],
+            device_id=peers.next[c % 2],
+            device_id_type=pl.DeviceIdType.MESH,
+        )
+
+    h_sems, d_sems = (h_s, h_r), (d_s, d_r)
     for c in range(imgs):
-        row_ring(c, 0, dy_ref.at[c], dy_out, d_ring, (d_s, d_r))
+        row_copy(dy_out, d_sems, c, 0, dy_ref.at[c]).start()
     for number in range(len(arrivals) - 1, len(arrivals) + 1):
         pass_x(number)
 
@@ -250,23 +288,23 @@
         if by:
             e_copy[by].wait_recv()
         of = peers.came(by)
-        src = ew_out.at[0, of] if by else ew_ref.at[member]
-        ex[by] = peers.send(src, ew_out.at[1, of], (ex_s, ex_r), by, peers.across)
-        ec[0, by] = peers.send(src, ew_out.at[2, of], (ec_s, ec_r), (0, by), peers.core)
+        src = we_s.at[0, of] if by else ew_ref.at[member]
+        ex[by] = peers.send(src, we_s.at[1, of], (ex_s, ex_r), by, peers.across)
+        ec[0, by] = peers.send(src, we_s.at[2, of], (ec_s, ec_r), (0, by), peers.core)
 
     def pass_ex(by):
         ex[by].wait_recv()
         of = peers.came(by)
-        ec[1, by] = peers.send(ew_out.at[1, of], ew_out.at[3, of], (ec_s, ec_r), (1, by), peers.core)
+        ec[1, by] = peers.send(we_s.at[1, of], we_s.at[3, of], (ec_s, ec_r), (1, by), peers.core)
 
     for number in range(E):
         pc[0, number].wait_recv()
         pc[1, number].wait_recv()
-    locals_[0].wait()
+    own_pack.wait()
     pass_e(0)
     keepers = [
         pltpu.make_async_copy(w_s, w_out, local.at[1]),
-        pltpu.make_async_copy(ew_ref.at[member], ew_out.at[0, member], local.at[2]),
+        pltpu.make_async_copy(ew_ref.at[member], we_s.at[0, member], local.at[2]),
     ] + [
         pltpu.make_async_copy(dy_ref.at[c], dy_out.at[member * imgs + c], local.at[3 + c]) for c in range(imgs)
     ]
@@ -279,35 +317,137 @@
             x_ref[c], par, lambda r: w_s[r], noise_ref[c], keep_ref[c],
             chunk_s.at[c], *(ref.at[c] for ref in (x1_ref, qkv_ref, o_ref, lse_ref, probs_ref)),
         )
-        row_ring(c, 0, chunk_s.at[c], h_out, h_ring, (h_s, h_r))
+        row_copy(h_out, h_sems, c, 0, chunk_s.at[c]).start()
         keepers.append(
             pltpu.make_async_copy(chunk_s.at[c], h_out.at[member * imgs + c], local.at[3 + imgs + c])
         )
         keepers[-1].start()
-        if c == 0:
-            for i in range(imgs):
-                d_ring[i, 0].wait_recv()
-                row_ring(i, 1, None, dy_out, d_ring, (d_s, d_r))
-
-    for k in range(1, E):
-        for c in range(imgs):
-            h_ring[c, k - 1].wait_recv()
-            if k < E - 1:
-                row_ring(c, k, None, h_out, h_ring, (h_s, h_r))
-        if k < E - 1:
-            for c in range(imgs):
-                d_ring[c, k].wait_recv()
-                if k + 1 < E - 1:
-                    row_ring(c, k + 1, None, dy_out, d_ring, (d_s, d_r))
-        for by in {2: (1, 7), 3: (2, 6), 4: (3, 5), 5: (4,)}.get(k, ()):
-            pass_e(by)
-        for by in {2: (0,), 3: (1, 7), 4: (2, 6), 5: (3, 5), 6: (4,)}.get(k, ()):
-            pass_ex(by)
+
+    far = (1, 7, 2, 6, 3, 5, 4)
+    for i, by in enumerate(far):
+        pass_e(by)
+        if i >= 1:
+            pass_ex((0, *far)[i - 1])
+    g_s[...] = jnp.zeros_like(g_s)
+    for by in (0, *far)[len(far) - 1 :]:
+        pass_ex(by)
     for by in range(E):
         ec[0, by].wait_recv()
         ec[1, by].wait_recv()
     for copy in keepers:
         copy.wait()
+
+    row16 = iota((16, D), 0)
+    eye = iota((PAD, PAD), 0) == iota((PAD, PAD), 1)
+
+    def sum_copy(flow, c, k):
+        return pltpu.make_async_remote_copy(
+            src_ref=pass_s.at[lax.rem(k, 2), flow, c],
+            dst_ref=t_in.at[k - 1, flow, c],
+            send_sem=t_ss.at[flow, c, k - 1],
+            recv_sem=t_r.at[flow, c, k - 1],
+            device_id=peers.next[c % 2],
+            device_id_type=pl.DeviceIdType.MESH,
+        )
+
+    own_sums = pltpu.make_async_copy(pass_s.at[0], t_in.at[E - 1], local.at[0])
+
+    def fetch_sums(k):
+        copies = []
+        for flow in range(2):
+            for c in range(imgs):
+                sum_copy(flow, c, k - 1).wait_recv()
+                copies.append(pltpu.make_async_copy(t_in.at[k - 2, flow, c], t_s.at[flow, c], stage.at[flow, c]))
+                copies[-1].start()
+        for copy in copies:
+            copy.wait()
+
+    def step(k, carry):
+        for c in range(imgs):
+            for out, sems in ((h_out, h_sems), (dy_out, d_sems)):
+
+                @pl.when(k > 0)
+                def _():
+                    row_copy(out, sems, c, k - 1).wait_recv()
+
+                @pl.when((k > 0) & (k < E - 1))
+                def _():
+                    row_copy(out, sems, c, k).start()
+
+        loads = []
+        for c in range(imgs):
+            for i, (out, held) in enumerate(((h_out, xs), (dy_out, dys))):
+                loads.append(pltpu.make_async_copy(out.at[block_at(c, k)], held.at[c], stage.at[i, c]))
+                loads[-1].start()
+        for copy in loads:
+            copy.wait()
+        columns = []
+        for c in range(imgs):
+            meta = xs[c, PAD - 16 :, :].astype(F32)
+            line = jnp.sum(jnp.where(row16 == 8 + member, meta, 0.0), axis=0, keepdims=True)[:, :PAD]
+            columns.append(jnp.sum(jnp.where(eye, line, 0.0), axis=1, keepdims=True))
+        y, dx, dgate = expert_step(
+            xs[...].reshape(imgs * PAD, D), dys[...].reshape(imgs * PAD, D), jnp.concatenate(columns, axis=0),
+            we_s, g_s, y_s, dx_s,
+        )
+        slot = lax.rem(k, 2)
+
+        @pl.when(k >= 3)
+        def _():
+            for flow in range(2):
+                for c in range(imgs):
+                    sum_copy(flow, c, k - 2).wait_send()
+
+        for c in range(imgs):
+            span = slice(c * PAD, (c + 1) * PAD)
+            line = jnp.sum(jnp.where(eye, dgate[span], 0.0), axis=0, keepdims=True)
+            line = jnp.concatenate([line, jnp.zeros((1, D - PAD), F32)], axis=1)
+            tail = dx[span][PAD - 16 :] + jnp.where(row16 == 8 + member, line, 0.0)
+            pass_s[slot, 0, c] = jnp.concatenate([dx[span][: PAD - 16], tail], axis=0).astype(BF16)
+            pass_s[slot, 1, c] = y[span]
+
+        @pl.when(k == 0)
+        def _():
+            own_sums.start()
+            own_sums.wait()
+
+        @pl.when(k >= 2)
+        def _():
+            fetch_sums(k)
+            pass_s[slot] = (pass_s[slot].astype(F32) + t_s[...].astype(F32)).astype(BF16)
+
+        @pl.when(k >= 1)
+        def _():
+            for flow in range(2):
+                for c in range(imgs):
+                    sum_copy(flow, c, k).start()
+
+        return carry
+
+    lax.fori_loop(0, E, step, 0)
+
+    for i in range(8):
+        r, kind = i // 2, i % 2
+        if i >= 2:
+            pltpu.make_async_copy(g_low.at[i % 2], g_out.at[r, :, kind], g_sem.at[i % 2]).wait()
+        g_low[i % 2] = g_s[r, kind].astype(BF16).reshape(E, d_own, FFS)
+        pltpu.make_async_copy(g_low.at[i % 2], g_out.at[r, :, kind], g_sem.at[i % 2]).start()
+    fetch_sums(E)
+    for c in range(imgs):
+        for flow in range(2):
+            sum_copy(flow, c, E - 2).wait_send()
+    own_sums = pltpu.make_async_copy(t_in.at[E - 1], pass_s.at[0], local.at[0])
+    own_sums.start()
+    own_sums.wait()
+    sums_out[...] = (pass_s[0].astype(F32) + t_s[...].astype(F32)).astype(BF16)
+    for i in range(2):
+        pltpu.make_async_copy(g_low.at[i], g_out.at[3, :, i], g_sem.at[i]).wait()
+    for c in range(imgs):
+        for flow in range(2):
+            sum_copy(flow, c, E - 1).wait_send()
+        for k in range(E - 1):
+            row_copy(h_out, h_sems, c, k).wait_send()
+            row_copy(dy_out, d_sems, c, k).wait_send()
     for copy in peers.sends:
         copy.wait_send()
 
@@ -319,29 +459,42 @@
     hbm = pl.BlockSpec(memory_space=pl.ANY)
     table = jax.ShapeDtypeStruct((E * imgs, PAD, D), BF16)
     dma = pltpu.SemaphoreType.DMA
+    pair = (2, imgs, PAD, D)
     return pl.pallas_call(
         functools.partial(front_kernel, imgs),
         out_shape=(
             table,
             table,
+            jax.ShapeDtypeStruct((E,) + pair, BF16),
             jax.ShapeDtypeStruct((4, E, 2, d_own, FFS), BF16),
+            jax.ShapeDtypeStruct(pair, BF16),
             jax.ShapeDtypeStruct((4, E * d_own, D + 128), BF16),
         )
         + attn_shapes(imgs),
         in_specs=[vm, hbm, hbm, vm, vm, vm],
-        out_specs=(hbm,) * 4 + (vm,) * 5,
+        out_specs=(hbm,) * 4 + (vm, hbm) + (vm,) * 5,
         scratch_shapes=[
             pltpu.VMEM((4, E * d_own, D + 128), BF16),
             pltpu.VMEM((imgs, PAD, D), BF16),
+            pltpu.VMEM((4, E, 2, d_own, FFS), BF16),
+            pltpu.VMEM((4, 2, D, FFS), F32),
+            pltpu.VMEM((imgs, PAD, D), BF16),
+            pltpu.VMEM((imgs, PAD, D), BF16),
+            pltpu.VMEM((imgs * PAD, D), F32),
+            pltpu.VMEM((imgs * PAD, D), F32),
+            pltpu.VMEM(pair, BF16),
+            pltpu.VMEM((2,) + pair, BF16),
+            pltpu.VMEM((2, E, d_own, FFS), BF16),
             dma((2, 4)), dma((2, 4)), dma((E,)), dma((E,)), dma((2, E)), dma((2, E)),
             dma((imgs, E - 1)), dma((imgs, E - 1)), dma((imgs, E - 1)), dma((imgs, E - 1)),
             dma((E,)), dma((E,)), dma((E,)), dma((E,)), dma((2, E)), dma((2, E)),
-            dma((3 + 2 * imgs,)),
+            dma((2, imgs, E - 1)), dma((2, imgs, E - 1)),
+            dma((3 + 2 * imgs,)), dma((2, imgs)), dma((2,)),
         ],
         compiler_params=pltpu.CompilerParams(
             vmem_limit_bytes=VMEM_LIMIT, collective_id=0, has_side_effects=True
         ),
-        cost_estimate=pl.CostEstimate(flops=6 * 10**9, bytes_accessed=10**8, transcendentals=2 * 10**6),
+        cost_estimate=pl.CostEstimate(flops=10**11, bytes_accessed=10**8, transcendentals=2 * 10**7),
         name="front",
     )(pack, ew, dy, x, noise, keep)
 
@@ -563,20 +716,22 @@
 
 
 def unpack_kernel(who_ref, *refs):
-    blocks, out_ref = refs[:E], refs[E]
+    blocks, (in_ref, out_ref) = refs[:E], refs[E:]
     for by in range(E):
-        out_ref[who_ref[by]] = blocks[by][...].astype(F32)
+        in_ref[who_ref[by]] = blocks[by][0].astype(F32)
+        out_ref[who_ref[by]] = blocks[by][1].astype(F32)
 
 
 def unpack(who, blocks):
     vm = pl.BlockSpec(memory_space=pltpu.VMEM)
+    whole = jax.ShapeDtypeStruct((E,) + blocks[0].shape[1:], F32)
     return pl.pallas_call(
         unpack_kernel,
-        out_shape=jax.ShapeDtypeStruct((E,) + blocks[0].shape, F32),
+        out_shape=(whole, whole),
         in_specs=[pl.BlockSpec(memory_space=pltpu.SMEM)] + [vm] * E,
-        out_specs=vm,
+        out_specs=(vm, vm),
         compiler_params=pltpu.CompilerParams(vmem_limit_bytes=VMEM_LIMIT),
-        cost_estimate=pl.CostEstimate(flops=10**6, bytes_accessed=4 * 10**6, transcendentals=0),
+        cost_estimate=pl.CostEstimate(flops=10**6, bytes_accessed=7 * 10**6, transcendentals=0),
         name="unpack",
     )(who, *blocks)
 
@@ -783,7 +938,13 @@
         weights = jnp.concatenate([two, self.other(two, 1)], axis=0)
         chunk, *saved = attn_forward(x, w, noise, keep)
         table = (E * x.shape[0], PAD, D)
-        return self.gather(chunk).reshape(table), self.gather(dy).reshape(table), weights, w, *saved
+        dh, y, rows, hid, tiles = experts(
+            self.member, self.gather(chunk).reshape(table), self.gather(dy).reshape(table), weights
+        )
+        sums = [self.scatter_sum(t.reshape((E,) + chunk.shape)) for t in (dh, y)]
+        g = [jnp.concatenate([expert_grads(tiles, rows, hid, kind, base) for base in (0, 2)]) for kind in (0, 1)]
+        g = jnp.stack([part.reshape(4, E, D // E, FFS) for part in g], axis=2)
+        return g, jnp.stack(sums), w, *saved
 
     def sum_both_ways(self, block_for):
         def chain(way, steps):
@@ -886,43 +1047,26 @@
     keep = jnp.stack(image_lanes(kept_pairs(routes), move.tensor, imgs))
     noise = jnp.stack(image_lanes(jnp.transpose(router_noise), move.tensor, imgs))
     if move.groups == 1:
-        h_all, dy_all, weights, w, *saved = front(pack, ew, dy, x, noise, keep)
+        _, _, _, g_low, sums, w, *saved = front(pack, ew, dy, x, noise, keep)
     else:
-        h_all, dy_all, weights, w, *saved = move.front(pack, ew, dy, x, noise, keep)
+        g_low, sums, w, *saved = move.front(pack, ew, dy, x, noise, keep)
     x1, qkv, o, lse, probs = saved
-
-    dh, y_all, rows, hid, tiles = experts(move.member, h_all, dy_all, weights)
-
-    def dh_for(c, k):
-        return lax.dynamic_index_in_dim(dh, move.behind(ways[c], k) * imgs + c, 0, False)
-
-    dh_sum = [dh_for(c, 1) for c in range(imgs)]
-    g_work = {3: (1, 2), 4: (1, 0), 5: (0, 2), 6: (0, 0)}
-    g_part = {}
-    for k in range(2, E + 1):
-        if k in g_work:
-            part = expert_grads(tiles, rows, hid, *g_work[k])
-            dh_sum, g_part[g_work[k]] = lax.optimization_barrier((dh_sum, part))
-        for c in range(imgs):
-            passed = move.along(dh_sum[c], ways[c])
-            dh_sum[c] = (passed.astype(F32) + dh_for(c, k % E).astype(F32)).astype(BF16)
-    y_all = after(y_all, dh_sum)
-    y_sum = move.scatter_sum(y_all.reshape(E, imgs, PAD, D))
-    g_exp = {}
-    for kind in (1, 0):
-        passed = move.other(g_part[kind, 2], 1).astype(F32)
-        pair = [(g_part[kind, 0][s].astype(F32) + passed[s]).astype(BF16) for s in range(2)]
-        total = (pair[0].astype(F32) + move.other(pair[1], 2).astype(F32)).astype(BF16)
-        total = move.sum_groups(total, 0)
-        blocks = []
-        for by in range(E):
-            to = lax.rem(move.member + by, E)
-            block = lax.dynamic_slice_in_dim(total, to * d_own, d_own, 0)
-            blocks.append(move.shift(block, by) if by else block)
-        g_exp[kind] = blocks
+    dh_sum, y_sum = sums[0], sums[1]
+
+    passed = move.other(g_low[2:], 1)
+    pair = [(g_low[s].astype(F32) + passed[s].astype(F32)).astype(BF16) for s in range(2)]
+    total = (pair[0].astype(F32) + move.other(pair[1], 2).astype(F32)).astype(BF16)
+    if move.groups > 1:
+        total = jnp.swapaxes(total, 1, 2).reshape(D, 2, FFS)
+        total = jnp.swapaxes(move.sum_groups(total, 0).reshape(E, d_own, 2, FFS), 1, 2)
+    g_exp = []
+    for by in range(E):
+        to = lax.rem(move.member + by, E)
+        block = lax.dynamic_index_in_dim(total, to, 0, False)
+        g_exp.append(move.shift(block, by) if by else block)
 
     pack0, pack1, packs, d_tok = attn_backward(
-        dh_sum, (x1, x, dy, probs, qkv, o, lse), w, n_dp
+        [dh_sum[c] for c in range(imgs)], (x1, x, dy, probs, qkv, o, lse), w, n_dp
     )
     passed = move.other(packs, 1)
     if move.groups > 1:
@@ -949,7 +1093,7 @@
     d_tokens = all_rows(d_tok)
     output = all_rows((x1 + y_sum.astype(F32)).astype(BF16))
     came = jnp.stack([lax.rem(move.member - by + E, E) for by in range(E)])
-    g_out, g_in = (unpack(came, g_exp[kind]) for kind in (1, 0))
+    g_in, g_out = unpack(came, g_exp)
     return (
         output,
         d_tokens,

time: 575 us -> 580 us (level)
  Pallas kernels: 301 us -> 364 us
  waiting for transfers between devices: 108 us -> 87.6 us
  other arithmetic: 38.7 us -> 22.1 us
  between operations: 15.2 us -> 1.39 us
  starting transfers between devices: 81.7 us -> 67.9 us
    pallas_call x1, Pallas kernels: 178 us -> 326 us  [front(): pl.pallas_call(functools.partial(front_kernel, imgs), out_shape=(table, t...]
    pallas_call x7 -> x1, Pallas kernels: 88.5 us -> 4.06 us  [unpack(): pl.pallas_call(unpack_kernel, out_shape=(whole, whole), in_specs=[pl.Bloc...]
    ppermute x21 -> x7, starting transfers between devices: 47.6 us -> 15.7 us  [along(): return lax.ppermute(value, 'dp', self.ring[way])]
    ppermute x14 -> x7, waiting for transfers between devices: 28.4 us -> 5.56 us  [shift(): return lax.ppermute(value, 'dp', perm)]
    ppermute x19 -> x17, waiting for transfers between devices: 55.7 us -> 76.7 us  [other(): return lax.ppermute(value, 'tensor', [(k, k ^ mask) for k in range(4)])]
    ppermute x14 -> x7, starting transfers between devices: 19.6 us -> 38.8 us  [shift(): return lax.ppermute(value, 'dp', perm)]
    ppermute x21 -> x7, waiting for transfers between devices: 23.4 us -> 5.32 us  [along(): return lax.ppermute(value, 'dp', self.ring[way])]
    convert_element_type x11 -> x1, other arithmetic: 16.4 us -> 4.99 us  [body(): (g_low[s].astype(F32) + passed[s].astype(F32)).astype(BF16)]
  transfers between devices with their start and end apart: 55 -> 31, of which waited for: 13 -> 11; matrix products, arithmetic and copies ran while one was open for 5% -> 4% of each run, Pallas kernels for 13% -> 6%
where the time goes in v4:
time: 580 us; the launch traced here: 570 us
  Pallas kernels  364 us (63%)
  waiting for transfers between devices  87.6 us (15%)
  starting transfers between devices  67.9 us (12%)
  local copies, waits for them, and re-layouts  27.2 us (5%)
  other arithmetic  22.1 us (4%)
    pallas_call x1, Pallas kernels, front(): pl.pallas_call(functools.partial(front_kernel, imgs), out_shape=(table, t...  326 us
    ppermute x17, waiting for transfers between devices, other(): return lax.ppermute(value, 'tensor', [(k, k ^ mask) for k in range(4)])  76.7 us
    ppermute x7, starting transfers between devices, shift(): return lax.ppermute(value, 'dp', perm)  38.8 us
    pallas_call x1, Pallas kernels, attn_backward(): pl.pallas_call(functools.partial(attn_backward_kernel, imgs), out_shape=(...  25.4 us
    ppermute x7, starting transfers between devices, along(): return lax.ppermute(value, 'dp', self.ring[way])  15.7 us
    ppermute x17, starting transfers between devices, other(): return lax.ppermute(value, 'tensor', [(k, k ^ mask) for k in range(4)])  13.3 us
  transfers between devices with their start and end apart: 31, of which 11 were waited for; matrix products, arithmetic and copies ran while one was open for 4% of the time, Pallas kernels for 6%

profile of v4, /device:TPU:24, one launch (start us, length us, event | category | flops | bytes accessed | tf_op | source)
XLA Modules:
  0.0 570.0 jit_solution(15368166151557927597)
XLA Ops:
  1.5 2.3 reduce-window.6
  6.4 1.6 constant_dynamic-slice_fusion.5
  21.0 1.6 pad_maximum_fusion.ew_ref
  22.6 325.8 %front.1 = (bf16[16,208,768]{2,1,0:T(8,128)(2,1)}, bf16[16,208,768]{2,1,0:T(8,128)(2,1)}, bf16[8,2,2,208,768]{4,3,2,1,0:T(8,128)(2,1)}, bf16[4,8,2,96,768]{4,3,2...) custom-call(bf16[96,896]{1,0:T(8,128)(2,1)} %pad.34.pack_ref, ...), custom_call_target="tpu_custom_call" | custom-call | flops 99999997952 | bytes 100000000 | tf_op jit(solution)/shard_map/front/pallas_call | solution.py:463
  348.4 5.0 slice.174
  354.3 25.4 %attn_backward.1 = (bf16[8,112,768]{2,1,0:T(8,128)(2,1)}, bf16[8,112,768]{2,1,0:T(8,128)(2,1)}, bf16[8,2,112,768]{3,2,1,0:T(8,128)(2,1)}, bf16[2,208,768]{2,1,0:T(8,128)(2,1)}) custom-call(bf16[208,768]{1,0:T(8,128)(2,1)} %get-tuple-element.96.refs_0_, bf16[208,768]{1,0:T(8,128)(2,1)} %get-tuple-element.95.refs_1_, ...), custom_call_target="tpu_custom_call" | custom-call | flops 12000000000 | bytes 20000000 | tf_op jit(solution)/shard_map/attn_backward/pallas_call | solution.py:852
  380.3 1.4 collective-permute-start.3
  381.7 3.5 collective-permute-done.6
  385.8 5.0 fusion.2
  390.8 1.4 collective-permute-start.23
  396.2 55.8 %collective-permute-done.7 = bf16[112,768]{1,0:T(8,128)(2,1)S(1)} collective-permute-done((bf16[112,768]{1,0:T(8,128)(2,1)S(1)}, bf16[112,768]{1,0:T(8,128)(2,1)S(1)}, u32[]{:S(2)}, u32[]{:S(2)}) %collective-permute-start.7) | collective-permute-done | bytes 172064 | tf_op jit(solution)/shard_map/ppermute | solution.py:905
  452.0 1.4 collective-permute-start.9
  453.4 15.9 %collective-permute-done.15 = bf16[112,768]{1,0:T(8,128)(2,1)S(1)} collective-permute-done((bf16[112,768]{1,0:T(8,128)(2,1)S(1)}, bf16[112,768]{1,0:T(8,128)(2,1)S(1)}, u32[]{:S(2)}, u32[]{:S(2)}) %collective-permute-start.15) | collective-permute-done | bytes 172064 | tf_op jit(solution)/shard_map/ppermute | solution.py:905
  469.3 8.9 %collective-permute-start.8 = (bf16[112,768]{1,0:T(8,128)(2,1)S(1)}, bf16[112,768]{1,0:T(8,128)(2,1)S(1)}, u32[]{:S(2)}, u32[]{:S(2)}) collective-permute-start(bf16[112,768]{1,0:T(8,128)(2,1)S(1)} %fusion.48), channel_id=1, source_target_pairs={{0,8},{8,16},{16,24},{24,28},{28,20},{20,12},{12,4},{4,0},{1,9},{9... | collective-permute-start | bytes 516104 | tf_op jit(solution)/shard_map/ppermute | solution.py:895
  478.2 1.5 collective-permute-start.11
  479.7 1.4 collective-permute-done.8
  481.2 1.5 collective-permute-start.17
  482.8 2.5 collective-permute-start.10
  485.5 1.4 collective-permute-done.17
  486.9 1.4 collective-permute-done.10
  488.3 2.5 collective-permute-done.16
  492.3 1.5 collective-permute-start.19
  498.0 4.2 lay_out.3
  502.3 4.4 lay_out.2
  507.3 1.5 fusion.31
  511.0 4.2 fusion
  517.6 1.8 collective-permute-start.25
  521.4 2.7 collective-permute-start.27
  525.0 2.2 collective-permute-done.24.refs_1_
  527.5 31.3 %collective-permute-start.30 = (bf16[2,96,768]{2,1,0:T(8,128)(2,1)S(1)}, bf16[2,96,768]{2,1,0:T(8,128)(2,1)}, u32[]{:S(2)}, u32[]{:S(2)}) collective-permute-start(bf16[2,96,768]{2,1,0:T(8,128)(2,1)S(1)} %get-tuple-element.73), channel_id=1, source_target_pairs={{0,28},{4,0},{8,4},{12,8},{16,12},{20,16},{24,20},{28,24},{1,29},{... | collective-permute-start | bytes 884744 | tf_op jit(solution)/shard_map/ppermute | solution.py:899
  561.8 2.8 collective-permute-done.26.refs_3_
  565.7 4.1 unpack.1
  (170 shorter events, 40.5 us)
Async XLA Ops:
  353.4 32.4 %collective-permute-start.22 = (bf16[2,8,2,96,768]{4,3,2,1,0:T(8,128)(2,1)}, bf16[2,8,2,96,768]{4,3,2,1,0:T(8,128)(2,1)}, u32[]{:S(2)}, u32[]{:S(2)}) collective-permute-start(bf16[2,8,2,96,768]{4,3,2,1,0:T(8,128)(2,1)} %slice.174), channel_id=1, source_target_pairs={{0,1},{1,0},{2,3},{3,2},{4,5},{5,4},{6,7},{7,6},{8,9},{9,8},{10,11... | collective-permute-start | bytes 14155784 | tf_op jit(solution)/shard_map/ppermute | solution.py:905
  379.8 5.4 collective-permute-start.6
  380.3 102.5 %collective-permute-start.3 = (bf16[2,208,768]{2,1,0:T(8,128)(2,1)}, bf16[2,208,768]{2,1,0:T(8,128)(2,1)}, u32[]{:S(2)}, u32[]{:S(2)}) collective-permute-start(bf16[2,208,768]{2,1,0:T(8,128)(2,1)} %get-tuple-element.32.refs_0_), channel_id=1, source_target_pairs={{0,2},{1,3},{2,0},{3,1},{4,6},{5,7},{6,4},{7,5},{8,10},{9,11},{10,... | collective-permute-start | bytes 1916936 | tf_op jit(solution)/shard_map/ppermute | solution.py:905
  390.8 120.2 %collective-permute-start.23 = (bf16[8,2,96,768]{3,2,1,0:T(8,128)(2,1)}, bf16[8,2,96,768]{3,2,1,0:T(8,128)(2,1)}, u32[]{:S(2)}, u32[]{:S(2)}) collective-permute-start(bf16[8,2,96,768]{3,2,1,0:T(8,128)(2,1)} %fusion.2), channel_id=1, source_target_pairs={{0,2},{1,3},{2,0},{3,1},{4,6},{5,7},{6,4},{7,5},{8,10},{9,11},{10,... | collective-permute-start | bytes 7077896 | tf_op jit(solution)/shard_map/ppermute | solution.py:905
  392.6 59.3 %collective-permute-start.7 = (bf16[112,768]{1,0:T(8,128)(2,1)S(1)}, bf16[112,768]{1,0:T(8,128)(2,1)S(1)}, u32[]{:S(2)}, u32[]{:S(2)}) collective-permute-start(bf16[112,768]{1,0:T(8,128)(2,1)S(1)} %get-tuple-element.87), channel_id=1, source_target_pairs={{0,2},{1,3},{2,0},{3,1},{4,6},{5,7},{6,4},{7,5},{8,10},{9,11},{10,... | collective-permute-start | bytes 516104 | tf_op jit(solution)/shard_map/ppermute | solution.py:905
  394.1 97.6 %copy-start.4 = (bf16[2,208,768]{2,1,0:T(8,128)(2,1)}, bf16[2,208,768]{2,1,0:T(8,128)(2,1)S(1)}, u32[]{:S(2)}) copy-start(bf16[2,208,768]{2,1,0:T(8,128)(2,1)S(1)} %fusion.3.refs_0_) | copy-start | bytes 1916932
  394.1 91.3 %collective-permute-start = (bf16[2,208,768]{2,1,0:T(8,128)(2,1)S(1)}, bf16[2,208,768]{2,1,0:T(8,128)(2,1)S(1)}, u32[]{:S(2)}, u32[]{:S(2)}) collective-permute-start(bf16[2,208,768]{2,1,0:T(8,128)(2,1)S(1)} %fusion.3.refs_0_), channel_id=1, source_target_pairs={{0,2},{1,3},{2,0},{3,1},{4,6},{5,7},{6,4},{7,5},{8,10},{9,11},{10,... | collective-permute-start | bytes 1916936 | tf_op jit(solution)/shard_map/ppermute | solution.py:905
  395.0 74.4 %collective-permute-start.15 = (bf16[112,768]{1,0:T(8,128)(2,1)S(1)}, bf16[112,768]{1,0:T(8,128)(2,1)S(1)}, u32[]{:S(2)}, u32[]{:S(2)}) collective-permute-start(bf16[112,768]{1,0:T(8,128)(2,1)S(1)} %get-tuple-element.91), channel_id=1, source_target_pairs={{0,2},{1,3},{2,0},{3,1},{4,6},{5,7},{6,4},{7,5},{8,10},{9,11},{10,... | collective-permute-start | bytes 516104 | tf_op jit(solution)/shard_map/ppermute | solution.py:905
  452.0 26.3 %collective-permute-start.9 = (bf16[112,768]{1,0:T(8,128)(2,1)S(1)}, bf16[112,768]{1,0:T(8,128)(2,1)S(1)}, u32[]{:S(2)}, u32[]{:S(2)}) collective-permute-start(bf16[112,768]{1,0:T(8,128)(2,1)S(1)} %get-tuple-element.94), channel_id=1, source_target_pairs={{0,2},{1,3},{2,0},{3,1},{4,6},{5,7},{6,4},{7,5},{8,10},{9,11},{10,... | collective-permute-start | bytes 516104 | tf_op jit(solution)/shard_map/ppermute | solution.py:905
  469.3 11.8 %collective-permute-start.8 = (bf16[112,768]{1,0:T(8,128)(2,1)S(1)}, bf16[112,768]{1,0:T(8,128)(2,1)S(1)}, u32[]{:S(2)}, u32[]{:S(2)}) collective-permute-start(bf16[112,768]{1,0:T(8,128)(2,1)S(1)} %fusion.48), channel_id=1, source_target_pairs={{0,8},{8,16},{16,24},{24,28},{28,20},{20,12},{12,4},{4,0},{1,9},{9... | collective-permute-start | bytes 516104 | tf_op jit(solution)/shard_map/ppermute | solution.py:895
  478.2 7.1 %collective-permute-start.11 = (bf16[112,768]{1,0:T(8,128)(2,1)S(1)}, bf16[112,768]{1,0:T(8,128)(2,1)S(1)}, u32[]{:S(2)}, u32[]{:S(2)}) collective-permute-start(bf16[112,768]{1,0:T(8,128)(2,1)S(1)} %get-tuple-element.93), channel_id=1, source_target_pairs={{0,2},{1,3},{2,0},{3,1},{4,6},{5,7},{6,4},{7,5},{8,10},{9,11},{10,... | collective-permute-start | bytes 516104 | tf_op jit(solution)/shard_map/ppermute | solution.py:905
  481.2 5.7 %collective-permute-start.17 = (bf16[112,768]{1,0:T(8,128)(2,1)S(1)}, bf16[112,768]{1,0:T(8,128)(2,1)S(1)}, u32[]{:S(2)}, u32[]{:S(2)}) collective-permute-start(bf16[112,768]{1,0:T(8,128)(2,1)S(1)} %get-tuple-element.90), channel_id=1, source_target_pairs={{0,2},{1,3},{2,0},{3,1},{4,6},{5,7},{6,4},{7,5},{8,10},{9,11},{10,... | collective-permute-start | bytes 516104 | tf_op jit(solution)/shard_map/ppermute | solution.py:905
  482.8 5.5 collective-permute-start.10
  485.4 5.4 collective-permute-start.16
  485.4 6.3 %collective-permute-start.4 = (bf16[2,208,768]{2,1,0:T(8,128)(2,1)S(1)}, bf16[2,208,768]{2,1,0:T(8,128)(2,1)S(1)}, u32[]{:S(2)}, u32[]{:S(2)}) collective-permute-start(bf16[2,208,768]{2,1,0:T(8,128)(2,1)S(1)} %copy-done.13), channel_id=1, source_target_pairs={{0,1},{1,0},{2,3},{3,2},{4,5},{5,4},{6,7},{7,6},{8,9},{9,8},{10,11... | collective-permute-start | bytes 1916936 | tf_op jit(solution)/shard_map/ppermute | solution.py:905
  486.9 5.4 collective-permute-start.1
  488.3 5.6 collective-permute-start.5
  490.8 4.0 collective-permute-start.2
  491.7 14.9 %collective-permute-start.13 = (bf16[112,768]{1,0:T(8,128)(2,1)S(1)}, bf16[112,768]{1,0:T(8,128)(2,1)}, u32[]{:S(2)}, u32[]{:S(2)}) collective-permute-start(bf16[112,768]{1,0:T(8,128)(2,1)S(1)} %get-tuple-element.92), channel_id=1, source_target_pairs={{0,2},{1,3},{2,0},{3,1},{4,6},{5,7},{6,4},{7,5},{8,10},{9,11},{10,... | collective-permute-start | bytes 516104 | tf_op jit(solution)/shard_map/ppermute | solution.py:905
  492.3 14.9 %collective-permute-start.19 = (bf16[112,768]{1,0:T(8,128)(2,1)S(1)}, bf16[112,768]{1,0:T(8,128)(2,1)}, u32[]{:S(2)}, u32[]{:S(2)}) collective-permute-start(bf16[112,768]{1,0:T(8,128)(2,1)S(1)} %get-tuple-element.89), channel_id=1, source_target_pairs={{0,2},{1,3},{2,0},{3,1},{4,6},{5,7},{6,4},{7,5},{8,10},{9,11},{10,... | collective-permute-start | bytes 516104 | tf_op jit(solution)/shard_map/ppermute | solution.py:905
  493.9 13.4 %collective-permute-start.12 = (bf16[112,768]{1,0:T(8,128)(2,1)}, bf16[112,768]{1,0:T(8,128)(2,1)}, u32[]{:S(2)}, u32[]{:S(2)}) collective-permute-start(bf16[112,768]{1,0:T(8,128)(2,1)} %get-tuple-element.83), channel_id=1, source_target_pairs={{0,8},{8,16},{16,24},{24,28},{28,20},{20,12},{12,4},{4,0},{1,9},{9... | collective-permute-start | bytes 516104 | tf_op jit(solution)/shard_map/ppermute | solution.py:895
  495.6 11.6 %collective-permute-start.18 = (bf16[112,768]{1,0:T(8,128)(2,1)}, bf16[112,768]{1,0:T(8,128)(2,1)}, u32[]{:S(2)}, u32[]{:S(2)}) collective-permute-start(bf16[112,768]{1,0:T(8,128)(2,1)} %get-tuple-element.84), channel_id=1, source_target_pairs={{8,0},{16,8},{24,16},{28,24},{20,28},{12,20},{4,12},{0,4},{9,1},{1... | collective-permute-start | bytes 516104 | tf_op jit(solution)/shard_map/ppermute | solution.py:895
  506.6 12.7 %collective-permute-start.21 = (bf16[112,768]{1,0:T(8,128)(2,1)S(1)}, bf16[112,768]{1,0:T(8,128)(2,1)S(1)}, u32[]{:S(2)}, u32[]{:S(2)}) collective-permute-start(bf16[112,768]{1,0:T(8,128)(2,1)S(1)} %get-tuple-element.88), channel_id=1, source_target_pairs={{0,2},{1,3},{2,0},{3,1},{4,6},{5,7},{6,4},{7,5},{8,10},{9,11},{10,... | collective-permute-start | bytes 516104 | tf_op jit(solution)/shard_map/ppermute | solution.py:905
  508.7 10.7 %collective-permute-start.14 = (bf16[112,768]{1,0:T(8,128)(2,1)S(1)}, bf16[112,768]{1,0:T(8,128)(2,1)S(1)}, u32[]{:S(2)}, u32[]{:S(2)}) collective-permute-start(bf16[112,768]{1,0:T(8,128)(2,1)S(1)} %get-tuple-element.81), channel_id=1, source_target_pairs={{0,8},{8,16},{16,24},{24,28},{28,20},{20,12},{12,4},{4,0},{1,9},{9... | collective-permute-start | bytes 516104 | tf_op jit(solution)/shard_map/ppermute | solution.py:895
  510.0 9.4 %collective-permute-start.20 = (bf16[112,768]{1,0:T(8,128)(2,1)S(1)}, bf16[112,768]{1,0:T(8,128)(2,1)S(1)}, u32[]{:S(2)}, u32[]{:S(2)}) collective-permute-start(bf16[112,768]{1,0:T(8,128)(2,1)S(1)} %get-tuple-element.82), channel_id=1, source_target_pairs={{8,0},{16,8},{24,16},{28,24},{20,28},{12,20},{4,12},{0,4},{9,1},{1... | collective-permute-start | bytes 516104 | tf_op jit(solution)/shard_map/ppermute | solution.py:895
  516.4 10.8 %collective-permute-start.24 = (bf16[2,96,768]{2,1,0:T(8,128)(2,1)S(1)}, bf16[2,96,768]{2,1,0:T(8,128)(2,1)S(1)}, u32[]{:S(2)}, u32[]{:S(2)}) collective-permute-start(bf16[2,96,768]{2,1,0:T(8,128)(2,1)S(1)} %get-tuple-element.79), channel_id=1, source_target_pairs={{0,4},{4,8},{8,12},{12,16},{16,20},{20,24},{24,28},{28,0},{1,5},{5... | collective-permute-start | bytes 884744 | tf_op jit(solution)/shard_map/ppermute | solution.py:899
  517.6 9.9 %collective-permute-start.25 = (bf16[2,96,768]{2,1,0:T(8,128)(2,1)S(1)}, bf16[2,96,768]{2,1,0:T(8,128)(2,1)S(1)}, u32[]{:S(2)}, u32[]{:S(2)}) collective-permute-start(bf16[2,96,768]{2,1,0:T(8,128)(2,1)S(1)} %get-tuple-element.78), channel_id=1, source_target_pairs={{0,8},{4,12},{8,16},{12,20},{16,24},{20,28},{24,0},{28,4},{1,9},{5... | collective-permute-start | bytes 884744 | tf_op jit(solution)/shard_map/ppermute | solution.py:899
  520.5 44.1 %collective-permute-start.26 = (bf16[2,96,768]{2,1,0:T(8,128)(2,1)}, bf16[2,96,768]{2,1,0:T(8,128)(2,1)S(1)}, u32[]{:S(2)}, u32[]{:S(2)}) collective-permute-start(bf16[2,96,768]{2,1,0:T(8,128)(2,1)} %get-tuple-element.77), channel_id=1, source_target_pairs={{0,12},{4,16},{8,20},{12,24},{16,28},{20,0},{24,4},{28,8},{1,13},{... | collective-permute-start | bytes 884744 | tf_op jit(solution)/shard_map/ppermute | solution.py:899
  521.4 43.4 %collective-permute-start.27 = (bf16[2,96,768]{2,1,0:T(8,128)(2,1)}, bf16[2,96,768]{2,1,0:T(8,128)(2,1)S(1)}, u32[]{:S(2)}, u32[]{:S(2)}) collective-permute-start(bf16[2,96,768]{2,1,0:T(8,128)(2,1)} %get-tuple-element.76), channel_id=1, source_target_pairs={{0,16},{4,20},{8,24},{12,28},{16,0},{20,4},{24,8},{28,12},{1,17},{... | collective-permute-start | bytes 884744 | tf_op jit(solution)/shard_map/ppermute | solution.py:899
  524.1 40.7 %collective-permute-start.28 = (bf16[2,96,768]{2,1,0:T(8,128)(2,1)}, bf16[2,96,768]{2,1,0:T(8,128)(2,1)S(1)}, u32[]{:S(2)}, u32[]{:S(2)}) collective-permute-start(bf16[2,96,768]{2,1,0:T(8,128)(2,1)} %get-tuple-element.75), channel_id=1, source_target_pairs={{0,20},{4,24},{8,28},{12,0},{16,4},{20,8},{24,12},{28,16},{1,21},{... | collective-permute-start | bytes 884744 | tf_op jit(solution)/shard_map/ppermute | solution.py:899
  527.2 37.6 %collective-permute-start.29 = (bf16[2,96,768]{2,1,0:T(8,128)(2,1)}, bf16[2,96,768]{2,1,0:T(8,128)(2,1)S(1)}, u32[]{:S(2)}, u32[]{:S(2)}) collective-permute-start(bf16[2,96,768]{2,1,0:T(8,128)(2,1)} %get-tuple-element.74), channel_id=1, source_target_pairs={{0,24},{4,28},{8,0},{12,4},{16,8},{20,12},{24,16},{28,20},{1,25},{... | collective-permute-start | bytes 884744 | tf_op jit(solution)/shard_map/ppermute | solution.py:899
  527.5 37.3 %collective-permute-start.30 = (bf16[2,96,768]{2,1,0:T(8,128)(2,1)S(1)}, bf16[2,96,768]{2,1,0:T(8,128)(2,1)}, u32[]{:S(2)}, u32[]{:S(2)}) collective-permute-start(bf16[2,96,768]{2,1,0:T(8,128)(2,1)S(1)} %get-tuple-element.73), channel_id=1, source_target_pairs={{0,28},{4,0},{8,4},{12,8},{16,12},{20,16},{24,20},{28,24},{1,29},{... | collective-permute-start | bytes 884744 | tf_op jit(solution)/shard_map/ppermute | solution.py:899
  (33 other events, 327.4 us)

commit v5 on v4

--- a/solution.py
+++ b/solution.py
@@ -762,58 +762,59 @@
     )(at, *parts)
 
 
-def attn_backward_kernel(imgs, *refs):
-    dh_in = refs[:imgs]
-    x1_in, x_in, dy_in, probs_in, qkv_in, o_in, lse_in, w_ref = refs[imgs : imgs + 8]
-    packs, dtok_ref = refs[imgs + 8 : imgs + 11], refs[imgs + 11]
-    dx1_s, low_s, h1_s, dh1_s, dqkv_s, o_s = refs[imgs + 12 :]
-    n_dp, d_own = packs[0].shape[0], packs[0].shape[1] - 16
-
-    def pack_of(r):
-        return packs[r] if r < 2 else packs[2].at[:, r - 2]
-
-    par = params_of(w_ref[0])
-    router = par[8:16].astype(BF16)
-    row_ok = iota((PAD, 1), 0) < SEQ
-    lane_ok = iota((E, PAD), 1) < SEQ
-    key_ok = iota((PAD, PAD), 1) < SEQ
-    small2g = jnp.zeros((1, D), F32)
-    small2b = jnp.zeros((1, D), F32)
-    g_router = jnp.zeros((E, D), F32)
-    for c in range(imgs):
-        span = slice(c * PAD, (c + 1) * PAD)
-        arrived = dh_in[c][...].astype(F32)
-        dgate = arrived[PAD - 8 :, :PAD]
-        probs = probs_in[c]
-        dlogits = probs * (dgate - jnp.sum(probs * dgate, axis=0, keepdims=True))
-        dlogits = jnp.where(lane_ok, dlogits, 0.0).astype(BF16)
-        unit, scale = normalise(x1_in[c])
-        h2 = (unit * par[2:3] + par[3:4]).astype(BF16)
-        g_router = g_router + dot(dlogits, h2)
-        dh2 = jnp.where(row_ok, arrived + dot_tn(dlogits, router), 0.0)
-        small2g = small2g + jnp.sum(dh2 * unit, axis=0, keepdims=True)
-        small2b = small2b + jnp.sum(dh2, axis=0, keepdims=True)
-        dx1 = dy_in[c].astype(F32) + norm_back(dh2, unit, scale, par[2:3])
-        dx1_s[span, :] = dx1
-        low_s[span, :] = dx1.astype(BF16)
-        unit1, _ = normalise(x_in[c].astype(F32))
-        h1_s[span, :] = (unit1 * par[0:1] + par[1:2]).astype(BF16)
-    low = low_s[...]
-    h1 = h1_s[...]
-    for r in range(4):
-        w = w_ref[r]
+class Backward:
+    def __init__(self, imgs, dh_of, saved, w_ref, dx1_s, low_s, h1_s, dh1_s, dqkv_s, o_s):
+        self.imgs, self.dh_of, self.saved, self.w_ref = imgs, dh_of, saved, w_ref
+        self.dx1_s, self.low_s, self.h1_s, self.dh1_s, self.dqkv_s, self.o_s = dx1_s, low_s, h1_s, dh1_s, dqkv_s, o_s
+        self.par = params_of(w_ref[0])
+        self.row_ok = iota((PAD, 1), 0) < SEQ
+        self.started = False
+
+    def span(self, c):
+        return slice(c * PAD, (c + 1) * PAD)
+
+    def first(self):
+        x1_in, x_in, dy_in, probs_in = self.saved[:4]
+        par, row_ok = self.par, self.row_ok
+        lane_ok = iota((E, PAD), 1) < SEQ
+        router = par[8:16].astype(BF16)
+        gain = jnp.zeros((1, D), F32)
+        bias = jnp.zeros((1, D), F32)
+        g_router = jnp.zeros((E, D), F32)
+        for c in range(self.imgs):
+            arrived = self.dh_of(c).astype(F32)
+            dgate = arrived[PAD - 8 :, :PAD]
+            probs = probs_in[c]
+            dlogits = probs * (dgate - jnp.sum(probs * dgate, axis=0, keepdims=True))
+            dlogits = jnp.where(lane_ok, dlogits, 0.0).astype(BF16)
+            unit, scale = normalise(x1_in[c])
+            h2 = (unit * par[2:3] + par[3:4]).astype(BF16)
+            g_router = g_router + dot(dlogits, h2)
+            dh2 = jnp.where(row_ok, arrived + dot_tn(dlogits, router), 0.0)
+            gain = gain + jnp.sum(dh2 * unit, axis=0, keepdims=True)
+            bias = bias + jnp.sum(dh2, axis=0, keepdims=True)
+            dx1 = dy_in[c].astype(F32) + norm_back(dh2, unit, scale, par[2:3])
+            self.dx1_s[self.span(c), :] = dx1
+            self.low_s[self.span(c), :] = dx1.astype(BF16)
+            unit1, _ = normalise(x_in[c].astype(F32))
+            self.h1_s[self.span(c), :] = (unit1 * par[0:1] + par[1:2]).astype(BF16)
+        self.small2 = [gain, bias, jnp.zeros((4, D), F32), g_router]
+
+    def heads(self, r):
+        qkv_in, o_in, lse_in = self.saved[4:]
+        key_ok = iota((PAD, PAD), 1) < SEQ
+        low, h1, w = self.low_s[...], self.h1_s[...], self.w_ref[r]
         dout = dot(low, w[:, 9 * HD : D]).astype(BF16)
-        for c in range(imgs):
-            span = slice(c * PAD, (c + 1) * PAD)
+        for c in range(self.imgs):
             qkv = qkv_in[c, r]
             lse = lse_in[c]
-            o_s[span, :] = o_in[c, r]
+            self.o_s[self.span(c), :] = o_in[c, r]
             dqs, dks, dvs = [], [], []
             for h in range(3):
                 q = qkv[:, h * HD : (h + 1) * HD]
                 k = qkv[:, (3 + h) * HD : (4 + h) * HD]
                 v = qkv[:, (6 + h) * HD : (7 + h) * HD]
-                do = dout[span, h * HD : (h + 1) * HD]
+                do = dout[self.span(c), h * HD : (h + 1) * HD]
                 s = dot_nt(q, k) * HD ** (-0.5)
                 p = jnp.where(key_ok, jnp.exp(s - lse[:, 3 * r + h : 3 * r + h + 1]), 0.0)
                 dvs.append(dot_tn(p.astype(BF16), do).astype(BF16))
@@ -821,34 +822,67 @@
                 ds = (p * (dp - jnp.sum(p * dp, axis=-1, keepdims=True))).astype(BF16)
                 dqs.append((dot(ds, k) * HD ** (-0.5)).astype(BF16))
                 dks.append((dot_tn(ds, q) * HD ** (-0.5)).astype(BF16))
-            dqkv_s[span, :] = jnp.concatenate(dqs + dks + dvs, axis=1)
-        dqkv = dqkv_s[...]
+            self.dqkv_s[self.span(c), :] = jnp.concatenate(dqs + dks + dvs, axis=1)
+        dqkv = self.dqkv_s[...]
         part = dot_nt(dqkv, w[:, : 9 * HD])
-        dh1_s[...] = part if r == 0 else dh1_s[...] + part
-        grad = jnp.concatenate([dot_tn(h1, dqkv), dot_tn(low, o_s[...])], axis=1).astype(BF16)
+        self.dh1_s[...] = self.dh1_s[...] + part if self.started else part
+        self.started = True
+        return jnp.concatenate([dot_tn(h1, dqkv), dot_tn(low, self.o_s[...])], axis=1).astype(BF16)
+
+    def last(self, dtok_ref):
+        x_in = self.saved[1]
+        gain = jnp.zeros((1, D), F32)
+        bias = jnp.zeros((1, D), F32)
+        for c in range(self.imgs):
+            dh1 = jnp.where(self.row_ok, self.dh1_s[self.span(c), :], 0.0)
+            unit, scale = normalise(x_in[c].astype(F32))
+            gain = gain + jnp.sum(dh1 * unit, axis=0, keepdims=True)
+            bias = bias + jnp.sum(dh1, axis=0, keepdims=True)
+            dtok_ref[c] = (self.dx1_s[self.span(c), :] + norm_back(dh1, unit, scale, self.par[0:1])).astype(BF16)
+        return jnp.concatenate([gain, bias] + self.small2, axis=0)
+
+
+def small_block(small, i, d_own):
+    line = jnp.concatenate([small[:, i * d_own : (i + 1) * d_own], jnp.zeros((16, D - d_own), F32)], axis=1)
+    return line.astype(BF16)
+
+
+def backward_scratch(imgs):
+    rows = imgs * PAD
+    return [
+        pltpu.VMEM((rows, D), F32),
+        pltpu.VMEM((rows, D), BF16),
+        pltpu.VMEM((rows, D), BF16),
+        pltpu.VMEM((rows, D), F32),
+        pltpu.VMEM((rows, 9 * HD), BF16),
+        pltpu.VMEM((rows, 3 * HD), BF16),
+    ]
+
+
+def attn_backward_kernel(imgs, *refs):
+    dh_in, saved, w_ref = refs[:imgs], refs[imgs : imgs + 7], refs[imgs + 7]
+    packs, dtok_ref = refs[imgs + 8 : imgs + 11], refs[imgs + 11]
+    n_dp, d_own = packs[0].shape[0], packs[0].shape[1] - 16
+    back = Backward(imgs, lambda c: dh_in[c][...], saved, w_ref, *refs[imgs + 12 :])
+
+    def pack_of(r):
+        return packs[r] if r < 2 else packs[2].at[:, r - 2]
+
+    back.first()
+    for r in range(4):
+        grad = back.heads(r)
         for i in range(n_dp):
             pack_of(r)[i, :d_own, :] = grad[i * d_own : (i + 1) * d_own]
-    small1g = jnp.zeros((1, D), F32)
-    small1b = jnp.zeros((1, D), F32)
-    for c in range(imgs):
-        span = slice(c * PAD, (c + 1) * PAD)
-        dh1 = jnp.where(row_ok, dh1_s[span, :], 0.0)
-        unit1, scale1 = normalise(x_in[c].astype(F32))
-        small1g = small1g + jnp.sum(dh1 * unit1, axis=0, keepdims=True)
-        small1b = small1b + jnp.sum(dh1, axis=0, keepdims=True)
-        dtok_ref[c] = (dx1_s[span, :] + norm_back(dh1, unit1, scale1, par[0:1])).astype(BF16)
-    small = jnp.concatenate([small1g, small1b, small2g, small2b, jnp.zeros((4, D), F32), g_router], axis=0)
+    small = back.last(dtok_ref)
     for i in range(n_dp):
-        line = jnp.concatenate([small[:, i * d_own : (i + 1) * d_own], jnp.zeros((16, D - d_own), F32)], axis=1)
         for r in range(4):
-            pack_of(r)[i, d_own:, :] = line.astype(BF16)
+            pack_of(r)[i, d_own:, :] = small_block(small, i, d_own)
 
 
 def attn_backward(dh, saved, w, n_dp):
     imgs = len(dh)
     pack = (n_dp, D // n_dp + 16, D)
     vm = pl.BlockSpec(memory_space=pltpu.VMEM)
-    rows = imgs * PAD
     return pl.pallas_call(
         functools.partial(attn_backward_kernel, imgs),
         out_shape=(
@@ -859,18 +893,191 @@
         ),
         in_specs=[vm] * (imgs + 8),
         out_specs=(vm,) * 4,
-        scratch_shapes=[
-            pltpu.VMEM((rows, D), F32),
-            pltpu.VMEM((rows, D), BF16),
-            pltpu.VMEM((rows, D), BF16),
-            pltpu.VMEM((rows, D), F32),
-            pltpu.VMEM((rows, 9 * HD), BF16),
-            pltpu.VMEM((rows, 3 * HD), BF16),
-        ],
+        scratch_shapes=backward_scratch(imgs),
         compiler_params=pltpu.CompilerParams(vmem_limit_bytes=VMEM_LIMIT),
         cost_estimate=pl.CostEstimate(flops=12 * 10**9, bytes_accessed=2 * 10**7, transcendentals=2 * 10**6),
         name="attn_backward",
     )(*dh, *saved, w)
+
+
+def back_kernel(
+    imgs, g_low, sums_ref, x1_ref, x_ref, dy_ref, probs_ref, qkv_ref, o_ref, lse_ref, w_ref,
+    g_out, out_all, dtok_all, total_ref,
+    ga_s, gc_s, gx_s, pk_s, pkc_s, pkr_s, sm_s, smr_s, cs_s, cr_s, fs_s, fr_s, or_s, dt_s,
+    dx1_s, low_s, h1_s, dh1_s, dqkv_s, o_s,
+    gc_ss, gc_r, gx_ss, gx_r, ga_ss, ga_r, pk_ss, pk_r, sm_ss, sm_r, c_ss, c_r, f_ss, f_r, row_ss, row_r, local,
+):
+    peers = Peers()
+    member = peers.member
+    tensor = lax.axis_index("tensor")
+    d_own = g_low.shape[3]
+    peers.meet()
+    loads = []
+
+    def here(src, dst):
+        copy = pltpu.make_async_copy(src, dst, local.at[len(loads)])
+        copy.start()
+        loads.append(copy)
+        return copy
+
+    def give_rows(kind, src, whole):
+        here(src, whole.at[tensor])
+        across = peers.send(src, whole.at[tensor], (row_ss, row_r), (kind, 0), peers.across)
+        core = peers.send(src, whole.at[tensor], (row_ss, row_r), (kind, 1), peers.core)
+
+        def onwards():
+            across.wait_recv()
+            other = lax.rem(tensor + 2, 4)
+            copy = peers.send(whole.at[other], whole.at[other], (row_ss, row_r), (kind, 2), peers.core)
+            return core, copy
+
+        return onwards
+
+    for c in range(imgs):
+        or_s[c] = (x1_ref[c] + sums_ref[1, c].astype(F32)).astype(BF16)
+    out_rows = give_rows(0, or_s, out_all)
+
+    g_core = [
+        peers.send(g_low.at[2 + s], gc_s.at[s], (gc_ss, gc_r), s, peers.core) for s in (1, 0)
+    ][::-1]
+    g_load = [here(g_low.at[s], ga_s.at[s]) for s in (1, 0)][::-1]
+    order = (4, 3, 5, 2, 6, 1, 7, 0)
+    gx = {}
+
+    def pass_across():
+        g_core[1].wait_recv()
+        g_load[1].wait()
+        for by in order:
+            to = peers.ahead(by)
+            ga_s[1, to] = (ga_s[1, to].astype(F32) + gc_s[1, to].astype(F32)).astype(BF16)
+            gx[by] = peers.send(ga_s.at[1, to], gx_s.at[to], (gx_ss, gx_r), by, peers.across)
+        g_core[0].wait_recv()
+        g_load[0].wait()
+
+    ga = {}
+
+    def pass_home(by):
+        gx[by].wait_recv()
+        to = peers.ahead(by)
+        part = ga_s[0, to].astype(F32) + gc_s[0, to].astype(F32)
+        ga_s[0, to] = (part + gx_s[to].astype(F32)).astype(BF16)
+        if by:
+            device = {"dp": peers.base + to}
+            ga[by] = peers.send(ga_s.at[0, to], g_out.at[member], (ga_ss, ga_r), by, device)
+        else:
+            here(ga_s.at[0, to], g_out.at[member])
+
+    saved = (x1_ref, x_ref, dy_ref, probs_ref, qkv_ref, o_ref, lse_ref)
+    back = Backward(imgs, lambda c: sums_ref[0, c], saved, w_ref, dx1_s, low_s, h1_s, dh1_s, dqkv_s, o_s)
+    back.first()
+    for r in (2, 3):
+        grad = back.heads(r)
+        for i in range(E):
+            pkc_s[i, r - 2] = grad[i * d_own : (i + 1) * d_own]
+        if r == 2:
+            pass_across()
+    pk_core = peers.send(pkc_s, pkr_s, (pk_ss, pk_r), 0, peers.core)
+    out_rows = out_rows()
+    for r in (0, 1):
+        grad = back.heads(r)
+        for i in range(E):
+            pk_s[i, r, :d_own] = grad[i * d_own : (i + 1) * d_own]
+        pass_home(order[r])
+    small = back.last(dt_s)
+    dtok_rows = give_rows(1, dt_s, dtok_all)
+    for i in range(E):
+        sm_s[i] = small_block(small, i, d_own)
+    sm_core = peers.send(sm_s, smr_s, (sm_ss, sm_r), 0, peers.core)
+    pk_core.wait_recv()
+    sm_core.wait_recv()
+
+    def term(of):
+        weights = pk_s[of, :, :d_own].astype(F32) + pkr_s[of].astype(F32)
+        both = sm_s[of].astype(F32) + smr_s[of].astype(F32)
+        return jnp.concatenate([weights, jnp.broadcast_to(both[None], (2,) + both.shape)], axis=1)
+
+    steps = (E // 2, E // 2 - 1)
+    hops = {}
+
+    def hop(way, i):
+        value = term(peers.behind(1 - way, steps[way] - i))
+        if i:
+            hops[way, i - 1].wait_recv()
+            value = value + cr_s[way, i - 1].astype(F32)
+        cs_s[way, i] = value.astype(BF16)
+        hops[way, i] = peers.send(cs_s.at[way, i], cr_s.at[way, i], (c_ss, c_r), (way, i), peers.next[way])
+
+    for i in range(E // 2):
+        hop(0, i)
+        if i < steps[1]:
+            hop(1, i)
+        pass_home(order[2 + i])
+    hops[1, steps[1] - 1].wait_recv()
+    hops[0, steps[0] - 1].wait_recv()
+    total = term(member) + cr_s[0, steps[0] - 1].astype(F32) + cr_s[1, steps[1] - 1].astype(F32)
+    fs_s[...] = total[1].astype(BF16)
+    final = peers.send(fs_s, fr_s, (f_ss, f_r), 0, peers.across)
+    pass_home(order[6])
+    pass_home(order[7])
+    dtok_rows = dtok_rows()
+    final.wait_recv()
+    total_ref[...] = total[0] + fr_s[...].astype(F32)
+    for by in range(1, E):
+        ga[by].wait_recv()
+    for copy in (*out_rows, *dtok_rows):
+        copy.wait_recv()
+    for copy in loads:
+        if all(copy is not other for other in g_load):
+            copy.wait()
+    for copy in peers.sends:
+        copy.wait_send()
+
+
+def back(g_low, sums, saved, w):
+    imgs = sums.shape[1]
+    d_own = g_low.shape[3]
+    vm = pl.BlockSpec(memory_space=pltpu.VMEM)
+    hbm = pl.BlockSpec(memory_space=pl.ANY)
+    dma = pltpu.SemaphoreType.DMA
+    part = (E, 2, d_own, D)
+    rows = (imgs, PAD, D)
+    hop = (2, E // 2, 2, d_own + 16, D)
+    return pl.pallas_call(
+        functools.partial(back_kernel, imgs),
+        out_shape=(
+            jax.ShapeDtypeStruct(part, BF16),
+            jax.ShapeDtypeStruct((4,) + rows, BF16),
+            jax.ShapeDtypeStruct((4,) + rows, BF16),
+            jax.ShapeDtypeStruct((d_own + 16, D), F32),
+        ),
+        in_specs=[hbm] + [vm] * 9,
+        out_specs=(hbm, hbm, hbm, vm),
+        scratch_shapes=[
+            pltpu.VMEM((2,) + part, BF16),
+            pltpu.VMEM((2,) + part, BF16),
+            pltpu.VMEM(part, BF16),
+            pltpu.VMEM((E, 2, d_own + 16, D), BF16),
+            pltpu.VMEM(part, BF16),
+            pltpu.VMEM(part, BF16),
+            pltpu.VMEM((E, 16, D), BF16),
+            pltpu.VMEM((E, 16, D), BF16),
+            pltpu.VMEM(hop, BF16),
+            pltpu.VMEM(hop, BF16),
+            pltpu.VMEM((d_own + 16, D), BF16),
+            pltpu.VMEM((d_own + 16, D), BF16),
+            pltpu.VMEM(rows, BF16),
+            pltpu.VMEM(rows, BF16),
+            *backward_scratch(imgs),
+            dma((2,)), dma((2,)), dma((E,)), dma((E,)), dma((E,)), dma((E,)), dma((1,)), dma((1,)),
+            dma((1,)), dma((1,)), dma((2, E // 2)), dma((2, E // 2)), dma((1,)), dma((1,)), dma((2, 3)), dma((2, 3)),
+            dma((5,)),
+        ],
+        compiler_params=pltpu.CompilerParams(
+            vmem_limit_bytes=VMEM_LIMIT, collective_id=1, has_side_effects=True
+        ),
+        cost_estimate=pl.CostEstimate(flops=12 * 10**9, bytes_accessed=10**8, transcendentals=2 * 10**6),
+        name="back",
+    )(g_low, sums, *saved, w)
 
 
 RING = (0, 2, 4, 6, 7, 5, 3, 1)
@@ -946,6 +1153,48 @@
         g = jnp.stack([part.reshape(4, E, D // E, FFS) for part in g], axis=2)
         return g, jnp.stack(sums), w, *saved
 
+    def back(self, g_low, sums, saved, x, dy, w):
+        x1, qkv, o, lse, probs = saved
+        dh_sum, y_sum = sums[0], sums[1]
+        imgs, d_own = x.shape[0], D // self.n_dp
+        passed = self.other(g_low[2:], 1)
+        pair = [(g_low[s].astype(F32) + passed[s].astype(F32)).astype(BF16) for s in range(2)]
+        total = (pair[0].astype(F32) + self.other(pair[1], 2).astype(F32)).astype(BF16)
+        if self.groups > 1:
+            total = jnp.swapaxes(total, 1, 2).reshape(D, 2, FFS)
+            total = jnp.swapaxes(self.sum_groups(total, 0).reshape(E, d_own, 2, FFS), 1, 2)
+        g_exp = []
+        for by in range(E):
+            to = lax.rem(self.member + by, E)
+            block = lax.dynamic_index_in_dim(total, to, 0, False)
+            g_exp.append(self.shift(block, by) if by else block)
+
+        pack0, pack1, packs, d_tok = attn_backward(
+            [dh_sum[c] for c in range(imgs)], (x1, x, dy, probs, qkv, o, lse), w, self.n_dp
+        )
+        passed = self.other(packs, 1)
+        if self.groups > 1:
+            pack0 = self.sum_groups((pack0.astype(F32) + passed[:, 0].astype(F32)).astype(BF16), 0)
+            pack1 = self.sum_groups((pack1.astype(F32) + passed[:, 1].astype(F32)).astype(BF16), 0)
+            passed = jnp.zeros((E, 2) + pack0.shape[1:], BF16)
+
+        def pack_for(member):
+            one, two = (lax.dynamic_index_in_dim(p, member, 0, False).astype(F32) for p in (pack0, pack1))
+            came = lax.dynamic_index_in_dim(passed, member, 0, False).astype(F32)
+            return one + came[0] + self.other((two + came[1]).astype(BF16), 2).astype(F32)
+
+        total = self.sum_both_ways(pack_for)
+        at = jnp.stack([_slot(self.tensor, t) for t in range(4)])
+
+        def all_rows(own):
+            across = self.other(own, 2)
+            return lay_out(at, [own, across, self.other(own, 1), self.other(across, 1)])
+
+        d_tokens = all_rows(d_tok)
+        output = all_rows((x1 + y_sum.astype(F32)).astype(BF16))
+        came = jnp.stack([lax.rem(self.member - by + E, E) for by in range(E)])
+        return output, d_tokens, *unpack(came, g_exp), total
+
     def sum_both_ways(self, block_for):
         def chain(way, steps):
             total = block_for(self.behind(1 - way, steps)).astype(BF16)
@@ -1048,52 +1297,17 @@
     noise = jnp.stack(image_lanes(jnp.transpose(router_noise), move.tensor, imgs))
     if move.groups == 1:
         _, _, _, g_low, sums, w, *saved = front(pack, ew, dy, x, noise, keep)
+        x1, qkv, o, lse, probs = saved
+        g_exp, output, d_tokens, total = back(g_low, sums, (x1, x, dy, probs, qkv, o, lse), w)
+        g_in, g_out = g_exp[:, 0].astype(F32), g_exp[:, 1].astype(F32)
+        output, d_tokens = (rows[:, :, :SEQ].reshape(token_count, D) for rows in (output, d_tokens))
     else:
         g_low, sums, w, *saved = move.front(pack, ew, dy, x, noise, keep)
-    x1, qkv, o, lse, probs = saved
-    dh_sum, y_sum = sums[0], sums[1]
-
-    passed = move.other(g_low[2:], 1)
-    pair = [(g_low[s].astype(F32) + passed[s].astype(F32)).astype(BF16) for s in range(2)]
-    total = (pair[0].astype(F32) + move.other(pair[1], 2).astype(F32)).astype(BF16)
-    if move.groups > 1:
-        total = jnp.swapaxes(total, 1, 2).reshape(D, 2, FFS)
-        total = jnp.swapaxes(move.sum_groups(total, 0).reshape(E, d_own, 2, FFS), 1, 2)
-    g_exp = []
-    for by in range(E):
-        to = lax.rem(move.member + by, E)
-        block = lax.dynamic_index_in_dim(total, to, 0, False)
-        g_exp.append(move.shift(block, by) if by else block)
-
-    pack0, pack1, packs, d_tok = attn_backward(
-        [dh_sum[c] for c in range(imgs)], (x1, x, dy, probs, qkv, o, lse), w, n_dp
-    )
-    passed = move.other(packs, 1)
-    if move.groups > 1:
-        pack0 = move.sum_groups((pack0.astype(F32) + passed[:, 0].astype(F32)).astype(BF16), 0)
-        pack1 = move.sum_groups((pack1.astype(F32) + passed[:, 1].astype(F32)).astype(BF16), 0)
-        passed = jnp.zeros((E, 2) + pack0.shape[1:], BF16)
-
-    def pack_for(member):
-        one, two = (lax.dynamic_index_in_dim(p, member, 0, False).astype(F32) for p in (pack0, pack1))
-        came = lax.dynamic_index_in_dim(passed, member, 0, False).astype(F32)
-        return one + came[0] + move.other((two + came[1]).astype(BF16), 2).astype(F32)
-
-    total = move.sum_both_ways(pack_for)
+        output, d_tokens, g_in, g_out, total = move.back(g_low, sums, saved, x, dy, w)
     g_qkv = total[:d_own, : 9 * HD].reshape(d_own, 3, 3 * HD)
     g_attn_out = jnp.transpose(total[:d_own, 9 * HD :])
     g_small = total[d_own:, :d_own]
 
-    at = jnp.stack([_slot(move.tensor, t) for t in range(4)])
-
-    def all_rows(own):
-        across = move.other(own, 2)
-        return lay_out(at, [own, across, move.other(own, 1), move.other(across, 1)])
-
-    d_tokens = all_rows(d_tok)
-    output = all_rows((x1 + y_sum.astype(F32)).astype(BF16))
-    came = jnp.stack([lax.rem(move.member - by + E, E) for by in range(E)])
-    g_in, g_out = unpack(came, g_exp)
     return (
         output,
         d_tokens,

time: 580 us -> 494 us (0.85)
  Pallas kernels: 364 us -> 452 us
  waiting for transfers between devices: 87.6 us -> 0 us
  starting transfers between devices: 67.9 us -> 0 us
  local copies, waits for them, and re-layouts: 27.2 us -> 18.3 us
  other arithmetic: 22.1 us -> 15.4 us
    pallas_call x4 -> x1, Pallas kernels: 38.1 us -> 126 us  [back(): pl.pallas_call(functools.partial(back_kernel, imgs), out_shape=(jax.Shape...]
    ppermute x31 -> x0, waiting for transfers between devices: 87.6 us -> none  [the longest x17 76.7 us: other(): return lax.ppermute(value, 'tensor', [(k, k ^ mask) for k in range(4)])]
    ppermute x31 -> x0, starting transfers between devices: 67.9 us -> none  [the longest x7 38.8 us: shift(): return lax.ppermute(value, 'dp', perm)]
    convert_element_type x9 -> x0, other arithmetic: 12.9 us -> none  [the longest x1 4.99 us: body(): (g_low[s].astype(F32) + passed[s].astype(F32)).astype(BF16)]
  transfers between devices with their start and end apart: 31 -> 0, of which waited for: 11 -> 0; matrix products, arithmetic and copies ran while one was open for 4% -> 0% of each run, Pallas kernels for 6% -> 0%
where the time goes in v5:
time: 494 us; the launch traced here: 487 us
  Pallas kernels  452 us (91%)
  local copies, waits for them, and re-layouts  18.3 us (4%)
  other arithmetic  15.4 us (3%)
    pallas_call x1, Pallas kernels, front(): pl.pallas_call(functools.partial(front_kernel, imgs), out_shape=(table, t...  326 us
    pallas_call x1, Pallas kernels, back(): pl.pallas_call(functools.partial(back_kernel, imgs), out_shape=(jax.Shape...  126 us

profile of v5, /device:TPU:24, one launch (start us, length us, event | category | flops | bytes accessed | tf_op | source)
XLA Modules:
  0.0 486.9 jit_solution(12330053393311127024)
XLA Ops:
  0.7 0.8 convert_bitcast_fusion.7
  1.5 0.7 convert_bitcast_fusion.6
  2.1 0.7 convert_bitcast_fusion.5
  2.8 0.7 convert_bitcast_fusion.4
  3.5 0.7 convert.56
  4.2 0.8 eq.15
  4.9 0.9 dynamic-slice_bitcast_fusion.1
  5.8 0.6 pad_maximum_fusion.3.noise_ref
  7.0 1.0 copy.32
  8.1 2.3 reduce-window.6
  10.4 0.3 slice_reduce_fusion
  10.7 0.2 reduce-window.9
  11.5 0.6 pad_maximum_fusion.4.keep_ref
  12.2 0.2 concatenate.8
  12.3 0.7 pad.34.pack_ref
  13.2 0.9 copy-done.1
  14.2 1.6 pad_maximum_fusion.ew_ref
  15.8 1.5 constant_dynamic-slice_fusion.3
  17.4 0.9 pad_maximum_fusion.2.x_ref
  18.4 0.9 pad_maximum_fusion.1.dy_ref
  19.2 325.7 %front.1 = (bf16[16,208,768]{2,1,0:T(8,128)(2,1)}, bf16[16,208,768]{2,1,0:T(8,128)(2,1)}, bf16[8,2,2,208,768]{4,3,2,1,0:T(8,128)(2,1)}, bf16[4,8,2,96,768]{4,3,2...) custom-call(bf16[96,896]{1,0:T(8,128)(2,1)} %pad.34.pack_ref, ...), custom_call_target="tpu_custom_call" | custom-call | flops 99999997952 | bytes 100000000 | tf_op jit(solution)/shard_map/front/pallas_call | solution.py:463
  345.0 126.4 %back.1 = (bf16[8,2,96,768]{3,2,1,0:T(8,128)(2,1)}, bf16[4,2,208,768]{3,2,1,0:T(8,128)(2,1)}, bf16[4,2,208,768]{3,2,1,0:T(8,128)(2,1)}, f32[112,768]{1,0:T(8,128)}) custom-call(bf16[4,8,2,96,768]{4,3,2,1,0:T(8,128)(2,1)} %get-tuple-element.23.g_low, bf16[2,2,208,768]{3,2,1,0:T(8,128)(2,1)} %get-tuple-element.24.sums_ref, ...), custom_call_target="tpu_custom_call" | custom-call | flops 12000000000 | bytes 100000000 | tf_op jit(solution)/shard_map/back/pallas_call | solution.py:1045
  471.3 1.9 slice.66
  473.2 2.1 reshape.53
  475.4 0.5 slice_bitcast_fusion.5
  475.9 0.6 slice_bitcast_fusion.4
  476.6 0.7 copy.41
  477.3 0.1 copy.39
  477.5 0.9 copy.40
  478.4 1.9 slice.67
  480.2 2.1 reshape.54
  482.4 4.3 convert_bitcast_fusion
  (35 shorter events, 1.7 us)
Async XLA Ops:
  0.6 12.4 %copy-start = (f32[8,96,768]{2,1,0:T(8,128)S(1)}, f32[8,96,768]{2,1,0:T(8,128)}, u32[]{:S(2)}) copy-start(f32[8,96,768]{2,1,0:T(8,128)} %param.21) | copy-start | bytes 7077892
  0.7 11.4 %copy-start.3 = (f32[96,3,192]{2,0,1:T(8,128)S(1)}, f32[96,3,192]{2,0,1:T(8,128)}, u32[]{:S(2)}) copy-start(f32[96,3,192]{2,0,1:T(8,128)} %param.16) | copy-start | bytes 663556
  12.3 1.7 copy-start.1
  473.2 2.2 copy-start.2

commit v6 on v5

--- a/solution.py
+++ b/solution.py
@@ -185,7 +185,7 @@
         return copy
 
 
-def expert_step(x, dy, gate, w_ref, g_ref, y_ref, dx_ref):
+def expert_step(x, dy, gate, w_ref, g_ref, y_ref, dx_ref, meanwhile):
     weight = jnp.maximum(gate, 0.0)
     d_rows = (dy.astype(F32) * weight).astype(BF16)
 
@@ -203,6 +203,7 @@
         dx_ref[...] += dot_nt(da, w1)
         g_ref[r, 0] += dot_tn(x, da)
         g_ref[r, 1] += dot_tn(d_rows, hid)
+        meanwhile(r)
         return carry
 
     y_ref[...] = jnp.zeros_like(y_ref)
@@ -213,11 +214,16 @@
     return (y * weight).astype(BF16), dx_ref[...], dgate
 
 
+GIVEN, PASSED, DY_AT = (1, 3, 4, 6, 7), (1, 3), 2
+NEXT_AT, SUMS_AT = 0, 3
+HOPS_AT = ()
+
+
 def front_kernel(
     imgs, pack_ref, ew_ref, dy_ref, x_ref, noise_ref, keep_ref,
-    h_out, dy_out, t_in, g_out, sums_out, w_out, x1_ref, qkv_ref, o_ref, lse_ref, probs_ref,
-    w_s, chunk_s, we_s, g_s, xs, dys, y_s, dx_s, t_s, pass_s, g_low,
-    p_s, p_r, px_s, px_r, pc_s, pc_r, d_s, d_r, h_s, h_r, e_s, e_r, ex_s, ex_r, ec_s, ec_r, t_ss, t_r, local, stage, g_sem,
+    h_out, dy_out, t_in, y_out, g_out, sum_out, w_out, x1_ref, qkv_ref, o_ref, lse_ref, probs_ref,
+    w_s, chunk_s, we_s, g_s, xs, dys, y_s, dx_s, t_s, own_s, y_low, pass_s, g_low,
+    p_s, p_r, px_s, px_r, pc_s, pc_r, d_s, d_r, h_s, h_r, e_s, e_r, ex_s, ex_r, ec_s, ec_r, t_ss, t_r, local, stage, y_sem, g_sem,
 ):
     peers = Peers()
     member = peers.member
@@ -241,26 +247,32 @@
 
     arrivals = [(0, k) if i == 0 else (1, k) for k in range(1, half + 1) for i in range(2 if k < half else 1)]
     owners = [member] + [peers.behind(way, k) for way, k in arrivals]
-    ring[0, 0] = peers.send(pack_ref, w_s.at[0, rows(member)], (p_s, p_r), (0, 0), peers.next[0])
-    pass_pack(0, member, pack_ref, 1, 0)
 
     def pass_x(number):
         px[number].wait_recv()
         at = rows(owners[number])
         pc[1, number] = peers.send(w_s.at[1, at], w_s.at[3, at], (pc_s, pc_r), (1, number), peers.core)
 
-    for number, (way, k) in enumerate(arrivals, 1):
-        ring[way, k - 1].wait_recv()
-        of = owners[number]
-        last = half if way == 0 else half - 1
-        pass_pack(number, of, w_s.at[0, rows(of)], way if k < last else None, k)
-        if number >= 2:
-            pass_x(number - 2)
-
-    e_copy = {}
-    for by in range(1, E):
-        to = peers.ahead(by)
-        e_copy[by] = peers.send(ew_ref.at[to], we_s.at[0, member], (e_s, e_r), by, {"dp": peers.base + to})
+    far = (1, 7, 2, 6, 3, 5, 4)
+    e_copy, ex, ec = {}, {}, {}
+
+    def give_e(part):
+        for by in part:
+            to = peers.ahead(by)
+            e_copy[by] = peers.send(ew_ref.at[to], we_s.at[0, member], (e_s, e_r), by, {"dp": peers.base + to})
+
+    def pass_e(by):
+        if by:
+            e_copy[by].wait_recv()
+        of = peers.came(by)
+        src = we_s.at[0, of] if by else ew_ref.at[member]
+        ex[by] = peers.send(src, we_s.at[1, of], (ex_s, ex_r), by, peers.across)
+        ec[0, by] = peers.send(src, we_s.at[2, of], (ec_s, ec_r), (0, by), peers.core)
+
+    def pass_ex(by):
+        ex[by].wait_recv()
+        of = peers.came(by)
+        ec[1, by] = peers.send(we_s.at[1, of], we_s.at[3, of], (ec_s, ec_r), (1, by), peers.core)
 
     def block_at(c, k):
         return peers.behind(c % 2, k) * imgs + c
@@ -277,42 +289,58 @@
         )
 
     h_sems, d_sems = (h_s, h_r), (d_s, d_r)
-    for c in range(imgs):
-        row_copy(dy_out, d_sems, c, 0, dy_ref.at[c]).start()
-    for number in range(len(arrivals) - 1, len(arrivals) + 1):
-        pass_x(number)
-
-    ex, ec = {}, {}
-
-    def pass_e(by):
-        if by:
-            e_copy[by].wait_recv()
-        of = peers.came(by)
-        src = we_s.at[0, of] if by else ew_ref.at[member]
-        ex[by] = peers.send(src, we_s.at[1, of], (ex_s, ex_r), by, peers.across)
-        ec[0, by] = peers.send(src, we_s.at[2, of], (ec_s, ec_r), (0, by), peers.core)
-
-    def pass_ex(by):
-        ex[by].wait_recv()
-        of = peers.came(by)
-        ec[1, by] = peers.send(we_s.at[1, of], we_s.at[3, of], (ec_s, ec_r), (1, by), peers.core)
-
-    for number in range(E):
-        pc[0, number].wait_recv()
-        pc[1, number].wait_recv()
-    own_pack.wait()
+
+    def row_hop(k):
+        for c in range(imgs):
+            for out, sems in ((h_out, h_sems), (dy_out, d_sems)):
+                row_copy(out, sems, c, k - 1).wait_recv()
+                row_copy(out, sems, c, k).start()
+
+    def give_dy():
+        for c in range(imgs):
+            row_copy(dy_out, d_sems, c, 0, dy_ref.at[c]).start()
+
+    ring[0, 0] = peers.send(pack_ref, w_s.at[0, rows(member)], (p_s, p_r), (0, 0), peers.next[0])
+    pass_pack(0, member, pack_ref, 1, 0)
+    give_e(far[:GIVEN[0]])
     pass_e(0)
+    if DY_AT == 0:
+        give_dy()
     keepers = [
-        pltpu.make_async_copy(w_s, w_out, local.at[1]),
         pltpu.make_async_copy(ew_ref.at[member], we_s.at[0, member], local.at[2]),
     ] + [
         pltpu.make_async_copy(dy_ref.at[c], dy_out.at[member * imgs + c], local.at[3 + c]) for c in range(imgs)
     ]
     for copy in keepers:
         copy.start()
+    for number, (way, k) in enumerate(arrivals, 1):
+        ring[way, k - 1].wait_recv()
+        of = owners[number]
+        last = half if way == 0 else half - 1
+        pass_pack(number, of, w_s.at[0, rows(of)], way if k < last else None, k)
+        if number >= 2:
+            pass_x(number - 2)
+        if number == 4:
+            give_e(far[GIVEN[0]:GIVEN[1]])
+    give_e(far[GIVEN[1]:GIVEN[2]])
+    if DY_AT == 1:
+        give_dy()
+    for number in range(len(arrivals) - 1, len(arrivals) + 1):
+        pass_x(number)
+    for number in range(E):
+        pc[0, number].wait_recv()
+        pc[1, number].wait_recv()
+    own_pack.wait()
+    keepers.append(pltpu.make_async_copy(w_s, w_out, local.at[1]))
+    keepers[-1].start()
 
     par = params_of(w_s[0])
+    done = 0
     for c in range(imgs):
+        for by in far[done : PASSED[c]]:
+            pass_e(by)
+            pass_ex((0, *far)[done])
+            done += 1
         attend(
             x_ref[c], par, lambda r: w_s[r], noise_ref[c], keep_ref[c],
             chunk_s.at[c], *(ref.at[c] for ref in (x1_ref, qkv_ref, o_ref, lse_ref, probs_ref)),
@@ -322,15 +350,17 @@
             pltpu.make_async_copy(chunk_s.at[c], h_out.at[member * imgs + c], local.at[3 + imgs + c])
         )
         keepers[-1].start()
-
-    far = (1, 7, 2, 6, 3, 5, 4)
+        give_e(far[GIVEN[2 + c]:GIVEN[3 + c]])
+    if DY_AT == 2:
+        give_dy()
     for i, by in enumerate(far):
-        pass_e(by)
-        if i >= 1:
-            pass_ex((0, *far)[i - 1])
+        if i >= done:
+            pass_e(by)
+            pass_ex((0, *far)[i])
+        if i in HOPS_AT:
+            row_hop(1 + HOPS_AT.index(i))
     g_s[...] = jnp.zeros_like(g_s)
-    for by in (0, *far)[len(far) - 1 :]:
-        pass_ex(by)
+    pass_ex(far[-1])
     for by in range(E):
         ec[0, by].wait_recv()
         ec[1, by].wait_recv()
@@ -340,90 +370,110 @@
     row16 = iota((16, D), 0)
     eye = iota((PAD, PAD), 0) == iota((PAD, PAD), 1)
 
-    def sum_copy(flow, c, k):
+    def sum_copy(c, k):
         return pltpu.make_async_remote_copy(
-            src_ref=pass_s.at[lax.rem(k, 2), flow, c],
-            dst_ref=t_in.at[k - 1, flow, c],
-            send_sem=t_ss.at[flow, c, k - 1],
-            recv_sem=t_r.at[flow, c, k - 1],
+            src_ref=pass_s.at[lax.rem(k, 2), c],
+            dst_ref=t_in.at[k - 1, c],
+            send_sem=t_ss.at[c, k - 1],
+            recv_sem=t_r.at[c, k - 1],
             device_id=peers.next[c % 2],
             device_id_type=pl.DeviceIdType.MESH,
         )
 
-    own_sums = pltpu.make_async_copy(pass_s.at[0], t_in.at[E - 1], local.at[0])
-
-    def fetch_sums(k):
-        copies = []
-        for flow in range(2):
-            for c in range(imgs):
-                sum_copy(flow, c, k - 1).wait_recv()
-                copies.append(pltpu.make_async_copy(t_in.at[k - 2, flow, c], t_s.at[flow, c], stage.at[flow, c]))
-                copies[-1].start()
+    def sums_to_hand(k):
+        return [pltpu.make_async_copy(t_in.at[k - 2, c], t_s.at[c], stage.at[2, c]) for c in range(imgs)]
+
+    def rows_to_hand(k):
+        slot = lax.rem(k, 2)
+        return [
+            pltpu.make_async_copy(out.at[block_at(c, k)], held.at[slot, c], stage.at[i, c])
+            for c in range(imgs)
+            for i, (out, held) in enumerate(((h_out, xs), (dy_out, dys)))
+        ]
+
+    def start(copies):
+        for copy in copies:
+            copy.start()
+
+    def finish(copies):
         for copy in copies:
             copy.wait()
 
+    def keep_y(k):
+        return pltpu.make_async_copy(y_low, y_out.at[k], y_sem)
+
     def step(k, carry):
-        for c in range(imgs):
-            for out, sems in ((h_out, h_sems), (dy_out, d_sems)):
-
-                @pl.when(k > 0)
-                def _():
-                    row_copy(out, sems, c, k - 1).wait_recv()
-
-                @pl.when((k > 0) & (k < E - 1))
-                def _():
-                    row_copy(out, sems, c, k).start()
-
-        loads = []
-        for c in range(imgs):
-            for i, (out, held) in enumerate(((h_out, xs), (dy_out, dys))):
-                loads.append(pltpu.make_async_copy(out.at[block_at(c, k)], held.at[c], stage.at[i, c]))
-                loads[-1].start()
-        for copy in loads:
-            copy.wait()
+        slot = lax.rem(k, 2)
+        finish(rows_to_hand(k))
+
+        def meanwhile(r):
+            for c in range(imgs):
+                for out, sems in ((h_out, h_sems), (dy_out, d_sems)):
+
+                    @pl.when((r == NEXT_AT) & (k >= len(HOPS_AT)) & (k < E - 1))
+                    def _():
+                        row_copy(out, sems, c, k).wait_recv()
+
+                    @pl.when((r == NEXT_AT) & (k >= len(HOPS_AT)) & (k < E - 2))
+                    def _():
+                        row_copy(out, sems, c, k + 1).start()
+
+            @pl.when((r == NEXT_AT) & (k < E - 1))
+            def _():
+                start(rows_to_hand(k + 1))
+
+            @pl.when((r == SUMS_AT) & (k >= 2))
+            def _():
+                for c in range(imgs):
+                    sum_copy(c, k - 1).wait_recv()
+                start(sums_to_hand(k))
+
         columns = []
         for c in range(imgs):
-            meta = xs[c, PAD - 16 :, :].astype(F32)
+            meta = xs[slot, c, PAD - 16 :, :].astype(F32)
             line = jnp.sum(jnp.where(row16 == 8 + member, meta, 0.0), axis=0, keepdims=True)[:, :PAD]
             columns.append(jnp.sum(jnp.where(eye, line, 0.0), axis=1, keepdims=True))
         y, dx, dgate = expert_step(
-            xs[...].reshape(imgs * PAD, D), dys[...].reshape(imgs * PAD, D), jnp.concatenate(columns, axis=0),
-            we_s, g_s, y_s, dx_s,
+            xs[slot].reshape(imgs * PAD, D), dys[slot].reshape(imgs * PAD, D), jnp.concatenate(columns, axis=0),
+            we_s, g_s, y_s, dx_s, meanwhile,
         )
-        slot = lax.rem(k, 2)
 
         @pl.when(k >= 3)
         def _():
-            for flow in range(2):
-                for c in range(imgs):
-                    sum_copy(flow, c, k - 2).wait_send()
+            for c in range(imgs):
+                sum_copy(c, k - 2).wait_send()
+
+        @pl.when(k >= 1)
+        def _():
+            keep_y(k - 1).wait()
 
         for c in range(imgs):
             span = slice(c * PAD, (c + 1) * PAD)
             line = jnp.sum(jnp.where(eye, dgate[span], 0.0), axis=0, keepdims=True)
             line = jnp.concatenate([line, jnp.zeros((1, D - PAD), F32)], axis=1)
             tail = dx[span][PAD - 16 :] + jnp.where(row16 == 8 + member, line, 0.0)
-            pass_s[slot, 0, c] = jnp.concatenate([dx[span][: PAD - 16], tail], axis=0).astype(BF16)
-            pass_s[slot, 1, c] = y[span]
+            pass_s[slot, c] = jnp.concatenate([dx[span][: PAD - 16], tail], axis=0).astype(BF16)
+            y_low[c] = y[span]
+
+        keep_y(k).start()
 
         @pl.when(k == 0)
         def _():
-            own_sums.start()
-            own_sums.wait()
+            own_s[...] = pass_s[0]
 
         @pl.when(k >= 2)
         def _():
-            fetch_sums(k)
+            finish(sums_to_hand(k))
             pass_s[slot] = (pass_s[slot].astype(F32) + t_s[...].astype(F32)).astype(BF16)
 
         @pl.when(k >= 1)
         def _():
-            for flow in range(2):
-                for c in range(imgs):
-                    sum_copy(flow, c, k).start()
+            for c in range(imgs):
+                sum_copy(c, k).start()
 
         return carry
 
+    start(rows_to_hand(0))
     lax.fori_loop(0, E, step, 0)
 
     for i in range(8):
@@ -432,19 +482,17 @@
             pltpu.make_async_copy(g_low.at[i % 2], g_out.at[r, :, kind], g_sem.at[i % 2]).wait()
         g_low[i % 2] = g_s[r, kind].astype(BF16).reshape(E, d_own, FFS)
         pltpu.make_async_copy(g_low.at[i % 2], g_out.at[r, :, kind], g_sem.at[i % 2]).start()
-    fetch_sums(E)
     for c in range(imgs):
-        for flow in range(2):
-            sum_copy(flow, c, E - 2).wait_send()
-    own_sums = pltpu.make_async_copy(t_in.at[E - 1], pass_s.at[0], local.at[0])
-    own_sums.start()
-    own_sums.wait()
-    sums_out[...] = (pass_s[0].astype(F32) + t_s[...].astype(F32)).astype(BF16)
+        sum_copy(c, E - 1).wait_recv()
+    start(sums_to_hand(E))
+    finish(sums_to_hand(E))
+    sum_out[...] = (own_s[...].astype(F32) + t_s[...].astype(F32)).astype(BF16)
+    keep_y(E - 1).wait()
     for i in range(2):
         pltpu.make_async_copy(g_low.at[i], g_out.at[3, :, i], g_sem.at[i]).wait()
     for c in range(imgs):
-        for flow in range(2):
-            sum_copy(flow, c, E - 1).wait_send()
+        sum_copy(c, E - 2).wait_send()
+        sum_copy(c, E - 1).wait_send()
         for k in range(E - 1):
             row_copy(h_out, h_sems, c, k).wait_send()
             row_copy(dy_out, d_sems, c, k).wait_send()
@@ -459,37 +507,40 @@
     hbm = pl.BlockSpec(memory_space=pl.ANY)
     table = jax.ShapeDtypeStruct((E * imgs, PAD, D), BF16)
     dma = pltpu.SemaphoreType.DMA
-    pair = (2, imgs, PAD, D)
+    rows = (imgs, PAD, D)
     return pl.pallas_call(
         functools.partial(front_kernel, imgs),
         out_shape=(
             table,
             table,
-            jax.ShapeDtypeStruct((E,) + pair, BF16),
+            jax.ShapeDtypeStruct((E - 1,) + rows, BF16),
+            jax.ShapeDtypeStruct((E,) + rows, BF16),
             jax.ShapeDtypeStruct((4, E, 2, d_own, FFS), BF16),
-            jax.ShapeDtypeStruct(pair, BF16),
+            jax.ShapeDtypeStruct(rows, BF16),
             jax.ShapeDtypeStruct((4, E * d_own, D + 128), BF16),
         )
         + attn_shapes(imgs),
         in_specs=[vm, hbm, hbm, vm, vm, vm],
-        out_specs=(hbm,) * 4 + (vm, hbm) + (vm,) * 5,
+        out_specs=(hbm,) * 5 + (vm, hbm) + (vm,) * 5,
         scratch_shapes=[
             pltpu.VMEM((4, E * d_own, D + 128), BF16),
             pltpu.VMEM((imgs, PAD, D), BF16),
             pltpu.VMEM((4, E, 2, d_own, FFS), BF16),
             pltpu.VMEM((4, 2, D, FFS), F32),
-            pltpu.VMEM((imgs, PAD, D), BF16),
-            pltpu.VMEM((imgs, PAD, D), BF16),
+            pltpu.VMEM((2, imgs, PAD, D), BF16),
+            pltpu.VMEM((2, imgs, PAD, D), BF16),
             pltpu.VMEM((imgs * PAD, D), F32),
             pltpu.VMEM((imgs * PAD, D), F32),
-            pltpu.VMEM(pair, BF16),
-            pltpu.VMEM((2,) + pair, BF16),
+            pltpu.VMEM(rows, BF16),
+            pltpu.VMEM(rows, BF16),
+            pltpu.VMEM(rows, BF16),
+            pltpu.VMEM((2,) + rows, BF16),
             pltpu.VMEM((2, E, d_own, FFS), BF16),
             dma((2, 4)), dma((2, 4)), dma((E,)), dma((E,)), dma((2, E)), dma((2, E)),
             dma((imgs, E - 1)), dma((imgs, E - 1)), dma((imgs, E - 1)), dma((imgs, E - 1)),
             dma((E,)), dma((E,)), dma((E,)), dma((E,)), dma((2, E)), dma((2, E)),
-            dma((2, imgs, E - 1)), dma((2, imgs, E - 1)),
-            dma((3 + 2 * imgs,)), dma((2, imgs)), dma((2,)),
+            dma((imgs, E - 1)), dma((imgs, E - 1)),
+            dma((3 + 2 * imgs,)), dma((3, imgs)), dma(()), dma((2,)),
         ],
         compiler_params=pltpu.CompilerParams(
             vmem_limit_bytes=VMEM_LIMIT, collective_id=0, has_side_effects=True
@@ -901,11 +952,11 @@
 
 
 def back_kernel(
-    imgs, g_low, sums_ref, x1_ref, x_ref, dy_ref, probs_ref, qkv_ref, o_ref, lse_ref, w_ref,
-    g_out, out_all, dtok_all, total_ref,
-    ga_s, gc_s, gx_s, pk_s, pkc_s, pkr_s, sm_s, smr_s, cs_s, cr_s, fs_s, fr_s, or_s, dt_s,
+    imgs, g_low, y_ref, dh_ref, x1_ref, x_ref, dy_ref, probs_ref, qkv_ref, o_ref, lse_ref, w_ref,
+    out_all, dtok_all, g_out, total_ref,
+    ga_s, gc_s, gx_s, pk_s, pkc_s, pkr_s, sm_s, smr_s, cs_s, cr_s, fs_s, fr_s, or_s, dt_s, y_s, yr_s,
     dx1_s, low_s, h1_s, dh1_s, dqkv_s, o_s,
-    gc_ss, gc_r, gx_ss, gx_r, ga_ss, ga_r, pk_ss, pk_r, sm_ss, sm_r, c_ss, c_r, f_ss, f_r, row_ss, row_r, local,
+    gc_ss, gc_r, gx_ss, gx_r, ga_ss, ga_r, pk_ss, pk_r, sm_ss, sm_r, c_ss, c_r, f_ss, f_r, row_ss, row_r, y_ss, y_r, local,
 ):
     peers = Peers()
     member = peers.member
@@ -933,14 +984,31 @@
 
         return onwards
 
-    for c in range(imgs):
-        or_s[c] = (x1_ref[c] + sums_ref[1, c].astype(F32)).astype(BF16)
-    out_rows = give_rows(0, or_s, out_all)
+    y_load = here(y_ref, y_s)
+    y_sent = {}
+
+    def y_hop(k):
+        for c in range(imgs):
+            if k == 1:
+                src = y_s.at[1, c]
+            else:
+                y_sent[c, k - 1].wait_recv()
+                src = yr_s.at[k - 2, c]
+                src[...] = (src[...].astype(F32) + y_s[k, c].astype(F32)).astype(BF16)
+            y_sent[c, k] = peers.send(src, yr_s.at[k - 1, c], (y_ss, y_r), (c, k - 1), peers.next[c % 2])
+
+    def y_last():
+        for c in range(imgs):
+            y_sent[c, E - 1].wait_recv()
+            total = yr_s[E - 2, c].astype(F32) + y_s[0, c].astype(F32)
+            or_s[c] = (x1_ref[c] + total).astype(BF16)
 
     g_core = [
         peers.send(g_low.at[2 + s], gc_s.at[s], (gc_ss, gc_r), s, peers.core) for s in (1, 0)
     ][::-1]
     g_load = [here(g_low.at[s], ga_s.at[s]) for s in (1, 0)][::-1]
+    y_load.wait()
+    y_hop(1)
     order = (4, 3, 5, 2, 6, 1, 7, 0)
     gx = {}
 
@@ -968,20 +1036,21 @@
             here(ga_s.at[0, to], g_out.at[member])
 
     saved = (x1_ref, x_ref, dy_ref, probs_ref, qkv_ref, o_ref, lse_ref)
-    back = Backward(imgs, lambda c: sums_ref[0, c], saved, w_ref, dx1_s, low_s, h1_s, dh1_s, dqkv_s, o_s)
+    back = Backward(imgs, lambda c: dh_ref[c], saved, w_ref, dx1_s, low_s, h1_s, dh1_s, dqkv_s, o_s)
     back.first()
     for r in (2, 3):
         grad = back.heads(r)
         for i in range(E):
             pkc_s[i, r - 2] = grad[i * d_own : (i + 1) * d_own]
+        y_hop(r)
         if r == 2:
             pass_across()
     pk_core = peers.send(pkc_s, pkr_s, (pk_ss, pk_r), 0, peers.core)
-    out_rows = out_rows()
     for r in (0, 1):
         grad = back.heads(r)
         for i in range(E):
             pk_s[i, r, :d_own] = grad[i * d_own : (i + 1) * d_own]
+        y_hop(4 + r)
         pass_home(order[r])
     small = back.last(dt_s)
     dtok_rows = give_rows(1, dt_s, dtok_all)
@@ -1011,6 +1080,11 @@
         hop(0, i)
         if i < steps[1]:
             hop(1, i)
+        if i < 2:
+            y_hop(6 + i)
+        if i == 2:
+            y_last()
+            out_rows = give_rows(0, or_s, out_all)
         pass_home(order[2 + i])
     hops[1, steps[1] - 1].wait_recv()
     hops[0, steps[0] - 1].wait_recv()
@@ -1020,6 +1094,7 @@
     pass_home(order[6])
     pass_home(order[7])
     dtok_rows = dtok_rows()
+    out_rows = out_rows()
     final.wait_recv()
     total_ref[...] = total[0] + fr_s[...].astype(F32)
     for by in range(1, E):
@@ -1027,14 +1102,14 @@
     for copy in (*out_rows, *dtok_rows):
         copy.wait_recv()
     for copy in loads:
-        if all(copy is not other for other in g_load):
+        if all(copy is not other for other in (y_load, *g_load)):
             copy.wait()
     for copy in peers.sends:
         copy.wait_send()
 
 
-def back(g_low, sums, saved, w):
-    imgs = sums.shape[1]
+def back(g_low, y, dh, saved, w):
+    imgs = dh.shape[0]
     d_own = g_low.shape[3]
     vm = pl.BlockSpec(memory_space=pltpu.VMEM)
     hbm = pl.BlockSpec(memory_space=pl.ANY)
@@ -1045,12 +1120,12 @@
     return pl.pallas_call(
         functools.partial(back_kernel, imgs),
         out_shape=(
-            jax.ShapeDtypeStruct(part, BF16),
             jax.ShapeDtypeStruct((4,) + rows, BF16),
             jax.ShapeDtypeStruct((4,) + rows, BF16),
+            jax.ShapeDtypeStruct(part, BF16),
             jax.ShapeDtypeStruct((d_own + 16, D), F32),
         ),
-        in_specs=[hbm] + [vm] * 9,
+        in_specs=[hbm, hbm] + [vm] * 9,
         out_specs=(hbm, hbm, hbm, vm),
         scratch_shapes=[
             pltpu.VMEM((2,) + part, BF16),
@@ -1067,17 +1142,136 @@
             pltpu.VMEM((d_own + 16, D), BF16),
             pltpu.VMEM(rows, BF16),
             pltpu.VMEM(rows, BF16),
+            pltpu.VMEM((E,) + rows, BF16),
+            pltpu.VMEM((E - 1,) + rows, BF16),
             *backward_scratch(imgs),
             dma((2,)), dma((2,)), dma((E,)), dma((E,)), dma((E,)), dma((E,)), dma((1,)), dma((1,)),
             dma((1,)), dma((1,)), dma((2, E // 2)), dma((2, E // 2)), dma((1,)), dma((1,)), dma((2, 3)), dma((2, 3)),
-            dma((5,)),
+            dma((imgs, E - 1)), dma((imgs, E - 1)), dma((6,)),
         ],
         compiler_params=pltpu.CompilerParams(
             vmem_limit_bytes=VMEM_LIMIT, collective_id=1, has_side_effects=True
         ),
         cost_estimate=pl.CostEstimate(flops=12 * 10**9, bytes_accessed=10**8, transcendentals=2 * 10**6),
         name="back",
-    )(g_low, sums, *saved, w)
+    )(g_low, y, dh, *saved, w)
+
+
+def eye_of(n, lanes):
+    return (iota((n, lanes), 0) == iota((n, lanes), 1)).astype(F32).astype(BF16)
+
+
+def prepare_kernel(
+    imgs, tensor_ref, tok_ref, cot_ref, qkv_ref, wo_ref, vec_ref, router_ref, win_ref, wout_ref, noise_ref, routes_ref,
+    pack_ref, ew_ref, x_ref, dy_ref, keep_out, noise_out, keep_s,
+):
+    tensor = tensor_ref[0]
+    d_own = wo_ref.shape[1]
+    wo = dot_tn(wo_ref[...].astype(BF16), eye_of(3 * HD, 3 * HD)).astype(BF16)
+    lines = jnp.concatenate([vec_ref[...], jnp.zeros((4, d_own), F32), router_ref[...]], axis=0).astype(BF16)
+    lines = dot_tn(lines, eye_of(16, 128)).astype(BF16)
+    pack_ref[...] = jnp.concatenate([qkv_ref[i].astype(BF16) for i in range(3)] + [wo, lines], axis=1)
+    for e in range(E):
+        ew_ref[e, 0] = win_ref[e].astype(BF16)
+        ew_ref[e, 1] = wout_ref[e].astype(BF16)
+    count = routes_ref.shape[1]
+    earlier = (iota((count, count), 0) <= iota((count, count), 1)).astype(F32).astype(BF16)
+    experts_ = iota((E, count), 0)
+    before = jnp.zeros((E, 1), F32)
+    keep = jnp.zeros((E, count), F32)
+    for choice in range(TOP):
+        named = experts_ == routes_ref[choice : choice + 1, :]
+        upto = before + dot(named.astype(F32).astype(BF16), earlier)
+        keep = keep + jnp.where(named & (upto <= CAP), 1.0, 0.0)
+        before = upto[:, count - 1 :]
+    keep_s[...] = keep
+    for t in range(4):
+
+        @pl.when(tensor == t)
+        def _():
+            for c in range(imgs):
+                at = (t * imgs + c) * SEQ
+                for src, dst in ((tok_ref, x_ref), (cot_ref, dy_ref)):
+                    dst[c, :SEQ, :] = src[at : at + SEQ, :]
+                    dst[c, SEQ:, :] = jnp.zeros((PAD - SEQ, D), BF16)
+                for src, dst in ((keep_s, keep_out), (noise_ref, noise_out)):
+                    dst[c] = jnp.concatenate([src[:, at : at + SEQ], jnp.zeros((E, PAD - SEQ), F32)], axis=1)
+
+
+def prepare(tensor, imgs, tokens, cotangent, w_qkv, w_attn_out, vectors, router, w_in, w_out, noise, routes):
+    vm = pl.BlockSpec(memory_space=pltpu.VMEM)
+    d_own = w_attn_out.shape[1]
+    rows = jax.ShapeDtypeStruct((imgs, PAD, D), BF16)
+    lanes = jax.ShapeDtypeStruct((imgs, E, PAD), F32)
+    return pl.pallas_call(
+        functools.partial(prepare_kernel, imgs),
+        out_shape=(
+            jax.ShapeDtypeStruct((d_own, D + 128), BF16),
+            jax.ShapeDtypeStruct((E, 2, d_own, FFS), BF16),
+            rows,
+            rows,
+            lanes,
+            lanes,
+        ),
+        in_specs=[pl.BlockSpec(memory_space=pltpu.SMEM)] + [vm] * 10,
+        out_specs=(vm,) * 6,
+        scratch_shapes=[pltpu.VMEM((E, tokens.shape[0]), F32)],
+        compiler_params=pltpu.CompilerParams(vmem_limit_bytes=VMEM_LIMIT),
+        cost_estimate=pl.CostEstimate(flops=10**8, bytes_accessed=15 * 10**6, transcendentals=0),
+        name="prepare",
+    )(tensor.reshape(1), tokens, cotangent, w_qkv, w_attn_out, vectors, router, w_in, w_out, noise, routes)
+
+
+def finish_kernel(imgs, out_in, dtok_in, g_in, total_ref, out_ref, dtok_ref, gi_ref, go_ref, qkv_ref, wo_ref, small_ref, rows_s, g_s, sem):
+    loads = [pltpu.make_async_copy(src, rows_s.at[i], sem.at[i]) for i, src in enumerate((out_in, dtok_in))]
+    loads.append(pltpu.make_async_copy(g_in, g_s, sem.at[2]))
+    for copy in loads:
+        copy.start()
+    d_own = gi_ref.shape[1]
+    total = total_ref[...]
+    for i in range(3):
+        qkv_ref[i] = total[:d_own, i * 3 * HD : (i + 1) * 3 * HD]
+    wo_ref[...] = jnp.transpose(total[:d_own, 9 * HD :])
+    small_ref[...] = total[d_own:, :d_own]
+    for which, dst in ((0, out_ref), (1, dtok_ref)):
+        loads[which].wait()
+        for i in range(4 * imgs):
+            dst[i * SEQ : (i + 1) * SEQ, :] = rows_s[which, i // imgs, i % imgs, :SEQ, :]
+    loads[2].wait()
+    for e in range(E):
+        gi_ref[e] = g_s[e, 0].astype(F32)
+        go_ref[e] = g_s[e, 1].astype(F32)
+
+
+def finish(out_all, dtok_all, g_exp, total):
+    imgs = out_all.shape[1]
+    d_own = g_exp.shape[2]
+    vm = pl.BlockSpec(memory_space=pltpu.VMEM)
+    hbm = pl.BlockSpec(memory_space=pl.ANY)
+    rows = jax.ShapeDtypeStruct((4 * imgs * SEQ, D), BF16)
+    grad = jax.ShapeDtypeStruct((E, d_own, FFS), F32)
+    return pl.pallas_call(
+        functools.partial(finish_kernel, imgs),
+        out_shape=(
+            rows,
+            rows,
+            grad,
+            grad,
+            jax.ShapeDtypeStruct((3, d_own, 3 * HD), F32),
+            jax.ShapeDtypeStruct((3 * HD, d_own), F32),
+            jax.ShapeDtypeStruct((16, d_own), F32),
+        ),
+        in_specs=[hbm, hbm, hbm, vm],
+        out_specs=(vm,) * 7,
+        scratch_shapes=[
+            pltpu.VMEM((2, 4, imgs, PAD, D), BF16),
+            pltpu.VMEM(g_exp.shape, BF16),
+            pltpu.SemaphoreType.DMA((3,)),
+        ],
+        compiler_params=pltpu.CompilerParams(vmem_limit_bytes=VMEM_LIMIT),
+        cost_estimate=pl.CostEstimate(flops=10**6, bytes_accessed=18 * 10**6, transcendentals=0),
+        name="finish",
+    )(out_all, dtok_all, g_exp, total)
 
 
 RING = (0, 2, 4, 6, 7, 5, 3, 1)
@@ -1285,29 +1479,35 @@
     d_own = w_qkv.shape[0]
     ways = [c % 2 for c in range(imgs)]
 
-    vectors = jnp.stack([ln1_gain, ln1_bias, ln2_gain, ln2_bias] + [jnp.zeros_like(ln1_gain)] * 4, axis=1)
-    pack = jnp.concatenate(
-        [w_qkv[:, 0], w_qkv[:, 1], w_qkv[:, 2], jnp.transpose(w_attn_out), vectors, router_weight], axis=1
-    )
-    pack = jnp.pad(pack, ((0, 0), (0, 128 - 16))).astype(BF16)
-    ew = jnp.stack([w_in, jnp.transpose(w_expert_out, (0, 2, 1))], axis=1).astype(BF16)
-    x = jnp.stack(image_blocks(tokens, move.tensor, imgs))
-    dy = jnp.stack(image_blocks(cotangent, move.tensor, imgs))
-    keep = jnp.stack(image_lanes(kept_pairs(routes), move.tensor, imgs))
-    noise = jnp.stack(image_lanes(jnp.transpose(router_noise), move.tensor, imgs))
+    w_out = jnp.transpose(w_expert_out, (0, 2, 1))
     if move.groups == 1:
-        _, _, _, g_low, sums, w, *saved = front(pack, ew, dy, x, noise, keep)
+        pack, ew, x, dy, keep, noise = prepare(
+            move.tensor, imgs, tokens, cotangent, jnp.transpose(w_qkv, (1, 0, 2)), w_attn_out,
+            jnp.stack([ln1_gain, ln1_bias, ln2_gain, ln2_bias]), jnp.transpose(router_weight),
+            w_in, w_out, jnp.transpose(router_noise), jnp.transpose(routes),
+        )
+        _, _, _, y, g_low, dh, w, *saved = front(pack, ew, dy, x, noise, keep)
         x1, qkv, o, lse, probs = saved
-        g_exp, output, d_tokens, total = back(g_low, sums, (x1, x, dy, probs, qkv, o, lse), w)
-        g_in, g_out = g_exp[:, 0].astype(F32), g_exp[:, 1].astype(F32)
-        output, d_tokens = (rows[:, :, :SEQ].reshape(token_count, D) for rows in (output, d_tokens))
+        output, d_tokens, g_in, g_out, g_qkv, g_attn_out, g_small = finish(
+            *back(g_low, y, dh, (x1, x, dy, probs, qkv, o, lse), w)
+        )
+        g_qkv = jnp.transpose(g_qkv, (1, 0, 2))
     else:
+        vectors = jnp.stack([ln1_gain, ln1_bias, ln2_gain, ln2_bias] + [jnp.zeros_like(ln1_gain)] * 4, axis=1)
+        pack = jnp.concatenate(
+            [w_qkv[:, 0], w_qkv[:, 1], w_qkv[:, 2], jnp.transpose(w_attn_out), vectors, router_weight], axis=1
+        )
+        pack = jnp.pad(pack, ((0, 0), (0, 128 - 16))).astype(BF16)
+        ew = jnp.stack([w_in, jnp.transpose(w_expert_out, (0, 2, 1))], axis=1).astype(BF16)
+        x = jnp.stack(image_blocks(tokens, move.tensor, imgs))
+        dy = jnp.stack(image_blocks(cotangent, move.tensor, imgs))
+        keep = jnp.stack(image_lanes(kept_pairs(routes), move.tensor, imgs))
+        noise = jnp.stack(image_lanes(jnp.transpose(router_noise), move.tensor, imgs))
         g_low, sums, w, *saved = move.front(pack, ew, dy, x, noise, keep)
         output, d_tokens, g_in, g_out, total = move.back(g_low, sums, saved, x, dy, w)
-    g_qkv = total[:d_own, : 9 * HD].reshape(d_own, 3, 3 * HD)
-    g_attn_out = jnp.transpose(total[:d_own, 9 * HD :])
-    g_small = total[d_own:, :d_own]
-
+        g_qkv = total[:d_own, : 9 * HD].reshape(d_own, 3, 3 * HD)
+        g_attn_out = jnp.transpose(total[:d_own, 9 * HD :])
+        g_small = total[d_own:, :d_own]
     return (
         output,
         d_tokens,

time: 494 us -> 440 us (0.89)
  the two profiles are of different devices: /device:TPU:24 before, /device:TPU:8 now
where the time goes in v6:
time: 440 us; the launch traced here: 432 us
  Pallas kernels  427 us (97%)
    pallas_call x1, Pallas kernels, front(): pl.pallas_call(functools.partial(front_kernel, imgs), out_shape=(table, t...  265 us
    pallas_call x1, Pallas kernels, back(): pl.pallas_call(functools.partial(back_kernel, imgs), out_shape=(jax.Shape...  146 us

profile of v6, /device:TPU:8, one launch (start us, length us, event | category | flops | bytes accessed | tf_op | source)
XLA Modules:
  0.0 431.9 jit_solution(6238042084766825991)
XLA Ops:
  0.6 1.3 pad_maximum_fusion.vec_ref
  1.9 7.6 %prepare.1 = (bf16[96,896]{1,0:T(8,128)(2,1)}, bf16[8,2,96,768]{3,2,1,0:T(8,128)(2,1)}, bf16[2,208,768]{2,1,0:T(8,128)(2,1)}, bf16[2,208,768]{2,1,0:T(8,128)(2,1...) custom-call(s32[1]{0:T(128)} %bitcast.tensor_ref, bf16[1576,768]{1,0:T(8,128)(2,1)} %tok_ref.1, bf16[1576,768]{1,0:T(8,128)(2,1)} %cot_ref.1, ...), custom_call_target="tpu_custom_call" | custom-call | flops 100000000 | bytes 15000000 | tf_op jit(solution)/shard_map/prepare/pallas_call | solution.py:1206
  9.5 265.1 %front.1 = (bf16[16,208,768]{2,1,0:T(8,128)(2,1)}, bf16[16,208,768]{2,1,0:T(8,128)(2,1)}, bf16[7,2,208,768]{3,2,1,0:T(8,128)(2,1)}, bf16[8,2,208,768]{3,2,1,0:T(...) custom-call(bf16[96,896]{1,0:T(8,128)(2,1)} %get-tuple-element.37.pa, ...), custom_call_target="tpu_custom_call" | custom-call | flops 99999997952 | bytes 100000000 | tf_op jit(solution)/shard_map/front/pallas_call | solution.py:511
  274.6 146.4 %back.1 = (bf16[4,2,208,768]{3,2,1,0:T(8,128)(2,1)}, bf16[4,2,208,768]{3,2,1,0:T(8,128)(2,1)}, bf16[8,2,96,768]{3,2,1,0:T(8,128)(2,1)}, f32[112,768]{1,0:T(8,128)}) custom-call(bf16[4,8,2,96,768]{4,3,2,1,0:T(8,128)(2,1)} %get-tuple-element.43.g_low, bf16[8,2,208,768]{3,2,1,0:T(8,128)(2,1)} %get-tuple-element.44.y_ref, ...), custom_call_target="tpu_custom_call" | custom-call | flops 12000000000 | bytes 100000000 | tf_op jit(solution)/shard_map/back/pallas_call | solution.py:1120
  421.0 8.0 %finish.1 = (bf16[1576,768]{1,0:T(8,128)(2,1)}, bf16[1576,768]{1,0:T(8,128)(2,1)}, f32[8,96,768]{2,1,0:T(8,128)}, f32[8,96,768]{2,1,0:T(8,128)}, f32[3,96,192]{2...) custom-call(bf16[4,2,208,768]{3,2,1,0:T(8,128)(2,1)} %get-tuple-element.52.out_in, ...), custom_call_target="tpu_custom_call" | custom-call | flops 1000000 | bytes 18000000 | tf_op jit(solution)/shard_map/finish/pallas_call | solution.py:1253
  429.1 1.4 slice_bitcast_fusion.1
  430.4 1.3 slice_bitcast_fusion

commit v7 on v6

--- a/solution.py
+++ b/solution.py
@@ -189,7 +189,8 @@
     weight = jnp.maximum(gate, 0.0)
     d_rows = (dy.astype(F32) * weight).astype(BF16)
 
-    def hidden(r, carry):
+    def hidden(i, carry):
+        r = 2 * lax.rem(i, 2) + lax.div(i, 2)
         w1 = w_ref[r, :, 0].reshape(D, FFS)
         w2 = w_ref[r, :, 1].reshape(D, FFS)
         a = dot(x, w1)
@@ -203,7 +204,7 @@
         dx_ref[...] += dot_nt(da, w1)
         g_ref[r, 0] += dot_tn(x, da)
         g_ref[r, 1] += dot_tn(d_rows, hid)
-        meanwhile(r)
+        meanwhile(i)
         return carry
 
     y_ref[...] = jnp.zeros_like(y_ref)
@@ -214,16 +215,17 @@
     return (y * weight).astype(BF16), dx_ref[...], dgate
 
 
-GIVEN, PASSED, DY_AT = (1, 3, 4, 6, 7), (1, 3), 2
-NEXT_AT, SUMS_AT = 0, 3
+GIVEN, PASSED, DY_AT = (1, 2, 4, 6, 7), (1, 3), 3
+HOP0, PASSED_EX = 5, 4
+NEXT_AT, SUMS_AT, Y_AT = 0, 3, 6
 HOPS_AT = ()
 
 
 def front_kernel(
     imgs, pack_ref, ew_ref, dy_ref, x_ref, noise_ref, keep_ref,
-    h_out, dy_out, t_in, y_out, g_out, sum_out, w_out, x1_ref, qkv_ref, o_ref, lse_ref, probs_ref,
+    h_out, dy_out, t_in, y_out, y_first, g_out, sum_out, w_out, x1_ref, qkv_ref, o_ref, lse_ref, probs_ref,
     w_s, chunk_s, we_s, g_s, xs, dys, y_s, dx_s, t_s, own_s, y_low, pass_s, g_low,
-    p_s, p_r, px_s, px_r, pc_s, pc_r, d_s, d_r, h_s, h_r, e_s, e_r, ex_s, ex_r, ec_s, ec_r, t_ss, t_r, local, stage, y_sem, g_sem,
+    p_s, p_r, px_s, px_r, pc_s, pc_r, d_s, d_r, h_s, h_r, e_s, e_r, ex_s, ex_r, ec_s, ec_r, t_ss, t_r, local, stage, y_sem, g_sem, yf_s, yf_r,
 ):
     peers = Peers()
     member = peers.member
@@ -269,10 +271,23 @@
         ex[by] = peers.send(src, we_s.at[1, of], (ex_s, ex_r), by, peers.across)
         ec[0, by] = peers.send(src, we_s.at[2, of], (ec_s, ec_r), (0, by), peers.core)
 
+    def slice_copy(to, of, sent, got, at, device):
+        return pltpu.make_async_remote_copy(
+            src_ref=we_s.at[0 if to == 1 else 1, of],
+            dst_ref=we_s.at[to, of],
+            send_sem=sent.at[at],
+            recv_sem=got.at[at],
+            device_id=device,
+            device_id_type=pl.DeviceIdType.MESH,
+        )
+
+    def ex_core(by):
+        return slice_copy(3, peers.came(by), ec_s, ec_r, (1, by), peers.core)
+
     def pass_ex(by):
-        ex[by].wait_recv()
         of = peers.came(by)
-        ec[1, by] = peers.send(we_s.at[1, of], we_s.at[3, of], (ec_s, ec_r), (1, by), peers.core)
+        slice_copy(1, of, ex_s, ex_r, by, peers.across).wait_recv()
+        ex_core(by).start()
 
     def block_at(c, k):
         return peers.behind(c % 2, k) * imgs + c
@@ -345,7 +360,8 @@
             x_ref[c], par, lambda r: w_s[r], noise_ref[c], keep_ref[c],
             chunk_s.at[c], *(ref.at[c] for ref in (x1_ref, qkv_ref, o_ref, lse_ref, probs_ref)),
         )
-        row_copy(h_out, h_sems, c, 0, chunk_s.at[c]).start()
+        if HOP0 == 0:
+            row_copy(h_out, h_sems, c, 0, chunk_s.at[c]).start()
         keepers.append(
             pltpu.make_async_copy(chunk_s.at[c], h_out.at[member * imgs + c], local.at[3 + imgs + c])
         )
@@ -353,17 +369,25 @@
         give_e(far[GIVEN[2 + c]:GIVEN[3 + c]])
     if DY_AT == 2:
         give_dy()
+
+    def first_hops():
+        for c in range(imgs):
+            row_copy(h_out, h_sems, c, 0, chunk_s.at[c]).start()
+        if DY_AT == 3:
+            give_dy()
+
     for i, by in enumerate(far):
         if i >= done:
             pass_e(by)
-            pass_ex((0, *far)[i])
+            if i <= PASSED_EX:
+                pass_ex((0, *far)[i])
+        if HOP0 and i == HOP0:
+            first_hops()
         if i in HOPS_AT:
             row_hop(1 + HOPS_AT.index(i))
     g_s[...] = jnp.zeros_like(g_s)
-    pass_ex(far[-1])
     for by in range(E):
         ec[0, by].wait_recv()
-        ec[1, by].wait_recv()
     for copy in keepers:
         copy.wait()
 
@@ -399,6 +423,16 @@
         for copy in copies:
             copy.wait()
 
+    def y_copy(c):
+        return pltpu.make_async_remote_copy(
+            src_ref=y_out.at[1, c],
+            dst_ref=y_first.at[c],
+            send_sem=yf_s.at[c],
+            recv_sem=yf_r.at[c],
+            device_id=peers.next[c % 2],
+            device_id_type=pl.DeviceIdType.MESH,
+        )
+
     def keep_y(k):
         return pltpu.make_async_copy(y_low, y_out.at[k], y_sem)
 
@@ -407,6 +441,16 @@
         finish(rows_to_hand(k))
 
         def meanwhile(r):
+            @pl.when((r == 0) & (k == 0))
+            def _():
+                for by in far[PASSED_EX:]:
+                    pass_ex(by)
+
+            @pl.when((r == 1) & (k == 0))
+            def _():
+                for by in range(E):
+                    ex_core(by).wait_recv()
+
             for c in range(imgs):
                 for out, sems in ((h_out, h_sems), (dy_out, d_sems)):
 
@@ -470,6 +514,11 @@
         def _():
             for c in range(imgs):
                 sum_copy(c, k).start()
+
+        @pl.when(k == Y_AT)
+        def _():
+            for c in range(imgs):
+                y_copy(c).start()
 
         return carry
 
@@ -488,6 +537,8 @@
     finish(sums_to_hand(E))
     sum_out[...] = (own_s[...].astype(F32) + t_s[...].astype(F32)).astype(BF16)
     keep_y(E - 1).wait()
+    for c in range(imgs):
+        y_copy(c).wait()
     for i in range(2):
         pltpu.make_async_copy(g_low.at[i], g_out.at[3, :, i], g_sem.at[i]).wait()
     for c in range(imgs):
@@ -496,6 +547,8 @@
         for k in range(E - 1):
             row_copy(h_out, h_sems, c, k).wait_send()
             row_copy(dy_out, d_sems, c, k).wait_send()
+    for by in range(E):
+        ex_core(by).wait_send()
     for copy in peers.sends:
         copy.wait_send()
 
@@ -515,13 +568,14 @@
             table,
             jax.ShapeDtypeStruct((E - 1,) + rows, BF16),
             jax.ShapeDtypeStruct((E,) + rows, BF16),
+            jax.ShapeDtypeStruct(rows, BF16),
             jax.ShapeDtypeStruct((4, E, 2, d_own, FFS), BF16),
             jax.ShapeDtypeStruct(rows, BF16),
             jax.ShapeDtypeStruct((4, E * d_own, D + 128), BF16),
         )
         + attn_shapes(imgs),
         in_specs=[vm, hbm, hbm, vm, vm, vm],
-        out_specs=(hbm,) * 5 + (vm, hbm) + (vm,) * 5,
+        out_specs=(hbm,) * 6 + (vm, hbm) + (vm,) * 5,
         scratch_shapes=[
             pltpu.VMEM((4, E * d_own, D + 128), BF16),
             pltpu.VMEM((imgs, PAD, D), BF16),
@@ -540,7 +594,7 @@
             dma((imgs, E - 1)), dma((imgs, E - 1)), dma((imgs, E - 1)), dma((imgs, E - 1)),
             dma((E,)), dma((E,)), dma((E,)), dma((E,)), dma((2, E)), dma((2, E)),
             dma((imgs, E - 1)), dma((imgs, E - 1)),
-            dma((3 + 2 * imgs,)), dma((3, imgs)), dma(()), dma((2,)),
+            dma((3 + 2 * imgs,)), dma((3, imgs)), dma(()), dma((2,)), dma((imgs,)), dma((imgs,)),
         ],
         compiler_params=pltpu.CompilerParams(
             vmem_limit_bytes=VMEM_LIMIT, collective_id=0, has_side_effects=True
@@ -951,8 +1005,11 @@
     )(*dh, *saved, w)
 
 
+HOMES = ((0,), (1, 2), (3,), (4,), (5, 6), (7,), ())
+
+
 def back_kernel(
-    imgs, g_low, y_ref, dh_ref, x1_ref, x_ref, dy_ref, probs_ref, qkv_ref, o_ref, lse_ref, w_ref,
+    imgs, g_low, y_ref, yf_ref, dh_ref, x1_ref, x_ref, dy_ref, probs_ref, qkv_ref, o_ref, lse_ref, w_ref,
     out_all, dtok_all, g_out, total_ref,
     ga_s, gc_s, gx_s, pk_s, pkc_s, pkr_s, sm_s, smr_s, cs_s, cr_s, fs_s, fr_s, or_s, dt_s, y_s, yr_s,
     dx1_s, low_s, h1_s, dh1_s, dqkv_s, o_s,
@@ -985,16 +1042,15 @@
         return onwards
 
     y_load = here(y_ref, y_s)
+    yf_load = here(yf_ref, yr_s.at[0])
     y_sent = {}
 
     def y_hop(k):
         for c in range(imgs):
-            if k == 1:
-                src = y_s.at[1, c]
-            else:
+            if k > 2:
                 y_sent[c, k - 1].wait_recv()
-                src = yr_s.at[k - 2, c]
-                src[...] = (src[...].astype(F32) + y_s[k, c].astype(F32)).astype(BF16)
+            src = yr_s.at[k - 2, c]
+            src[...] = (src[...].astype(F32) + y_s[k, c].astype(F32)).astype(BF16)
             y_sent[c, k] = peers.send(src, yr_s.at[k - 1, c], (y_ss, y_r), (c, k - 1), peers.next[c % 2])
 
     def y_last():
@@ -1008,7 +1064,8 @@
     ][::-1]
     g_load = [here(g_low.at[s], ga_s.at[s]) for s in (1, 0)][::-1]
     y_load.wait()
-    y_hop(1)
+    yf_load.wait()
+    y_hop(2)
     order = (4, 3, 5, 2, 6, 1, 7, 0)
     gx = {}
 
@@ -1035,6 +1092,10 @@
         else:
             here(ga_s.at[0, to], g_out.at[member])
 
+    def homes(at):
+        for number in HOMES[at]:
+            pass_home(order[number])
+
     saved = (x1_ref, x_ref, dy_ref, probs_ref, qkv_ref, o_ref, lse_ref)
     back = Backward(imgs, lambda c: dh_ref[c], saved, w_ref, dx1_s, low_s, h1_s, dh1_s, dqkv_s, o_s)
     back.first()
@@ -1042,7 +1103,7 @@
         grad = back.heads(r)
         for i in range(E):
             pkc_s[i, r - 2] = grad[i * d_own : (i + 1) * d_own]
-        y_hop(r)
+        y_hop(r + 1)
         if r == 2:
             pass_across()
     pk_core = peers.send(pkc_s, pkr_s, (pk_ss, pk_r), 0, peers.core)
@@ -1050,8 +1111,8 @@
         grad = back.heads(r)
         for i in range(E):
             pk_s[i, r, :d_own] = grad[i * d_own : (i + 1) * d_own]
-        y_hop(4 + r)
-        pass_home(order[r])
+        y_hop(5 + r)
+        homes(r)
     small = back.last(dt_s)
     dtok_rows = give_rows(1, dt_s, dtok_all)
     for i in range(E):
@@ -1080,19 +1141,18 @@
         hop(0, i)
         if i < steps[1]:
             hop(1, i)
-        if i < 2:
-            y_hop(6 + i)
-        if i == 2:
+        if i == 0:
+            y_hop(7)
+        if i == 1:
             y_last()
             out_rows = give_rows(0, or_s, out_all)
-        pass_home(order[2 + i])
+        homes(2 + i)
     hops[1, steps[1] - 1].wait_recv()
     hops[0, steps[0] - 1].wait_recv()
     total = term(member) + cr_s[0, steps[0] - 1].astype(F32) + cr_s[1, steps[1] - 1].astype(F32)
     fs_s[...] = total[1].astype(BF16)
     final = peers.send(fs_s, fr_s, (f_ss, f_r), 0, peers.across)
-    pass_home(order[6])
-    pass_home(order[7])
+    homes(6)
     dtok_rows = dtok_rows()
     out_rows = out_rows()
     final.wait_recv()
@@ -1102,13 +1162,13 @@
     for copy in (*out_rows, *dtok_rows):
         copy.wait_recv()
     for copy in loads:
-        if all(copy is not other for other in (y_load, *g_load)):
+        if all(copy is not other for other in (y_load, yf_load, *g_load)):
             copy.wait()
     for copy in peers.sends:
         copy.wait_send()
 
 
-def back(g_low, y, dh, saved, w):
+def back(g_low, y, y_first, dh, saved, w):
     imgs = dh.shape[0]
     d_own = g_low.shape[3]
     vm = pl.BlockSpec(memory_space=pltpu.VMEM)
@@ -1125,7 +1185,7 @@
             jax.ShapeDtypeStruct(part, BF16),
             jax.ShapeDtypeStruct((d_own + 16, D), F32),
         ),
-        in_specs=[hbm, hbm] + [vm] * 9,
+        in_specs=[hbm, hbm, hbm] + [vm] * 9,
         out_specs=(hbm, hbm, hbm, vm),
         scratch_shapes=[
             pltpu.VMEM((2,) + part, BF16),
@@ -1147,14 +1207,14 @@
             *backward_scratch(imgs),
             dma((2,)), dma((2,)), dma((E,)), dma((E,)), dma((E,)), dma((E,)), dma((1,)), dma((1,)),
             dma((1,)), dma((1,)), dma((2, E // 2)), dma((2, E // 2)), dma((1,)), dma((1,)), dma((2, 3)), dma((2, 3)),
-            dma((imgs, E - 1)), dma((imgs, E - 1)), dma((6,)),
+            dma((imgs, E - 1)), dma((imgs, E - 1)), dma((7,)),
         ],
         compiler_params=pltpu.CompilerParams(
             vmem_limit_bytes=VMEM_LIMIT, collective_id=1, has_side_effects=True
         ),
         cost_estimate=pl.CostEstimate(flops=12 * 10**9, bytes_accessed=10**8, transcendentals=2 * 10**6),
         name="back",
-    )(g_low, y, dh, *saved, w)
+    )(g_low, y, y_first, dh, *saved, w)
 
 
 def eye_of(n, lanes):
@@ -1162,13 +1222,14 @@
 
 
 def prepare_kernel(
-    imgs, tensor_ref, tok_ref, cot_ref, qkv_ref, wo_ref, vec_ref, router_ref, win_ref, wout_ref, noise_ref, routes_ref,
+    imgs, tensor_ref, tok_ref, cot_ref, qkv_ref, wo_ref, v0_ref, v1_ref, v2_ref, v3_ref, router_ref, win_ref, wout_ref, noise_ref, routes_ref,
     pack_ref, ew_ref, x_ref, dy_ref, keep_out, noise_out, keep_s,
 ):
     tensor = tensor_ref[0]
     d_own = wo_ref.shape[1]
     wo = dot_tn(wo_ref[...].astype(BF16), eye_of(3 * HD, 3 * HD)).astype(BF16)
-    lines = jnp.concatenate([vec_ref[...], jnp.zeros((4, d_own), F32), router_ref[...]], axis=0).astype(BF16)
+    vectors = [ref[...] for ref in (v0_ref, v1_ref, v2_ref, v3_ref)]
+    lines = jnp.concatenate(vectors + [jnp.zeros((4, d_own), F32), router_ref[...]], axis=0).astype(BF16)
     lines = dot_tn(lines, eye_of(16, 128)).astype(BF16)
     pack_ref[...] = jnp.concatenate([qkv_ref[i].astype(BF16) for i in range(3)] + [wo, lines], axis=1)
     for e in range(E):
@@ -1213,16 +1274,16 @@
             lanes,
             lanes,
         ),
-        in_specs=[pl.BlockSpec(memory_space=pltpu.SMEM)] + [vm] * 10,
+        in_specs=[pl.BlockSpec(memory_space=pltpu.SMEM)] + [vm] * 13,
         out_specs=(vm,) * 6,
         scratch_shapes=[pltpu.VMEM((E, tokens.shape[0]), F32)],
         compiler_params=pltpu.CompilerParams(vmem_limit_bytes=VMEM_LIMIT),
         cost_estimate=pl.CostEstimate(flops=10**8, bytes_accessed=15 * 10**6, transcendentals=0),
         name="prepare",
-    )(tensor.reshape(1), tokens, cotangent, w_qkv, w_attn_out, vectors, router, w_in, w_out, noise, routes)
-
-
-def finish_kernel(imgs, out_in, dtok_in, g_in, total_ref, out_ref, dtok_ref, gi_ref, go_ref, qkv_ref, wo_ref, small_ref, rows_s, g_s, sem):
+    )(tensor.reshape(1), tokens, cotangent, w_qkv, w_attn_out, *vectors, router, w_in, w_out, noise, routes)
+
+
+def finish_kernel(imgs, out_in, dtok_in, g_in, total_ref, out_ref, dtok_ref, gi_ref, go_ref, qkv_ref, wo_ref, s0_ref, s1_ref, s2_ref, s3_ref, router_ref, rows_s, g_s, sem):
     loads = [pltpu.make_async_copy(src, rows_s.at[i], sem.at[i]) for i, src in enumerate((out_in, dtok_in))]
     loads.append(pltpu.make_async_copy(g_in, g_s, sem.at[2]))
     for copy in loads:
@@ -1232,7 +1293,9 @@
     for i in range(3):
         qkv_ref[i] = total[:d_own, i * 3 * HD : (i + 1) * 3 * HD]
     wo_ref[...] = jnp.transpose(total[:d_own, 9 * HD :])
-    small_ref[...] = total[d_own:, :d_own]
+    for i, ref in enumerate((s0_ref, s1_ref, s2_ref, s3_ref)):
+        ref[...] = total[d_own + i : d_own + i + 1, :d_own]
+    router_ref[...] = total[d_own + 8 :, :d_own]
     for which, dst in ((0, out_ref), (1, dtok_ref)):
         loads[which].wait()
         for i in range(4 * imgs):
@@ -1259,10 +1322,11 @@
             grad,
             jax.ShapeDtypeStruct((3, d_own, 3 * HD), F32),
             jax.ShapeDtypeStruct((3 * HD, d_own), F32),
-            jax.ShapeDtypeStruct((16, d_own), F32),
+            *[jax.ShapeDtypeStruct((1, d_own), F32)] * 4,
+            jax.ShapeDtypeStruct((E, d_own), F32),
         ),
         in_specs=[hbm, hbm, hbm, vm],
-        out_specs=(vm,) * 7,
+        out_specs=(vm,) * 11,
         scratch_shapes=[
             pltpu.VMEM((2, 4, imgs, PAD, D), BF16),
             pltpu.VMEM(g_exp.shape, BF16),
@@ -1483,14 +1547,15 @@
     if move.groups == 1:
         pack, ew, x, dy, keep, noise = prepare(
             move.tensor, imgs, tokens, cotangent, jnp.transpose(w_qkv, (1, 0, 2)), w_attn_out,
-            jnp.stack([ln1_gain, ln1_bias, ln2_gain, ln2_bias]), jnp.transpose(router_weight),
+            [v.reshape(1, d_own) for v in (ln1_gain, ln1_bias, ln2_gain, ln2_bias)], jnp.transpose(router_weight),
             w_in, w_out, jnp.transpose(router_noise), jnp.transpose(routes),
         )
-        _, _, _, y, g_low, dh, w, *saved = front(pack, ew, dy, x, noise, keep)
+        _, _, _, y, y_first, g_low, dh, w, *saved = front(pack, ew, dy, x, noise, keep)
         x1, qkv, o, lse, probs = saved
-        output, d_tokens, g_in, g_out, g_qkv, g_attn_out, g_small = finish(
-            *back(g_low, y, dh, (x1, x, dy, probs, qkv, o, lse), w)
+        output, d_tokens, g_in, g_out, g_qkv, g_attn_out, *g_vectors, g_router = finish(
+            *back(g_low, y, y_first, dh, (x1, x, dy, probs, qkv, o, lse), w)
         )
+        g_vectors = [v.reshape(d_own) for v in g_vectors]
         g_qkv = jnp.transpose(g_qkv, (1, 0, 2))
     else:
         vectors = jnp.stack([ln1_gain, ln1_bias, ln2_gain, ln2_bias] + [jnp.zeros_like(ln1_gain)] * 4, axis=1)
@@ -1507,17 +1572,18 @@
         output, d_tokens, g_in, g_out, total = move.back(g_low, sums, saved, x, dy, w)
         g_qkv = total[:d_own, : 9 * HD].reshape(d_own, 3, 3 * HD)
         g_attn_out = jnp.transpose(total[:d_own, 9 * HD :])
-        g_small = total[d_own:, :d_own]
+        g_vectors = [total[d_own + i, :d_own] for i in range(4)]
+        g_router = total[d_own + 8 :, :d_own]
     return (
         output,
         d_tokens,
-        g_small[0],
-        g_small[1],
+        g_vectors[0],
+        g_vectors[1],
         g_qkv,
         g_attn_out,
-        g_small[2],
-        g_small[3],
-        jnp.transpose(g_small[8:16]),
+        g_vectors[2],
+        g_vectors[3],
+        jnp.transpose(g_router),
         g_in,
         jnp.transpose(g_out, (0, 2, 1)),
     )

time: 440 us -> 413 us (0.939)
  the two profiles are of different devices: /device:TPU:8 before, /device:TPU:24 now
where the time goes in v7:
time: 413 us; the launch traced here: 408 us
  Pallas kernels  408 us (99%)
    pallas_call x1, Pallas kernels, front(): pl.pallas_call(functools.partial(front_kernel, imgs), out_shape=(table, t...  251 us
    pallas_call x1, Pallas kernels, back(): pl.pallas_call(functools.partial(back_kernel, imgs), out_shape=(jax.Shape...  141 us

profile of v7, /device:TPU:24, one launch (start us, length us, event | category | flops | bytes accessed | tf_op | source)
XLA Modules:
  0.0 408.4 jit_solution(5990636016485075518)
XLA Ops:
  0.7 7.7 %prepare.1 = (bf16[96,896]{1,0:T(8,128)(2,1)}, bf16[8,2,96,768]{3,2,1,0:T(8,128)(2,1)}, bf16[2,208,768]{2,1,0:T(8,128)(2,1)}, bf16[2,208,768]{2,1,0:T(8,128)(2,1...) custom-call(s32[1]{0:T(128)} %bitcast.tensor_ref, bf16[1576,768]{1,0:T(8,128)(2,1)} %tok_ref.1, bf16[1576,768]{1,0:T(8,128)(2,1)} %cot_ref.1, ...), custom_call_target="tpu_custom_call" | custom-call | flops 100000000 | bytes 15000000 | tf_op jit(solution)/shard_map/prepare/pallas_call | solution.py:1267
  8.3 250.7 %front.1 = (bf16[16,208,768]{2,1,0:T(8,128)(2,1)}, bf16[16,208,768]{2,1,0:T(8,128)(2,1)}, bf16[7,2,208,768]{3,2,1,0:T(8,128)(2,1)}, bf16[8,2,208,768]{3,2,1,0:T(...) custom-call(bf16[96,896]{1,0:T(8,128)(2,1)} %get-tuple-element.42.pa, ...), custom_call_target="tpu_custom_call" | custom-call | flops 99999997952 | bytes 100000000 | tf_op jit(solution)/shard_map/front/pallas_call | solution.py:564
  259.1 141.0 %back.1 = (bf16[4,2,208,768]{3,2,1,0:T(8,128)(2,1)}, bf16[4,2,208,768]{3,2,1,0:T(8,128)(2,1)}, bf16[8,2,96,768]{3,2,1,0:T(8,128)(2,1)}, f32[112,768]{1,0:T(8,128)}) custom-call(bf16[4,8,2,96,768]{4,3,2,1,0:T(8,128)(2,1)} %get-tuple-element.48.g_low, bf16[8,2,208,768]{3,2,1,0:T(8,128)(2,1)} %get-tuple-element.49.y_ref, ...), custom_call_target="tpu_custom_call" | custom-call | flops 12000000000 | bytes 100000000 | tf_op jit(solution)/shard_map/back/pallas_call | solution.py:1180
  400.1 8.1 %finish.1 = (bf16[1576,768]{1,0:T(8,128)(2,1)}, bf16[1576,768]{1,0:T(8,128)(2,1)}, f32[8,96,768]{2,1,0:T(8,128)}, f32[8,96,768]{2,1,0:T(8,128)}, f32[3,96,192]{2...) custom-call(bf16[4,2,208,768]{3,2,1,0:T(8,128)(2,1)} %get-tuple-elem, ...), custom_call_target="tpu_custom_call" | custom-call | flops 1000000 | bytes 18000000 | tf_op jit(solution)/shard_map/finish/pallas_call | solution.py:1316

commit v8 on v7

--- a/solution.py
+++ b/solution.py
@@ -217,13 +217,13 @@
 
 GIVEN, PASSED, DY_AT = (1, 2, 4, 6, 7), (1, 3), 3
 HOP0, PASSED_EX = 5, 4
-NEXT_AT, SUMS_AT, Y_AT = 0, 3, 6
+NEXT_AT, SUMS_AT, Y_AT = 0, 2, 5
 HOPS_AT = ()
 
 
 def front_kernel(
     imgs, pack_ref, ew_ref, dy_ref, x_ref, noise_ref, keep_ref,
-    h_out, dy_out, t_in, y_out, y_first, g_out, sum_out, w_out, x1_ref, qkv_ref, o_ref, lse_ref, probs_ref,
+    h_out, dy_out, t_in, y_out, y_first, y_second, g_out, sum_out, w_out, x1_ref, qkv_ref, o_ref, lse_ref, probs_ref,
     w_s, chunk_s, we_s, g_s, xs, dys, y_s, dx_s, t_s, own_s, y_low, pass_s, g_low,
     p_s, p_r, px_s, px_r, pc_s, pc_r, d_s, d_r, h_s, h_r, e_s, e_r, ex_s, ex_r, ec_s, ec_r, t_ss, t_r, local, stage, y_sem, g_sem, yf_s, yf_r,
 ):
@@ -423,12 +423,12 @@
         for copy in copies:
             copy.wait()
 
-    def y_copy(c):
+    def y_copy(c, hop):
         return pltpu.make_async_remote_copy(
-            src_ref=y_out.at[1, c],
-            dst_ref=y_first.at[c],
-            send_sem=yf_s.at[c],
-            recv_sem=yf_r.at[c],
+            src_ref=y_out.at[1, c] if hop == 0 else xs.at[0, c],
+            dst_ref=y_first.at[c] if hop == 0 else y_second.at[c],
+            send_sem=yf_s.at[hop, c],
+            recv_sem=yf_r.at[hop, c],
             device_id=peers.next[c % 2],
             device_id_type=pl.DeviceIdType.MESH,
         )
@@ -518,14 +518,23 @@
         @pl.when(k == Y_AT)
         def _():
             for c in range(imgs):
-                y_copy(c).start()
+                y_copy(c, 0).start()
 
         return carry
 
     start(rows_to_hand(0))
     lax.fori_loop(0, E, step, 0)
 
+    for c in range(imgs):
+        y_copy(c, 0).wait()
+    y_loads = [pltpu.make_async_copy(y_first, xs.at[0], stage.at[0, 0]), pltpu.make_async_copy(y_out.at[2], dys.at[0], stage.at[1, 0])]
+    start(y_loads)
     for i in range(8):
+        if i == 2:
+            finish(y_loads)
+            xs[0] = (xs[0].astype(F32) + dys[0].astype(F32)).astype(BF16)
+            for c in range(imgs):
+                y_copy(c, 1).start()
         r, kind = i // 2, i % 2
         if i >= 2:
             pltpu.make_async_copy(g_low.at[i % 2], g_out.at[r, :, kind], g_sem.at[i % 2]).wait()
@@ -538,7 +547,7 @@
     sum_out[...] = (own_s[...].astype(F32) + t_s[...].astype(F32)).astype(BF16)
     keep_y(E - 1).wait()
     for c in range(imgs):
-        y_copy(c).wait()
+        y_copy(c, 1).wait()
     for i in range(2):
         pltpu.make_async_copy(g_low.at[i], g_out.at[3, :, i], g_sem.at[i]).wait()
     for c in range(imgs):
@@ -569,13 +578,14 @@
             jax.ShapeDtypeStruct((E - 1,) + rows, BF16),
             jax.ShapeDtypeStruct((E,) + rows, BF16),
             jax.ShapeDtypeStruct(rows, BF16),
+            jax.ShapeDtypeStruct(rows, BF16),
             jax.ShapeDtypeStruct((4, E, 2, d_own, FFS), BF16),
             jax.ShapeDtypeStruct(rows, BF16),
             jax.ShapeDtypeStruct((4, E * d_own, D + 128), BF16),
         )
         + attn_shapes(imgs),
         in_specs=[vm, hbm, hbm, vm, vm, vm],
-        out_specs=(hbm,) * 6 + (vm, hbm) + (vm,) * 5,
+        out_specs=(hbm,) * 7 + (vm, hbm) + (vm,) * 5,
         scratch_shapes=[
             pltpu.VMEM((4, E * d_own, D + 128), BF16),
             pltpu.VMEM((imgs, PAD, D), BF16),
@@ -594,7 +604,7 @@
             dma((imgs, E - 1)), dma((imgs, E - 1)), dma((imgs, E - 1)), dma((imgs, E - 1)),
             dma((E,)), dma((E,)), dma((E,)), dma((E,)), dma((2, E)), dma((2, E)),
             dma((imgs, E - 1)), dma((imgs, E - 1)),
-            dma((3 + 2 * imgs,)), dma((3, imgs)), dma(()), dma((2,)), dma((imgs,)), dma((imgs,)),
+            dma((3 + 2 * imgs,)), dma((3, imgs)), dma(()), dma((2,)), dma((2, imgs)), dma((2, imgs)),
         ],
         compiler_params=pltpu.CompilerParams(
             vmem_limit_bytes=VMEM_LIMIT, collective_id=0, has_side_effects=True
@@ -1005,7 +1015,7 @@
     )(*dh, *saved, w)
 
 
-HOMES = ((0,), (1, 2), (3,), (4,), (5, 6), (7,), ())
+HOMES = ((), (0,), (1, 2), (3,), (4, 5), (6, 7), ())
 
 
 def back_kernel(
@@ -1042,12 +1052,12 @@
         return onwards
 
     y_load = here(y_ref, y_s)
-    yf_load = here(yf_ref, yr_s.at[0])
+    yf_load = here(yf_ref, yr_s.at[1])
     y_sent = {}
 
     def y_hop(k):
         for c in range(imgs):
-            if k > 2:
+            if k > 3:
                 y_sent[c, k - 1].wait_recv()
             src = yr_s.at[k - 2, c]
             src[...] = (src[...].astype(F32) + y_s[k, c].astype(F32)).astype(BF16)
@@ -1065,7 +1075,7 @@
     g_load = [here(g_low.at[s], ga_s.at[s]) for s in (1, 0)][::-1]
     y_load.wait()
     yf_load.wait()
-    y_hop(2)
+    y_hop(3)
     order = (4, 3, 5, 2, 6, 1, 7, 0)
     gx = {}
 
@@ -1103,7 +1113,7 @@
         grad = back.heads(r)
         for i in range(E):
             pkc_s[i, r - 2] = grad[i * d_own : (i + 1) * d_own]
-        y_hop(r + 1)
+        y_hop(r + 2)
         if r == 2:
             pass_across()
     pk_core = peers.send(pkc_s, pkr_s, (pk_ss, pk_r), 0, peers.core)
@@ -1111,7 +1121,7 @@
         grad = back.heads(r)
         for i in range(E):
             pk_s[i, r, :d_own] = grad[i * d_own : (i + 1) * d_own]
-        y_hop(5 + r)
+        y_hop(6 + r)
         homes(r)
     small = back.last(dt_s)
     dtok_rows = give_rows(1, dt_s, dtok_all)
@@ -1142,8 +1152,6 @@
         if i < steps[1]:
             hop(1, i)
         if i == 0:
-            y_hop(7)
-        if i == 1:
             y_last()
             out_rows = give_rows(0, or_s, out_all)
         homes(2 + i)
@@ -1168,7 +1176,7 @@
         copy.wait_send()
 
 
-def back(g_low, y, y_first, dh, saved, w):
+def back(g_low, y, y_begun, dh, saved, w):
     imgs = dh.shape[0]
     d_own = g_low.shape[3]
     vm = pl.BlockSpec(memory_space=pltpu.VMEM)
@@ -1214,7 +1222,7 @@
         ),
         cost_estimate=pl.CostEstimate(flops=12 * 10**9, bytes_accessed=10**8, transcendentals=2 * 10**6),
         name="back",
-    )(g_low, y, y_first, dh, *saved, w)
+    )(g_low, y, y_begun, dh, *saved, w)
 
 
 def eye_of(n, lanes):
@@ -1550,10 +1558,10 @@
             [v.reshape(1, d_own) for v in (ln1_gain, ln1_bias, ln2_gain, ln2_bias)], jnp.transpose(router_weight),
             w_in, w_out, jnp.transpose(router_noise), jnp.transpose(routes),
         )
-        _, _, _, y, y_first, g_low, dh, w, *saved = front(pack, ew, dy, x, noise, keep)
+        _, _, _, y, _, y_begun, g_low, dh, w, *saved = front(pack, ew, dy, x, noise, keep)
         x1, qkv, o, lse, probs = saved
         output, d_tokens, g_in, g_out, g_qkv, g_attn_out, *g_vectors, g_router = finish(
-            *back(g_low, y, y_first, dh, (x1, x, dy, probs, qkv, o, lse), w)
+            *back(g_low, y, y_begun, dh, (x1, x, dy, probs, qkv, o, lse), w)
         )
         g_vectors = [v.reshape(d_own) for v in g_vectors]
         g_qkv = jnp.transpose(g_qkv, (1, 0, 2))

time: 413 us -> 409 us (level)
    pallas_call x1, Pallas kernels: 141 us -> 134 us  [back(): pl.pallas_call(functools.partial(back_kernel, imgs), out_shape=(jax.Shape...]
    pallas_call x1, Pallas kernels: 251 us -> 255 us  [front(): pl.pallas_call(functools.partial(front_kernel, imgs), out_shape=(table, t...]
where the time goes in v8:
time: 409 us; the launch traced here: 406 us
  Pallas kernels  405 us (99%)
    pallas_call x1, Pallas kernels, front(): pl.pallas_call(functools.partial(front_kernel, imgs), out_shape=(table, t...  255 us
    pallas_call x1, Pallas kernels, back(): pl.pallas_call(functools.partial(back_kernel, imgs), out_shape=(jax.Shape...  134 us

profile of v8, /device:TPU:24, one launch (start us, length us, event | category | flops | bytes accessed | tf_op | source)
XLA Modules:
  0.0 406.0 jit_solution(7202317130807370815)
XLA Ops:
  0.7 7.7 %prepare.1 = (bf16[96,896]{1,0:T(8,128)(2,1)}, bf16[8,2,96,768]{3,2,1,0:T(8,128)(2,1)}, bf16[2,208,768]{2,1,0:T(8,128)(2,1)}, bf16[2,208,768]{2,1,0:T(8,128)(2,1...) custom-call(s32[1]{0:T(128)} %bitcast.tensor_ref, bf16[1576,768]{1,0:T(8,128)(2,1)} %tok_ref.1, bf16[1576,768]{1,0:T(8,128)(2,1)} %cot_ref.1, ...), custom_call_target="tpu_custom_call" | custom-call | flops 100000000 | bytes 15000000 | tf_op jit(solution)/shard_map/prepare/pallas_call | solution.py:1275
  8.3 255.2 %front.1 = (bf16[16,208,768]{2,1,0:T(8,128)(2,1)}, bf16[16,208,768]{2,1,0:T(8,128)(2,1)}, bf16[7,2,208,768]{3,2,1,0:T(8,128)(2,1)}, bf16[8,2,208,768]{3,2,1,0:T(...) custom-call(bf16[96,896]{1,0:T(8,128)(2,1)} %get-tuple-element.42.pa, ...), custom_call_target="tpu_custom_call" | custom-call | flops 99999997952 | bytes 100000000 | tf_op jit(solution)/shard_map/front/pallas_call | solution.py:573
  263.6 134.2 %back.1 = (bf16[4,2,208,768]{3,2,1,0:T(8,128)(2,1)}, bf16[4,2,208,768]{3,2,1,0:T(8,128)(2,1)}, bf16[8,2,96,768]{3,2,1,0:T(8,128)(2,1)}, f32[112,768]{1,0:T(8,128)}) custom-call(bf16[4,8,2,96,768]{4,3,2,1,0:T(8,128)(2,1)} %get-tuple-element.48.g_low, bf16[8,2,208,768]{3,2,1,0:T(8,128)(2,1)} %get-tuple-element.49.y_ref, ...), custom_call_target="tpu_custom_call" | custom-call | flops 12000000000 | bytes 100000000 | tf_op jit(solution)/shard_map/back/pallas_call | solution.py:1188
  397.8 8.1 %finish.1 = (bf16[1576,768]{1,0:T(8,128)(2,1)}, bf16[1576,768]{1,0:T(8,128)(2,1)}, f32[8,96,768]{2,1,0:T(8,128)}, f32[8,96,768]{2,1,0:T(8,128)}, f32[3,96,192]{2...) custom-call(bf16[4,2,208,768]{3,2,1,0:T(8,128)(2,1)} %get-tuple-elem, ...), custom_call_target="tpu_custom_call" | custom-call | flops 1000000 | bytes 18000000 | tf_op jit(solution)/shard_map/finish/pallas_call | solution.py:1324

commit v9 on v8

--- a/solution.py
+++ b/solution.py
@@ -1155,13 +1155,13 @@
             y_last()
             out_rows = give_rows(0, or_s, out_all)
         homes(2 + i)
+    dtok_rows = dtok_rows()
     hops[1, steps[1] - 1].wait_recv()
     hops[0, steps[0] - 1].wait_recv()
     total = term(member) + cr_s[0, steps[0] - 1].astype(F32) + cr_s[1, steps[1] - 1].astype(F32)
     fs_s[...] = total[1].astype(BF16)
     final = peers.send(fs_s, fr_s, (f_ss, f_r), 0, peers.across)
     homes(6)
-    dtok_rows = dtok_rows()
     out_rows = out_rows()
     final.wait_recv()
     total_ref[...] = total[0] + fr_s[...].astype(F32)

time: 409 us -> 409 us (level)
  no operation moved by 1% of the time
where the time goes in v9:
time: 409 us; the launch traced here: 406 us
  Pallas kernels  405 us (99%)
    pallas_call x1, Pallas kernels, front(): pl.pallas_call(functools.partial(front_kernel, imgs), out_shape=(table, t...  255 us
    pallas_call x1, Pallas kernels, back(): pl.pallas_call(functools.partial(back_kernel, imgs), out_shape=(jax.Shape...  134 us

profile of v9, /device:TPU:24, one launch (start us, length us, event | category | flops | bytes accessed | tf_op | source)
XLA Modules:
  0.0 406.0 jit_solution(4860844552021795561)
XLA Ops:
  0.7 7.7 %prepare.1 = (bf16[96,896]{1,0:T(8,128)(2,1)}, bf16[8,2,96,768]{3,2,1,0:T(8,128)(2,1)}, bf16[2,208,768]{2,1,0:T(8,128)(2,1)}, bf16[2,208,768]{2,1,0:T(8,128)(2,1...) custom-call(s32[1]{0:T(128)} %bitcast.tensor_ref, bf16[1576,768]{1,0:T(8,128)(2,1)} %tok_ref.1, bf16[1576,768]{1,0:T(8,128)(2,1)} %cot_ref.1, ...), custom_call_target="tpu_custom_call" | custom-call | flops 100000000 | bytes 15000000 | tf_op jit(solution)/shard_map/prepare/pallas_call | solution.py:1275
  8.3 255.2 %front.1 = (bf16[16,208,768]{2,1,0:T(8,128)(2,1)}, bf16[16,208,768]{2,1,0:T(8,128)(2,1)}, bf16[7,2,208,768]{3,2,1,0:T(8,128)(2,1)}, bf16[8,2,208,768]{3,2,1,0:T(...) custom-call(bf16[96,896]{1,0:T(8,128)(2,1)} %get-tuple-element.42.pa, ...), custom_call_target="tpu_custom_call" | custom-call | flops 99999997952 | bytes 100000000 | tf_op jit(solution)/shard_map/front/pallas_call | solution.py:573
  263.6 134.2 %back.1 = (bf16[4,2,208,768]{3,2,1,0:T(8,128)(2,1)}, bf16[4,2,208,768]{3,2,1,0:T(8,128)(2,1)}, bf16[8,2,96,768]{3,2,1,0:T(8,128)(2,1)}, f32[112,768]{1,0:T(8,128)}) custom-call(bf16[4,8,2,96,768]{4,3,2,1,0:T(8,128)(2,1)} %get-tuple-element.48.g_low, bf16[8,2,208,768]{3,2,1,0:T(8,128)(2,1)} %get-tuple-element.49.y_ref, ...), custom_call_target="tpu_custom_call" | custom-call | flops 12000000000 | bytes 100000000 | tf_op jit(solution)/shard_map/back/pallas_call | solution.py:1188
  397.8 8.1 %finish.1 = (bf16[1576,768]{1,0:T(8,128)(2,1)}, bf16[1576,768]{1,0:T(8,128)(2,1)}, f32[8,96,768]{2,1,0:T(8,128)}, f32[8,96,768]{2,1,0:T(8,128)}, f32[3,96,192]{2...) custom-call(bf16[4,2,208,768]{3,2,1,0:T(8,128)(2,1)} %get-tuple-elem, ...), custom_call_target="tpu_custom_call" | custom-call | flops 1000000 | bytes 18000000 | tf_op jit(solution)/shard_map/finish/pallas_call | solution.py:1324
